TPU v7x, 32 devices: a whole 2x2x4 slice. The times are simulated.
32 devices in a mesh: outer: 8 (over z, x), inner: 4 (over y, core).
Axes of the slice: x: 2, y: 2, z: 4, core: 2. Of those that a mesh axis runs over, the one named last changes fastest.
Arguments:
- tokens: bfloat16 [4096, 1024], P(('outer', 'inner')), may hold values from -6 to 6
- router_weight: bfloat16 [1024, 32], replicated, may hold values from -0.1875 to 0.1875
- in_weight: bfloat16 [32, 1024, 4096], P(('outer', 'inner')), may hold values from -0.1875 to 0.1875
- out_weight: bfloat16 [32, 4096, 1024], P(('outer', 'inner')), may hold values from -0.09375 to 0.09375
- expert_ids: int32 [4096, 2], P(('outer', 'inner')), may hold values from 0 to 31, as said below
- slot_ids: int32 [4096, 2], P(('outer', 'inner')), may hold values from 0 to 12, as said below
- cotangent: bfloat16 [4096, 1024], P(('outer', 'inner')), may hold values from -6 to 6
Outputs:
- mixed: bfloat16 [4096, 1024], P(('outer', 'inner'))
- grad_tokens: bfloat16 [4096, 1024], P(('outer', 'inner'))
- grad_router: float32 [1024, 32], replicated
Inputs may be any that keep to these rules, and one draw needn't show every extreme that they name: `expert_ids`: the two ids of a token differ. slot_ids[t, k] is the number of earlier choices naming the same expert among the rows of the same device, all first choices in token order counted before all second choices, capped at 12; the value 12 marks a dropped choice.
All inputs are finite; a program needn't handle non-finite values.
Results may differ from a plain program's by a relative error of at most 0.017.
Values may be sent and summed in bfloat16 or wider, within the bound.
No kernel may reach another device: no remote copies, remote signals or barrier semaphores. Data moves between devices by JAX's collectives and lax.ppermute only.
A program may use at most 64 MiB of HBM per device.

v0:
```python
import functools

import jax
import jax.numpy as jnp
from jax import lax
from jax.experimental import pallas as pl
from jax.experimental.pallas import tpu as pltpu
from jax.sharding import PartitionSpec as P

AXES = ("outer", "inner")
F32 = jnp.float32
BF16 = jnp.bfloat16
GROUP = 8
VMEM_BYTES = 60 * 1024 * 1024


class Layout:
    def __init__(self, capacity, model_width):
        self.full, left = divmod(capacity, GROUP)
        self.rest = 0
        if left:
            self.rest = 1
            while self.rest < left:
                self.rest *= 2
        if self.rest == GROUP:
            self.full, self.rest = self.full + 1, 0
        self.capacity = capacity
        self.width = model_width
        self.cuts = GROUP // self.rest if self.rest else 1
        self.piece = model_width // self.cuts
        self.base = self.full * model_width
        self.columns = self.base + (self.piece if self.rest else 0)
        self.rows = self.full * GROUP + self.rest


def dot(a, b):
    return jnp.dot(a, b, preferred_element_type=F32)


def dot_nt(a, b):
    return lax.dot_general(a, b, (((1,), (1,)), ((), ())), preferred_element_type=F32)


def iota(shape, dim):
    return lax.broadcasted_iota(jnp.int32, shape, dim)


def as_column(row):
    count = row.shape[1]
    eye = iota((count, count), 0) == iota((count, count), 1)
    return jnp.sum(jnp.where(eye, row, 0.0), axis=1, keepdims=True)


def as_row(column):
    count = column.shape[0]
    eye = iota((count, count), 0) == iota((count, count), 1)
    return jnp.sum(jnp.where(eye, column, 0.0), axis=0, keepdims=True)


def targets(lay, ids, slots):
    found = []
    kept = slots < lay.capacity
    for group in range(lay.full):
        inside = kept & (slots >= group * GROUP) & (slots < (group + 1) * GROUP)
        found.append(jnp.where(inside, ids * GROUP + slots - group * GROUP, -1))
    if lay.rest:
        inside = kept & (slots >= lay.full * GROUP)
        found.append(jnp.where(inside, ids * GROUP + slots - lay.full * GROUP, -1))
    return found


def shifted(row, by):
    return jnp.where(row >= 0, row + by, -1)


def place(lay, row_targets, values, out_ref):
    count = out_ref.shape[0]
    toks = values[0].shape[0]
    row_at = iota((count, toks), 0)
    stacked = jnp.concatenate(values, axis=0) if len(values) > 1 else values[0]

    def onehot(rows):
        hit = functools.reduce(jnp.logical_or, [row_at == row for row in rows])
        return jnp.where(hit, 1.0, 0.0).astype(BF16)

    for group in range(lay.full):
        hot = [onehot([t[group] for t in ranks]) for ranks in row_targets]
        hot = jnp.concatenate(hot, axis=1) if len(hot) > 1 else hot[0]
        out_ref[:, group * lay.width : (group + 1) * lay.width] = dot(hot, stacked).astype(BF16)
    if lay.rest:
        hot, pieces = [], []
        for cut in range(lay.cuts):
            for ranks in row_targets:
                hot.append(onehot([shifted(t[lay.full], cut * lay.rest) for t in ranks]))
            pieces.append(stacked[:, cut * lay.piece : (cut + 1) * lay.piece])
        out_ref[:, lay.base :] = dot(
            jnp.concatenate(hot, axis=1), jnp.concatenate(pieces, axis=0)
        ).astype(BF16)


def pick(lay, ranks, message_ref):
    count = message_ref.shape[0]
    toks = ranks[0][0].shape[0]
    row_at = iota((toks, count), 1)

    def onehot(rows):
        hit = functools.reduce(jnp.logical_or, [row_at == row for row in rows])
        return jnp.where(hit, 1.0, 0.0).astype(BF16)

    whole = [onehot([t[group] for t in ranks]) for group in range(lay.full)]
    pieces = []
    for cut in range(lay.cuts):
        left = cut * lay.piece
        total = None
        for group in range(lay.full):
            start = group * lay.width + left
            term = dot(whole[group], message_ref[:, start : start + lay.piece])
            total = term if total is None else total + term
        if lay.rest:
            hot = onehot([shifted(t[lay.full], cut * lay.rest) for t in ranks])
            term = dot(hot, message_ref[:, lay.base : lay.base + lay.piece])
            total = term if total is None else total + term
        pieces.append(total)
    return jnp.concatenate(pieces, axis=1) if len(pieces) > 1 else pieces[0]


def rest_selection(lay, count):
    small = count // GROUP * lay.rest
    row = iota((small, count), 0)
    col = iota((small, count), 1)
    shift = lay.rest.bit_length() - 1
    home = lax.shift_right_logical(row, shift) * GROUP + (row & (lay.rest - 1))
    return [jnp.where(col == home + cut * lay.rest, 1.0, 0.0).astype(BF16) for cut in range(lay.cuts)]


def unpack(lay, message_ref, out_ref):
    count = message_ref.shape[0]
    for group in range(lay.full):
        out_ref[group * count : (group + 1) * count, :] = message_ref[
            :, group * lay.width : (group + 1) * lay.width
        ]
    if lay.rest:
        tail = message_ref[:, lay.base :]
        for cut, chosen in enumerate(rest_selection(lay, count)):
            out_ref[lay.full * count :, cut * lay.piece : (cut + 1) * lay.piece] = dot(
                chosen, tail
            ).astype(BF16)


def pack(lay, rows_ref, message_ref):
    count = message_ref.shape[0]
    for group in range(lay.full):
        message_ref[:, group * lay.width : (group + 1) * lay.width] = rows_ref[
            group * count : (group + 1) * count, :
        ].astype(BF16)
    if lay.rest:
        total = None
        for cut, chosen in enumerate(rest_selection(lay, count)):
            part = rows_ref[
                lay.full * count :, cut * lay.piece : (cut + 1) * lay.piece
            ].astype(BF16)
            term = lax.dot_general(
                chosen, part, (((0,), (0,)), ((), ())), preferred_element_type=F32
            )
            total = term if total is None else total + term
        message_ref[:, lay.base :] = total.astype(BF16)


def send_tokens_kernel(lay, ids_ref, slots_ref, tokens_ref, out_ref):
    first = targets(lay, ids_ref[0:1, :], slots_ref[0:1, :])
    second = targets(lay, ids_ref[1:2, :], slots_ref[1:2, :])
    place(lay, [[first, second]], [tokens_ref[...]], out_ref)


def send_grads_kernel(
    lay, ids_ref, slots_ref, tokens_ref, router_ref, cot_ref, out_ref, gates_ref
):
    logits = dot_nt(router_ref[...], tokens_ref[...])
    expert_at = iota(logits.shape, 0)
    picked = [
        jnp.sum(jnp.where(expert_at == ids_ref[k : k + 1, :], logits, 0.0), axis=0, keepdims=True)
        for k in range(2)
    ]
    gates = [jax.nn.sigmoid(picked[0] - picked[1]), jax.nn.sigmoid(picked[1] - picked[0])]
    gates_ref[0:1, :] = gates[0]
    gates_ref[1:2, :] = gates[1]
    cot = cot_ref[...].astype(F32)
    scaled = [(as_column(gate) * cot).astype(BF16) for gate in gates]
    ranks = [[targets(lay, ids_ref[k : k + 1, :], slots_ref[k : k + 1, :])] for k in range(2)]
    place(lay, ranks, scaled, out_ref)


def forward_kernel(lay, message_ref, win_ref, wout_ref, out_ref, hidden_ref, rows_ref, total_ref):
    step = pl.program_id(0)

    @pl.when(step == 0)
    def _():
        unpack(lay, message_ref, rows_ref)

    hidden = jnp.maximum(dot(rows_ref[...], win_ref[0]), 0.0).astype(BF16)
    hidden_ref[...] = hidden
    term = dot(hidden, wout_ref[0])

    @pl.when(step == 0)
    def _():
        total_ref[...] = term

    @pl.when(step > 0)
    def _():
        total_ref[...] += term

    @pl.when(step == pl.num_programs(0) - 1)
    def _():
        pack(lay, total_ref, out_ref)


def backward_kernel(lay, message_ref, hidden_ref, win_ref, wout_ref, out_ref, rows_ref, total_ref):
    step = pl.program_id(0)

    @pl.when(step == 0)
    def _():
        unpack(lay, message_ref, rows_ref)

    back = dot_nt(rows_ref[...], wout_ref[0])
    back = jnp.where(hidden_ref[...].astype(F32) > 0.0, back, 0.0).astype(BF16)
    term = dot_nt(back, win_ref[0])

    @pl.when(step == 0)
    def _():
        total_ref[...] = term

    @pl.when(step > 0)
    def _():
        total_ref[...] += term

    @pl.when(step == pl.num_programs(0) - 1)
    def _():
        pack(lay, total_ref, out_ref)


def column_targets(lay, ids_ref, slots_ref):
    ids = [as_column(ids_ref[k : k + 1, :].astype(F32)).astype(jnp.int32) for k in range(2)]
    slots = [as_column(slots_ref[k : k + 1, :].astype(F32)).astype(jnp.int32) for k in range(2)]
    return ids, [targets(lay, ids[k], slots[k]) for k in range(2)]


def split_in_two(x):
    high = x.astype(BF16)
    return high, (x - high.astype(F32)).astype(BF16)


def mix_kernel(
    lay,
    ids_ref,
    slots_ref,
    gates_ref,
    message_ref,
    cot_ref,
    tokens_ref,
    router_ref,
    mixed_ref,
    back_ref,
    partial_ref,
):
    experts = router_ref.shape[0]
    toks = tokens_ref.shape[0]
    ids, ranks = column_targets(lay, ids_ref, slots_ref)
    gates = [as_column(gates_ref[k : k + 1, :]) for k in range(2)]
    cot = cot_ref[...].astype(F32)
    choice = [pick(lay, [ranks[k]], message_ref) for k in range(2)]
    mixed_ref[...] = (gates[0] * choice[0] + gates[1] * choice[1]).astype(BF16)
    actions = [jnp.sum(choice[k] * cot, axis=1, keepdims=True) for k in range(2)]
    slope = gates[0] * gates[1] * (actions[0] - actions[1])

    expert_at = iota((toks, experts), 1)
    signs = jnp.where(expert_at == ids[0], 1.0, 0.0) - jnp.where(expert_at == ids[1], 1.0, 0.0)
    high, low = split_in_two(signs * slope)
    router = router_ref[...]
    back_ref[...] = dot(high, router) + dot(low, router)

    expert_at = iota((experts, toks), 0)
    signs = jnp.where(expert_at == ids_ref[0:1, :], 1.0, 0.0) - jnp.where(
        expert_at == ids_ref[1:2, :], 1.0, 0.0
    )
    high, low = split_in_two(signs * as_row(slope))
    tokens = tokens_ref[...]
    partial_ref[...] = (dot(high, tokens) + dot(low, tokens)) * (1.0 / toks)


def grad_kernel(lay, ids_ref, slots_ref, message_ref, back_ref, out_ref):
    _, ranks = column_targets(lay, ids_ref, slots_ref)
    out_ref[...] = (pick(lay, ranks, message_ref) + back_ref[...]).astype(BF16)


def call(kernel, out_shape, flops, args):
    moved = sum(a.size * a.dtype.itemsize for a in args)
    moved += sum(o.size * o.dtype.itemsize for o in jax.tree.leaves(out_shape))
    return pl.pallas_call(
        kernel,
        out_shape=out_shape,
        compiler_params=pltpu.CompilerParams(vmem_limit_bytes=VMEM_BYTES),
        cost_estimate=pl.CostEstimate(flops=flops, bytes_accessed=moved, transcendentals=0),
    )(*args)


def expert_call(kernel, lay, message, hidden, in_weight, out_weight):
    count = message.shape[0]
    ff = in_weight.shape[2]
    tile = min(512, ff)
    rows = count // GROUP * lay.rows
    whole = pl.BlockSpec(message.shape, lambda j: (0, 0))
    win = pl.BlockSpec((1, lay.width, tile), lambda j: (0, 0, j))
    wout = pl.BlockSpec((1, tile, lay.width), lambda j: (0, j, 0))
    hid = pl.BlockSpec((rows, tile), lambda j: (0, j))
    forward = hidden is None
    operands = (message, in_weight, out_weight) if forward else (message, hidden, in_weight, out_weight)
    message_out = jax.ShapeDtypeStruct(message.shape, BF16)
    return pl.pallas_call(
        functools.partial(kernel, lay),
        grid=(ff // tile,),
        in_specs=[whole, win, wout] if forward else [whole, hid, win, wout],
        out_specs=[whole, hid] if forward else whole,
        out_shape=[message_out, jax.ShapeDtypeStruct((rows, ff), BF16)] if forward else message_out,
        scratch_shapes=[pltpu.VMEM((rows, lay.width), BF16), pltpu.VMEM((rows, lay.width), F32)],
        compiler_params=pltpu.CompilerParams(vmem_limit_bytes=VMEM_BYTES),
        cost_estimate=pl.CostEstimate(
            flops=4 * rows * lay.width * ff,
            bytes_accessed=4 * lay.width * ff + 2 * rows * ff + 4 * message.size,
            transcendentals=0,
        ),
    )(*operands)


def exchange(x):
    return lax.all_to_all(x, AXES, split_axis=0, concat_axis=0, tiled=True)


def from_device(x, bits, devices):
    return lax.ppermute(x, AXES, [(d, d ^ bits) for d in range(devices)])


def sum_over_devices(x, devices):
    half = x.shape[0] // 2
    core = lax.axis_index("inner") % 2
    own = lax.dynamic_slice_in_dim(x, core * half, half, 0)
    other = lax.dynamic_slice_in_dim(x, (1 - core) * half, half, 0)
    own = own + from_device(other, 1, devices)
    bit = 2
    while bit < devices:
        if 2 * bit < devices:
            near = own + from_device(own, bit, devices)
            far = from_device(own, 2 * bit, devices) + from_device(own, 3 * bit, devices)
            own = near + far
        else:
            own = own + from_device(own, bit, devices)
        bit *= 4
    other = from_device(own, 1, devices)
    first = core == 0
    return jnp.concatenate([jnp.where(first, own, other), jnp.where(first, other, own)], axis=0)


def on_device(tokens, router_weight, in_weight, out_weight, expert_ids, slot_ids, cotangent):
    tok_rows, model_width = tokens.shape
    experts = router_weight.shape[1]
    devices = lax.axis_size("outer") * lax.axis_size("inner")
    lay = Layout(3 * tok_rows // experts, model_width)
    message = jax.ShapeDtypeStruct((experts * GROUP, lay.columns), BF16)
    ids, slots, router = expert_ids.T, slot_ids.T, router_weight.T
    place_flops = 4 * experts * GROUP * tok_rows * model_width

    sent_tokens = call(
        functools.partial(send_tokens_kernel, lay), message, place_flops, (ids, slots, tokens)
    )
    sent_grads, gates = call(
        functools.partial(send_grads_kernel, lay),
        [message, jax.ShapeDtypeStruct((2, tok_rows), F32)],
        2 * place_flops,
        (ids, slots, tokens, router, cotangent),
    )
    arrived = exchange(sent_tokens)
    arrived, sent_grads = lax.optimization_barrier((arrived, sent_grads))
    grad_rows = exchange(sent_grads)
    produced, hidden = expert_call(forward_kernel, lay, arrived, None, in_weight, out_weight)
    produced, grad_rows = lax.optimization_barrier((produced, grad_rows))
    produced_back = exchange(produced)
    returned = expert_call(backward_kernel, lay, grad_rows, hidden, in_weight, out_weight)
    returned, produced_back = lax.optimization_barrier((returned, produced_back))
    returned_back = exchange(returned)

    mixed, router_back, partial_grad = call(
        functools.partial(mix_kernel, lay),
        [
            jax.ShapeDtypeStruct((tok_rows, model_width), BF16),
            jax.ShapeDtypeStruct((tok_rows, model_width), F32),
            jax.ShapeDtypeStruct((experts, model_width), F32),
        ],
        2 * place_flops,
        (ids, slots, gates, produced_back, cotangent, tokens, router),
    )
    grad_router = sum_over_devices(partial_grad, devices).T
    grad_tokens = call(
        functools.partial(grad_kernel, lay),
        jax.ShapeDtypeStruct((tok_rows, model_width), BF16),
        place_flops,
        (ids, slots, returned_back, router_back),
    )
    return (mixed, grad_tokens, grad_router)


def solution(mesh):
    placed = (
        P(AXES, None),
        P(),
        P(AXES, None, None),
        P(AXES, None, None),
        P(AXES, None),
        P(AXES, None),
        P(AXES, None),
    )
    return jax.shard_map(
        on_device,
        mesh=mesh,
        in_specs=placed,
        out_specs=(P(AXES, None), P(AXES, None), P()),
        check_vma=False,
    )
```

profile of v0, /device:TPU:0, one launch (start us, length us, event | category | flops | bytes accessed | tf_op | source)
XLA Modules:
  0.0 114.5 jit_solution(15935169966471320645)
XLA Ops:
  0.6 2.2 %shard_map.95 = bf16[256,1536]{1,0:T(8,128)(2,1)} custom-call(s32[2,128]{1,0:T(2,128)} %bitcast.23, s32[2,128]{1,0:T(2,128)} %bitcast.27, bf16[128,1024]{1,0:T(8,128)(2,1)} %tokens_ref.5), custom_call_target="tpu_custom_call" | custom-call | flops 134217728 | bytes 1050624 | tf_op jit(solution)/shard_map/pallas_call | solution.py:298
  2.9 7.3 %all-to-all-start = ((bf16[32,8,1536]{2,1,0:T(8,128)(2,1)}), bf16[32,8,1536]{2,1,0:T(8,128)(2,1)S(1)}, u32[]{:S(2)}, u32[]{:S(2)}) async-start(bf16[32,8,1536]{2,1,0:T(8,128)(2,1)} %bitcast.15), calls=%async_computation | async-start | bytes 1572864 | tf_op jit(solution)/shard_map/all_to_all | solution.py:335
  10.2 2.9 %shard_map.94 = (bf16[256,1536]{1,0:T(8,128)(2,1)}, f32[2,128]{1,0:T(2,128)}) custom-call(s32[2,128]{1,0:T(2,128)} %bitcast.24, s32[2,128]{1,0:T(2,128)} %bitcast.28, bf16[128,1024]{1,0:T(8,128)(2,1)} %tokens_ref.5, bf16[32,1024]{1,0:T(8,128)(2,1)} %bitcast.21, bf16[128,1024]{1,0:T(8,128)(2,1)} %cot_ref.3), custom_call_target="tpu_custom_call" | custom-call | flops 268435456 | bytes 1379328 | tf_op jit(solution)/shard_map/pallas_call | solution.py:298
  13.0 17.7 %all-to-all-done = bf16[32,8,1536]{2,1,0:T(8,128)(2,1)S(1)} async-done(((bf16[32,8,1536]{2,1,0:T(8,128)(2,1)}), bf16[32,8,1536]{2,1,0:T(8,128)(2,1)S(1)}, u32[]{:S(2)}, u32[]{:S(2)}) %all-to-all-start) | async-done | bytes 786464 | tf_op jit(solution)/shard_map/all_to_all | solution.py:335
  30.8 0.0 copy-start.2
  30.8 3.6 %all-to-all-start.1 = ((bf16[32,8,1536]{2,1,0:T(8,128)(2,1)}), bf16[32,8,1536]{2,1,0:T(8,128)(2,1)S(1)}, u32[]{:S(2)}, u32[]{:S(2)}) async-start(bf16[32,8,1536]{2,1,0:T(8,128)(2,1)} %bitcast.19), calls=%async_computation.1 | async-start | bytes 1572864 | tf_op jit(solution)/shard_map/all_to_all | solution.py:335
  34.4 0.0 copy-done.2
  34.4 14.7 %shard_map.96 = (bf16[256,1536]{1,0:T(8,128)(2,1)}, bf16[384,4096]{1,0:T(8,128)(2,1)}) custom-call(bf16[256,1536]{1,0:T(8,128)(2,1)} %bitcast.17, bf16[1,1024,4096]{2,1,0:T(8,128)(2,1)} %win_ref.3, bf16[1,4096,1024]{2,1,0:T(8,128)(2,1)} %wout_ref.3), custom_call_target="tpu_custom_call" | custom-call | flops 6442450944 | bytes 21495808 | tf_op jit(solution)/shard_map/pallas_call | solution.py:318
  49.1 5.9 %all-to-all-done.1 = bf16[32,8,1536]{2,1,0:T(8,128)(2,1)S(1)} async-done(((bf16[32,8,1536]{2,1,0:T(8,128)(2,1)}), bf16[32,8,1536]{2,1,0:T(8,128)(2,1)S(1)}, u32[]{:S(2)}, u32[]{:S(2)}) %all-to-all-start.1) | async-done | bytes 786464 | tf_op jit(solution)/shard_map/all_to_all | solution.py:335
  55.0 0.0 copy-start.3
  55.0 3.6 %all-to-all-start.2 = ((bf16[32,8,1536]{2,1,0:T(8,128)(2,1)}), bf16[32,8,1536]{2,1,0:T(8,128)(2,1)S(1)}, u32[]{:S(2)}, u32[]{:S(2)}) async-start(bf16[32,8,1536]{2,1,0:T(8,128)(2,1)} %bitcast.20), calls=%async_computation.2 | async-start | bytes 1572864 | tf_op jit(solution)/shard_map/all_to_all | solution.py:335
  58.7 0.0 copy-done.3
  58.7 15.1 %shard_map.97 = bf16[256,1536]{1,0:T(8,128)(2,1)} custom-call(bf16[256,1536]{1,0:T(8,128)(2,1)} %bitcast.18, bf16[384,4096]{1,0:T(8,128)(2,1)} %get-tuple-element.22.hidden_ref, bf16[1,1024,4096]{2,1,0:T(8,128)(2,1)} %win_ref.3, bf16[1,4096,1024]{2,1,0:T(8,128)(2,1)} %wout_ref.3), custom_call_target="tpu_custom_call" | custom-call | flops 6442450944 | bytes 21495808 | tf_op jit(solution)/shard_map/pallas_call | solution.py:318
  73.8 5.5 %all-to-all-done.2 = bf16[32,8,1536]{2,1,0:T(8,128)(2,1)S(1)} async-done(((bf16[32,8,1536]{2,1,0:T(8,128)(2,1)}), bf16[32,8,1536]{2,1,0:T(8,128)(2,1)S(1)}, u32[]{:S(2)}, u32[]{:S(2)}) %all-to-all-start.2) | async-done | bytes 786464 | tf_op jit(solution)/shard_map/all_to_all | solution.py:335
  79.3 0.0 copy-start.1
  79.3 3.6 %all-to-all-start.3 = ((bf16[32,8,1536]{2,1,0:T(8,128)(2,1)}), bf16[32,8,1536]{2,1,0:T(8,128)(2,1)S(1)}, u32[]{:S(2)}, u32[]{:S(2)}) async-start(bf16[32,8,1536]{2,1,0:T(8,128)(2,1)} %bitcast.16), calls=%async_computation.3 | async-start | bytes 1572864 | tf_op jit(solution)/shard_map/all_to_all | solution.py:335
  82.9 0.0 copy-done.1
  82.9 3.0 %shard_map.98 = (bf16[128,1024]{1,0:T(8,128)(2,1)}, f32[128,1024]{1,0:T(8,128)}, f32[32,1024]{1,0:T(8,128)}) custom-call(s32[2,128]{1,0:T(2,128)} %bitcast.25, s32[2,128]{1,0:T(2,128)} %bitcast.29, f32[2,128]{1,0:T(2,128)} %get-tuple-element.16.gates_ref, bf16[256,1536]{1,0:T(8,128)(2,1)} %bitcast.14, bf16[128,1024]{1,0:T(8,128)(2,1)} %cot_ref.3, ...), custom_call_target="tpu_custom_call" | custom-call | flops 268435456 | bytes 2296832 | tf_op jit(solution)/shard_map/pallas_call | solution.py:298
  85.9 0.8 constant_dynamic-slice_fusion
  86.8 0.2 collective-permute-start
  87.0 1.0 collective-permute-done
  88.0 0.8 dynamic-slice_add_fusion
  88.9 2.7 %collective-permute-start.3 = (f32[16,1024]{1,0:T(8,128)S(1)}, f32[16,1024]{1,0:T(8,128)S(1)}, u32[]{:S(2)}, u32[]{:S(2)}) collective-permute-start(f32[16,1024]{1,0:T(8,128)S(1)} %dynamic-slice_add_fusion), channel_id=1, source_target_pairs={{0,6},{1,7},{2,4},{3,5},{4,2},{5,3},{6,0},{7,1},{8,14},{9,15},{10,... | collective-permute-start | bytes 196616 | tf_op jit(solution)/shard_map/ppermute | solution.py:339
  91.6 0.6 collective-permute-start.2
  92.2 0.3 collective-permute-start.1
  92.4 3.4 %collective-permute-done.3 = f32[16,1024]{1,0:T(8,128)S(1)} collective-permute-done((f32[16,1024]{1,0:T(8,128)S(1)}, f32[16,1024]{1,0:T(8,128)S(1)}, u32[]{:S(2)}, u32[]{:S(2)}) %collective-permute-start.3) | collective-permute-done | bytes 65568 | tf_op jit(solution)/shard_map/ppermute | solution.py:339
  95.8 1.5 %collective-permute-done.2 = f32[16,1024]{1,0:T(8,128)S(1)} collective-permute-done((f32[16,1024]{1,0:T(8,128)S(1)}, f32[16,1024]{1,0:T(8,128)S(1)}, u32[]{:S(2)}, u32[]{:S(2)}) %collective-permute-start.2) | collective-permute-done | bytes 65568 | tf_op jit(solution)/shard_map/ppermute | solution.py:339
  97.3 0.0 collective-permute-done.1
  97.3 4.2 %collective-permute-start.6 = (f32[16,1024]{1,0:T(8,128)S(1)}, f32[16,1024]{1,0:T(8,128)S(1)}, u32[]{:S(2)}, u32[]{:S(2)}) collective-permute-start(f32[16,1024]{1,0:T(8,128)S(1)} %add_add_fusion.1), channel_id=1, source_target_pairs={{0,24},{1,25},{2,26},{3,27},{4,28},{5,29},{6,30},{7,31},{8,16},{9,... | collective-permute-start | bytes 196616 | tf_op jit(solution)/shard_map/ppermute | solution.py:339
  101.5 0.0 collective-permute-start.5
  101.5 0.6 collective-permute-start.4
  102.1 2.4 %collective-permute-done.6 = f32[16,1024]{1,0:T(8,128)S(1)} collective-permute-done((f32[16,1024]{1,0:T(8,128)S(1)}, f32[16,1024]{1,0:T(8,128)S(1)}, u32[]{:S(2)}, u32[]{:S(2)}) %collective-permute-start.6) | collective-permute-done | bytes 65568 | tf_op jit(solution)/shard_map/ppermute | solution.py:339
  104.5 4.7 %collective-permute-done.5 = f32[16,1024]{1,0:T(8,128)S(1)} collective-permute-done((f32[16,1024]{1,0:T(8,128)S(1)}, f32[16,1024]{1,0:T(8,128)S(1)}, u32[]{:S(2)}, u32[]{:S(2)}) %collective-permute-start.5) | collective-permute-done | bytes 65568 | tf_op jit(solution)/shard_map/ppermute | solution.py:339
  109.1 0.0 collective-permute-done.4
  109.2 0.1 collective-permute-start.7
  109.2 1.2 %collective-permute-done.7 = f32[16,1024]{1,0:T(8,128)S(1)} collective-permute-done((f32[16,1024]{1,0:T(8,128)S(1)}, f32[16,1024]{1,0:T(8,128)S(1)}, u32[]{:S(2)}, u32[]{:S(2)}) %collective-permute-start.7) | collective-permute-done | bytes 65568 | tf_op jit(solution)/shard_map/ppermute | solution.py:339
  110.5 0.7 maximum_bitcast_fusion
  111.2 0.0 all-to-all-done.3
  111.2 0.0 copy-start
  111.2 0.9 copy-done
  112.1 2.4 %shard_map.99 = bf16[128,1024]{1,0:T(8,128)(2,1)} custom-call(s32[2,128]{1,0:T(2,128)} %bitcast.26, s32[2,128]{1,0:T(2,128)} %bitcast.30, bf16[256,1536]{1,0:T(8,128)(2,1)} %bitcast.13, f32[128,1024]{1,0:T(8,128)} %get-tuple-element.27.back_ref), custom_call_target="tpu_custom_call" | custom-call | flops 134217728 | bytes 1574912 | tf_op jit(solution)/shard_map/pallas_call | solution.py:298
  (3 shorter events, 0.0 us)
Async XLA Ops:
  2.9 27.9 %all-to-all-start = ((bf16[32,8,1536]{2,1,0:T(8,128)(2,1)}), bf16[32,8,1536]{2,1,0:T(8,128)(2,1)S(1)}, u32[]{:S(2)}, u32[]{:S(2)}) async-start(bf16[32,8,1536]{2,1,0:T(8,128)(2,1)} %bitcast.15), calls=%async_computation | async-start | bytes 1572864 | tf_op jit(solution)/shard_map/all_to_all | solution.py:335
  30.8 3.6 %copy-start.2 = (bf16[32,8,1536]{2,1,0:T(8,128)(2,1)}, bf16[32,8,1536]{2,1,0:T(8,128)(2,1)S(1)}, u32[]{:S(2)}) copy-start(bf16[32,8,1536]{2,1,0:T(8,128)(2,1)S(1)} %all-to-all-done) | copy-start | bytes 2359300
  30.8 24.2 %all-to-all-start.1 = ((bf16[32,8,1536]{2,1,0:T(8,128)(2,1)}), bf16[32,8,1536]{2,1,0:T(8,128)(2,1)S(1)}, u32[]{:S(2)}, u32[]{:S(2)}) async-start(bf16[32,8,1536]{2,1,0:T(8,128)(2,1)} %bitcast.19), calls=%async_computation.1 | async-start | bytes 1572864 | tf_op jit(solution)/shard_map/all_to_all | solution.py:335
  55.0 3.6 %copy-start.3 = (bf16[32,8,1536]{2,1,0:T(8,128)(2,1)}, bf16[32,8,1536]{2,1,0:T(8,128)(2,1)S(1)}, u32[]{:S(2)}) copy-start(bf16[32,8,1536]{2,1,0:T(8,128)(2,1)S(1)} %all-to-all-done.1) | copy-start | bytes 2359300
  55.0 24.2 %all-to-all-start.2 = ((bf16[32,8,1536]{2,1,0:T(8,128)(2,1)}), bf16[32,8,1536]{2,1,0:T(8,128)(2,1)S(1)}, u32[]{:S(2)}, u32[]{:S(2)}) async-start(bf16[32,8,1536]{2,1,0:T(8,128)(2,1)} %bitcast.20), calls=%async_computation.2 | async-start | bytes 1572864 | tf_op jit(solution)/shard_map/all_to_all | solution.py:335
  79.3 3.6 %copy-start.1 = (bf16[32,8,1536]{2,1,0:T(8,128)(2,1)}, bf16[32,8,1536]{2,1,0:T(8,128)(2,1)S(1)}, u32[]{:S(2)}) copy-start(bf16[32,8,1536]{2,1,0:T(8,128)(2,1)S(1)} %all-to-all-done.2) | copy-start | bytes 2359300
  79.3 31.9 %all-to-all-start.3 = ((bf16[32,8,1536]{2,1,0:T(8,128)(2,1)}), bf16[32,8,1536]{2,1,0:T(8,128)(2,1)S(1)}, u32[]{:S(2)}, u32[]{:S(2)}) async-start(bf16[32,8,1536]{2,1,0:T(8,128)(2,1)} %bitcast.16), calls=%async_computation.3 | async-start | bytes 1572864 | tf_op jit(solution)/shard_map/all_to_all | solution.py:335
  86.8 1.3 %collective-permute-start = (f32[16,1024]{1,0:T(8,128)S(1)}, f32[16,1024]{1,0:T(8,128)S(1)}, u32[]{:S(2)}, u32[]{:S(2)}) collective-permute-start(f32[16,1024]{1,0:T(8,128)S(1)} %constant_dynamic-slice_fusion), channel_id=1, source_target_pairs={{0,1},{1,0},{2,3},{3,2},{4,5},{5,4},{6,7},{7,6},{8,9},{9,8},{10,11... | collective-permute-start | bytes 196616 | tf_op jit(solution)/shard_map/ppermute | solution.py:339
  88.9 6.9 %collective-permute-start.3 = (f32[16,1024]{1,0:T(8,128)S(1)}, f32[16,1024]{1,0:T(8,128)S(1)}, u32[]{:S(2)}, u32[]{:S(2)}) collective-permute-start(f32[16,1024]{1,0:T(8,128)S(1)} %dynamic-slice_add_fusion), channel_id=1, source_target_pairs={{0,6},{1,7},{2,4},{3,5},{4,2},{5,3},{6,0},{7,1},{8,14},{9,15},{10,... | collective-permute-start | bytes 196616 | tf_op jit(solution)/shard_map/ppermute | solution.py:339
  91.6 5.7 %collective-permute-start.2 = (f32[16,1024]{1,0:T(8,128)S(1)}, f32[16,1024]{1,0:T(8,128)S(1)}, u32[]{:S(2)}, u32[]{:S(2)}) collective-permute-start(f32[16,1024]{1,0:T(8,128)S(1)} %dynamic-slice_add_fusion), channel_id=1, source_target_pairs={{0,4},{1,5},{2,6},{3,7},{4,0},{5,1},{6,2},{7,3},{8,12},{9,13},{10,... | collective-permute-start | bytes 196616 | tf_op jit(solution)/shard_map/ppermute | solution.py:339
  92.2 5.1 %collective-permute-start.1 = (f32[16,1024]{1,0:T(8,128)S(1)}, f32[16,1024]{1,0:T(8,128)S(1)}, u32[]{:S(2)}, u32[]{:S(2)}) collective-permute-start(f32[16,1024]{1,0:T(8,128)S(1)} %dynamic-slice_add_fusion), channel_id=1, source_target_pairs={{0,2},{1,3},{2,0},{3,1},{4,6},{5,7},{6,4},{7,5},{8,10},{9,11},{10,... | collective-permute-start | bytes 196616 | tf_op jit(solution)/shard_map/ppermute | solution.py:339
  97.3 7.2 %collective-permute-start.6 = (f32[16,1024]{1,0:T(8,128)S(1)}, f32[16,1024]{1,0:T(8,128)S(1)}, u32[]{:S(2)}, u32[]{:S(2)}) collective-permute-start(f32[16,1024]{1,0:T(8,128)S(1)} %add_add_fusion.1), channel_id=1, source_target_pairs={{0,24},{1,25},{2,26},{3,27},{4,28},{5,29},{6,30},{7,31},{8,16},{9,... | collective-permute-start | bytes 196616 | tf_op jit(solution)/shard_map/ppermute | solution.py:339
  101.5 7.7 %collective-permute-start.5 = (f32[16,1024]{1,0:T(8,128)S(1)}, f32[16,1024]{1,0:T(8,128)S(1)}, u32[]{:S(2)}, u32[]{:S(2)}) collective-permute-start(f32[16,1024]{1,0:T(8,128)S(1)} %add_add_fusion.1), channel_id=1, source_target_pairs={{0,16},{1,17},{2,18},{3,19},{4,20},{5,21},{6,22},{7,23},{8,24},{9,... | collective-permute-start | bytes 196616 | tf_op jit(solution)/shard_map/ppermute | solution.py:339
  101.5 7.6 %collective-permute-start.4 = (f32[16,1024]{1,0:T(8,128)S(1)}, f32[16,1024]{1,0:T(8,128)S(1)}, u32[]{:S(2)}, u32[]{:S(2)}) collective-permute-start(f32[16,1024]{1,0:T(8,128)S(1)} %add_add_fusion.1), channel_id=1, source_target_pairs={{0,8},{1,9},{2,10},{3,11},{4,12},{5,13},{6,14},{7,15},{8,0},{9,1},... | collective-permute-start | bytes 196616 | tf_op jit(solution)/shard_map/ppermute | solution.py:339
  109.2 1.3 %collective-permute-start.7 = (f32[16,1024]{1,0:T(8,128)S(1)}, f32[16,1024]{1,0:T(8,128)S(1)}, u32[]{:S(2)}, u32[]{:S(2)}) collective-permute-start(f32[16,1024]{1,0:T(8,128)S(1)} %add_add_fusion), channel_id=1, source_target_pairs={{0,1},{1,0},{2,3},{3,2},{4,5},{5,4},{6,7},{7,6},{8,9},{9,8},{10,11... | collective-permute-start | bytes 196616 | tf_op jit(solution)/shard_map/ppermute | solution.py:339
  111.2 0.9 copy-start
where the time goes:
time: 116 us; the launch traced here: 114 us
  waiting for transfers between devices  43.3 us (37%)
  Pallas kernels  40.3 us (35%)
  starting transfers between devices  26.8 us (23%)
  local copies, waits for them, and re-layouts  1.74 us (2%)
  other arithmetic  1.56 us (1%)
    pallas_call x2, Pallas kernels, expert_call(): pl.pallas_call(functools.partial(kernel, lay), grid=(ff // tile,), in_spe...  29.8 us
    all_to_all x4, waiting for transfers between devices, exchange(): return lax.all_to_all(x, AXES, split_axis=0, concat_axis=0, tiled=True)  29.2 us
    all_to_all x4, starting transfers between devices, exchange(): return lax.all_to_all(x, AXES, split_axis=0, concat_axis=0, tiled=True)  18.2 us
    ppermute x8, waiting for transfers between devices, from_device(): return lax.ppermute(x, AXES, [(d, d ^ bits) for d in range(devices)])  14.1 us
    pallas_call x4, Pallas kernels, call(): pl.pallas_call(kernel, out_shape=out_shape, compiler_params=pltpu.Compile...  10.5 us
    ppermute x8, starting transfers between devices, from_device(): return lax.ppermute(x, AXES, [(d, d ^ bits) for d in range(devices)])  8.67 us
  transfers between devices with their start and end apart: 12, of which 9 were waited for; matrix products, arithmetic and copies ran while one was open for 2% of the time, Pallas kernels for 31%

commit v1 on v0

--- a/solution.py
+++ b/solution.py
@@ -73,8 +73,41 @@
     return jnp.where(row >= 0, row + by, -1)
 
 
-def place(lay, row_targets, values, out_ref):
-    count = out_ref.shape[0]
+class Order:
+    def __init__(self, high, low, by_high):
+        self.high, self.low, self.by_high = high, low, by_high
+        self.arrays = high if by_high else low
+        self.inside = low if by_high else high
+        self.rows = self.inside * GROUP
+
+    def position(self, block):
+        if self.by_high:
+            return block
+        shift = self.low.bit_length() - 1
+        return (block & (self.low - 1)) * self.high + lax.shift_right_logical(block, shift)
+
+    def block(self, position):
+        if self.by_high:
+            return position
+        part, high = divmod(position, self.high)
+        return high * self.low + part
+
+
+def this_device():
+    return lax.axis_index("outer") * lax.axis_size("inner") + lax.axis_index("inner")
+
+
+def read_all(refs):
+    return jnp.concatenate([ref[...] for ref in refs], axis=0)
+
+
+def write_all(order, refs, start, values):
+    for at, ref in enumerate(refs):
+        ref[:, start : start + values.shape[1]] = values[at * order.rows : (at + 1) * order.rows, :]
+
+
+def place(lay, order, row_targets, values, out_refs):
+    count = order.arrays * order.rows
     toks = values[0].shape[0]
     row_at = iota((count, toks), 0)
     stacked = jnp.concatenate(values, axis=0) if len(values) > 1 else values[0]
@@ -86,20 +119,19 @@
     for group in range(lay.full):
         hot = [onehot([t[group] for t in ranks]) for ranks in row_targets]
         hot = jnp.concatenate(hot, axis=1) if len(hot) > 1 else hot[0]
-        out_ref[:, group * lay.width : (group + 1) * lay.width] = dot(hot, stacked).astype(BF16)
+        write_all(order, out_refs, group * lay.width, dot(hot, stacked).astype(BF16))
     if lay.rest:
         hot, pieces = [], []
         for cut in range(lay.cuts):
             for ranks in row_targets:
                 hot.append(onehot([shifted(t[lay.full], cut * lay.rest) for t in ranks]))
             pieces.append(stacked[:, cut * lay.piece : (cut + 1) * lay.piece])
-        out_ref[:, lay.base :] = dot(
-            jnp.concatenate(hot, axis=1), jnp.concatenate(pieces, axis=0)
-        ).astype(BF16)
-
-
-def pick(lay, ranks, message_ref):
-    count = message_ref.shape[0]
+        placed = dot(jnp.concatenate(hot, axis=1), jnp.concatenate(pieces, axis=0))
+        write_all(order, out_refs, lay.base, placed.astype(BF16))
+
+
+def pick(lay, ranks, message):
+    count = message.shape[0]
     toks = ranks[0][0].shape[0]
     row_at = iota((toks, count), 1)
 
@@ -114,48 +146,58 @@
         total = None
         for group in range(lay.full):
             start = group * lay.width + left
-            term = dot(whole[group], message_ref[:, start : start + lay.piece])
+            term = dot(whole[group], message[:, start : start + lay.piece])
             total = term if total is None else total + term
         if lay.rest:
             hot = onehot([shifted(t[lay.full], cut * lay.rest) for t in ranks])
-            term = dot(hot, message_ref[:, lay.base : lay.base + lay.piece])
+            term = dot(hot, message[:, lay.base : lay.base + lay.piece])
             total = term if total is None else total + term
         pieces.append(total)
     return jnp.concatenate(pieces, axis=1) if len(pieces) > 1 else pieces[0]
 
 
-def rest_selection(lay, count):
+def rest_selection(lay, order):
+    count = order.arrays * order.rows
     small = count // GROUP * lay.rest
     row = iota((small, count), 0)
     col = iota((small, count), 1)
     shift = lay.rest.bit_length() - 1
-    home = lax.shift_right_logical(row, shift) * GROUP + (row & (lay.rest - 1))
+    home = order.position(lax.shift_right_logical(row, shift)) * GROUP + (row & (lay.rest - 1))
     return [jnp.where(col == home + cut * lay.rest, 1.0, 0.0).astype(BF16) for cut in range(lay.cuts)]
 
 
-def unpack(lay, message_ref, out_ref):
-    count = message_ref.shape[0]
+def unpack(lay, order, message_refs, out_ref):
+    count = order.arrays * order.rows
+    message = read_all(message_refs)
     for group in range(lay.full):
-        out_ref[group * count : (group + 1) * count, :] = message_ref[
-            :, group * lay.width : (group + 1) * lay.width
-        ]
+        part = message[:, group * lay.width : (group + 1) * lay.width]
+        if not order.by_high:
+            part = part.astype(F32)
+            blocks = [
+                part[at * GROUP : (at + 1) * GROUP, :]
+                for at in sorted(range(count // GROUP), key=order.block)
+            ]
+            part = jnp.concatenate(blocks, axis=0).astype(BF16)
+        out_ref[group * count : (group + 1) * count, :] = part
     if lay.rest:
-        tail = message_ref[:, lay.base :]
-        for cut, chosen in enumerate(rest_selection(lay, count)):
+        tail = message[:, lay.base :]
+        for cut, chosen in enumerate(rest_selection(lay, order)):
             out_ref[lay.full * count :, cut * lay.piece : (cut + 1) * lay.piece] = dot(
                 chosen, tail
             ).astype(BF16)
 
 
-def pack(lay, rows_ref, message_ref):
-    count = message_ref.shape[0]
+def pack(lay, order, rows_ref, message_refs):
+    count = order.arrays * order.rows
     for group in range(lay.full):
-        message_ref[:, group * lay.width : (group + 1) * lay.width] = rows_ref[
-            group * count : (group + 1) * count, :
-        ].astype(BF16)
+        part = rows_ref[group * count : (group + 1) * count, :]
+        if not order.by_high:
+            blocks = [order.block(at) * GROUP for at in range(count // GROUP)]
+            part = jnp.concatenate([part[at : at + GROUP, :] for at in blocks], axis=0)
+        write_all(order, message_refs, group * lay.width, part.astype(BF16))
     if lay.rest:
         total = None
-        for cut, chosen in enumerate(rest_selection(lay, count)):
+        for cut, chosen in enumerate(rest_selection(lay, order)):
             part = rows_ref[
                 lay.full * count :, cut * lay.piece : (cut + 1) * lay.piece
             ].astype(BF16)
@@ -163,17 +205,28 @@
                 chosen, part, (((0,), (0,)), ((), ())), preferred_element_type=F32
             )
             total = term if total is None else total + term
-        message_ref[:, lay.base :] = total.astype(BF16)
-
-
-def send_tokens_kernel(lay, ids_ref, slots_ref, tokens_ref, out_ref):
-    first = targets(lay, ids_ref[0:1, :], slots_ref[0:1, :])
-    second = targets(lay, ids_ref[1:2, :], slots_ref[1:2, :])
-    place(lay, [[first, second]], [tokens_ref[...]], out_ref)
+        write_all(order, message_refs, lay.base, total.astype(BF16))
+
+
+def repack_kernel(order, *refs):
+    sources, outs = refs[: order.arrays], refs[order.arrays :]
+    for part, out_ref in enumerate(outs):
+        blocks = [ref[part * GROUP : (part + 1) * GROUP, :] for ref in sources]
+        out_ref[...] = jnp.concatenate(blocks, axis=0)
+
+
+def blocks_of(order, ids):
+    return order.position(ids ^ this_device())
+
+
+def send_tokens_kernel(lay, order, ids_ref, slots_ref, tokens_ref, *out_refs):
+    blocks = blocks_of(order, ids_ref[...])
+    ranks = [targets(lay, blocks[k : k + 1, :], slots_ref[k : k + 1, :]) for k in range(2)]
+    place(lay, order, [ranks], [tokens_ref[...]], out_refs)
 
 
 def send_grads_kernel(
-    lay, ids_ref, slots_ref, tokens_ref, router_ref, cot_ref, out_ref, gates_ref
+    lay, order, ids_ref, slots_ref, tokens_ref, router_ref, cot_ref, gates_ref, *out_refs
 ):
     logits = dot_nt(router_ref[...], tokens_ref[...])
     expert_at = iota(logits.shape, 0)
@@ -186,16 +239,20 @@
     gates_ref[1:2, :] = gates[1]
     cot = cot_ref[...].astype(F32)
     scaled = [(as_column(gate) * cot).astype(BF16) for gate in gates]
-    ranks = [[targets(lay, ids_ref[k : k + 1, :], slots_ref[k : k + 1, :])] for k in range(2)]
-    place(lay, ranks, scaled, out_ref)
-
-
-def forward_kernel(lay, message_ref, win_ref, wout_ref, out_ref, hidden_ref, rows_ref, total_ref):
+    blocks = blocks_of(order, ids_ref[...])
+    ranks = [[targets(lay, blocks[k : k + 1, :], slots_ref[k : k + 1, :])] for k in range(2)]
+    place(lay, order, ranks, scaled, out_refs)
+
+
+def forward_kernel(lay, order, out_order, *refs):
+    message_refs = refs[: order.arrays]
+    win_ref, wout_ref, hidden_ref = refs[order.arrays : order.arrays + 3]
+    out_refs, (rows_ref, total_ref) = refs[order.arrays + 3 : -2], refs[-2:]
     step = pl.program_id(0)
 
     @pl.when(step == 0)
     def _():
-        unpack(lay, message_ref, rows_ref)
+        unpack(lay, order, message_refs, rows_ref)
 
     hidden = jnp.maximum(dot(rows_ref[...], win_ref[0]), 0.0).astype(BF16)
     hidden_ref[...] = hidden
@@ -211,15 +268,18 @@
 
     @pl.when(step == pl.num_programs(0) - 1)
     def _():
-        pack(lay, total_ref, out_ref)
-
-
-def backward_kernel(lay, message_ref, hidden_ref, win_ref, wout_ref, out_ref, rows_ref, total_ref):
+        pack(lay, out_order, total_ref, out_refs)
+
+
+def backward_kernel(lay, order, out_order, *refs):
+    message_refs = refs[: order.arrays]
+    win_ref, wout_ref, hidden_ref = refs[order.arrays : order.arrays + 3]
+    out_refs, (rows_ref, total_ref) = refs[order.arrays + 3 : -2], refs[-2:]
     step = pl.program_id(0)
 
     @pl.when(step == 0)
     def _():
-        unpack(lay, message_ref, rows_ref)
+        unpack(lay, order, message_refs, rows_ref)
 
     back = dot_nt(rows_ref[...], wout_ref[0])
     back = jnp.where(hidden_ref[...].astype(F32) > 0.0, back, 0.0).astype(BF16)
@@ -235,13 +295,13 @@
 
     @pl.when(step == pl.num_programs(0) - 1)
     def _():
-        pack(lay, total_ref, out_ref)
-
-
-def column_targets(lay, ids_ref, slots_ref):
+        pack(lay, out_order, total_ref, out_refs)
+
+
+def column_targets(lay, order, ids_ref, slots_ref):
     ids = [as_column(ids_ref[k : k + 1, :].astype(F32)).astype(jnp.int32) for k in range(2)]
     slots = [as_column(slots_ref[k : k + 1, :].astype(F32)).astype(jnp.int32) for k in range(2)]
-    return ids, [targets(lay, ids[k], slots[k]) for k in range(2)]
+    return ids, [targets(lay, blocks_of(order, ids[k]), slots[k]) for k in range(2)]
 
 
 def split_in_two(x):
@@ -249,25 +309,15 @@
     return high, (x - high.astype(F32)).astype(BF16)
 
 
-def mix_kernel(
-    lay,
-    ids_ref,
-    slots_ref,
-    gates_ref,
-    message_ref,
-    cot_ref,
-    tokens_ref,
-    router_ref,
-    mixed_ref,
-    back_ref,
-    partial_ref,
-):
+def mix_kernel(lay, order, ids_ref, slots_ref, gates_ref, cot_ref, tokens_ref, router_ref, *refs):
+    message_refs, (mixed_ref, back_ref, partial_ref) = refs[: order.arrays], refs[order.arrays :]
     experts = router_ref.shape[0]
     toks = tokens_ref.shape[0]
-    ids, ranks = column_targets(lay, ids_ref, slots_ref)
+    ids, ranks = column_targets(lay, order, ids_ref, slots_ref)
     gates = [as_column(gates_ref[k : k + 1, :]) for k in range(2)]
     cot = cot_ref[...].astype(F32)
-    choice = [pick(lay, [ranks[k]], message_ref) for k in range(2)]
+    message = read_all(message_refs)
+    choice = [pick(lay, [ranks[k]], message) for k in range(2)]
     mixed_ref[...] = (gates[0] * choice[0] + gates[1] * choice[1]).astype(BF16)
     actions = [jnp.sum(choice[k] * cot, axis=1, keepdims=True) for k in range(2)]
     slope = gates[0] * gates[1] * (actions[0] - actions[1])
@@ -287,9 +337,11 @@
     partial_ref[...] = (dot(high, tokens) + dot(low, tokens)) * (1.0 / toks)
 
 
-def grad_kernel(lay, ids_ref, slots_ref, message_ref, back_ref, out_ref):
-    _, ranks = column_targets(lay, ids_ref, slots_ref)
-    out_ref[...] = (pick(lay, ranks, message_ref) + back_ref[...]).astype(BF16)
+def grad_kernel(lay, order, ids_ref, slots_ref, back_ref, *refs):
+    message_refs, out_ref = refs[: order.arrays], refs[order.arrays]
+    _, ranks = column_targets(lay, order, ids_ref, slots_ref)
+    message = read_all(message_refs)
+    out_ref[...] = (pick(lay, ranks, message) + back_ref[...]).astype(BF16)
 
 
 def call(kernel, out_shape, flops, args):
@@ -303,36 +355,57 @@
     )(*args)
 
 
-def expert_call(kernel, lay, message, hidden, in_weight, out_weight):
-    count = message.shape[0]
+def messages_of(lay, order):
+    return [jax.ShapeDtypeStruct((order.rows, lay.columns), BF16)] * order.arrays
+
+
+def expert_call(kernel, lay, order, out_order, message, hidden, in_weight, out_weight):
     ff = in_weight.shape[2]
     tile = min(512, ff)
-    rows = count // GROUP * lay.rows
-    whole = pl.BlockSpec(message.shape, lambda j: (0, 0))
+    rows = order.arrays * order.inside * lay.rows
     win = pl.BlockSpec((1, lay.width, tile), lambda j: (0, 0, j))
     wout = pl.BlockSpec((1, tile, lay.width), lambda j: (0, j, 0))
     hid = pl.BlockSpec((rows, tile), lambda j: (0, j))
+
+    def whole(of):
+        return [pl.BlockSpec((of.rows, lay.columns), lambda j: (0, 0))] * of.arrays
+
     forward = hidden is None
-    operands = (message, in_weight, out_weight) if forward else (message, hidden, in_weight, out_weight)
-    message_out = jax.ShapeDtypeStruct(message.shape, BF16)
+    hidden_shape = [jax.ShapeDtypeStruct((rows, ff), BF16)]
     return pl.pallas_call(
-        functools.partial(kernel, lay),
+        functools.partial(kernel, lay, order, out_order),
         grid=(ff // tile,),
-        in_specs=[whole, win, wout] if forward else [whole, hid, win, wout],
-        out_specs=[whole, hid] if forward else whole,
-        out_shape=[message_out, jax.ShapeDtypeStruct((rows, ff), BF16)] if forward else message_out,
+        in_specs=whole(order) + [win, wout] + ([] if forward else [hid]),
+        out_specs=([hid] if forward else []) + whole(out_order),
+        out_shape=(hidden_shape if forward else []) + messages_of(lay, out_order),
         scratch_shapes=[pltpu.VMEM((rows, lay.width), BF16), pltpu.VMEM((rows, lay.width), F32)],
         compiler_params=pltpu.CompilerParams(vmem_limit_bytes=VMEM_BYTES),
         cost_estimate=pl.CostEstimate(
             flops=4 * rows * lay.width * ff,
-            bytes_accessed=4 * lay.width * ff + 2 * rows * ff + 4 * message.size,
+            bytes_accessed=4 * lay.width * ff + 2 * rows * ff + 4 * rows * lay.width,
             transcendentals=0,
         ),
-    )(*operands)
-
-
-def exchange(x):
-    return lax.all_to_all(x, AXES, split_axis=0, concat_axis=0, tiled=True)
+    )(*message, in_weight, out_weight, *([] if forward else [hidden]))
+
+
+def repack(lay, order, message):
+    other = Order(order.high, order.low, not order.by_high)
+    return call(
+        functools.partial(repack_kernel, order), messages_of(lay, other), 0, tuple(message)
+    )
+
+
+def step_of(order, message):
+    devices = order.high * order.low
+    unit = order.low if order.by_high else 1
+    return [message[0]] + [
+        from_device(message[part], part * unit, devices) for part in range(1, order.arrays)
+    ]
+
+
+def tied(first, second):
+    out = lax.optimization_barrier(tuple(first) + tuple(second))
+    return list(out[: len(first)]), list(out[len(first) :])
 
 
 def from_device(x, bits, devices):
@@ -364,45 +437,59 @@
     experts = router_weight.shape[1]
     devices = lax.axis_size("outer") * lax.axis_size("inner")
     lay = Layout(3 * tok_rows // experts, model_width)
-    message = jax.ShapeDtypeStruct((experts * GROUP, lay.columns), BF16)
+    high = 4 if devices >= 16 else 1
+    by_high, by_low = (Order(high, devices // high, flag) for flag in (True, False))
     ids, slots, router = expert_ids.T, slot_ids.T, router_weight.T
     place_flops = 4 * experts * GROUP * tok_rows * model_width
 
     sent_tokens = call(
-        functools.partial(send_tokens_kernel, lay), message, place_flops, (ids, slots, tokens)
-    )
-    sent_grads, gates = call(
-        functools.partial(send_grads_kernel, lay),
-        [message, jax.ShapeDtypeStruct((2, tok_rows), F32)],
+        functools.partial(send_tokens_kernel, lay, by_high),
+        messages_of(lay, by_high),
+        place_flops,
+        (ids, slots, tokens),
+    )
+    token_half = step_of(by_high, sent_tokens)
+
+    gates, *sent_grads = call(
+        functools.partial(send_grads_kernel, lay, by_low),
+        [jax.ShapeDtypeStruct((2, tok_rows), F32)] + messages_of(lay, by_low),
         2 * place_flops,
         (ids, slots, tokens, router, cotangent),
     )
-    arrived = exchange(sent_tokens)
-    arrived, sent_grads = lax.optimization_barrier((arrived, sent_grads))
-    grad_rows = exchange(sent_grads)
-    produced, hidden = expert_call(forward_kernel, lay, arrived, None, in_weight, out_weight)
-    produced, grad_rows = lax.optimization_barrier((produced, grad_rows))
-    produced_back = exchange(produced)
-    returned = expert_call(backward_kernel, lay, grad_rows, hidden, in_weight, out_weight)
-    returned, produced_back = lax.optimization_barrier((returned, produced_back))
-    returned_back = exchange(returned)
+    grad_half = repack(lay, by_low, step_of(by_low, sent_grads))
+    token_half, grad_half = tied(token_half, grad_half)
+    grad_rows = step_of(by_high, grad_half)
+    arrived = step_of(by_low, repack(lay, by_high, token_half))
+
+    hidden, *produced = expert_call(
+        forward_kernel, lay, by_low, by_high, arrived, None, in_weight, out_weight
+    )
+    produced, grad_rows = tied(produced, grad_rows)
+    produced_half = step_of(by_high, produced)
+    returned = expert_call(
+        backward_kernel, lay, by_high, by_low, grad_rows, hidden, in_weight, out_weight
+    )
+    returned_half = repack(lay, by_low, step_of(by_low, returned))
+    produced_half, returned_half = tied(produced_half, returned_half)
+    returned_back = step_of(by_high, returned_half)
+    produced_back = step_of(by_low, repack(lay, by_high, produced_half))
 
     mixed, router_back, partial_grad = call(
-        functools.partial(mix_kernel, lay),
+        functools.partial(mix_kernel, lay, by_low),
         [
             jax.ShapeDtypeStruct((tok_rows, model_width), BF16),
             jax.ShapeDtypeStruct((tok_rows, model_width), F32),
             jax.ShapeDtypeStruct((experts, model_width), F32),
         ],
         2 * place_flops,
-        (ids, slots, gates, produced_back, cotangent, tokens, router),
+        (ids, slots, gates, cotangent, tokens, router, *produced_back),
     )
     grad_router = sum_over_devices(partial_grad, devices).T
     grad_tokens = call(
-        functools.partial(grad_kernel, lay),
+        functools.partial(grad_kernel, lay, by_high),
         jax.ShapeDtypeStruct((tok_rows, model_width), BF16),
         place_flops,
-        (ids, slots, returned_back, router_back),
+        (ids, slots, router_back, *returned_back),
     )
     return (mixed, grad_tokens, grad_router)
 

time: 116 us -> 163 us (1.41)
  starting transfers between devices: 26.8 us -> 59.5 us
  Pallas kernels: 40.3 us -> 48.7 us
  local copies, waits for them, and re-layouts: 1.74 us -> 6.36 us
  waiting for transfers between devices: 43.3 us -> 45.4 us
    ppermute x8 -> x48, starting transfers between devices: 8.67 us -> 59.5 us  [from_device(): return lax.ppermute(x, AXES, [(d, d ^ bits) for d in range(devices)])]
    ppermute x8 -> x48, waiting for transfers between devices: 14.1 us -> 45.4 us  [from_device(): return lax.ppermute(x, AXES, [(d, d ^ bits) for d in range(devices)])]
    all_to_all x4 -> x0, waiting for transfers between devices: 29.2 us -> none  [exchange(): return lax.all_to_all(x, AXES, split_axis=0, concat_axis=0, tiled=True)]
    all_to_all x4 -> x0, starting transfers between devices: 18.2 us -> none  [exchange(): return lax.all_to_all(x, AXES, split_axis=0, concat_axis=0, tiled=True)]
    pallas_call x4 -> x8, Pallas kernels: 10.5 us -> 19 us  [call(): pl.pallas_call(kernel, out_shape=out_shape, compiler_params=pltpu.Compile...]
    unnamed x8 -> x86, local copies, waits for them, and re-layouts: 0.9 us -> 5.52 us
  transfers between devices with their start and end apart: 12 -> 48, of which waited for: 9 -> 21; matrix products, arithmetic and copies ran while one was open for 2% -> 0% of each run, Pallas kernels for 31% -> 15%
where the time goes in v1:
time: 163 us; the launch traced here: 162 us
  starting transfers between devices  59.5 us (37%)
  Pallas kernels  48.7 us (30%)
  waiting for transfers between devices  45.4 us (28%)
  local copies, waits for them, and re-layouts  6.36 us (4%)
    ppermute x48, starting transfers between devices, from_device(): return lax.ppermute(x, AXES, [(d, d ^ bits) for d in range(devices)])  59.5 us
    ppermute x48, waiting for transfers between devices, from_device(): return lax.ppermute(x, AXES, [(d, d ^ bits) for d in range(devices)])  45.4 us
    pallas_call x2, Pallas kernels, expert_call(): pl.pallas_call(functools.partial(kernel, lay, order, out_order), grid=(ff...  29.8 us
    pallas_call x8, Pallas kernels, call(): pl.pallas_call(kernel, out_shape=out_shape, compiler_params=pltpu.Compile...  19 us
    unnamed x86, local copies, waits for them, and re-layouts  5.52 us
  transfers between devices with their start and end apart: 48, of which 21 were waited for; matrix products, arithmetic and copies ran while one was open for 0% of the time, Pallas kernels for 15%

profile of v1, /device:TPU:0, one launch (start us, length us, event | category | flops | bytes accessed | tf_op | source)
XLA Modules:
  0.0 162.5 jit_solution(5428210759862806276)
XLA Ops:
  0.6 2.8 %shard_map.94 = (f32[2,128]{1,0:T(2,128)}, bf16[32,1536]{1,0:T(8,128)(2,1)}, bf16[32,1536]{1,0:T(8,128)(2,1)}, bf16[32,1536]{1,0:T(8,128)(2,1)}, bf16[32,1536]{1...) custom-call(s32[2,128]{1,0:T(2,128)} %bitcast.7, ...), custom_call_target="tpu_custom_call" | custom-call | flops 268435456 | bytes 1379328 | tf_op jit(solution)/shard_map/pallas_call | solution.py:350
  3.9 2.5 %collective-permute-start.4 = (bf16[32,1536]{1,0:T(8,128)(2,1)}, bf16[32,1536]{1,0:T(8,128)(2,1)S(1)}, u32[]{:S(2)}, u32[]{:S(2)}) collective-permute-start(bf16[32,1536]{1,0:T(8,128)(2,1)} %get-tuple-element.87), channel_id=1, source_target_pairs={{0,2},{1,3},{2,0},{3,1},{4,6},{5,7},{6,4},{7,5},{8,10},{9,11},{10,... | collective-permute-start | bytes 294920 | tf_op jit(solution)/shard_map/ppermute | solution.py:412
  6.6 1.7 %collective-permute-start.6 = (bf16[32,1536]{1,0:T(8,128)(2,1)}, bf16[32,1536]{1,0:T(8,128)(2,1)S(1)}, u32[]{:S(2)}, u32[]{:S(2)}) collective-permute-start(bf16[32,1536]{1,0:T(8,128)(2,1)} %get-tuple-element.89), channel_id=1, source_target_pairs={{0,4},{1,5},{2,6},{3,7},{4,0},{5,1},{6,2},{7,3},{8,12},{9,13},{10,... | collective-permute-start | bytes 294920 | tf_op jit(solution)/shard_map/ppermute | solution.py:412
  8.2 2.2 %shard_map.95 = (bf16[64,1536]{1,0:T(8,128)(2,1)}, bf16[64,1536]{1,0:T(8,128)(2,1)}, bf16[64,1536]{1,0:T(8,128)(2,1)}, bf16[64,1536]{1,0:T(8,128)(2,1)}) custom-call(s32[2,128]{1,0:T(2,128)} %bitcast.8, s32[2,128]{1,0:T(2,128)} %bitcast.12, bf16[128,1024]{1,0:T(8,128)(2,1)} %tokens_ref.5), custom_call_target="tpu_custom_call" | custom-call | flops 134217728 | bytes 1050624 | tf_op jit(solution)/shard_map/pallas_call | solution.py:350
  10.4 1.8 %collective-permute-start = (bf16[64,1536]{1,0:T(8,128)(2,1)}, bf16[64,1536]{1,0:T(8,128)(2,1)S(1)}, u32[]{:S(2)}, u32[]{:S(2)}) collective-permute-start(bf16[64,1536]{1,0:T(8,128)(2,1)} %get-tuple-element.82), channel_id=1, source_target_pairs={{0,8},{1,9},{2,10},{3,11},{4,12},{5,13},{6,14},{7,15},{8,0},{9,1},... | collective-permute-start | bytes 589832 | tf_op jit(solution)/shard_map/ppermute | solution.py:412
  12.2 2.6 %collective-permute-start.1 = (bf16[64,1536]{1,0:T(8,128)(2,1)}, bf16[64,1536]{1,0:T(8,128)(2,1)S(1)}, u32[]{:S(2)}, u32[]{:S(2)}) collective-permute-start(bf16[64,1536]{1,0:T(8,128)(2,1)} %get-tuple-element.83), channel_id=1, source_target_pairs={{0,16},{1,17},{2,18},{3,19},{4,20},{5,21},{6,22},{7,23},{8,24},{9,... | collective-permute-start | bytes 589832 | tf_op jit(solution)/shard_map/ppermute | solution.py:412
  14.8 0.8 collective-permute-start.2
  15.6 2.4 %collective-permute-start.8 = (bf16[32,1536]{1,0:T(8,128)(2,1)}, bf16[32,1536]{1,0:T(8,128)(2,1)S(1)}, u32[]{:S(2)}, u32[]{:S(2)}) collective-permute-start(bf16[32,1536]{1,0:T(8,128)(2,1)} %get-tuple-element.91), channel_id=1, source_target_pairs={{0,6},{1,7},{2,4},{3,5},{4,2},{5,3},{6,0},{7,1},{8,14},{9,15},{10,... | collective-permute-start | bytes 294920 | tf_op jit(solution)/shard_map/ppermute | solution.py:412
  18.1 3.6 %collective-permute-done.8.refs_6_ = bf16[32,1536]{1,0:T(8,128)(2,1)S(1)} collective-permute-done((bf16[32,1536]{1,0:T(8,128)(2,1)}, bf16[32,1536]{1,0:T(8,128)(2,1)S(1)}, u32[]{:S(2)}, u32[]{:S(2)}) %collective-permute-start.8) | collective-permute-done | bytes 98336 | tf_op jit(solution)/shard_map/ppermute | solution.py:412
  21.7 2.4 %collective-permute-done.9.refs_7_ = bf16[32,1536]{1,0:T(8,128)(2,1)S(1)} collective-permute-done((bf16[32,1536]{1,0:T(8,128)(2,1)}, bf16[32,1536]{1,0:T(8,128)(2,1)S(1)}, u32[]{:S(2)}, u32[]{:S(2)}) %collective-permute-start.9) | collective-permute-done | bytes 98336 | tf_op jit(solution)/shard_map/ppermute | solution.py:412
  24.7 2.1 %shard_map.96 = (bf16[64,1536]{1,0:T(8,128)(2,1)}, bf16[64,1536]{1,0:T(8,128)(2,1)}, bf16[64,1536]{1,0:T(8,128)(2,1)}, bf16[64,1536]{1,0:T(8,128)(2,1)}) custom-call(bf16[32,1536]{1,0:T(8,128)(2,1)} %get-tuple-element.85.refs_0_, bf16[32,1536]{1,0:T(8,128)(2,1)} %copy-done.15, bf16[32,1536]{1,0:T(8,128)(2,1)} %copy-done.17, bf16[32,1536]{1,0:T(8,128)(2,1)} %copy-done.19, ...), custom_call_target="tpu_custom_call" | custom-call | bytes 1572864 | tf_op jit(solution)/shard_map/pallas_call | solution.py:350
  26.9 2.6 %collective-permute-done.1.refs_2_ = bf16[64,1536]{1,0:T(8,128)(2,1)S(1)} collective-permute-done((bf16[64,1536]{1,0:T(8,128)(2,1)}, bf16[64,1536]{1,0:T(8,128)(2,1)S(1)}, u32[]{:S(2)}, u32[]{:S(2)}) %collective-permute-start.1) | collective-permute-done | bytes 196640 | tf_op jit(solution)/shard_map/ppermute | solution.py:412
  29.5 0.7 copy-done.5
  30.3 2.1 %shard_map.97 = (bf16[32,1536]{1,0:T(8,128)(2,1)}, bf16[32,1536]{1,0:T(8,128)(2,1)}, bf16[32,1536]{1,0:T(8,128)(2,1)}, bf16[32,1536]{1,0:T(8,128)(2,1)}, bf16[32...) custom-call(bf16[64,1536]{1,0:T(8,128)(2,1)} %get-tuple-element.97.refs_0_, ...), custom_call_target="tpu_custom_call" | custom-call | bytes 1572864 | tf_op jit(solution)/shard_map/pallas_call | solution.py:350
  32.4 1.6 collective-permute-start.11
  34.2 1.5 collective-permute-start.13
  35.9 2.4 %collective-permute-start.15 = (bf16[32,1536]{1,0:T(8,128)(2,1)}, bf16[32,1536]{1,0:T(8,128)(2,1)S(1)}, u32[]{:S(2)}, u32[]{:S(2)}) collective-permute-start(bf16[32,1536]{1,0:T(8,128)(2,1)} %get-tuple-element.107), channel_id=1, source_target_pairs={{0,6},{1,7},{2,4},{3,5},{4,2},{5,3},{6,0},{7,1},{8,14},{9,15},{10,... | collective-permute-start | bytes 294920 | tf_op jit(solution)/shard_map/ppermute | solution.py:412
  38.4 1.2 collective-permute-start.16
  39.5 4.0 %collective-permute-start.17 = (bf16[64,1536]{1,0:T(8,128)(2,1)}, bf16[64,1536]{1,0:T(8,128)(2,1)S(1)}, u32[]{:S(2)}, u32[]{:S(2)}) collective-permute-start(bf16[64,1536]{1,0:T(8,128)(2,1)} %get-tuple-element.114), channel_id=1, source_target_pairs={{0,8},{1,9},{2,10},{3,11},{4,12},{5,13},{6,14},{7,15},{8,0},{9,1},... | collective-permute-start | bytes 589832 | tf_op jit(solution)/shard_map/ppermute | solution.py:412
  43.5 1.5 collective-permute-start.18
  45.1 1.3 collective-permute-start.19
  47.1 14.7 %shard_map.98 = (bf16[384,4096]{1,0:T(8,128)(2,1)}, bf16[64,1536]{1,0:T(8,128)(2,1)}, bf16[64,1536]{1,0:T(8,128)(2,1)}, bf16[64,1536]{1,0:T(8,128)(2,1)}, bf16[64,1536]{1,0:T(8,128)(2,1)}) custom-call(bf16[32,1536]{1,0:T(8,128)(2,1)} %get-tuple-element.101.refs_0_, bf16[32,1536]{1,0:T(8,128)(2,1)} %copy-done.36, bf16[32,1536]{1,0:T(8,128)(2,1)} %copy-done.37, ...), custom_call_target="tpu_custom_call" | custom-call | flops 6442450944 | bytes 21495808 | tf_op jit(solution)/shard_map/pallas_call | solution.py:375
  62.6 15.1 %shard_map.99 = (bf16[32,1536]{1,0:T(8,128)(2,1)}, bf16[32,1536]{1,0:T(8,128)(2,1)}, bf16[32,1536]{1,0:T(8,128)(2,1)}, bf16[32,1536]{1,0:T(8,128)(2,1)}, bf16[32...) custom-call(bf16[64,1536]{1,0:T(8,128)(2,1)} %get-tuple-element.121.refs_0_, ...), custom_call_target="tpu_custom_call" | custom-call | flops 6442450944 | bytes 21495808 | tf_op jit(solution)/shard_map/pallas_call | solution.py:375
  78.1 1.2 collective-permute-start.24
  79.5 1.5 collective-permute-start.26
  81.6 3.8 %collective-permute-start.20 = (bf16[64,1536]{1,0:T(8,128)(2,1)S(1)}, bf16[64,1536]{1,0:T(8,128)(2,1)S(1)}, u32[]{:S(2)}, u32[]{:S(2)}) collective-permute-start(bf16[64,1536]{1,0:T(8,128)(2,1)S(1)} %copy-done.32), channel_id=1, source_target_pairs={{0,8},{1,9},{2,10},{3,11},{4,12},{5,13},{6,14},{7,15},{8,0},{9,1},... | collective-permute-start | bytes 589832 | tf_op jit(solution)/shard_map/ppermute | solution.py:412
  85.3 3.3 %collective-permute-start.21 = (bf16[64,1536]{1,0:T(8,128)(2,1)S(1)}, bf16[64,1536]{1,0:T(8,128)(2,1)S(1)}, u32[]{:S(2)}, u32[]{:S(2)}) collective-permute-start(bf16[64,1536]{1,0:T(8,128)(2,1)S(1)} %copy-done.31), channel_id=1, source_target_pairs={{0,16},{1,17},{2,18},{3,19},{4,20},{5,21},{6,22},{7,23},{8,24},{9,... | collective-permute-start | bytes 589832 | tf_op jit(solution)/shard_map/ppermute | solution.py:412
  88.7 1.4 collective-permute-start.22
  90.1 1.4 collective-permute-start.28
  91.5 4.5 %collective-permute-done.28.refs_6_ = bf16[32,1536]{1,0:T(8,128)(2,1)S(1)} collective-permute-done((bf16[32,1536]{1,0:T(8,128)(2,1)}, bf16[32,1536]{1,0:T(8,128)(2,1)S(1)}, u32[]{:S(2)}, u32[]{:S(2)}) %collective-permute-start.28) | collective-permute-done | bytes 98336 | tf_op jit(solution)/shard_map/ppermute | solution.py:412
  96.0 1.6 %collective-permute-done.29.refs_7_ = bf16[32,1536]{1,0:T(8,128)(2,1)S(1)} collective-permute-done((bf16[32,1536]{1,0:T(8,128)(2,1)}, bf16[32,1536]{1,0:T(8,128)(2,1)S(1)}, u32[]{:S(2)}, u32[]{:S(2)}) %collective-permute-start.29) | collective-permute-done | bytes 98336 | tf_op jit(solution)/shard_map/ppermute | solution.py:412
  98.3 2.1 %shard_map.100 = (bf16[64,1536]{1,0:T(8,128)(2,1)}, bf16[64,1536]{1,0:T(8,128)(2,1)}, bf16[64,1536]{1,0:T(8,128)(2,1)}, bf16[64,1536]{1,0:T(8,128)(2,1)}) custom-call(bf16[32,1536]{1,0:T(8,128)(2,1)} %get-tuple-element.126.refs_0_, bf16[32,1536]{1,0:T(8,128)(2,1)} %copy-done.18, bf16[32,1536]{1,0:T(8,128)(2,1)} %copy-done.20, bf16[32,1536]{1,0:T(8,128)(2,1)} %copy-done.22, ...), custom_call_target="tpu_custom_call" | custom-call | bytes 1572864 | tf_op jit(solution)/shard_map/pallas_call | solution.py:350
  100.5 2.4 %collective-permute-done.21.refs_2_ = bf16[64,1536]{1,0:T(8,128)(2,1)S(1)} collective-permute-done((bf16[64,1536]{1,0:T(8,128)(2,1)S(1)}, bf16[64,1536]{1,0:T(8,128)(2,1)S(1)}, u32[]{:S(2)}, u32[]{:S(2)}) %collective-permute-start.21) | collective-permute-done | bytes 196640 | tf_op jit(solution)/shard_map/ppermute | solution.py:412
  102.9 0.7 copy-done.6
  103.6 2.1 %shard_map.101 = (bf16[32,1536]{1,0:T(8,128)(2,1)}, bf16[32,1536]{1,0:T(8,128)(2,1)}, bf16[32,1536]{1,0:T(8,128)(2,1)}, bf16[32,1536]{1,0:T(8,128)(2,1)}, bf16[3...) custom-call(bf16[64,1536]{1,0:T(8,128)(2,1)} %get-tuple-element.138.refs_0_,, ...), custom_call_target="tpu_custom_call" | custom-call | bytes 1572864 | tf_op jit(solution)/shard_map/pallas_call | solution.py:350
  106.2 1.4 collective-permute-start.32
  107.6 1.5 collective-permute-start.33
  109.3 1.3 collective-permute-start.35
  110.6 1.0 collective-permute-done.31.refs_2_
  112.0 0.8 collective-permute-done.32.refs_3_
  113.4 1.3 collective-permute-done.34.refs_5_
  114.6 2.9 %collective-permute-done.35.refs_6_ = bf16[32,1536]{1,0:T(8,128)(2,1)S(1)} collective-permute-done((bf16[32,1536]{1,0:T(8,128)(2,1)}, bf16[32,1536]{1,0:T(8,128)(2,1)S(1)}, u32[]{:S(2)}, u32[]{:S(2)}) %collective-permute-start.35) | collective-permute-done | bytes 98336 | tf_op jit(solution)/shard_map/ppermute | solution.py:412
  117.5 0.9 collective-permute-done.36.refs_7_
  119.1 3.1 %shard_map.102 = (bf16[128,1024]{1,0:T(8,128)(2,1)}, f32[128,1024]{1,0:T(8,128)}, f32[32,1024]{1,0:T(8,128)}) custom-call(s32[2,128]{1,0:T(2,128)} %bitcast.9, s32[2,128]{1,0:T(2,128)} %bitcast.13, f32[2,128]{1,0:T(2,128)} %get-tuple-element.80.gates_ref, bf16[128,1024]{1,0:T(8,128)(2,1)} %cot_ref.3, bf16[128,1024]{1,0:T(8,128)(2,1)} %tokens_ref.5, ...), custom_call_target="tpu_custom_call" | custom-call | flops 268435456 | bytes 2296832 | tf_op jit(solution)/shard_map/pallas_call | solution.py:350
  122.1 0.8 constant_dynamic-slice_fusion
  123.4 0.9 collective-permute-done.40
  124.3 0.8 dynamic-slice_add_fusion
  125.1 1.5 collective-permute-start.42
  126.7 1.6 collective-permute-start.43
  128.7 0.9 collective-permute-done.42
  129.5 2.5 %collective-permute-done.43 = f32[16,1024]{1,0:T(8,128)S(1)} collective-permute-done((f32[16,1024]{1,0:T(8,128)S(1)}, f32[16,1024]{1,0:T(8,128)S(1)}, u32[]{:S(2)}, u32[]{:S(2)}) %collective-permute-start.43) | collective-permute-done | bytes 65568 | tf_op jit(solution)/shard_map/ppermute | solution.py:412
  132.1 1.1 collective-permute-done.41
  133.2 4.6 %collective-permute-start.45 = (f32[16,1024]{1,0:T(8,128)S(1)}, f32[16,1024]{1,0:T(8,128)S(1)}, u32[]{:S(2)}, u32[]{:S(2)}) collective-permute-start(f32[16,1024]{1,0:T(8,128)S(1)} %add_add_fusion.1), channel_id=1, source_target_pairs={{0,16},{1,17},{2,18},{3,19},{4,20},{5,21},{6,22},{7,23},{8,24},{9,... | collective-permute-start | bytes 196616 | tf_op jit(solution)/shard_map/ppermute | solution.py:412
  137.8 1.4 collective-permute-start.46
  139.2 2.0 %collective-permute-start.37 = (bf16[64,1536]{1,0:T(8,128)(2,1)}, bf16[64,1536]{1,0:T(8,128)(2,1)S(1)}, u32[]{:S(2)}, u32[]{:S(2)}) collective-permute-start(bf16[64,1536]{1,0:T(8,128)(2,1)} %get-tuple-element.153), channel_id=1, source_target_pairs={{0,8},{1,9},{2,10},{3,11},{4,12},{5,13},{6,14},{7,15},{8,0},{9,1},... | collective-permute-start | bytes 589832 | tf_op jit(solution)/shard_map/ppermute | solution.py:412
  141.2 1.0 collective-permute-start.38
  142.8 0.9 collective-permute-start.39
  143.7 0.7 collective-permute-done.46
  144.4 3.7 %collective-permute-done.44 = f32[16,1024]{1,0:T(8,128)S(1)} collective-permute-done((f32[16,1024]{1,0:T(8,128)S(1)}, f32[16,1024]{1,0:T(8,128)S(1)}, u32[]{:S(2)}, u32[]{:S(2)}) %collective-permute-start.44) | collective-permute-done | bytes 65568 | tf_op jit(solution)/shard_map/ppermute | solution.py:412
  148.1 4.0 %collective-permute-done.37.refs_1_ = bf16[64,1536]{1,0:T(8,128)(2,1)S(1)} collective-permute-done((bf16[64,1536]{1,0:T(8,128)(2,1)}, bf16[64,1536]{1,0:T(8,128)(2,1)S(1)}, u32[]{:S(2)}, u32[]{:S(2)}) %collective-permute-start.37) | collective-permute-done | bytes 196640 | tf_op jit(solution)/shard_map/ppermute | solution.py:412
  152.2 6.4 %collective-permute-done.38.refs_2_ = bf16[64,1536]{1,0:T(8,128)(2,1)S(1)} collective-permute-done((bf16[64,1536]{1,0:T(8,128)(2,1)}, bf16[64,1536]{1,0:T(8,128)(2,1)S(1)}, u32[]{:S(2)}, u32[]{:S(2)}) %collective-permute-start.38) | collective-permute-done | bytes 196640 | tf_op jit(solution)/shard_map/ppermute | solution.py:412
  158.6 0.7 copy-done.1
  159.3 2.5 %shard_map.103 = bf16[128,1024]{1,0:T(8,128)(2,1)} custom-call(s32[2,128]{1,0:T(2,128)} %bitcast.10, s32[2,128]{1,0:T(2,128)} %bitcast.14, f32[128,1024]{1,0:T(8,128)} %get-tuple-element.151.back_ref, bf16[64,1536]{1,0:T(8,128)(2,1)} %get-tuple-element.152.refs_0_, bf16[64,1536]{1,0:T(8,128)(2,1)} %copy-done, bf16[64,1536]{1,0:T(8,128)(2,1)} %copy-done.1, ...), custom_call_target="tpu_custom_call" | custom-call | flops 134217728 | bytes 1574912 | tf_op jit(solution)/shard_map/pallas_call | solution.py:350
  161.8 0.7 maximum_bitcast_fusion
  (134 shorter events, 9.1 us)
Async XLA Ops:
  3.4 7.0 %collective-permute-start.3 = (bf16[32,1536]{1,0:T(8,128)(2,1)}, bf16[32,1536]{1,0:T(8,128)(2,1)S(1)}, u32[]{:S(2)}, u32[]{:S(2)}) collective-permute-start(bf16[32,1536]{1,0:T(8,128)(2,1)} %get-tuple-element.86), channel_id=1, source_target_pairs={{0,1},{1,0},{2,3},{3,2},{4,5},{5,4},{6,7},{7,6},{8,9},{9,8},{10,11... | collective-permute-start | bytes 294920 | tf_op jit(solution)/shard_map/ppermute | solution.py:412
  3.9 8.3 %collective-permute-start.4 = (bf16[32,1536]{1,0:T(8,128)(2,1)}, bf16[32,1536]{1,0:T(8,128)(2,1)S(1)}, u32[]{:S(2)}, u32[]{:S(2)}) collective-permute-start(bf16[32,1536]{1,0:T(8,128)(2,1)} %get-tuple-element.87), channel_id=1, source_target_pairs={{0,2},{1,3},{2,0},{3,1},{4,6},{5,7},{6,4},{7,5},{8,10},{9,11},{10,... | collective-permute-start | bytes 294920 | tf_op jit(solution)/shard_map/ppermute | solution.py:412
  6.4 8.4 %collective-permute-start.5 = (bf16[32,1536]{1,0:T(8,128)(2,1)}, bf16[32,1536]{1,0:T(8,128)(2,1)S(1)}, u32[]{:S(2)}, u32[]{:S(2)}) collective-permute-start(bf16[32,1536]{1,0:T(8,128)(2,1)} %get-tuple-element.88), channel_id=1, source_target_pairs={{0,3},{1,2},{2,1},{3,0},{4,7},{5,6},{6,5},{7,4},{8,11},{9,10},{10,... | collective-permute-start | bytes 294920 | tf_op jit(solution)/shard_map/ppermute | solution.py:412
  6.6 9.0 %collective-permute-start.6 = (bf16[32,1536]{1,0:T(8,128)(2,1)}, bf16[32,1536]{1,0:T(8,128)(2,1)S(1)}, u32[]{:S(2)}, u32[]{:S(2)}) collective-permute-start(bf16[32,1536]{1,0:T(8,128)(2,1)} %get-tuple-element.89), channel_id=1, source_target_pairs={{0,4},{1,5},{2,6},{3,7},{4,0},{5,1},{6,2},{7,3},{8,12},{9,13},{10,... | collective-permute-start | bytes 294920 | tf_op jit(solution)/shard_map/ppermute | solution.py:412
  8.2 9.8 %collective-permute-start.7 = (bf16[32,1536]{1,0:T(8,128)(2,1)}, bf16[32,1536]{1,0:T(8,128)(2,1)S(1)}, u32[]{:S(2)}, u32[]{:S(2)}) collective-permute-start(bf16[32,1536]{1,0:T(8,128)(2,1)} %get-tuple-element.90), channel_id=1, source_target_pairs={{0,5},{1,4},{2,7},{3,6},{4,1},{5,0},{6,3},{7,2},{8,13},{9,12},{10,... | collective-permute-start | bytes 294920 | tf_op jit(solution)/shard_map/ppermute | solution.py:412
  10.4 13.7 %copy-start.15 = (bf16[32,1536]{1,0:T(8,128)(2,1)}, bf16[32,1536]{1,0:T(8,128)(2,1)S(1)}, u32[]{:S(2)}) copy-start(bf16[32,1536]{1,0:T(8,128)(2,1)S(1)} %collective-permute-done.3.refs_1_) | copy-start | bytes 294916
  10.4 16.5 %collective-permute-start = (bf16[64,1536]{1,0:T(8,128)(2,1)}, bf16[64,1536]{1,0:T(8,128)(2,1)S(1)}, u32[]{:S(2)}, u32[]{:S(2)}) collective-permute-start(bf16[64,1536]{1,0:T(8,128)(2,1)} %get-tuple-element.82), channel_id=1, source_target_pairs={{0,8},{1,9},{2,10},{3,11},{4,12},{5,13},{6,14},{7,15},{8,0},{9,1},... | collective-permute-start | bytes 589832 | tf_op jit(solution)/shard_map/ppermute | solution.py:412
  12.2 11.9 %copy-start.17 = (bf16[32,1536]{1,0:T(8,128)(2,1)}, bf16[32,1536]{1,0:T(8,128)(2,1)S(1)}, u32[]{:S(2)}) copy-start(bf16[32,1536]{1,0:T(8,128)(2,1)S(1)} %collective-permute-done.4.refs_2_) | copy-start | bytes 294916
  12.2 17.3 %collective-permute-start.1 = (bf16[64,1536]{1,0:T(8,128)(2,1)}, bf16[64,1536]{1,0:T(8,128)(2,1)S(1)}, u32[]{:S(2)}, u32[]{:S(2)}) collective-permute-start(bf16[64,1536]{1,0:T(8,128)(2,1)} %get-tuple-element.83), channel_id=1, source_target_pairs={{0,16},{1,17},{2,18},{3,19},{4,20},{5,21},{6,22},{7,23},{8,24},{9,... | collective-permute-start | bytes 589832 | tf_op jit(solution)/shard_map/ppermute | solution.py:412
  14.8 9.3 %copy-start.19 = (bf16[32,1536]{1,0:T(8,128)(2,1)}, bf16[32,1536]{1,0:T(8,128)(2,1)S(1)}, u32[]{:S(2)}) copy-start(bf16[32,1536]{1,0:T(8,128)(2,1)S(1)} %collective-permute-done.5.refs_3_) | copy-start | bytes 294916
  14.8 14.7 %collective-permute-start.2 = (bf16[64,1536]{1,0:T(8,128)(2,1)}, bf16[64,1536]{1,0:T(8,128)(2,1)S(1)}, u32[]{:S(2)}, u32[]{:S(2)}) collective-permute-start(bf16[64,1536]{1,0:T(8,128)(2,1)} %get-tuple-element.84), channel_id=1, source_target_pairs={{0,24},{1,25},{2,26},{3,27},{4,28},{5,29},{6,30},{7,31},{8,16},{9,... | collective-permute-start | bytes 589832 | tf_op jit(solution)/shard_map/ppermute | solution.py:412
  15.6 8.5 %copy-start.21 = (bf16[32,1536]{1,0:T(8,128)(2,1)}, bf16[32,1536]{1,0:T(8,128)(2,1)S(1)}, u32[]{:S(2)}) copy-start(bf16[32,1536]{1,0:T(8,128)(2,1)S(1)} %collective-permute-done.6.refs_4_) | copy-start | bytes 294916
  15.6 6.1 %collective-permute-start.8 = (bf16[32,1536]{1,0:T(8,128)(2,1)}, bf16[32,1536]{1,0:T(8,128)(2,1)S(1)}, u32[]{:S(2)}, u32[]{:S(2)}) collective-permute-start(bf16[32,1536]{1,0:T(8,128)(2,1)} %get-tuple-element.91), channel_id=1, source_target_pairs={{0,6},{1,7},{2,4},{3,5},{4,2},{5,3},{6,0},{7,1},{8,14},{9,15},{10,... | collective-permute-start | bytes 294920 | tf_op jit(solution)/shard_map/ppermute | solution.py:412
  18.0 6.0 %collective-permute-start.9 = (bf16[32,1536]{1,0:T(8,128)(2,1)}, bf16[32,1536]{1,0:T(8,128)(2,1)S(1)}, u32[]{:S(2)}, u32[]{:S(2)}) collective-permute-start(bf16[32,1536]{1,0:T(8,128)(2,1)} %get-tuple-element.92), channel_id=1, source_target_pairs={{0,7},{1,6},{2,5},{3,4},{4,3},{5,2},{6,1},{7,0},{8,15},{9,14},{10,... | collective-permute-start | bytes 294920 | tf_op jit(solution)/shard_map/ppermute | solution.py:412
  32.4 3.5 %collective-permute-start.10 = (bf16[32,1536]{1,0:T(8,128)(2,1)}, bf16[32,1536]{1,0:T(8,128)(2,1)S(1)}, u32[]{:S(2)}, u32[]{:S(2)}) collective-permute-start(bf16[32,1536]{1,0:T(8,128)(2,1)} %get-tuple-element.102), channel_id=1, source_target_pairs={{0,1},{1,0},{2,3},{3,2},{4,5},{5,4},{6,7},{7,6},{8,9},{9,8},{10,11... | collective-permute-start | bytes 294920 | tf_op jit(solution)/shard_map/ppermute | solution.py:412
  32.4 6.0 %collective-permute-start.11 = (bf16[32,1536]{1,0:T(8,128)(2,1)}, bf16[32,1536]{1,0:T(8,128)(2,1)S(1)}, u32[]{:S(2)}, u32[]{:S(2)}) collective-permute-start(bf16[32,1536]{1,0:T(8,128)(2,1)} %get-tuple-element.103), channel_id=1, source_target_pairs={{0,2},{1,3},{2,0},{3,1},{4,6},{5,7},{6,4},{7,5},{8,10},{9,11},{10,... | collective-permute-start | bytes 294920 | tf_op jit(solution)/shard_map/ppermute | solution.py:412
  33.9 5.6 %collective-permute-start.12 = (bf16[32,1536]{1,0:T(8,128)(2,1)}, bf16[32,1536]{1,0:T(8,128)(2,1)S(1)}, u32[]{:S(2)}, u32[]{:S(2)}) collective-permute-start(bf16[32,1536]{1,0:T(8,128)(2,1)} %get-tuple-element.104), channel_id=1, source_target_pairs={{0,3},{1,2},{2,1},{3,0},{4,7},{5,6},{6,5},{7,4},{8,11},{9,10},{10,... | collective-permute-start | bytes 294920 | tf_op jit(solution)/shard_map/ppermute | solution.py:412
  34.2 9.3 %collective-permute-start.13 = (bf16[32,1536]{1,0:T(8,128)(2,1)}, bf16[32,1536]{1,0:T(8,128)(2,1)S(1)}, u32[]{:S(2)}, u32[]{:S(2)}) collective-permute-start(bf16[32,1536]{1,0:T(8,128)(2,1)} %get-tuple-element.105), channel_id=1, source_target_pairs={{0,4},{1,5},{2,6},{3,7},{4,0},{5,1},{6,2},{7,3},{8,12},{9,13},{10,... | collective-permute-start | bytes 294920 | tf_op jit(solution)/shard_map/ppermute | solution.py:412
  35.7 9.3 %collective-permute-start.14 = (bf16[32,1536]{1,0:T(8,128)(2,1)}, bf16[32,1536]{1,0:T(8,128)(2,1)S(1)}, u32[]{:S(2)}, u32[]{:S(2)}) collective-permute-start(bf16[32,1536]{1,0:T(8,128)(2,1)} %get-tuple-element.106), channel_id=1, source_target_pairs={{0,5},{1,4},{2,7},{3,6},{4,1},{5,0},{6,3},{7,2},{8,13},{9,12},{10,... | collective-permute-start | bytes 294920 | tf_op jit(solution)/shard_map/ppermute | solution.py:412
  35.9 10.5 %copy-start.36 = (bf16[32,1536]{1,0:T(8,128)(2,1)}, bf16[32,1536]{1,0:T(8,128)(2,1)S(1)}, u32[]{:S(2)}) copy-start(bf16[32,1536]{1,0:T(8,128)(2,1)S(1)} %collective-permute-done.10.refs_1_) | copy-start | bytes 294916
  35.9 10.5 %collective-permute-start.15 = (bf16[32,1536]{1,0:T(8,128)(2,1)}, bf16[32,1536]{1,0:T(8,128)(2,1)S(1)}, u32[]{:S(2)}, u32[]{:S(2)}) collective-permute-start(bf16[32,1536]{1,0:T(8,128)(2,1)} %get-tuple-element.107), channel_id=1, source_target_pairs={{0,6},{1,7},{2,4},{3,5},{4,2},{5,3},{6,0},{7,1},{8,14},{9,15},{10,... | collective-permute-start | bytes 294920 | tf_op jit(solution)/shard_map/ppermute | solution.py:412
  38.4 8.1 %copy-start.37 = (bf16[32,1536]{1,0:T(8,128)(2,1)}, bf16[32,1536]{1,0:T(8,128)(2,1)S(1)}, u32[]{:S(2)}) copy-start(bf16[32,1536]{1,0:T(8,128)(2,1)S(1)} %collective-permute-done.11.refs_2_) | copy-start | bytes 294916
  38.4 8.0 %collective-permute-start.16 = (bf16[32,1536]{1,0:T(8,128)(2,1)}, bf16[32,1536]{1,0:T(8,128)(2,1)S(1)}, u32[]{:S(2)}, u32[]{:S(2)}) collective-permute-start(bf16[32,1536]{1,0:T(8,128)(2,1)} %get-tuple-element.108), channel_id=1, source_target_pairs={{0,7},{1,6},{2,5},{3,4},{4,3},{5,2},{6,1},{7,0},{8,15},{9,14},{10,... | collective-permute-start | bytes 294920 | tf_op jit(solution)/shard_map/ppermute | solution.py:412
  39.5 6.9 %copy-start.38 = (bf16[32,1536]{1,0:T(8,128)(2,1)}, bf16[32,1536]{1,0:T(8,128)(2,1)S(1)}, u32[]{:S(2)}) copy-start(bf16[32,1536]{1,0:T(8,128)(2,1)S(1)} %collective-permute-done.12.refs_3_) | copy-start | bytes 294916
  39.5 22.2 %collective-permute-start.17 = (bf16[64,1536]{1,0:T(8,128)(2,1)}, bf16[64,1536]{1,0:T(8,128)(2,1)S(1)}, u32[]{:S(2)}, u32[]{:S(2)}) collective-permute-start(bf16[64,1536]{1,0:T(8,128)(2,1)} %get-tuple-element.114), channel_id=1, source_target_pairs={{0,8},{1,9},{2,10},{3,11},{4,12},{5,13},{6,14},{7,15},{8,0},{9,1},... | collective-permute-start | bytes 589832 | tf_op jit(solution)/shard_map/ppermute | solution.py:412
  43.5 18.2 %collective-permute-start.18 = (bf16[64,1536]{1,0:T(8,128)(2,1)}, bf16[64,1536]{1,0:T(8,128)(2,1)S(1)}, u32[]{:S(2)}, u32[]{:S(2)}) collective-permute-start(bf16[64,1536]{1,0:T(8,128)(2,1)} %get-tuple-element.115), channel_id=1, source_target_pairs={{0,16},{1,17},{2,18},{3,19},{4,20},{5,21},{6,22},{7,23},{8,24},{9,... | collective-permute-start | bytes 589832 | tf_op jit(solution)/shard_map/ppermute | solution.py:412
  45.1 16.7 %collective-permute-start.19 = (bf16[64,1536]{1,0:T(8,128)(2,1)}, bf16[64,1536]{1,0:T(8,128)(2,1)S(1)}, u32[]{:S(2)}, u32[]{:S(2)}) collective-permute-start(bf16[64,1536]{1,0:T(8,128)(2,1)} %get-tuple-element.116), channel_id=1, source_target_pairs={{0,24},{1,25},{2,26},{3,27},{4,28},{5,29},{6,30},{7,31},{8,16},{9,... | collective-permute-start | bytes 589832 | tf_op jit(solution)/shard_map/ppermute | solution.py:412
  62.6 19.0 %copy-start.32 = (bf16[64,1536]{1,0:T(8,128)(2,1)S(1)}, bf16[64,1536]{1,0:T(8,128)(2,1)}, u32[]{:S(2)}) copy-start(bf16[64,1536]{1,0:T(8,128)(2,1)} %get-tuple-element.118) | copy-start | bytes 589828
  62.6 22.8 %copy-start.31 = (bf16[64,1536]{1,0:T(8,128)(2,1)S(1)}, bf16[64,1536]{1,0:T(8,128)(2,1)}, u32[]{:S(2)}) copy-start(bf16[64,1536]{1,0:T(8,128)(2,1)} %get-tuple-element.119) | copy-start | bytes 589828
  62.6 26.1 %copy-start.30 = (bf16[64,1536]{1,0:T(8,128)(2,1)S(1)}, bf16[64,1536]{1,0:T(8,128)(2,1)}, u32[]{:S(2)}) copy-start(bf16[64,1536]{1,0:T(8,128)(2,1)} %get-tuple-element.120) | copy-start | bytes 589828
  77.7 3.9 %collective-permute-start.23 = (bf16[32,1536]{1,0:T(8,128)(2,1)}, bf16[32,1536]{1,0:T(8,128)(2,1)S(1)}, u32[]{:S(2)}, u32[]{:S(2)}) collective-permute-start(bf16[32,1536]{1,0:T(8,128)(2,1)} %get-tuple-element.127), channel_id=1, source_target_pairs={{0,1},{1,0},{2,3},{3,2},{4,5},{5,4},{6,7},{7,6},{8,9},{9,8},{10,11... | collective-permute-start | bytes 294920 | tf_op jit(solution)/shard_map/ppermute | solution.py:412
  78.1 7.3 %collective-permute-start.24 = (bf16[32,1536]{1,0:T(8,128)(2,1)}, bf16[32,1536]{1,0:T(8,128)(2,1)S(1)}, u32[]{:S(2)}, u32[]{:S(2)}) collective-permute-start(bf16[32,1536]{1,0:T(8,128)(2,1)} %get-tuple-element.128), channel_id=1, source_target_pairs={{0,2},{1,3},{2,0},{3,1},{4,6},{5,7},{6,4},{7,5},{8,10},{9,11},{10,... | collective-permute-start | bytes 294920 | tf_op jit(solution)/shard_map/ppermute | solution.py:412
  79.2 9.4 %collective-permute-start.25 = (bf16[32,1536]{1,0:T(8,128)(2,1)}, bf16[32,1536]{1,0:T(8,128)(2,1)S(1)}, u32[]{:S(2)}, u32[]{:S(2)}) collective-permute-start(bf16[32,1536]{1,0:T(8,128)(2,1)} %get-tuple-element.129), channel_id=1, source_target_pairs={{0,3},{1,2},{2,1},{3,0},{4,7},{5,6},{6,5},{7,4},{8,11},{9,10},{10,... | collective-permute-start | bytes 294920 | tf_op jit(solution)/shard_map/ppermute | solution.py:412
  79.5 10.5 %collective-permute-start.26 = (bf16[32,1536]{1,0:T(8,128)(2,1)}, bf16[32,1536]{1,0:T(8,128)(2,1)S(1)}, u32[]{:S(2)}, u32[]{:S(2)}) collective-permute-start(bf16[32,1536]{1,0:T(8,128)(2,1)} %get-tuple-element.130), channel_id=1, source_target_pairs={{0,4},{1,5},{2,6},{3,7},{4,0},{5,1},{6,2},{7,3},{8,12},{9,13},{10,... | collective-permute-start | bytes 294920 | tf_op jit(solution)/shard_map/ppermute | solution.py:412
  81.1 10.4 %collective-permute-start.27 = (bf16[32,1536]{1,0:T(8,128)(2,1)}, bf16[32,1536]{1,0:T(8,128)(2,1)S(1)}, u32[]{:S(2)}, u32[]{:S(2)}) collective-permute-start(bf16[32,1536]{1,0:T(8,128)(2,1)} %get-tuple-element.131), channel_id=1, source_target_pairs={{0,5},{1,4},{2,7},{3,6},{4,1},{5,0},{6,3},{7,2},{8,13},{9,12},{10,... | collective-permute-start | bytes 294920 | tf_op jit(solution)/shard_map/ppermute | solution.py:412
  81.6 16.1 %copy-start.18 = (bf16[32,1536]{1,0:T(8,128)(2,1)}, bf16[32,1536]{1,0:T(8,128)(2,1)S(1)}, u32[]{:S(2)}) copy-start(bf16[32,1536]{1,0:T(8,128)(2,1)S(1)} %collective-permute-done.23.refs_1_) | copy-start | bytes 294916
  81.6 18.9 %collective-permute-start.20 = (bf16[64,1536]{1,0:T(8,128)(2,1)S(1)}, bf16[64,1536]{1,0:T(8,128)(2,1)S(1)}, u32[]{:S(2)}, u32[]{:S(2)}) collective-permute-start(bf16[64,1536]{1,0:T(8,128)(2,1)S(1)} %copy-done.32), channel_id=1, source_target_pairs={{0,8},{1,9},{2,10},{3,11},{4,12},{5,13},{6,14},{7,15},{8,0},{9,1},... | collective-permute-start | bytes 589832 | tf_op jit(solution)/shard_map/ppermute | solution.py:412
  85.3 12.3 %copy-start.20 = (bf16[32,1536]{1,0:T(8,128)(2,1)}, bf16[32,1536]{1,0:T(8,128)(2,1)S(1)}, u32[]{:S(2)}) copy-start(bf16[32,1536]{1,0:T(8,128)(2,1)S(1)} %collective-permute-done.24.refs_2_) | copy-start | bytes 294916
  85.3 17.5 %collective-permute-start.21 = (bf16[64,1536]{1,0:T(8,128)(2,1)S(1)}, bf16[64,1536]{1,0:T(8,128)(2,1)S(1)}, u32[]{:S(2)}, u32[]{:S(2)}) collective-permute-start(bf16[64,1536]{1,0:T(8,128)(2,1)S(1)} %copy-done.31), channel_id=1, source_target_pairs={{0,16},{1,17},{2,18},{3,19},{4,20},{5,21},{6,22},{7,23},{8,24},{9,... | collective-permute-start | bytes 589832 | tf_op jit(solution)/shard_map/ppermute | solution.py:412
  88.7 9.0 %copy-start.22 = (bf16[32,1536]{1,0:T(8,128)(2,1)}, bf16[32,1536]{1,0:T(8,128)(2,1)S(1)}, u32[]{:S(2)}) copy-start(bf16[32,1536]{1,0:T(8,128)(2,1)S(1)} %collective-permute-done.25.refs_3_) | copy-start | bytes 294916
  88.7 14.2 %collective-permute-start.22 = (bf16[64,1536]{1,0:T(8,128)(2,1)S(1)}, bf16[64,1536]{1,0:T(8,128)(2,1)S(1)}, u32[]{:S(2)}, u32[]{:S(2)}) collective-permute-start(bf16[64,1536]{1,0:T(8,128)(2,1)S(1)} %copy-done.30), channel_id=1, source_target_pairs={{0,24},{1,25},{2,26},{3,27},{4,28},{5,29},{6,30},{7,31},{8,16},{9,... | collective-permute-start | bytes 589832 | tf_op jit(solution)/shard_map/ppermute | solution.py:412
  90.1 7.6 %copy-start.24 = (bf16[32,1536]{1,0:T(8,128)(2,1)}, bf16[32,1536]{1,0:T(8,128)(2,1)S(1)}, u32[]{:S(2)}) copy-start(bf16[32,1536]{1,0:T(8,128)(2,1)S(1)} %collective-permute-done.26.refs_4_) | copy-start | bytes 294916
  90.1 6.0 %collective-permute-start.28 = (bf16[32,1536]{1,0:T(8,128)(2,1)}, bf16[32,1536]{1,0:T(8,128)(2,1)S(1)}, u32[]{:S(2)}, u32[]{:S(2)}) collective-permute-start(bf16[32,1536]{1,0:T(8,128)(2,1)} %get-tuple-element.132), channel_id=1, source_target_pairs={{0,6},{1,7},{2,4},{3,5},{4,2},{5,3},{6,0},{7,1},{8,14},{9,15},{10,... | collective-permute-start | bytes 294920 | tf_op jit(solution)/shard_map/ppermute | solution.py:412
  91.5 6.2 %collective-permute-start.29 = (bf16[32,1536]{1,0:T(8,128)(2,1)}, bf16[32,1536]{1,0:T(8,128)(2,1)S(1)}, u32[]{:S(2)}, u32[]{:S(2)}) collective-permute-start(bf16[32,1536]{1,0:T(8,128)(2,1)} %get-tuple-element.133), channel_id=1, source_target_pairs={{0,7},{1,6},{2,5},{3,4},{4,3},{5,2},{6,1},{7,0},{8,15},{9,14},{10,... | collective-permute-start | bytes 294920 | tf_op jit(solution)/shard_map/ppermute | solution.py:412
  105.7 3.5 %collective-permute-start.30 = (bf16[32,1536]{1,0:T(8,128)(2,1)}, bf16[32,1536]{1,0:T(8,128)(2,1)S(1)}, u32[]{:S(2)}, u32[]{:S(2)}) collective-permute-start(bf16[32,1536]{1,0:T(8,128)(2,1)} %get-tuple-element.143), channel_id=1, source_target_pairs={{0,1},{1,0},{2,3},{3,2},{4,5},{5,4},{6,7},{7,6},{8,9},{9,8},{10,11... | collective-permute-start | bytes 294920 | tf_op jit(solution)/shard_map/ppermute | solution.py:412
  105.7 5.9 %collective-permute-start.31 = (bf16[32,1536]{1,0:T(8,128)(2,1)}, bf16[32,1536]{1,0:T(8,128)(2,1)S(1)}, u32[]{:S(2)}, u32[]{:S(2)}) collective-permute-start(bf16[32,1536]{1,0:T(8,128)(2,1)} %get-tuple-element.144), channel_id=1, source_target_pairs={{0,2},{1,3},{2,0},{3,1},{4,6},{5,7},{6,4},{7,5},{8,10},{9,11},{10,... | collective-permute-start | bytes 294920 | tf_op jit(solution)/shard_map/ppermute | solution.py:412
  106.2 6.6 %collective-permute-start.32 = (bf16[32,1536]{1,0:T(8,128)(2,1)}, bf16[32,1536]{1,0:T(8,128)(2,1)S(1)}, u32[]{:S(2)}, u32[]{:S(2)}) collective-permute-start(bf16[32,1536]{1,0:T(8,128)(2,1)} %get-tuple-element.145), channel_id=1, source_target_pairs={{0,3},{1,2},{2,1},{3,0},{4,7},{5,6},{6,5},{7,4},{8,11},{9,10},{10,... | collective-permute-start | bytes 294920 | tf_op jit(solution)/shard_map/ppermute | solution.py:412
  107.6 5.8 %collective-permute-start.33 = (bf16[32,1536]{1,0:T(8,128)(2,1)}, bf16[32,1536]{1,0:T(8,128)(2,1)S(1)}, u32[]{:S(2)}, u32[]{:S(2)}) collective-permute-start(bf16[32,1536]{1,0:T(8,128)(2,1)} %get-tuple-element.146), channel_id=1, source_target_pairs={{0,4},{1,5},{2,6},{3,7},{4,0},{5,1},{6,2},{7,3},{8,12},{9,13},{10,... | collective-permute-start | bytes 294920 | tf_op jit(solution)/shard_map/ppermute | solution.py:412
  109.1 5.6 %collective-permute-start.34 = (bf16[32,1536]{1,0:T(8,128)(2,1)}, bf16[32,1536]{1,0:T(8,128)(2,1)S(1)}, u32[]{:S(2)}, u32[]{:S(2)}) collective-permute-start(bf16[32,1536]{1,0:T(8,128)(2,1)} %get-tuple-element.147), channel_id=1, source_target_pairs={{0,5},{1,4},{2,7},{3,6},{4,1},{5,0},{6,3},{7,2},{8,13},{9,12},{10,... | collective-permute-start | bytes 294920 | tf_op jit(solution)/shard_map/ppermute | solution.py:412
  109.3 9.2 %copy-start.9 = (bf16[32,1536]{1,0:T(8,128)(2,1)}, bf16[32,1536]{1,0:T(8,128)(2,1)S(1)}, u32[]{:S(2)}) copy-start(bf16[32,1536]{1,0:T(8,128)(2,1)S(1)} %collective-permute-done.30.refs_1_) | copy-start | bytes 294916
  109.3 8.2 %collective-permute-start.35 = (bf16[32,1536]{1,0:T(8,128)(2,1)}, bf16[32,1536]{1,0:T(8,128)(2,1)S(1)}, u32[]{:S(2)}, u32[]{:S(2)}) collective-permute-start(bf16[32,1536]{1,0:T(8,128)(2,1)} %get-tuple-element.148), channel_id=1, source_target_pairs={{0,6},{1,7},{2,4},{3,5},{4,2},{5,3},{6,0},{7,1},{8,14},{9,15},{10,... | collective-permute-start | bytes 294920 | tf_op jit(solution)/shard_map/ppermute | solution.py:412
  111.6 6.9 %copy-start.10 = (bf16[32,1536]{1,0:T(8,128)(2,1)}, bf16[32,1536]{1,0:T(8,128)(2,1)S(1)}, u32[]{:S(2)}) copy-start(bf16[32,1536]{1,0:T(8,128)(2,1)S(1)} %collective-permute-done.31.refs_2_) | copy-start | bytes 294916
  111.6 6.9 %collective-permute-start.36 = (bf16[32,1536]{1,0:T(8,128)(2,1)}, bf16[32,1536]{1,0:T(8,128)(2,1)S(1)}, u32[]{:S(2)}, u32[]{:S(2)}) collective-permute-start(bf16[32,1536]{1,0:T(8,128)(2,1)} %get-tuple-element.149), channel_id=1, source_target_pairs={{0,7},{1,6},{2,5},{3,4},{4,3},{5,2},{6,1},{7,0},{8,15},{9,14},{10,... | collective-permute-start | bytes 294920 | tf_op jit(solution)/shard_map/ppermute | solution.py:412
  123.0 1.3 collective-permute-start.40
  125.1 4.4 %collective-permute-start.42 = (f32[16,1024]{1,0:T(8,128)S(1)}, f32[16,1024]{1,0:T(8,128)S(1)}, u32[]{:S(2)}, u32[]{:S(2)}) collective-permute-start(f32[16,1024]{1,0:T(8,128)S(1)} %dynamic-slice_add_fusion), channel_id=1, source_target_pairs={{0,4},{1,5},{2,6},{3,7},{4,0},{5,1},{6,2},{7,3},{8,12},{9,13},{10,... | collective-permute-start | bytes 196616 | tf_op jit(solution)/shard_map/ppermute | solution.py:412
  126.7 5.4 %collective-permute-start.43 = (f32[16,1024]{1,0:T(8,128)S(1)}, f32[16,1024]{1,0:T(8,128)S(1)}, u32[]{:S(2)}, u32[]{:S(2)}) collective-permute-start(f32[16,1024]{1,0:T(8,128)S(1)} %dynamic-slice_add_fusion), channel_id=1, source_target_pairs={{0,6},{1,7},{2,4},{3,5},{4,2},{5,3},{6,0},{7,1},{8,14},{9,15},{10,... | collective-permute-start | bytes 196616 | tf_op jit(solution)/shard_map/ppermute | solution.py:412
  128.2 5.0 %collective-permute-start.41 = (f32[16,1024]{1,0:T(8,128)S(1)}, f32[16,1024]{1,0:T(8,128)S(1)}, u32[]{:S(2)}, u32[]{:S(2)}) collective-permute-start(f32[16,1024]{1,0:T(8,128)S(1)} %dynamic-slice_add_fusion), channel_id=1, source_target_pairs={{0,2},{1,3},{2,0},{3,1},{4,6},{5,7},{6,4},{7,5},{8,10},{9,11},{10,... | collective-permute-start | bytes 196616 | tf_op jit(solution)/shard_map/ppermute | solution.py:412
  133.2 9.6 %collective-permute-start.45 = (f32[16,1024]{1,0:T(8,128)S(1)}, f32[16,1024]{1,0:T(8,128)S(1)}, u32[]{:S(2)}, u32[]{:S(2)}) collective-permute-start(f32[16,1024]{1,0:T(8,128)S(1)} %add_add_fusion.1), channel_id=1, source_target_pairs={{0,16},{1,17},{2,18},{3,19},{4,20},{5,21},{6,22},{7,23},{8,24},{9,... | collective-permute-start | bytes 196616 | tf_op jit(solution)/shard_map/ppermute | solution.py:412
  137.8 6.6 %collective-permute-start.46 = (f32[16,1024]{1,0:T(8,128)S(1)}, f32[16,1024]{1,0:T(8,128)S(1)}, u32[]{:S(2)}, u32[]{:S(2)}) collective-permute-start(f32[16,1024]{1,0:T(8,128)S(1)} %add_add_fusion.1), channel_id=1, source_target_pairs={{0,24},{1,25},{2,26},{3,27},{4,28},{5,29},{6,30},{7,31},{8,16},{9,... | collective-permute-start | bytes 196616 | tf_op jit(solution)/shard_map/ppermute | solution.py:412
  139.2 8.8 %collective-permute-start.44 = (f32[16,1024]{1,0:T(8,128)S(1)}, f32[16,1024]{1,0:T(8,128)S(1)}, u32[]{:S(2)}, u32[]{:S(2)}) collective-permute-start(f32[16,1024]{1,0:T(8,128)S(1)} %add_add_fusion.1), channel_id=1, source_target_pairs={{0,8},{1,9},{2,10},{3,11},{4,12},{5,13},{6,14},{7,15},{8,0},{9,1},... | collective-permute-start | bytes 196616 | tf_op jit(solution)/shard_map/ppermute | solution.py:412
  139.2 13.0 %collective-permute-start.37 = (bf16[64,1536]{1,0:T(8,128)(2,1)}, bf16[64,1536]{1,0:T(8,128)(2,1)S(1)}, u32[]{:S(2)}, u32[]{:S(2)}) collective-permute-start(bf16[64,1536]{1,0:T(8,128)(2,1)} %get-tuple-element.153), channel_id=1, source_target_pairs={{0,8},{1,9},{2,10},{3,11},{4,12},{5,13},{6,14},{7,15},{8,0},{9,1},... | collective-permute-start | bytes 589832 | tf_op jit(solution)/shard_map/ppermute | solution.py:412
  141.2 17.4 %collective-permute-start.38 = (bf16[64,1536]{1,0:T(8,128)(2,1)}, bf16[64,1536]{1,0:T(8,128)(2,1)S(1)}, u32[]{:S(2)}, u32[]{:S(2)}) collective-permute-start(bf16[64,1536]{1,0:T(8,128)(2,1)} %get-tuple-element.154), channel_id=1, source_target_pairs={{0,16},{1,17},{2,18},{3,19},{4,20},{5,21},{6,22},{7,23},{8,24},{9,... | collective-permute-start | bytes 589832 | tf_op jit(solution)/shard_map/ppermute | solution.py:412
  142.8 15.8 %collective-permute-start.39 = (bf16[64,1536]{1,0:T(8,128)(2,1)}, bf16[64,1536]{1,0:T(8,128)(2,1)S(1)}, u32[]{:S(2)}, u32[]{:S(2)}) collective-permute-start(bf16[64,1536]{1,0:T(8,128)(2,1)} %get-tuple-element.155), channel_id=1, source_target_pairs={{0,24},{1,25},{2,26},{3,27},{4,28},{5,29},{6,30},{7,31},{8,16},{9,... | collective-permute-start | bytes 589832 | tf_op jit(solution)/shard_map/ppermute | solution.py:412
  148.0 13.8 %collective-permute-start.47 = (f32[16,1024]{1,0:T(8,128)S(1)}, f32[16,1024]{1,0:T(8,128)S(1)}, u32[]{:S(2)}, u32[]{:S(2)}) collective-permute-start(f32[16,1024]{1,0:T(8,128)S(1)} %add_add_fusion), channel_id=1, source_target_pairs={{0,1},{1,0},{2,3},{3,2},{4,5},{5,4},{6,7},{7,6},{8,9},{9,8},{10,11... | collective-permute-start | bytes 196616 | tf_op jit(solution)/shard_map/ppermute | solution.py:412
  (27 other events, 57.5 us)

commit v2 on v1

--- a/solution.py
+++ b/solution.py
@@ -74,23 +74,22 @@
 
 
 class Order:
-    def __init__(self, high, low, by_high):
-        self.high, self.low, self.by_high = high, low, by_high
-        self.arrays = high if by_high else low
-        self.inside = low if by_high else high
-        self.rows = self.inside * GROUP
+    def __init__(self, half, apart):
+        self.half, self.apart = half, apart
+        self.arrays = 2 if apart else 1
+        self.rows = 2 * half * GROUP // self.arrays
+        self.blocks = 2 * half
 
     def position(self, block):
-        if self.by_high:
+        if self.apart:
             return block
-        shift = self.low.bit_length() - 1
-        return (block & (self.low - 1)) * self.high + lax.shift_right_logical(block, shift)
+        shift = self.half.bit_length() - 1
+        return (block & (self.half - 1)) * 2 + lax.shift_right_logical(block, shift)
 
     def block(self, position):
-        if self.by_high:
+        if self.apart:
             return position
-        part, high = divmod(position, self.high)
-        return high * self.low + part
+        return (position % 2) * self.half + position // 2
 
 
 def this_device():
@@ -107,7 +106,7 @@
 
 
 def place(lay, order, row_targets, values, out_refs):
-    count = order.arrays * order.rows
+    count = len(out_refs) * order.rows
     toks = values[0].shape[0]
     row_at = iota((count, toks), 0)
     stacked = jnp.concatenate(values, axis=0) if len(values) > 1 else values[0]
@@ -171,7 +170,7 @@
     message = read_all(message_refs)
     for group in range(lay.full):
         part = message[:, group * lay.width : (group + 1) * lay.width]
-        if not order.by_high:
+        if not order.apart:
             part = part.astype(F32)
             blocks = [
                 part[at * GROUP : (at + 1) * GROUP, :]
@@ -191,7 +190,7 @@
     count = order.arrays * order.rows
     for group in range(lay.full):
         part = rows_ref[group * count : (group + 1) * count, :]
-        if not order.by_high:
+        if not order.apart:
             blocks = [order.block(at) * GROUP for at in range(count // GROUP)]
             part = jnp.concatenate([part[at : at + GROUP, :] for at in blocks], axis=0)
         write_all(order, message_refs, group * lay.width, part.astype(BF16))
@@ -208,40 +207,61 @@
         write_all(order, message_refs, lay.base, total.astype(BF16))
 
 
-def repack_kernel(order, *refs):
-    sources, outs = refs[: order.arrays], refs[order.arrays :]
-    for part, out_ref in enumerate(outs):
-        blocks = [ref[part * GROUP : (part + 1) * GROUP, :] for ref in sources]
-        out_ref[...] = jnp.concatenate(blocks, axis=0)
-
-
-def blocks_of(order, ids):
-    return order.position(ids ^ this_device())
-
-
-def send_tokens_kernel(lay, order, ids_ref, slots_ref, tokens_ref, *out_refs):
-    blocks = blocks_of(order, ids_ref[...])
-    ranks = [targets(lay, blocks[k : k + 1, :], slots_ref[k : k + 1, :]) for k in range(2)]
-    place(lay, order, [ranks], [tokens_ref[...]], out_refs)
+def blocks_of(order, ids, mirrored):
+    device = lax.axis_index("outer") * lax.axis_size("inner") + lax.axis_index("inner")
+    inside = ids - (device & -order.half)
+    inside = jnp.where((inside >= 0) & (inside < order.half), inside, -1)
+    return jnp.where(inside >= 0, order.position(inside + mirrored * order.half), -1)
+
+
+def row_targets(lay, order, routes_ref, mirrored, k):
+    blocks = blocks_of(order, routes_ref[k : k + 1, :], mirrored)
+    slots = jnp.where(blocks >= 0, routes_ref[2 + k : 3 + k, :], lay.capacity)
+    return targets(lay, blocks, slots)
+
+
+def column_targets(lay, order, routes_ref, mirrored, k):
+    ids = as_column(routes_ref[k : k + 1, :].astype(F32)).astype(jnp.int32)
+    slots = as_column(routes_ref[2 + k : 3 + k, :].astype(F32)).astype(jnp.int32)
+    blocks = blocks_of(order, ids, mirrored)
+    return targets(lay, blocks, jnp.where(blocks >= 0, slots, lay.capacity))
+
+
+def send_tokens_kernel(lay, order, routes_ref, tokens_ref, out_ref):
+    ranks = [row_targets(lay, order, routes_ref, 0, k) for k in range(2)]
+    place(lay, order, [ranks], [tokens_ref[...]], [out_ref])
 
 
 def send_grads_kernel(
-    lay, order, ids_ref, slots_ref, tokens_ref, router_ref, cot_ref, gates_ref, *out_refs
+    lay,
+    order,
+    routes_ref,
+    tokens_ref,
+    cot_ref,
+    mirror_routes_ref,
+    mirror_tokens_ref,
+    mirror_cot_ref,
+    router_ref,
+    gates_ref,
+    out_ref,
 ):
-    logits = dot_nt(router_ref[...], tokens_ref[...])
-    expert_at = iota(logits.shape, 0)
-    picked = [
-        jnp.sum(jnp.where(expert_at == ids_ref[k : k + 1, :], logits, 0.0), axis=0, keepdims=True)
-        for k in range(2)
-    ]
-    gates = [jax.nn.sigmoid(picked[0] - picked[1]), jax.nn.sigmoid(picked[1] - picked[0])]
-    gates_ref[0:1, :] = gates[0]
-    gates_ref[1:2, :] = gates[1]
-    cot = cot_ref[...].astype(F32)
-    scaled = [(as_column(gate) * cot).astype(BF16) for gate in gates]
-    blocks = blocks_of(order, ids_ref[...])
-    ranks = [[targets(lay, blocks[k : k + 1, :], slots_ref[k : k + 1, :])] for k in range(2)]
-    place(lay, order, ranks, scaled, out_refs)
+    router = router_ref[...]
+    ranks, scaled = [], []
+    parts = ((routes_ref, tokens_ref, cot_ref), (mirror_routes_ref, mirror_tokens_ref, mirror_cot_ref))
+    for mirrored, (routes, tokens, cotangent) in enumerate(parts):
+        logits = dot_nt(router, tokens[...])
+        expert_at = iota(logits.shape, 0)
+        picked = [
+            jnp.sum(jnp.where(expert_at == routes[k : k + 1, :], logits, 0.0), axis=0, keepdims=True)
+            for k in range(2)
+        ]
+        gates = [jax.nn.sigmoid(picked[0] - picked[1]), jax.nn.sigmoid(picked[1] - picked[0])]
+        cot = cotangent[...].astype(F32)
+        for k in range(2):
+            gates_ref[2 * mirrored + k : 2 * mirrored + k + 1, :] = gates[k]
+            scaled.append((as_column(gates[k]) * cot).astype(BF16))
+            ranks.append([row_targets(lay, order, routes, mirrored, k)])
+    place(lay, order, ranks, scaled, [out_ref])
 
 
 def forward_kernel(lay, order, out_order, *refs):
@@ -298,50 +318,51 @@
         pack(lay, out_order, total_ref, out_refs)
 
 
-def column_targets(lay, order, ids_ref, slots_ref):
-    ids = [as_column(ids_ref[k : k + 1, :].astype(F32)).astype(jnp.int32) for k in range(2)]
-    slots = [as_column(slots_ref[k : k + 1, :].astype(F32)).astype(jnp.int32) for k in range(2)]
-    return ids, [targets(lay, blocks_of(order, ids[k]), slots[k]) for k in range(2)]
-
-
 def split_in_two(x):
     high = x.astype(BF16)
     return high, (x - high.astype(F32)).astype(BF16)
 
 
-def mix_kernel(lay, order, ids_ref, slots_ref, gates_ref, cot_ref, tokens_ref, router_ref, *refs):
-    message_refs, (mixed_ref, back_ref, partial_ref) = refs[: order.arrays], refs[order.arrays :]
+def mix_kernel(lay, order, mirrored, routes_ref, gates_ref, cot_ref, message_ref, mixed_ref, actions_ref):
+    cot = cot_ref[...].astype(F32)
+    message = message_ref[...]
+    mixed = None
+    for k in range(2):
+        choice = pick(lay, [column_targets(lay, order, routes_ref, mirrored, k)], message)
+        gate = as_column(gates_ref[2 * mirrored + k : 2 * mirrored + k + 1, :])
+        mixed = gate * choice if mixed is None else mixed + gate * choice
+        action = jnp.sum(choice * cot, axis=1, keepdims=True)
+        actions_ref[k : k + 1, :] = as_row(action)
+    mixed_ref[...] = mixed.astype(mixed_ref.dtype)
+
+
+def slope_kernel(
+    routes_ref, gates_ref, actions_ref, mirror_actions_ref, tokens_ref, router_ref, back_ref, partial_ref
+):
     experts = router_ref.shape[0]
     toks = tokens_ref.shape[0]
-    ids, ranks = column_targets(lay, order, ids_ref, slots_ref)
-    gates = [as_column(gates_ref[k : k + 1, :]) for k in range(2)]
-    cot = cot_ref[...].astype(F32)
-    message = read_all(message_refs)
-    choice = [pick(lay, [ranks[k]], message) for k in range(2)]
-    mixed_ref[...] = (gates[0] * choice[0] + gates[1] * choice[1]).astype(BF16)
-    actions = [jnp.sum(choice[k] * cot, axis=1, keepdims=True) for k in range(2)]
-    slope = gates[0] * gates[1] * (actions[0] - actions[1])
-
-    expert_at = iota((toks, experts), 1)
-    signs = jnp.where(expert_at == ids[0], 1.0, 0.0) - jnp.where(expert_at == ids[1], 1.0, 0.0)
-    high, low = split_in_two(signs * slope)
-    router = router_ref[...]
-    back_ref[...] = dot(high, router) + dot(low, router)
-
+    actions = actions_ref[...] + mirror_actions_ref[...]
+    slope = gates_ref[0:1, :] * gates_ref[1:2, :] * (actions[0:1, :] - actions[1:2, :])
     expert_at = iota((experts, toks), 0)
-    signs = jnp.where(expert_at == ids_ref[0:1, :], 1.0, 0.0) - jnp.where(
-        expert_at == ids_ref[1:2, :], 1.0, 0.0
-    )
-    high, low = split_in_two(signs * as_row(slope))
-    tokens = tokens_ref[...]
-    partial_ref[...] = (dot(high, tokens) + dot(low, tokens)) * (1.0 / toks)
-
-
-def grad_kernel(lay, order, ids_ref, slots_ref, back_ref, *refs):
-    message_refs, out_ref = refs[: order.arrays], refs[order.arrays]
-    _, ranks = column_targets(lay, order, ids_ref, slots_ref)
-    message = read_all(message_refs)
-    out_ref[...] = (pick(lay, ranks, message) + back_ref[...]).astype(BF16)
+    signs = jnp.where(expert_at == routes_ref[0:1, :], 1.0, 0.0) - jnp.where(
+        expert_at == routes_ref[1:2, :], 1.0, 0.0
+    )
+    parts = split_in_two(signs * slope)
+    tokens, router = tokens_ref[...], router_ref[...]
+    partial_ref[...] = (dot(parts[0], tokens) + dot(parts[1], tokens)) * (1.0 / toks)
+    back = [
+        lax.dot_general(part, router, (((0,), (0,)), ((), ())), preferred_element_type=F32)
+        for part in parts
+    ]
+    back_ref[...] = back[0] + back[1]
+
+
+def grad_kernel(lay, order, mirrored, routes_ref, message_ref, *refs):
+    ranks = [column_targets(lay, order, routes_ref, mirrored, k) for k in range(2)]
+    total = pick(lay, ranks, message_ref[...])
+    if len(refs) > 1:
+        total = total + refs[0][...]
+    refs[-1][...] = total.astype(refs[-1].dtype)
 
 
 def call(kernel, out_shape, flops, args):
@@ -362,7 +383,7 @@
 def expert_call(kernel, lay, order, out_order, message, hidden, in_weight, out_weight):
     ff = in_weight.shape[2]
     tile = min(512, ff)
-    rows = order.arrays * order.inside * lay.rows
+    rows = order.blocks * lay.rows
     win = pl.BlockSpec((1, lay.width, tile), lambda j: (0, 0, j))
     wout = pl.BlockSpec((1, tile, lay.width), lambda j: (0, j, 0))
     hid = pl.BlockSpec((rows, tile), lambda j: (0, j))
@@ -388,24 +409,14 @@
     )(*message, in_weight, out_weight, *([] if forward else [hidden]))
 
 
-def repack(lay, order, message):
-    other = Order(order.high, order.low, not order.by_high)
-    return call(
-        functools.partial(repack_kernel, order), messages_of(lay, other), 0, tuple(message)
-    )
-
-
-def step_of(order, message):
-    devices = order.high * order.low
-    unit = order.low if order.by_high else 1
-    return [message[0]] + [
-        from_device(message[part], part * unit, devices) for part in range(1, order.arrays)
-    ]
-
-
 def tied(first, second):
-    out = lax.optimization_barrier(tuple(first) + tuple(second))
-    return list(out[: len(first)]), list(out[len(first) :])
+    return lax.optimization_barrier((first, second))
+
+
+def exchange(x, devices):
+    half = devices // 2
+    groups = [list(range(half)), list(range(half, devices))]
+    return lax.all_to_all(x, AXES, split_axis=0, concat_axis=0, tiled=True, axis_index_groups=groups)
 
 
 def from_device(x, bits, devices):
@@ -437,60 +448,85 @@
     experts = router_weight.shape[1]
     devices = lax.axis_size("outer") * lax.axis_size("inner")
     lay = Layout(3 * tok_rows // experts, model_width)
-    high = 4 if devices >= 16 else 1
-    by_high, by_low = (Order(high, devices // high, flag) for flag in (True, False))
-    ids, slots, router = expert_ids.T, slot_ids.T, router_weight.T
+    half = devices // 2
+    apart, joined = Order(half, True), Order(half, False)
+    router = router_weight.T
     place_flops = 4 * experts * GROUP * tok_rows * model_width
-
-    sent_tokens = call(
-        functools.partial(send_tokens_kernel, lay, by_high),
-        messages_of(lay, by_high),
+    wide = jax.ShapeDtypeStruct((tok_rows, model_width), F32)
+    narrow = jax.ShapeDtypeStruct((tok_rows, model_width), BF16)
+    pair = jax.ShapeDtypeStruct((2, tok_rows), F32)
+
+    routes = jnp.concatenate([expert_ids.T, slot_ids.T], axis=0)
+    mirror_tokens = from_device(tokens, half, devices)
+    mirror_routes = from_device(routes, half, devices)
+    mirror_tokens, late_cotangent = tied(mirror_tokens, cotangent)
+    mirror_cot = from_device(late_cotangent, half, devices)
+
+    def send_tokens(where, rows):
+        message = messages_of(lay, apart)[0]
+        return call(
+            functools.partial(send_tokens_kernel, lay, apart), message, place_flops, (where, rows)
+        )
+
+    arrived = exchange(send_tokens(routes, tokens), devices)
+    sent_mirror = send_tokens(mirror_routes, mirror_tokens)
+    arrived, sent_mirror = tied(arrived, sent_mirror)
+    arrived_mirror = exchange(sent_mirror, devices)
+    gates, sent_grads = call(
+        functools.partial(send_grads_kernel, lay, joined),
+        [jax.ShapeDtypeStruct((4, tok_rows), F32)] + messages_of(lay, joined),
+        4 * place_flops,
+        (routes, tokens, cotangent, mirror_routes, mirror_tokens, mirror_cot, router),
+    )
+    arrived_mirror, sent_grads = tied(arrived_mirror, sent_grads)
+    grad_rows = exchange(sent_grads, devices)
+
+    hidden, produced = expert_call(
+        forward_kernel, lay, apart, joined, [arrived, arrived_mirror], None, in_weight, out_weight
+    )
+    produced, grad_rows = tied(produced, grad_rows)
+    produced_back = exchange(produced, devices)
+    (returned,) = expert_call(
+        backward_kernel, lay, joined, joined, [grad_rows], hidden, in_weight, out_weight
+    )
+    returned, produced_back = tied(returned, produced_back)
+    returned_back = exchange(returned, devices)
+
+    def mix(mirrored, where, cot, out):
+        return call(
+            functools.partial(mix_kernel, lay, joined, mirrored),
+            [out, pair],
+            2 * place_flops,
+            (where, gates, cot, produced_back),
+        )
+
+    their_mixed, their_actions = mix(1, mirror_routes, mirror_cot, narrow)
+    mirror_actions = from_device(their_actions, half, devices)
+    mirror_mixed = from_device(their_mixed, half, devices)
+    own_mixed, actions = mix(0, routes, cotangent, wide)
+    router_back, partial_grad = call(
+        slope_kernel,
+        [wide, jax.ShapeDtypeStruct((experts, model_width), F32)],
+        place_flops // 4,
+        (routes, gates, actions, mirror_actions, tokens, router),
+    )
+    grad_router = sum_over_devices(partial_grad, devices).T
+    mixed = (own_mixed + mirror_mixed.astype(F32)).astype(BF16)
+
+    their_grad = call(
+        functools.partial(grad_kernel, lay, joined, 1),
+        narrow,
         place_flops,
-        (ids, slots, tokens),
-    )
-    token_half = step_of(by_high, sent_tokens)
-
-    gates, *sent_grads = call(
-        functools.partial(send_grads_kernel, lay, by_low),
-        [jax.ShapeDtypeStruct((2, tok_rows), F32)] + messages_of(lay, by_low),
-        2 * place_flops,
-        (ids, slots, tokens, router, cotangent),
-    )
-    grad_half = repack(lay, by_low, step_of(by_low, sent_grads))
-    token_half, grad_half = tied(token_half, grad_half)
-    grad_rows = step_of(by_high, grad_half)
-    arrived = step_of(by_low, repack(lay, by_high, token_half))
-
-    hidden, *produced = expert_call(
-        forward_kernel, lay, by_low, by_high, arrived, None, in_weight, out_weight
-    )
-    produced, grad_rows = tied(produced, grad_rows)
-    produced_half = step_of(by_high, produced)
-    returned = expert_call(
-        backward_kernel, lay, by_high, by_low, grad_rows, hidden, in_weight, out_weight
-    )
-    returned_half = repack(lay, by_low, step_of(by_low, returned))
-    produced_half, returned_half = tied(produced_half, returned_half)
-    returned_back = step_of(by_high, returned_half)
-    produced_back = step_of(by_low, repack(lay, by_high, produced_half))
-
-    mixed, router_back, partial_grad = call(
-        functools.partial(mix_kernel, lay, by_low),
-        [
-            jax.ShapeDtypeStruct((tok_rows, model_width), BF16),
-            jax.ShapeDtypeStruct((tok_rows, model_width), F32),
-            jax.ShapeDtypeStruct((experts, model_width), F32),
-        ],
-        2 * place_flops,
-        (ids, slots, gates, cotangent, tokens, router, *produced_back),
-    )
-    grad_router = sum_over_devices(partial_grad, devices).T
-    grad_tokens = call(
-        functools.partial(grad_kernel, lay, by_high),
-        jax.ShapeDtypeStruct((tok_rows, model_width), BF16),
+        (mirror_routes, returned_back),
+    )
+    mirror_grad = from_device(their_grad, half, devices)
+    own_grad = call(
+        functools.partial(grad_kernel, lay, joined, 0),
+        wide,
         place_flops,
-        (ids, slots, router_back, *returned_back),
-    )
+        (routes, returned_back, router_back),
+    )
+    grad_tokens = (own_grad + mirror_grad.astype(F32)).astype(BF16)
     return (mixed, grad_tokens, grad_router)
 
 

time: 163 us -> 164 us (level)
  starting transfers between devices: 59.5 us -> 46.2 us
  waiting for transfers between devices: 45.4 us -> 55.3 us
  other arithmetic: 1.56 us -> 6.43 us
  local copies, waits for them, and re-layouts: 6.36 us -> 4.31 us
    ppermute x48 -> x14, starting transfers between devices: 59.5 us -> 21.4 us  [from_device(): return lax.ppermute(x, AXES, [(d, d ^ bits) for d in range(devices)])]
    all_to_all x0 -> x5, starting transfers between devices: none -> 24.9 us  [exchange(): lax.all_to_all(x, AXES, split_axis=0, concat_axis=0, tiled=True, axis_ind...]
    ppermute x48 -> x14, waiting for transfers between devices: 45.4 us -> 55.3 us  [from_device(): return lax.ppermute(x, AXES, [(d, d ^ bits) for d in range(devices)])]
    convert_element_type x0 -> x2, other arithmetic: none -> 3.6 us  [the longest x1 1.8 us: on_device(): mixed = (own_mixed + mirror_mixed.astype(F32)).astype(BF16)]
    unnamed x86 -> x18, local copies, waits for them, and re-layouts: 5.52 us -> 3.47 us
  transfers between devices with their start and end apart: 48 -> 19, of which waited for: 21 -> 10; matrix products, arithmetic and copies ran while one was open for 0% -> 3% of each run, Pallas kernels for 15% -> 29%
where the time goes in v2:
time: 164 us; the launch traced here: 162 us
  waiting for transfers between devices  55.3 us (34%)
  Pallas kernels  49.2 us (30%)
  starting transfers between devices  46.2 us (28%)
  other arithmetic  6.43 us (4%)
  local copies, waits for them, and re-layouts  4.31 us (3%)
    ppermute x14, waiting for transfers between devices, from_device(): return lax.ppermute(x, AXES, [(d, d ^ bits) for d in range(devices)])  55.3 us
    pallas_call x2, Pallas kernels, expert_call(): pl.pallas_call(functools.partial(kernel, lay, order, out_order), grid=(ff...  29.7 us
    all_to_all x5, starting transfers between devices, exchange(): lax.all_to_all(x, AXES, split_axis=0, concat_axis=0, tiled=True, axis_ind...  24.9 us
    ppermute x14, starting transfers between devices, from_device(): return lax.ppermute(x, AXES, [(d, d ^ bits) for d in range(devices)])  21.4 us
    pallas_call x8, Pallas kernels, call(): pl.pallas_call(kernel, out_shape=out_shape, compiler_params=pltpu.Compile...  19.4 us
    unnamed x18, local copies, waits for them, and re-layouts  3.47 us
  transfers between devices with their start and end apart: 19, of which 10 were waited for; matrix products, arithmetic and copies ran while one was open for 3% of the time, Pallas kernels for 29%

profile of v2, /device:TPU:0, one launch (start us, length us, event | category | flops | bytes accessed | tf_op | source)
XLA Modules:
  0.0 162.3 jit_solution(876542494927879196)
XLA Ops:
  0.6 1.3 pad_add_fusion.routes_ref
  1.9 2.0 %shard_map.95 = bf16[128,1536]{1,0:T(8,128)(2,1)} custom-call(s32[4,128]{1,0:T(4,128)} %pad_add_fusion.routes_ref, bf16[128,1024]{1,0:T(8,128)(2,1)} %tokens_ref.5), custom_call_target="tpu_custom_call" | custom-call | flops 134217728 | bytes 657408 | tf_op jit(solution)/shard_map/pallas_call | solution.py:371
  3.9 6.3 %all-to-all-start = ((bf16[16,8,1536]{2,1,0:T(8,128)(2,1)}), bf16[16,8,1536]{2,1,0:T(8,128)(2,1)S(1)}, u32[]{:S(2)}, u32[]{:S(2)}) async-start(bf16[16,8,1536]{2,1,0:T(8,128)(2,1)} %bitcast.20), calls=%async_computation | async-start | bytes 786432 | tf_op jit(solution)/shard_map/all_to_all | solution.py:419
  10.2 2.7 %collective-permute-start.1 = (bf16[128,1024]{1,0:T(8,128)(2,1)}, bf16[128,1024]{1,0:T(8,128)(2,1)S(1)}, u32[]{:S(2)}, u32[]{:S(2)}) collective-permute-start(bf16[128,1024]{1,0:T(8,128)(2,1)} %tokens_ref.5), channel_id=1, source_target_pairs={{0,16},{1,17},{2,18},{3,19},{4,20},{5,21},{6,22},{7,23},{8,24},{9,... | collective-permute-start | bytes 786440 | tf_op jit(solution)/shard_map/ppermute | solution.py:423
  12.8 0.3 collective-permute-start
  13.2 12.5 %collective-permute-done.1.mirror_tokens_ref.tokens_ref = bf16[128,1024]{1,0:T(8,128)(2,1)S(1)} collective-permute-done((bf16[128,1024]{1,0:T(8,128)(2,1)}, bf16[128,1024]{1,0:T(8,128)(2,1)S(1)}, u32[]{:S(2)}, u32[]{:S(2)}) %collective-permute-start.1) | collective-permute-done | bytes 262176 | tf_op jit(solution)/shard_map/ppermute | solution.py:423
  25.7 0.0 collective-permute-done.mirror_routes_ref.routes_ref
  25.7 0.7 copy-done.5
  26.4 0.6 copy-done.7
  26.9 2.0 %shard_map.96 = bf16[128,1536]{1,0:T(8,128)(2,1)} custom-call(s32[4,128]{1,0:T(4,128)} %copy-done.7, bf16[128,1024]{1,0:T(8,128)(2,1)} %copy-done.5), custom_call_target="tpu_custom_call" | custom-call | flops 134217728 | bytes 657408 | tf_op jit(solution)/shard_map/pallas_call | solution.py:371
  28.9 0.0 all-to-all-done
  28.9 4.2 %all-to-all-start.1 = ((bf16[16,8,1536]{2,1,0:T(8,128)(2,1)}), bf16[16,8,1536]{2,1,0:T(8,128)(2,1)S(1)}, u32[]{:S(2)}, u32[]{:S(2)}) async-start(bf16[16,8,1536]{2,1,0:T(8,128)(2,1)} %bitcast.19), calls=%async_computation.1 | async-start | bytes 786432 | tf_op jit(solution)/shard_map/all_to_all | solution.py:419
  33.1 3.3 %collective-permute-start.2 = (bf16[128,1024]{1,0:T(8,128)(2,1)}, bf16[128,1024]{1,0:T(8,128)(2,1)S(1)}, u32[]{:S(2)}, u32[]{:S(2)}) collective-permute-start(bf16[128,1024]{1,0:T(8,128)(2,1)} %cot_ref.3), channel_id=1, source_target_pairs={{0,16},{1,17},{2,18},{3,19},{4,20},{5,21},{6,22},{7,23},{8,24},{9,... | collective-permute-start | bytes 786440 | tf_op jit(solution)/shard_map/ppermute | solution.py:423
  36.4 12.7 %collective-permute-done.2.mirror_cot_ref.cot_ref = bf16[128,1024]{1,0:T(8,128)(2,1)S(1)} collective-permute-done((bf16[128,1024]{1,0:T(8,128)(2,1)}, bf16[128,1024]{1,0:T(8,128)(2,1)S(1)}, u32[]{:S(2)}, u32[]{:S(2)}) %collective-permute-start.2) | collective-permute-done | bytes 262176 | tf_op jit(solution)/shard_map/ppermute | solution.py:423
  49.1 0.7 copy-done.6
  49.8 3.2 %shard_map.94 = (f32[4,128]{1,0:T(4,128)}, bf16[256,1536]{1,0:T(8,128)(2,1)}) custom-call(s32[4,128]{1,0:T(4,128)} %pad_add_fusion.routes_ref, bf16[128,1024]{1,0:T(8,128)(2,1)} %tokens_ref.5, bf16[128,1024]{1,0:T(8,128)(2,1)} %cot_ref.3, s32[4,128]{1,0:T(4,128)} %copy-done.7, bf16[128,1024]{1,0:T(8,128)(2,1)} %copy-done.5, bf16[128,1024]{1,0:T(8,128)(2,1)} %copy-done.6, ...), custom_call_target="tpu_custom_call" | custom-call | flops 536870912 | bytes 1906688 | tf_op jit(solution)/shard_map/pallas_call | solution.py:371
  53.1 0.0 all-to-all-done.1
  53.1 4.2 %all-to-all-start.2 = ((bf16[16,16,1536]{2,1,0:T(8,128)(2,1)}), bf16[16,16,1536]{2,1,0:T(8,128)(2,1)S(1)}, u32[]{:S(2)}, u32[]{:S(2)}) async-start(bf16[16,16,1536]{2,1,0:T(8,128)(2,1)} %bitcast.23), calls=%async_computation.2 | async-start | bytes 1572864 | tf_op jit(solution)/shard_map/all_to_all | solution.py:419
  57.2 0.0 copy-done.3
  57.3 0.0 copy-done.4
  57.3 14.7 %shard_map.97 = (bf16[384,4096]{1,0:T(8,128)(2,1)}, bf16[256,1536]{1,0:T(8,128)(2,1)}) custom-call(bf16[128,1536]{1,0:T(8,128)(2,1)} %bitcast.25, bf16[128,1536]{1,0:T(8,128)(2,1)} %bitcast.26, bf16[1,1024,4096]{2,1,0:T(8,128)(2,1)} %refs_1_.1, bf16[1,4096,1024]{2,1,0:T(8,128)(2,1)} %refs_2_.3), custom_call_target="tpu_custom_call" | custom-call | flops 6442450944 | bytes 21495808 | tf_op jit(solution)/shard_map/pallas_call | solution.py:396
  72.0 0.0 all-to-all-done.2
  72.0 0.0 copy-start.2
  72.0 5.1 %all-to-all-start.3 = ((bf16[16,16,1536]{2,1,0:T(8,128)(2,1)}), bf16[16,16,1536]{2,1,0:T(8,128)(2,1)S(1)}, u32[]{:S(2)}, u32[]{:S(2)}) async-start(bf16[16,16,1536]{2,1,0:T(8,128)(2,1)} %bitcast.24), calls=%async_computation.3 | async-start | bytes 1572864 | tf_op jit(solution)/shard_map/all_to_all | solution.py:419
  77.1 0.0 copy-done.2
  77.1 15.0 %shard_map.98 = bf16[256,1536]{1,0:T(8,128)(2,1)} custom-call(bf16[256,1536]{1,0:T(8,128)(2,1)} %bitcast.22, bf16[1,1024,4096]{2,1,0:T(8,128)(2,1)} %refs_1_.1, bf16[1,4096,1024]{2,1,0:T(8,128)(2,1)} %refs_2_.3, bf16[384,4096]{1,0:T(8,128)(2,1)} %get-tuple-element.33.refs_3_), custom_call_target="tpu_custom_call" | custom-call | flops 6442450944 | bytes 21495808 | tf_op jit(solution)/shard_map/pallas_call | solution.py:396
  92.1 0.0 all-to-all-done.3
  92.2 5.1 %all-to-all-start.4 = ((bf16[16,16,1536]{2,1,0:T(8,128)(2,1)}), bf16[16,16,1536]{2,1,0:T(8,128)(2,1)S(1)}, u32[]{:S(2)}, u32[]{:S(2)}) async-start(bf16[16,16,1536]{2,1,0:T(8,128)(2,1)} %bitcast.21), calls=%async_computation.4 | async-start | bytes 1572864 | tf_op jit(solution)/shard_map/all_to_all | solution.py:419
  97.3 0.0 copy-done.1
  97.3 2.6 %shard_map.100 = (bf16[128,1024]{1,0:T(8,128)(2,1)}, f32[2,128]{1,0:T(2,128)}) custom-call(s32[4,128]{1,0:T(4,128)} %copy-done.7, f32[4,128]{1,0:T(4,128)} %get-tuple-element.25.gates_ref, bf16[128,1024]{1,0:T(8,128)(2,1)} %copy-done.6, bf16[256,1536]{1,0:T(8,128)(2,1)} %bitcast.17), custom_call_target="tpu_custom_call" | custom-call | flops 268435456 | bytes 1315840 | tf_op jit(solution)/shard_map/pallas_call | solution.py:371
  99.9 3.3 %collective-permute-start.4 = (f32[2,128]{1,0:T(2,128)}, f32[2,128]{1,0:T(2,128)S(1)}, u32[]{:S(2)}, u32[]{:S(2)}) collective-permute-start(f32[2,128]{1,0:T(2,128)} %get-tuple-element.40), channel_id=1, source_target_pairs={{0,16},{1,17},{2,18},{3,19},{4,20},{5,21},{6,22},{7,23},{8,24},{9,... | collective-permute-start | bytes 3080 | tf_op jit(solution)/shard_map/ppermute | solution.py:423
  103.2 2.7 %shard_map.99 = (f32[128,1024]{1,0:T(8,128)}, f32[2,128]{1,0:T(2,128)}) custom-call(s32[4,128]{1,0:T(4,128)} %pad_add_fusion.routes_ref, f32[4,128]{1,0:T(4,128)} %get-tuple-element.25.gates_ref, bf16[128,1024]{1,0:T(8,128)(2,1)} %cot_ref.3, bf16[256,1536]{1,0:T(8,128)(2,1)} %bitcast.18), custom_call_target="tpu_custom_call" | custom-call | flops 268435456 | bytes 1577984 | tf_op jit(solution)/shard_map/pallas_call | solution.py:371
  105.9 1.0 collective-permute-done.4.mirror_actions_ref
  106.9 0.6 copy-done.8
  107.5 2.1 %shard_map.101 = (f32[128,1024]{1,0:T(8,128)}, f32[32,1024]{1,0:T(8,128)}) custom-call(s32[4,128]{1,0:T(4,128)} %pad_add_fusion.routes_ref, f32[4,128]{1,0:T(4,128)} %get-tuple-element.25.gates_ref, f32[2,128]{1,0:T(2,128)} %get-tuple-element.39.actions_ref, f32[2,128]{1,0:T(2,128)} %copy-done.8, bf16[128,1024]{1,0:T(8,128)(2,1)} %tokens_ref.5, ...), custom_call_target="tpu_custom_call" | custom-call | flops 33554432 | bytes 989184 | tf_op jit(solution)/shard_map/pallas_call | solution.py:371
  109.6 0.8 constant_dynamic-slice_fusion
  110.5 0.0 collective-permute-start.6
  110.5 1.3 collective-permute-done.6
  111.7 0.8 dynamic-slice_add_fusion
  112.6 2.6 %collective-permute-start.9 = (f32[16,1024]{1,0:T(8,128)S(1)}, f32[16,1024]{1,0:T(8,128)S(1)}, u32[]{:S(2)}, u32[]{:S(2)}) collective-permute-start(f32[16,1024]{1,0:T(8,128)S(1)} %dynamic-slice_add_fusion), channel_id=1, source_target_pairs={{0,6},{1,7},{2,4},{3,5},{4,2},{5,3},{6,0},{7,1},{8,14},{9,15},{10,... | collective-permute-start | bytes 196616 | tf_op jit(solution)/shard_map/ppermute | solution.py:423
  115.2 0.6 collective-permute-start.8
  115.8 0.3 collective-permute-start.7
  116.1 1.9 %collective-permute-done.9 = f32[16,1024]{1,0:T(8,128)S(1)} collective-permute-done((f32[16,1024]{1,0:T(8,128)S(1)}, f32[16,1024]{1,0:T(8,128)S(1)}, u32[]{:S(2)}, u32[]{:S(2)}) %collective-permute-start.9) | collective-permute-done | bytes 65568 | tf_op jit(solution)/shard_map/ppermute | solution.py:423
  118.0 1.4 collective-permute-done.8
  119.4 0.6 collective-permute-done.7
  120.1 4.2 %collective-permute-start.12 = (f32[16,1024]{1,0:T(8,128)S(1)}, f32[16,1024]{1,0:T(8,128)S(1)}, u32[]{:S(2)}, u32[]{:S(2)}) collective-permute-start(f32[16,1024]{1,0:T(8,128)S(1)} %add_add_fusion.1), channel_id=1, source_target_pairs={{0,24},{1,25},{2,26},{3,27},{4,28},{5,29},{6,30},{7,31},{8,16},{9,... | collective-permute-start | bytes 196616 | tf_op jit(solution)/shard_map/ppermute | solution.py:423
  124.2 2.4 %collective-permute-start.11 = (f32[16,1024]{1,0:T(8,128)S(1)}, f32[16,1024]{1,0:T(8,128)S(1)}, u32[]{:S(2)}, u32[]{:S(2)}) collective-permute-start(f32[16,1024]{1,0:T(8,128)S(1)} %add_add_fusion.1), channel_id=1, source_target_pairs={{0,16},{1,17},{2,18},{3,19},{4,20},{5,21},{6,22},{7,23},{8,24},{9,... | collective-permute-start | bytes 196616 | tf_op jit(solution)/shard_map/ppermute | solution.py:423
  126.6 0.0 collective-permute-start.10
  126.6 1.5 collective-permute-start.3
  128.2 0.0 collective-permute-done.12
  128.2 9.2 %collective-permute-done.11 = f32[16,1024]{1,0:T(8,128)S(1)} collective-permute-done((f32[16,1024]{1,0:T(8,128)S(1)}, f32[16,1024]{1,0:T(8,128)S(1)}, u32[]{:S(2)}, u32[]{:S(2)}) %collective-permute-start.11) | collective-permute-done | bytes 65568 | tf_op jit(solution)/shard_map/ppermute | solution.py:423
  137.4 0.0 collective-permute-done.10
  137.4 0.1 collective-permute-start.13
  137.5 4.5 %collective-permute-done.3 = bf16[128,1024]{1,0:T(8,128)(2,1)S(1)} collective-permute-done((bf16[128,1024]{1,0:T(8,128)(2,1)}, bf16[128,1024]{1,0:T(8,128)(2,1)S(1)}, u32[]{:S(2)}, u32[]{:S(2)}) %collective-permute-start.3) | collective-permute-done | bytes 262176 | tf_op jit(solution)/shard_map/ppermute | solution.py:423
  141.9 1.8 %add_convert_fusion.1 = bf16[128,1024]{1,0:T(8,128)(2,1)} fusion(f32[128,1024]{1,0:T(8,128)} %get-tuple-element.36, bf16[128,1024]{1,0:T(8,128)(2,1)S(1)} %collective-permute-done.3), kind=kLoop, calls=%fused_computation.1 | loop fusion | flops 393216 | bytes 1048576 | tf_op jit(solution)/shard_map/convert_element_type | solution.py:514
  143.7 0.0 all-to-all-done.4
  143.7 0.9 copy-done
  144.6 2.3 %shard_map.103 = bf16[128,1024]{1,0:T(8,128)(2,1)} custom-call(s32[4,128]{1,0:T(4,128)} %copy-done.7, bf16[256,1536]{1,0:T(8,128)(2,1)} %bitcast.15), custom_call_target="tpu_custom_call" | custom-call | flops 134217728 | bytes 1050624 | tf_op jit(solution)/shard_map/pallas_call | solution.py:371
  146.9 0.0 collective-permute-start.5
  146.9 0.0 collective-permute-done.13
  147.0 0.7 maximum_bitcast_fusion
  147.6 2.5 %shard_map.102 = f32[128,1024]{1,0:T(8,128)} custom-call(s32[4,128]{1,0:T(4,128)} %pad_add_fusion.routes_ref, bf16[256,1536]{1,0:T(8,128)(2,1)} %bitcast.16, f32[128,1024]{1,0:T(8,128)} %get-tuple-element.41.refs_0_), custom_call_target="tpu_custom_call" | custom-call | flops 134217728 | bytes 1837056 | tf_op jit(solution)/shard_map/pallas_call | solution.py:371
  150.2 10.3 %collective-permute-done.5 = bf16[128,1024]{1,0:T(8,128)(2,1)S(1)} collective-permute-done((bf16[128,1024]{1,0:T(8,128)(2,1)}, bf16[128,1024]{1,0:T(8,128)(2,1)S(1)}, u32[]{:S(2)}, u32[]{:S(2)}) %collective-permute-start.5) | collective-permute-done | bytes 262176 | tf_op jit(solution)/shard_map/ppermute | solution.py:423
  160.5 1.8 %add_convert_fusion = bf16[128,1024]{1,0:T(8,128)(2,1)} fusion(f32[128,1024]{1,0:T(8,128)} %shard_map.102, bf16[128,1024]{1,0:T(8,128)(2,1)S(1)} %collective-permute-done.5), kind=kLoop, calls=%fused_computation | loop fusion | flops 393216 | bytes 1048576 | tf_op jit(solution)/shard_map/convert_element_type | solution.py:529
  (11 shorter events, 0.1 us)
Async XLA Ops:
  3.9 25.0 %all-to-all-start = ((bf16[16,8,1536]{2,1,0:T(8,128)(2,1)}), bf16[16,8,1536]{2,1,0:T(8,128)(2,1)S(1)}, u32[]{:S(2)}, u32[]{:S(2)}) async-start(bf16[16,8,1536]{2,1,0:T(8,128)(2,1)} %bitcast.20), calls=%async_computation | async-start | bytes 786432 | tf_op jit(solution)/shard_map/all_to_all | solution.py:419
  10.2 15.5 %collective-permute-start.1 = (bf16[128,1024]{1,0:T(8,128)(2,1)}, bf16[128,1024]{1,0:T(8,128)(2,1)S(1)}, u32[]{:S(2)}, u32[]{:S(2)}) collective-permute-start(bf16[128,1024]{1,0:T(8,128)(2,1)} %tokens_ref.5), channel_id=1, source_target_pairs={{0,16},{1,17},{2,18},{3,19},{4,20},{5,21},{6,22},{7,23},{8,24},{9,... | collective-permute-start | bytes 786440 | tf_op jit(solution)/shard_map/ppermute | solution.py:423
  12.8 12.8 %collective-permute-start = (s32[4,128]{1,0:T(4,128)}, s32[4,128]{1,0:T(4,128)S(1)}, u32[]{:S(2)}, u32[]{:S(2)}) collective-permute-start(s32[4,128]{1,0:T(4,128)} %pad_add_fusion.routes_ref), channel_id=1, source_target_pairs={{0,16},{1,17},{2,18},{3,19},{4,20},{5,21},{6,22},{7,23},{8,24},{9,... | collective-permute-start | bytes 6152 | tf_op jit(solution)/shard_map/ppermute | solution.py:423
  25.7 0.7 copy-start.5
  26.4 0.6 copy-start.7
  28.9 28.3 %copy-start.3 = (bf16[16,8,1536]{2,1,0:T(8,128)(2,1)}, bf16[16,8,1536]{2,1,0:T(8,128)(2,1)S(1)}, u32[]{:S(2)}) copy-start(bf16[16,8,1536]{2,1,0:T(8,128)(2,1)S(1)} %all-to-all-done) | copy-start | bytes 1179652
  28.9 24.1 %all-to-all-start.1 = ((bf16[16,8,1536]{2,1,0:T(8,128)(2,1)}), bf16[16,8,1536]{2,1,0:T(8,128)(2,1)S(1)}, u32[]{:S(2)}, u32[]{:S(2)}) async-start(bf16[16,8,1536]{2,1,0:T(8,128)(2,1)} %bitcast.19), calls=%async_computation.1 | async-start | bytes 786432 | tf_op jit(solution)/shard_map/all_to_all | solution.py:419
  33.1 16.0 %collective-permute-start.2 = (bf16[128,1024]{1,0:T(8,128)(2,1)}, bf16[128,1024]{1,0:T(8,128)(2,1)S(1)}, u32[]{:S(2)}, u32[]{:S(2)}) collective-permute-start(bf16[128,1024]{1,0:T(8,128)(2,1)} %cot_ref.3), channel_id=1, source_target_pairs={{0,16},{1,17},{2,18},{3,19},{4,20},{5,21},{6,22},{7,23},{8,24},{9,... | collective-permute-start | bytes 786440 | tf_op jit(solution)/shard_map/ppermute | solution.py:423
  49.1 0.7 copy-start.6
  53.1 4.2 %copy-start.4 = (bf16[16,8,1536]{2,1,0:T(8,128)(2,1)}, bf16[16,8,1536]{2,1,0:T(8,128)(2,1)S(1)}, u32[]{:S(2)}) copy-start(bf16[16,8,1536]{2,1,0:T(8,128)(2,1)S(1)} %all-to-all-done.1) | copy-start | bytes 1179652
  53.1 18.9 %all-to-all-start.2 = ((bf16[16,16,1536]{2,1,0:T(8,128)(2,1)}), bf16[16,16,1536]{2,1,0:T(8,128)(2,1)S(1)}, u32[]{:S(2)}, u32[]{:S(2)}) async-start(bf16[16,16,1536]{2,1,0:T(8,128)(2,1)} %bitcast.23), calls=%async_computation.2 | async-start | bytes 1572864 | tf_op jit(solution)/shard_map/all_to_all | solution.py:419
  72.0 5.1 %copy-start.2 = (bf16[16,16,1536]{2,1,0:T(8,128)(2,1)}, bf16[16,16,1536]{2,1,0:T(8,128)(2,1)S(1)}, u32[]{:S(2)}) copy-start(bf16[16,16,1536]{2,1,0:T(8,128)(2,1)S(1)} %all-to-all-done.2) | copy-start | bytes 2359300
  72.0 20.1 %all-to-all-start.3 = ((bf16[16,16,1536]{2,1,0:T(8,128)(2,1)}), bf16[16,16,1536]{2,1,0:T(8,128)(2,1)S(1)}, u32[]{:S(2)}, u32[]{:S(2)}) async-start(bf16[16,16,1536]{2,1,0:T(8,128)(2,1)} %bitcast.24), calls=%async_computation.3 | async-start | bytes 1572864 | tf_op jit(solution)/shard_map/all_to_all | solution.py:419
  92.1 5.1 %copy-start.1 = (bf16[16,16,1536]{2,1,0:T(8,128)(2,1)}, bf16[16,16,1536]{2,1,0:T(8,128)(2,1)S(1)}, u32[]{:S(2)}) copy-start(bf16[16,16,1536]{2,1,0:T(8,128)(2,1)S(1)} %all-to-all-done.3) | copy-start | bytes 2359300
  92.2 51.6 %all-to-all-start.4 = ((bf16[16,16,1536]{2,1,0:T(8,128)(2,1)}), bf16[16,16,1536]{2,1,0:T(8,128)(2,1)S(1)}, u32[]{:S(2)}, u32[]{:S(2)}) async-start(bf16[16,16,1536]{2,1,0:T(8,128)(2,1)} %bitcast.21), calls=%async_computation.4 | async-start | bytes 1572864 | tf_op jit(solution)/shard_map/all_to_all | solution.py:419
  99.9 7.0 %collective-permute-start.4 = (f32[2,128]{1,0:T(2,128)}, f32[2,128]{1,0:T(2,128)S(1)}, u32[]{:S(2)}, u32[]{:S(2)}) collective-permute-start(f32[2,128]{1,0:T(2,128)} %get-tuple-element.40), channel_id=1, source_target_pairs={{0,16},{1,17},{2,18},{3,19},{4,20},{5,21},{6,22},{7,23},{8,24},{9,... | collective-permute-start | bytes 3080 | tf_op jit(solution)/shard_map/ppermute | solution.py:423
  106.9 0.6 copy-start.8
  110.5 1.3 collective-permute-start.6
  112.6 5.4 %collective-permute-start.9 = (f32[16,1024]{1,0:T(8,128)S(1)}, f32[16,1024]{1,0:T(8,128)S(1)}, u32[]{:S(2)}, u32[]{:S(2)}) collective-permute-start(f32[16,1024]{1,0:T(8,128)S(1)} %dynamic-slice_add_fusion), channel_id=1, source_target_pairs={{0,6},{1,7},{2,4},{3,5},{4,2},{5,3},{6,0},{7,1},{8,14},{9,15},{10,... | collective-permute-start | bytes 196616 | tf_op jit(solution)/shard_map/ppermute | solution.py:423
  115.2 4.3 %collective-permute-start.8 = (f32[16,1024]{1,0:T(8,128)S(1)}, f32[16,1024]{1,0:T(8,128)S(1)}, u32[]{:S(2)}, u32[]{:S(2)}) collective-permute-start(f32[16,1024]{1,0:T(8,128)S(1)} %dynamic-slice_add_fusion), channel_id=1, source_target_pairs={{0,4},{1,5},{2,6},{3,7},{4,0},{5,1},{6,2},{7,3},{8,12},{9,13},{10,... | collective-permute-start | bytes 196616 | tf_op jit(solution)/shard_map/ppermute | solution.py:423
  115.8 4.3 %collective-permute-start.7 = (f32[16,1024]{1,0:T(8,128)S(1)}, f32[16,1024]{1,0:T(8,128)S(1)}, u32[]{:S(2)}, u32[]{:S(2)}) collective-permute-start(f32[16,1024]{1,0:T(8,128)S(1)} %dynamic-slice_add_fusion), channel_id=1, source_target_pairs={{0,2},{1,3},{2,0},{3,1},{4,6},{5,7},{6,4},{7,5},{8,10},{9,11},{10,... | collective-permute-start | bytes 196616 | tf_op jit(solution)/shard_map/ppermute | solution.py:423
  120.1 8.1 %collective-permute-start.12 = (f32[16,1024]{1,0:T(8,128)S(1)}, f32[16,1024]{1,0:T(8,128)S(1)}, u32[]{:S(2)}, u32[]{:S(2)}) collective-permute-start(f32[16,1024]{1,0:T(8,128)S(1)} %add_add_fusion.1), channel_id=1, source_target_pairs={{0,24},{1,25},{2,26},{3,27},{4,28},{5,29},{6,30},{7,31},{8,16},{9,... | collective-permute-start | bytes 196616 | tf_op jit(solution)/shard_map/ppermute | solution.py:423
  124.2 13.1 %collective-permute-start.11 = (f32[16,1024]{1,0:T(8,128)S(1)}, f32[16,1024]{1,0:T(8,128)S(1)}, u32[]{:S(2)}, u32[]{:S(2)}) collective-permute-start(f32[16,1024]{1,0:T(8,128)S(1)} %add_add_fusion.1), channel_id=1, source_target_pairs={{0,16},{1,17},{2,18},{3,19},{4,20},{5,21},{6,22},{7,23},{8,24},{9,... | collective-permute-start | bytes 196616 | tf_op jit(solution)/shard_map/ppermute | solution.py:423
  126.6 10.7 %collective-permute-start.10 = (f32[16,1024]{1,0:T(8,128)S(1)}, f32[16,1024]{1,0:T(8,128)S(1)}, u32[]{:S(2)}, u32[]{:S(2)}) collective-permute-start(f32[16,1024]{1,0:T(8,128)S(1)} %add_add_fusion.1), channel_id=1, source_target_pairs={{0,8},{1,9},{2,10},{3,11},{4,12},{5,13},{6,14},{7,15},{8,0},{9,1},... | collective-permute-start | bytes 196616 | tf_op jit(solution)/shard_map/ppermute | solution.py:423
  126.6 15.3 %collective-permute-start.3 = (bf16[128,1024]{1,0:T(8,128)(2,1)}, bf16[128,1024]{1,0:T(8,128)(2,1)S(1)}, u32[]{:S(2)}, u32[]{:S(2)}) collective-permute-start(bf16[128,1024]{1,0:T(8,128)(2,1)} %get-tuple-element.37), channel_id=1, source_target_pairs={{0,16},{1,17},{2,18},{3,19},{4,20},{5,21},{6,22},{7,23},{8,24},{9,... | collective-permute-start | bytes 786440 | tf_op jit(solution)/shard_map/ppermute | solution.py:423
  137.4 9.6 %collective-permute-start.13 = (f32[16,1024]{1,0:T(8,128)S(1)}, f32[16,1024]{1,0:T(8,128)S(1)}, u32[]{:S(2)}, u32[]{:S(2)}) collective-permute-start(f32[16,1024]{1,0:T(8,128)S(1)} %add_add_fusion), channel_id=1, source_target_pairs={{0,1},{1,0},{2,3},{3,2},{4,5},{5,4},{6,7},{7,6},{8,9},{9,8},{10,11... | collective-permute-start | bytes 196616 | tf_op jit(solution)/shard_map/ppermute | solution.py:423
  143.7 0.9 copy-start
  146.9 13.5 %collective-permute-start.5 = (bf16[128,1024]{1,0:T(8,128)(2,1)}, bf16[128,1024]{1,0:T(8,128)(2,1)S(1)}, u32[]{:S(2)}, u32[]{:S(2)}) collective-permute-start(bf16[128,1024]{1,0:T(8,128)(2,1)} %shard_map.103), channel_id=1, source_target_pairs={{0,16},{1,17},{2,18},{3,19},{4,20},{5,21},{6,22},{7,23},{8,24},{9,... | collective-permute-start | bytes 786440 | tf_op jit(solution)/shard_map/ppermute | solution.py:423

commit v3 on v0

--- a/solution.py
+++ b/solution.py
@@ -339,7 +339,11 @@
     return lax.ppermute(x, AXES, [(d, d ^ bits) for d in range(devices)])
 
 
-def sum_over_devices(x, devices):
+def sum_of_pairs(own, near, far, both):
+    return (own + near) + (far + both)
+
+
+def sum_over_devices(x, devices, beside):
     half = x.shape[0] // 2
     core = lax.axis_index("inner") % 2
     own = lax.dynamic_slice_in_dim(x, core * half, half, 0)
@@ -347,16 +351,18 @@
     own = own + from_device(other, 1, devices)
     bit = 2
     while bit < devices:
-        if 2 * bit < devices:
-            near = own + from_device(own, bit, devices)
-            far = from_device(own, 2 * bit, devices) + from_device(own, 3 * bit, devices)
-            own = near + far
-        else:
-            own = own + from_device(own, bit, devices)
+        sent = own if bit == 2 else own.astype(BF16)
+        steps = [1, 2, 3] if 2 * bit < devices else [1]
+        terms = [from_device(sent, step * bit, devices) for step in steps]
+        if bit * 4 >= devices:
+            beside, sent, *terms = lax.optimization_barrier((beside, sent, *terms))
+        terms = [term.astype(F32) for term in [sent] + terms]
+        own = sum_of_pairs(*terms) if len(terms) == 4 else terms[0] + terms[1]
         bit *= 4
     other = from_device(own, 1, devices)
     first = core == 0
-    return jnp.concatenate([jnp.where(first, own, other), jnp.where(first, other, own)], axis=0)
+    total = jnp.concatenate([jnp.where(first, own, other), jnp.where(first, other, own)], axis=0)
+    return total, beside
 
 
 def on_device(tokens, router_weight, in_weight, out_weight, expert_ids, slot_ids, cotangent):
@@ -397,14 +403,14 @@
         2 * place_flops,
         (ids, slots, gates, produced_back, cotangent, tokens, router),
     )
-    grad_router = sum_over_devices(partial_grad, devices).T
     grad_tokens = call(
         functools.partial(grad_kernel, lay),
         jax.ShapeDtypeStruct((tok_rows, model_width), BF16),
         place_flops,
         (ids, slots, returned_back, router_back),
     )
-    return (mixed, grad_tokens, grad_router)
+    grad_router, grad_tokens = sum_over_devices(partial_grad, devices, grad_tokens)
+    return (mixed, grad_tokens, grad_router.T)
 
 
 def solution(mesh):

time: 116 us -> 112 us (0.966)
  waiting for transfers between devices: 43.3 us -> 39.6 us
    ppermute x8, waiting for transfers between devices: 14.1 us -> 7.1 us  [from_device(): return lax.ppermute(x, AXES, [(d, d ^ bits) for d in range(devices)])]
    all_to_all x4, waiting for transfers between devices: 29.2 us -> 32.5 us  [exchange(): return lax.all_to_all(x, AXES, split_axis=0, concat_axis=0, tiled=True)]
  transfers between devices with their start and end apart: 12 -> 12, of which waited for: 9 -> 8; matrix products, arithmetic and copies ran while one was open for 2% -> 2% of each run, Pallas kernels for 31% -> 34%
where the time goes in v3:
time: 112 us; the launch traced here: 111 us
  Pallas kernels  40.3 us (36%)
  waiting for transfers between devices  39.6 us (35%)
  starting transfers between devices  26.8 us (24%)
  local copies, waits for them, and re-layouts  1.74 us (2%)
  other arithmetic  1.56 us (1%)
    all_to_all x4, waiting for transfers between devices, exchange(): return lax.all_to_all(x, AXES, split_axis=0, concat_axis=0, tiled=True)  32.5 us
    pallas_call x2, Pallas kernels, expert_call(): pl.pallas_call(functools.partial(kernel, lay), grid=(ff // tile,), in_spe...  29.8 us
    all_to_all x4, starting transfers between devices, exchange(): return lax.all_to_all(x, AXES, split_axis=0, concat_axis=0, tiled=True)  18.2 us
    pallas_call x4, Pallas kernels, call(): pl.pallas_call(kernel, out_shape=out_shape, compiler_params=pltpu.Compile...  10.5 us
    ppermute x8, starting transfers between devices, from_device(): return lax.ppermute(x, AXES, [(d, d ^ bits) for d in range(devices)])  8.67 us
    ppermute x8, waiting for transfers between devices, from_device(): return lax.ppermute(x, AXES, [(d, d ^ bits) for d in range(devices)])  7.1 us
  transfers between devices with their start and end apart: 12, of which 8 were waited for; matrix products, arithmetic and copies ran while one was open for 2% of the time, Pallas kernels for 34%

profile of v3, /device:TPU:0, one launch (start us, length us, event | category | flops | bytes accessed | tf_op | source)
XLA Modules:
  0.0 110.8 jit_solution(17830814166279034205)
XLA Ops:
  0.6 2.2 %shard_map.95 = bf16[256,1536]{1,0:T(8,128)(2,1)} custom-call(s32[2,128]{1,0:T(2,128)} %bitcast.23, s32[2,128]{1,0:T(2,128)} %bitcast.27, bf16[128,1024]{1,0:T(8,128)(2,1)} %tokens_ref.5), custom_call_target="tpu_custom_call" | custom-call | flops 134217728 | bytes 1050624 | tf_op jit(solution)/shard_map/pallas_call | solution.py:298
  2.9 7.3 %all-to-all-start = ((bf16[32,8,1536]{2,1,0:T(8,128)(2,1)}), bf16[32,8,1536]{2,1,0:T(8,128)(2,1)S(1)}, u32[]{:S(2)}, u32[]{:S(2)}) async-start(bf16[32,8,1536]{2,1,0:T(8,128)(2,1)} %bitcast.15), calls=%async_computation | async-start | bytes 1572864 | tf_op jit(solution)/shard_map/all_to_all | solution.py:335
  10.2 2.9 %shard_map.94 = (bf16[256,1536]{1,0:T(8,128)(2,1)}, f32[2,128]{1,0:T(2,128)}) custom-call(s32[2,128]{1,0:T(2,128)} %bitcast.24, s32[2,128]{1,0:T(2,128)} %bitcast.28, bf16[128,1024]{1,0:T(8,128)(2,1)} %tokens_ref.5, bf16[32,1024]{1,0:T(8,128)(2,1)} %bitcast.21, bf16[128,1024]{1,0:T(8,128)(2,1)} %cot_ref.3), custom_call_target="tpu_custom_call" | custom-call | flops 268435456 | bytes 1379328 | tf_op jit(solution)/shard_map/pallas_call | solution.py:298
  13.0 17.7 %all-to-all-done = bf16[32,8,1536]{2,1,0:T(8,128)(2,1)S(1)} async-done(((bf16[32,8,1536]{2,1,0:T(8,128)(2,1)}), bf16[32,8,1536]{2,1,0:T(8,128)(2,1)S(1)}, u32[]{:S(2)}, u32[]{:S(2)}) %all-to-all-start) | async-done | bytes 786464 | tf_op jit(solution)/shard_map/all_to_all | solution.py:335
  30.8 0.0 copy-start.2
  30.8 3.6 %all-to-all-start.1 = ((bf16[32,8,1536]{2,1,0:T(8,128)(2,1)}), bf16[32,8,1536]{2,1,0:T(8,128)(2,1)S(1)}, u32[]{:S(2)}, u32[]{:S(2)}) async-start(bf16[32,8,1536]{2,1,0:T(8,128)(2,1)} %bitcast.19), calls=%async_computation.1 | async-start | bytes 1572864 | tf_op jit(solution)/shard_map/all_to_all | solution.py:335
  34.4 0.0 copy-done.2
  34.4 14.7 %shard_map.96 = (bf16[256,1536]{1,0:T(8,128)(2,1)}, bf16[384,4096]{1,0:T(8,128)(2,1)}) custom-call(bf16[256,1536]{1,0:T(8,128)(2,1)} %bitcast.17, bf16[1,1024,4096]{2,1,0:T(8,128)(2,1)} %win_ref.3, bf16[1,4096,1024]{2,1,0:T(8,128)(2,1)} %wout_ref.3), custom_call_target="tpu_custom_call" | custom-call | flops 6442450944 | bytes 21495808 | tf_op jit(solution)/shard_map/pallas_call | solution.py:318
  49.1 5.9 %all-to-all-done.1 = bf16[32,8,1536]{2,1,0:T(8,128)(2,1)S(1)} async-done(((bf16[32,8,1536]{2,1,0:T(8,128)(2,1)}), bf16[32,8,1536]{2,1,0:T(8,128)(2,1)S(1)}, u32[]{:S(2)}, u32[]{:S(2)}) %all-to-all-start.1) | async-done | bytes 786464 | tf_op jit(solution)/shard_map/all_to_all | solution.py:335
  55.0 0.0 copy-start.3
  55.0 3.6 %all-to-all-start.2 = ((bf16[32,8,1536]{2,1,0:T(8,128)(2,1)}), bf16[32,8,1536]{2,1,0:T(8,128)(2,1)S(1)}, u32[]{:S(2)}, u32[]{:S(2)}) async-start(bf16[32,8,1536]{2,1,0:T(8,128)(2,1)} %bitcast.20), calls=%async_computation.2 | async-start | bytes 1572864 | tf_op jit(solution)/shard_map/all_to_all | solution.py:335
  58.7 0.0 copy-done.3
  58.7 15.1 %shard_map.97 = bf16[256,1536]{1,0:T(8,128)(2,1)} custom-call(bf16[256,1536]{1,0:T(8,128)(2,1)} %bitcast.18, bf16[384,4096]{1,0:T(8,128)(2,1)} %get-tuple-element.27.hidden_ref, bf16[1,1024,4096]{2,1,0:T(8,128)(2,1)} %win_ref.3, bf16[1,4096,1024]{2,1,0:T(8,128)(2,1)} %wout_ref.3), custom_call_target="tpu_custom_call" | custom-call | flops 6442450944 | bytes 21495808 | tf_op jit(solution)/shard_map/pallas_call | solution.py:318
  73.8 5.5 %all-to-all-done.2 = bf16[32,8,1536]{2,1,0:T(8,128)(2,1)S(1)} async-done(((bf16[32,8,1536]{2,1,0:T(8,128)(2,1)}), bf16[32,8,1536]{2,1,0:T(8,128)(2,1)S(1)}, u32[]{:S(2)}, u32[]{:S(2)}) %all-to-all-start.2) | async-done | bytes 786464 | tf_op jit(solution)/shard_map/all_to_all | solution.py:335
  79.3 0.0 copy-start.1
  79.3 3.6 %all-to-all-start.3 = ((bf16[32,8,1536]{2,1,0:T(8,128)(2,1)}), bf16[32,8,1536]{2,1,0:T(8,128)(2,1)S(1)}, u32[]{:S(2)}, u32[]{:S(2)}) async-start(bf16[32,8,1536]{2,1,0:T(8,128)(2,1)} %bitcast.16), calls=%async_computation.3 | async-start | bytes 1572864 | tf_op jit(solution)/shard_map/all_to_all | solution.py:335
  82.9 0.0 copy-done.1
  82.9 3.0 %shard_map.98 = (bf16[128,1024]{1,0:T(8,128)(2,1)}, f32[128,1024]{1,0:T(8,128)}, f32[32,1024]{1,0:T(8,128)}) custom-call(s32[2,128]{1,0:T(2,128)} %bitcast.25, s32[2,128]{1,0:T(2,128)} %bitcast.29, f32[2,128]{1,0:T(2,128)} %get-tuple-element.21.gates_ref, bf16[256,1536]{1,0:T(8,128)(2,1)} %bitcast.14, bf16[128,1024]{1,0:T(8,128)(2,1)} %cot_ref.3, ...), custom_call_target="tpu_custom_call" | custom-call | flops 268435456 | bytes 2296832 | tf_op jit(solution)/shard_map/pallas_call | solution.py:298
  85.9 0.8 constant_dynamic-slice_fusion
  86.8 0.2 collective-permute-start
  87.0 1.0 collective-permute-done
  88.0 0.8 dynamic-slice_add_fusion
  88.9 2.7 %collective-permute-start.3 = (f32[16,1024]{1,0:T(8,128)S(1)}, f32[16,1024]{1,0:T(8,128)S(1)}, u32[]{:S(2)}, u32[]{:S(2)}) collective-permute-start(f32[16,1024]{1,0:T(8,128)S(1)} %dynamic-slice_add_fusion), channel_id=1, source_target_pairs={{0,6},{1,7},{2,4},{3,5},{4,2},{5,3},{6,0},{7,1},{8,14},{9,15},{10,... | collective-permute-start | bytes 196616 | tf_op jit(solution)/shard_map/ppermute | solution.py:339
  91.6 0.6 collective-permute-start.2
  92.2 0.3 collective-permute-start.1
  92.4 3.4 %collective-permute-done.3 = f32[16,1024]{1,0:T(8,128)S(1)} collective-permute-done((f32[16,1024]{1,0:T(8,128)S(1)}, f32[16,1024]{1,0:T(8,128)S(1)}, u32[]{:S(2)}, u32[]{:S(2)}) %collective-permute-start.3) | collective-permute-done | bytes 65568 | tf_op jit(solution)/shard_map/ppermute | solution.py:339
  95.8 1.5 %collective-permute-done.2 = f32[16,1024]{1,0:T(8,128)S(1)} collective-permute-done((f32[16,1024]{1,0:T(8,128)S(1)}, f32[16,1024]{1,0:T(8,128)S(1)}, u32[]{:S(2)}, u32[]{:S(2)}) %collective-permute-start.2) | collective-permute-done | bytes 65568 | tf_op jit(solution)/shard_map/ppermute | solution.py:339
  97.3 0.0 collective-permute-done.1
  97.3 4.2 %collective-permute-start.6 = (bf16[16,1024]{1,0:T(8,128)(2,1)S(1)}, bf16[16,1024]{1,0:T(8,128)(2,1)S(1)}, u32[]{:S(2)}, u32[]{:S(2)}) collective-permute-start(bf16[16,1024]{1,0:T(8,128)(2,1)S(1)} %add_convert_fusion), channel_id=1, source_target_pairs={{0,24},{1,25},{2,26},{3,27},{4,28},{5,29},{6,30},{7,31},{8,16},{9,... | collective-permute-start | bytes 98312 | tf_op jit(solution)/shard_map/ppermute | solution.py:339
  101.5 0.0 collective-permute-start.5
  101.5 0.6 collective-permute-start.4
  102.1 3.3 %all-to-all-done.3 = bf16[32,8,1536]{2,1,0:T(8,128)(2,1)S(1)} async-done(((bf16[32,8,1536]{2,1,0:T(8,128)(2,1)}), bf16[32,8,1536]{2,1,0:T(8,128)(2,1)S(1)}, u32[]{:S(2)}, u32[]{:S(2)}) %all-to-all-start.3) | async-done | bytes 786464 | tf_op jit(solution)/shard_map/all_to_all | solution.py:335
  105.4 0.0 copy-start
  105.4 0.9 copy-done
  106.3 2.4 %shard_map.99 = bf16[128,1024]{1,0:T(8,128)(2,1)} custom-call(s32[2,128]{1,0:T(2,128)} %bitcast.26, s32[2,128]{1,0:T(2,128)} %bitcast.30, bf16[256,1536]{1,0:T(8,128)(2,1)} %bitcast.13, f32[128,1024]{1,0:T(8,128)} %get-tuple-element.32.back_ref), custom_call_target="tpu_custom_call" | custom-call | flops 134217728 | bytes 1574912 | tf_op jit(solution)/shard_map/pallas_call | solution.py:298
  108.7 0.0 collective-permute-done.6
  108.7 0.0 collective-permute-done.5
  108.7 0.0 collective-permute-done.4
  108.8 0.1 collective-permute-start.7
  108.9 1.2 %collective-permute-done.7 = f32[16,1024]{1,0:T(8,128)S(1)} collective-permute-done((f32[16,1024]{1,0:T(8,128)S(1)}, f32[16,1024]{1,0:T(8,128)S(1)}, u32[]{:S(2)}, u32[]{:S(2)}) %collective-permute-start.7) | collective-permute-done | bytes 65568 | tf_op jit(solution)/shard_map/ppermute | solution.py:339
  110.1 0.7 maximum_bitcast_fusion
  (3 shorter events, 0.0 us)
Async XLA Ops:
  2.9 27.9 %all-to-all-start = ((bf16[32,8,1536]{2,1,0:T(8,128)(2,1)}), bf16[32,8,1536]{2,1,0:T(8,128)(2,1)S(1)}, u32[]{:S(2)}, u32[]{:S(2)}) async-start(bf16[32,8,1536]{2,1,0:T(8,128)(2,1)} %bitcast.15), calls=%async_computation | async-start | bytes 1572864 | tf_op jit(solution)/shard_map/all_to_all | solution.py:335
  30.8 3.6 %copy-start.2 = (bf16[32,8,1536]{2,1,0:T(8,128)(2,1)}, bf16[32,8,1536]{2,1,0:T(8,128)(2,1)S(1)}, u32[]{:S(2)}) copy-start(bf16[32,8,1536]{2,1,0:T(8,128)(2,1)S(1)} %all-to-all-done) | copy-start | bytes 2359300
  30.8 24.2 %all-to-all-start.1 = ((bf16[32,8,1536]{2,1,0:T(8,128)(2,1)}), bf16[32,8,1536]{2,1,0:T(8,128)(2,1)S(1)}, u32[]{:S(2)}, u32[]{:S(2)}) async-start(bf16[32,8,1536]{2,1,0:T(8,128)(2,1)} %bitcast.19), calls=%async_computation.1 | async-start | bytes 1572864 | tf_op jit(solution)/shard_map/all_to_all | solution.py:335
  55.0 3.6 %copy-start.3 = (bf16[32,8,1536]{2,1,0:T(8,128)(2,1)}, bf16[32,8,1536]{2,1,0:T(8,128)(2,1)S(1)}, u32[]{:S(2)}) copy-start(bf16[32,8,1536]{2,1,0:T(8,128)(2,1)S(1)} %all-to-all-done.1) | copy-start | bytes 2359300
  55.0 24.2 %all-to-all-start.2 = ((bf16[32,8,1536]{2,1,0:T(8,128)(2,1)}), bf16[32,8,1536]{2,1,0:T(8,128)(2,1)S(1)}, u32[]{:S(2)}, u32[]{:S(2)}) async-start(bf16[32,8,1536]{2,1,0:T(8,128)(2,1)} %bitcast.20), calls=%async_computation.2 | async-start | bytes 1572864 | tf_op jit(solution)/shard_map/all_to_all | solution.py:335
  79.3 3.6 %copy-start.1 = (bf16[32,8,1536]{2,1,0:T(8,128)(2,1)}, bf16[32,8,1536]{2,1,0:T(8,128)(2,1)S(1)}, u32[]{:S(2)}) copy-start(bf16[32,8,1536]{2,1,0:T(8,128)(2,1)S(1)} %all-to-all-done.2) | copy-start | bytes 2359300
  79.3 26.1 %all-to-all-start.3 = ((bf16[32,8,1536]{2,1,0:T(8,128)(2,1)}), bf16[32,8,1536]{2,1,0:T(8,128)(2,1)S(1)}, u32[]{:S(2)}, u32[]{:S(2)}) async-start(bf16[32,8,1536]{2,1,0:T(8,128)(2,1)} %bitcast.16), calls=%async_computation.3 | async-start | bytes 1572864 | tf_op jit(solution)/shard_map/all_to_all | solution.py:335
  86.8 1.3 %collective-permute-start = (f32[16,1024]{1,0:T(8,128)S(1)}, f32[16,1024]{1,0:T(8,128)S(1)}, u32[]{:S(2)}, u32[]{:S(2)}) collective-permute-start(f32[16,1024]{1,0:T(8,128)S(1)} %constant_dynamic-slice_fusion), channel_id=1, source_target_pairs={{0,1},{1,0},{2,3},{3,2},{4,5},{5,4},{6,7},{7,6},{8,9},{9,8},{10,11... | collective-permute-start | bytes 196616 | tf_op jit(solution)/shard_map/ppermute | solution.py:339
  88.9 6.9 %collective-permute-start.3 = (f32[16,1024]{1,0:T(8,128)S(1)}, f32[16,1024]{1,0:T(8,128)S(1)}, u32[]{:S(2)}, u32[]{:S(2)}) collective-permute-start(f32[16,1024]{1,0:T(8,128)S(1)} %dynamic-slice_add_fusion), channel_id=1, source_target_pairs={{0,6},{1,7},{2,4},{3,5},{4,2},{5,3},{6,0},{7,1},{8,14},{9,15},{10,... | collective-permute-start | bytes 196616 | tf_op jit(solution)/shard_map/ppermute | solution.py:339
  91.6 5.7 %collective-permute-start.2 = (f32[16,1024]{1,0:T(8,128)S(1)}, f32[16,1024]{1,0:T(8,128)S(1)}, u32[]{:S(2)}, u32[]{:S(2)}) collective-permute-start(f32[16,1024]{1,0:T(8,128)S(1)} %dynamic-slice_add_fusion), channel_id=1, source_target_pairs={{0,4},{1,5},{2,6},{3,7},{4,0},{5,1},{6,2},{7,3},{8,12},{9,13},{10,... | collective-permute-start | bytes 196616 | tf_op jit(solution)/shard_map/ppermute | solution.py:339
  92.2 5.1 %collective-permute-start.1 = (f32[16,1024]{1,0:T(8,128)S(1)}, f32[16,1024]{1,0:T(8,128)S(1)}, u32[]{:S(2)}, u32[]{:S(2)}) collective-permute-start(f32[16,1024]{1,0:T(8,128)S(1)} %dynamic-slice_add_fusion), channel_id=1, source_target_pairs={{0,2},{1,3},{2,0},{3,1},{4,6},{5,7},{6,4},{7,5},{8,10},{9,11},{10,... | collective-permute-start | bytes 196616 | tf_op jit(solution)/shard_map/ppermute | solution.py:339
  97.3 11.4 %collective-permute-start.6 = (bf16[16,1024]{1,0:T(8,128)(2,1)S(1)}, bf16[16,1024]{1,0:T(8,128)(2,1)S(1)}, u32[]{:S(2)}, u32[]{:S(2)}) collective-permute-start(bf16[16,1024]{1,0:T(8,128)(2,1)S(1)} %add_convert_fusion), channel_id=1, source_target_pairs={{0,24},{1,25},{2,26},{3,27},{4,28},{5,29},{6,30},{7,31},{8,16},{9,... | collective-permute-start | bytes 98312 | tf_op jit(solution)/shard_map/ppermute | solution.py:339
  101.5 7.3 %collective-permute-start.5 = (bf16[16,1024]{1,0:T(8,128)(2,1)S(1)}, bf16[16,1024]{1,0:T(8,128)(2,1)S(1)}, u32[]{:S(2)}, u32[]{:S(2)}) collective-permute-start(bf16[16,1024]{1,0:T(8,128)(2,1)S(1)} %add_convert_fusion), channel_id=1, source_target_pairs={{0,16},{1,17},{2,18},{3,19},{4,20},{5,21},{6,22},{7,23},{8,24},{9,... | collective-permute-start | bytes 98312 | tf_op jit(solution)/shard_map/ppermute | solution.py:339
  101.5 7.2 %collective-permute-start.4 = (bf16[16,1024]{1,0:T(8,128)(2,1)S(1)}, bf16[16,1024]{1,0:T(8,128)(2,1)S(1)}, u32[]{:S(2)}, u32[]{:S(2)}) collective-permute-start(bf16[16,1024]{1,0:T(8,128)(2,1)S(1)} %add_convert_fusion), channel_id=1, source_target_pairs={{0,8},{1,9},{2,10},{3,11},{4,12},{5,13},{6,14},{7,15},{8,0},{9,1},... | collective-permute-start | bytes 98312 | tf_op jit(solution)/shard_map/ppermute | solution.py:339
  105.4 0.9 copy-start
  108.8 1.3 %collective-permute-start.7 = (f32[16,1024]{1,0:T(8,128)S(1)}, f32[16,1024]{1,0:T(8,128)S(1)}, u32[]{:S(2)}, u32[]{:S(2)}) collective-permute-start(f32[16,1024]{1,0:T(8,128)S(1)} %add_add_fusion), channel_id=1, source_target_pairs={{0,1},{1,0},{2,3},{3,2},{4,5},{5,4},{6,7},{7,6},{8,9},{9,8},{10,11... | collective-permute-start | bytes 196616 | tf_op jit(solution)/shard_map/ppermute | solution.py:339

commit v4 on v3

--- a/solution.py
+++ b/solution.py
@@ -12,6 +12,7 @@
 BF16 = jnp.bfloat16
 GROUP = 8
 VMEM_BYTES = 60 * 1024 * 1024
+SMALL_VMEM_BYTES = 24 * 1024 * 1024
 
 
 class Layout:
@@ -292,13 +293,13 @@
     out_ref[...] = (pick(lay, ranks, message_ref) + back_ref[...]).astype(BF16)
 
 
-def call(kernel, out_shape, flops, args):
+def call(kernel, out_shape, flops, args, vmem_bytes=VMEM_BYTES):
     moved = sum(a.size * a.dtype.itemsize for a in args)
     moved += sum(o.size * o.dtype.itemsize for o in jax.tree.leaves(out_shape))
     return pl.pallas_call(
         kernel,
         out_shape=out_shape,
-        compiler_params=pltpu.CompilerParams(vmem_limit_bytes=VMEM_BYTES),
+        compiler_params=pltpu.CompilerParams(vmem_limit_bytes=vmem_bytes),
         cost_estimate=pl.CostEstimate(flops=flops, bytes_accessed=moved, transcendentals=0),
     )(*args)
 
@@ -402,12 +403,14 @@
         ],
         2 * place_flops,
         (ids, slots, gates, produced_back, cotangent, tokens, router),
+        SMALL_VMEM_BYTES,
     )
     grad_tokens = call(
         functools.partial(grad_kernel, lay),
         jax.ShapeDtypeStruct((tok_rows, model_width), BF16),
         place_flops,
         (ids, slots, returned_back, router_back),
+        SMALL_VMEM_BYTES,
     )
     grad_router, grad_tokens = sum_over_devices(partial_grad, devices, grad_tokens)
     return (mixed, grad_tokens, grad_router.T)

time: 112 us -> 109 us (0.973)
  waiting for transfers between devices: 39.6 us -> 42.5 us
  Pallas kernels: 40.3 us -> 37.5 us
  local copies, waits for them, and re-layouts: 1.74 us -> 0.05 us
    pallas_call x4, Pallas kernels: 10.5 us -> 7.65 us  [call(): pl.pallas_call(kernel, out_shape=out_shape, compiler_params=pltpu.Compile...]
    all_to_all x4, waiting for transfers between devices: 32.5 us -> 34.1 us  [exchange(): return lax.all_to_all(x, AXES, split_axis=0, concat_axis=0, tiled=True)]
    ppermute x8, waiting for transfers between devices: 7.1 us -> 8.41 us  [from_device(): return lax.ppermute(x, AXES, [(d, d ^ bits) for d in range(devices)])]
  transfers between devices with their start and end apart: 12 -> 12, of which waited for: 8 -> 9; matrix products, arithmetic and copies ran while one was open for 2% -> 0% of each run, Pallas kernels for 34% -> 33%
where the time goes in v4:
time: 109 us
  waiting for transfers between devices  42.5 us (39%)
  Pallas kernels  37.5 us (34%)
  starting transfers between devices  26.9 us (25%)
    all_to_all x4, waiting for transfers between devices, exchange(): return lax.all_to_all(x, AXES, split_axis=0, concat_axis=0, tiled=True)  34.1 us
    pallas_call x2, Pallas kernels, expert_call(): pl.pallas_call(functools.partial(kernel, lay), grid=(ff // tile,), in_spe...  29.8 us
    all_to_all x4, starting transfers between devices, exchange(): return lax.all_to_all(x, AXES, split_axis=0, concat_axis=0, tiled=True)  18.2 us
    ppermute x8, starting transfers between devices, from_device(): return lax.ppermute(x, AXES, [(d, d ^ bits) for d in range(devices)])  8.76 us
    ppermute x8, waiting for transfers between devices, from_device(): return lax.ppermute(x, AXES, [(d, d ^ bits) for d in range(devices)])  8.41 us
    pallas_call x4, Pallas kernels, call(): pl.pallas_call(kernel, out_shape=out_shape, compiler_params=pltpu.Compile...  7.65 us
  transfers between devices with their start and end apart: 12, of which 9 were waited for; matrix products, arithmetic and copies ran while one was open for 0% of the time, Pallas kernels for 33%

profile of v4, /device:TPU:0, one launch (start us, length us, event | category | flops | bytes accessed | tf_op | source)
XLA Modules:
  0.0 108.5 jit_solution(10324887854461934500)
XLA Ops:
  0.6 2.2 %shard_map.95 = bf16[256,1536]{1,0:T(8,128)(2,1)} custom-call(s32[2,128]{1,0:T(2,128)} %bitcast.17, s32[2,128]{1,0:T(2,128)} %bitcast.21, bf16[128,1024]{1,0:T(8,128)(2,1)} %tokens_ref.5), custom_call_target="tpu_custom_call" | custom-call | flops 134217728 | bytes 1050624 | tf_op jit(solution)/shard_map/pallas_call | solution.py:299
  2.8 7.3 %all-to-all-start = ((bf16[32,8,1536]{2,1,0:T(8,128)(2,1)}), bf16[32,8,1536]{2,1,0:T(8,128)(2,1)S(1)}, u32[]{:S(2)}, u32[]{:S(2)}) async-start(bf16[32,8,1536]{2,1,0:T(8,128)(2,1)} %bitcast.25), calls=%async_computation | async-start | bytes 1572864 | tf_op jit(solution)/shard_map/all_to_all | solution.py:336
  10.2 2.9 %shard_map.94 = (bf16[256,1536]{1,0:T(8,128)(2,1)}, f32[2,128]{1,0:T(2,128)}) custom-call(s32[2,128]{1,0:T(2,128)} %bitcast.18, s32[2,128]{1,0:T(2,128)} %bitcast.22, bf16[128,1024]{1,0:T(8,128)(2,1)} %tokens_ref.5, bf16[32,1024]{1,0:T(8,128)(2,1)} %bitcast.15, bf16[128,1024]{1,0:T(8,128)(2,1)} %cot_ref.3), custom_call_target="tpu_custom_call" | custom-call | flops 268435456 | bytes 1379328 | tf_op jit(solution)/shard_map/pallas_call | solution.py:299
  13.0 17.8 %all-to-all-done = bf16[32,8,1536]{2,1,0:T(8,128)(2,1)S(1)} async-done(((bf16[32,8,1536]{2,1,0:T(8,128)(2,1)}), bf16[32,8,1536]{2,1,0:T(8,128)(2,1)S(1)}, u32[]{:S(2)}, u32[]{:S(2)}) %all-to-all-start) | async-done | bytes 786464 | tf_op jit(solution)/shard_map/all_to_all | solution.py:336
  30.8 0.0 copy-start.6
  30.8 3.6 %all-to-all-start.1 = ((bf16[32,8,1536]{2,1,0:T(8,128)(2,1)}), bf16[32,8,1536]{2,1,0:T(8,128)(2,1)S(1)}, u32[]{:S(2)}, u32[]{:S(2)}) async-start(bf16[32,8,1536]{2,1,0:T(8,128)(2,1)} %bitcast.29), calls=%async_computation.1 | async-start | bytes 1572864 | tf_op jit(solution)/shard_map/all_to_all | solution.py:336
  34.4 0.0 copy-done.6
  34.4 14.7 %shard_map.96 = (bf16[256,1536]{1,0:T(8,128)(2,1)}, bf16[384,4096]{1,0:T(8,128)(2,1)}) custom-call(bf16[256,1536]{1,0:T(8,128)(2,1)} %bitcast.27, bf16[1,1024,4096]{2,1,0:T(8,128)(2,1)} %win_ref.3, bf16[1,4096,1024]{2,1,0:T(8,128)(2,1)} %wout_ref.3), custom_call_target="tpu_custom_call" | custom-call | flops 6442450944 | bytes 21495808 | tf_op jit(solution)/shard_map/pallas_call | solution.py:319
  49.1 5.9 %all-to-all-done.1 = bf16[32,8,1536]{2,1,0:T(8,128)(2,1)S(1)} async-done(((bf16[32,8,1536]{2,1,0:T(8,128)(2,1)}), bf16[32,8,1536]{2,1,0:T(8,128)(2,1)S(1)}, u32[]{:S(2)}, u32[]{:S(2)}) %all-to-all-start.1) | async-done | bytes 786464 | tf_op jit(solution)/shard_map/all_to_all | solution.py:336
  55.0 0.0 copy-start.7
  55.0 3.6 %all-to-all-start.2 = ((bf16[32,8,1536]{2,1,0:T(8,128)(2,1)}), bf16[32,8,1536]{2,1,0:T(8,128)(2,1)S(1)}, u32[]{:S(2)}, u32[]{:S(2)}) async-start(bf16[32,8,1536]{2,1,0:T(8,128)(2,1)} %bitcast.30), calls=%async_computation.2 | async-start | bytes 1572864 | tf_op jit(solution)/shard_map/all_to_all | solution.py:336
  58.7 0.0 copy-done.7
  58.7 0.0 copy-start
  58.7 0.0 copy-start.1
  58.7 0.0 copy-start.2
  58.7 0.0 copy-start.3
  58.7 0.0 copy-start.4
  58.7 0.0 copy-start.5
  58.7 15.1 %shard_map.97 = bf16[256,1536]{1,0:T(8,128)(2,1)} custom-call(bf16[256,1536]{1,0:T(8,128)(2,1)} %bitcast.28, bf16[384,4096]{1,0:T(8,128)(2,1)} %get-tuple-element.27.hidden_ref, bf16[1,1024,4096]{2,1,0:T(8,128)(2,1)} %win_ref.3, bf16[1,4096,1024]{2,1,0:T(8,128)(2,1)} %wout_ref.3), custom_call_target="tpu_custom_call" | custom-call | flops 6442450944 | bytes 21495808 | tf_op jit(solution)/shard_map/pallas_call | solution.py:319
  73.9 5.4 %all-to-all-done.2 = bf16[32,8,1536]{2,1,0:T(8,128)(2,1)S(1)} async-done(((bf16[32,8,1536]{2,1,0:T(8,128)(2,1)}), bf16[32,8,1536]{2,1,0:T(8,128)(2,1)S(1)}, u32[]{:S(2)}, u32[]{:S(2)}) %all-to-all-start.2) | async-done | bytes 786464 | tf_op jit(solution)/shard_map/all_to_all | solution.py:336
  79.3 3.6 %all-to-all-start.3 = ((bf16[32,8,1536]{2,1,0:T(8,128)(2,1)}), bf16[32,8,1536]{2,1,0:T(8,128)(2,1)S(1)}, u32[]{:S(2)}, u32[]{:S(2)}) async-start(bf16[32,8,1536]{2,1,0:T(8,128)(2,1)} %bitcast.26), calls=%async_computation.3 | async-start | bytes 1572864 | tf_op jit(solution)/shard_map/all_to_all | solution.py:336
  82.9 0.0 copy-done
  82.9 0.0 copy-done.1
  82.9 0.0 copy-done.2
  82.9 0.0 copy-done.3
  83.0 0.0 copy-done.4
  83.0 0.0 copy-done.5
  83.0 1.5 %shard_map.98 = (bf16[128,1024]{1,0:T(8,128)(2,1)}, f32[128,1024]{1,0:T(8,128)S(1)}, f32[32,1024]{1,0:T(8,128)S(1)}) custom-call(s32[2,128]{1,0:T(2,128)S(1)} %bitcast.19, s32[2,128]{1,0:T(2,128)S(1)} %bitcast.23, f32[2,128]{1,0:T(2,128)S(1)} %copy-done.5, bf16[256,1536]{1,0:T(8,128)(2,1)S(1)} %bitcast.14, bf16[128,1024]{1,0:T(8,128)(2,1)S(1)} %copy-done.1, ...), custom_call_target="tpu_custom_call" | custom-call | flops 268435456 | bytes 2296832 | tf_op jit(solution)/shard_map/pallas_call | solution.py:299
  84.4 0.2 collective-permute-start
  84.7 1.0 collective-permute-done
  85.7 2.7 %collective-permute-start.3 = (f32[16,1024]{1,0:T(8,128)S(1)}, f32[16,1024]{1,0:T(8,128)S(1)}, u32[]{:S(2)}, u32[]{:S(2)}) collective-permute-start(f32[16,1024]{1,0:T(8,128)S(1)} %dynamic-slice_add_fusion), channel_id=1, source_target_pairs={{0,6},{1,7},{2,4},{3,5},{4,2},{5,3},{6,0},{7,1},{8,14},{9,15},{10,... | collective-permute-start | bytes 196616 | tf_op jit(solution)/shard_map/ppermute | solution.py:340
  88.5 0.6 collective-permute-start.2
  89.0 0.3 collective-permute-start.1
  89.3 4.2 %collective-permute-done.3 = f32[16,1024]{1,0:T(8,128)S(1)} collective-permute-done((f32[16,1024]{1,0:T(8,128)S(1)}, f32[16,1024]{1,0:T(8,128)S(1)}, u32[]{:S(2)}, u32[]{:S(2)}) %collective-permute-start.3) | collective-permute-done | bytes 65568 | tf_op jit(solution)/shard_map/ppermute | solution.py:340
  93.5 1.7 %collective-permute-done.2 = f32[16,1024]{1,0:T(8,128)S(1)} collective-permute-done((f32[16,1024]{1,0:T(8,128)S(1)}, f32[16,1024]{1,0:T(8,128)S(1)}, u32[]{:S(2)}, u32[]{:S(2)}) %collective-permute-start.2) | collective-permute-done | bytes 65568 | tf_op jit(solution)/shard_map/ppermute | solution.py:340
  95.2 0.2 collective-permute-done.1
  95.5 4.2 %collective-permute-start.6 = (bf16[16,1024]{1,0:T(8,128)(2,1)S(1)}, bf16[16,1024]{1,0:T(8,128)(2,1)S(1)}, u32[]{:S(2)}, u32[]{:S(2)}) collective-permute-start(bf16[16,1024]{1,0:T(8,128)(2,1)S(1)} %add_convert_fusion), channel_id=1, source_target_pairs={{0,24},{1,25},{2,26},{3,27},{4,28},{5,29},{6,30},{7,31},{8,16},{9,... | collective-permute-start | bytes 98312 | tf_op jit(solution)/shard_map/ppermute | solution.py:340
  99.7 0.0 collective-permute-start.5
  99.7 0.6 collective-permute-start.4
  100.3 5.1 %all-to-all-done.3 = bf16[32,8,1536]{2,1,0:T(8,128)(2,1)S(1)} async-done(((bf16[32,8,1536]{2,1,0:T(8,128)(2,1)}), bf16[32,8,1536]{2,1,0:T(8,128)(2,1)S(1)}, u32[]{:S(2)}, u32[]{:S(2)}) %all-to-all-start.3) | async-done | bytes 786464 | tf_op jit(solution)/shard_map/all_to_all | solution.py:336
  105.4 1.1 %shard_map.99 = bf16[128,1024]{1,0:T(8,128)(2,1)} custom-call(s32[2,128]{1,0:T(2,128)S(1)} %bitcast.20, s32[2,128]{1,0:T(2,128)S(1)} %bitcast.24, bf16[256,1536]{1,0:T(8,128)(2,1)S(1)} %bitcast.13, f32[128,1024]{1,0:T(8,128)S(1)} %get-tuple-element.32.back_ref), custom_call_target="tpu_custom_call" | custom-call | flops 134217728 | bytes 1574912 | tf_op jit(solution)/shard_map/pallas_call | solution.py:299
  106.5 0.0 collective-permute-done.6
  106.5 0.0 collective-permute-done.5
  106.5 0.0 collective-permute-done.4
  106.5 0.1 collective-permute-start.7
  106.6 1.2 %collective-permute-done.7 = f32[16,1024]{1,0:T(8,128)S(1)} collective-permute-done((f32[16,1024]{1,0:T(8,128)S(1)}, f32[16,1024]{1,0:T(8,128)S(1)}, u32[]{:S(2)}, u32[]{:S(2)}) %collective-permute-start.7) | collective-permute-done | bytes 65568 | tf_op jit(solution)/shard_map/ppermute | solution.py:340
  107.9 0.7 maximum_bitcast_fusion
  (5 shorter events, 0.1 us)
Async XLA Ops:
  2.8 27.9 %all-to-all-start = ((bf16[32,8,1536]{2,1,0:T(8,128)(2,1)}), bf16[32,8,1536]{2,1,0:T(8,128)(2,1)S(1)}, u32[]{:S(2)}, u32[]{:S(2)}) async-start(bf16[32,8,1536]{2,1,0:T(8,128)(2,1)} %bitcast.25), calls=%async_computation | async-start | bytes 1572864 | tf_op jit(solution)/shard_map/all_to_all | solution.py:336
  30.8 3.6 %copy-start.6 = (bf16[32,8,1536]{2,1,0:T(8,128)(2,1)}, bf16[32,8,1536]{2,1,0:T(8,128)(2,1)S(1)}, u32[]{:S(2)}) copy-start(bf16[32,8,1536]{2,1,0:T(8,128)(2,1)S(1)} %all-to-all-done) | copy-start | bytes 2359300
  30.8 24.2 %all-to-all-start.1 = ((bf16[32,8,1536]{2,1,0:T(8,128)(2,1)}), bf16[32,8,1536]{2,1,0:T(8,128)(2,1)S(1)}, u32[]{:S(2)}, u32[]{:S(2)}) async-start(bf16[32,8,1536]{2,1,0:T(8,128)(2,1)} %bitcast.29), calls=%async_computation.1 | async-start | bytes 1572864 | tf_op jit(solution)/shard_map/all_to_all | solution.py:336
  55.0 3.6 %copy-start.7 = (bf16[32,8,1536]{2,1,0:T(8,128)(2,1)}, bf16[32,8,1536]{2,1,0:T(8,128)(2,1)S(1)}, u32[]{:S(2)}) copy-start(bf16[32,8,1536]{2,1,0:T(8,128)(2,1)S(1)} %all-to-all-done.1) | copy-start | bytes 2359300
  55.0 24.2 %all-to-all-start.2 = ((bf16[32,8,1536]{2,1,0:T(8,128)(2,1)}), bf16[32,8,1536]{2,1,0:T(8,128)(2,1)S(1)}, u32[]{:S(2)}, u32[]{:S(2)}) async-start(bf16[32,8,1536]{2,1,0:T(8,128)(2,1)} %bitcast.30), calls=%async_computation.2 | async-start | bytes 1572864 | tf_op jit(solution)/shard_map/all_to_all | solution.py:336
  58.7 24.3 %copy-start = (bf16[128,1024]{1,0:T(8,128)(2,1)S(1)}, bf16[128,1024]{1,0:T(8,128)(2,1)}, u32[]{:S(2)}) copy-start(bf16[128,1024]{1,0:T(8,128)(2,1)} %tokens_ref.5) | copy-start | bytes 786436
  58.7 24.3 %copy-start.1 = (bf16[128,1024]{1,0:T(8,128)(2,1)S(1)}, bf16[128,1024]{1,0:T(8,128)(2,1)}, u32[]{:S(2)}) copy-start(bf16[128,1024]{1,0:T(8,128)(2,1)} %cot_ref.3) | copy-start | bytes 786436
  58.7 24.3 %copy-start.2 = (bf16[1024,32]{0,1:T(8,128)(2,1)S(1)}, bf16[1024,32]{0,1:T(8,128)(2,1)}, u32[]{:S(2)}) copy-start(bf16[1024,32]{0,1:T(8,128)(2,1)} %param.8) | copy-start | bytes 196612
  58.7 24.2 %copy-start.3 = (s32[128,2]{0,1:T(2,128)S(1)}, s32[128,2]{0,1:T(2,128)}, u32[]{:S(2)}) copy-start(s32[128,2]{0,1:T(2,128)} %param.11) | copy-start | bytes 3076
  58.7 24.2 %copy-start.4 = (s32[128,2]{0,1:T(2,128)S(1)}, s32[128,2]{0,1:T(2,128)}, u32[]{:S(2)}) copy-start(s32[128,2]{0,1:T(2,128)} %param.12) | copy-start | bytes 3076
  58.7 24.2 %copy-start.5 = (f32[2,128]{1,0:T(2,128)S(1)}, f32[2,128]{1,0:T(2,128)}, u32[]{:S(2)}) copy-start(f32[2,128]{1,0:T(2,128)} %get-tuple-element.21.gates_ref) | copy-start | bytes 3076
  79.3 26.1 %all-to-all-start.3 = ((bf16[32,8,1536]{2,1,0:T(8,128)(2,1)}), bf16[32,8,1536]{2,1,0:T(8,128)(2,1)S(1)}, u32[]{:S(2)}, u32[]{:S(2)}) async-start(bf16[32,8,1536]{2,1,0:T(8,128)(2,1)} %bitcast.26), calls=%async_computation.3 | async-start | bytes 1572864 | tf_op jit(solution)/shard_map/all_to_all | solution.py:336
  84.4 1.3 %collective-permute-start = (f32[16,1024]{1,0:T(8,128)S(1)}, f32[16,1024]{1,0:T(8,128)S(1)}, u32[]{:S(2)}, u32[]{:S(2)}) collective-permute-start(f32[16,1024]{1,0:T(8,128)S(1)} %constant_dynamic-slice_fusion), channel_id=1, source_target_pairs={{0,1},{1,0},{2,3},{3,2},{4,5},{5,4},{6,7},{7,6},{8,9},{9,8},{10,11... | collective-permute-start | bytes 196616 | tf_op jit(solution)/shard_map/ppermute | solution.py:340
  85.7 7.8 %collective-permute-start.3 = (f32[16,1024]{1,0:T(8,128)S(1)}, f32[16,1024]{1,0:T(8,128)S(1)}, u32[]{:S(2)}, u32[]{:S(2)}) collective-permute-start(f32[16,1024]{1,0:T(8,128)S(1)} %dynamic-slice_add_fusion), channel_id=1, source_target_pairs={{0,6},{1,7},{2,4},{3,5},{4,2},{5,3},{6,0},{7,1},{8,14},{9,15},{10,... | collective-permute-start | bytes 196616 | tf_op jit(solution)/shard_map/ppermute | solution.py:340
  88.5 6.7 %collective-permute-start.2 = (f32[16,1024]{1,0:T(8,128)S(1)}, f32[16,1024]{1,0:T(8,128)S(1)}, u32[]{:S(2)}, u32[]{:S(2)}) collective-permute-start(f32[16,1024]{1,0:T(8,128)S(1)} %dynamic-slice_add_fusion), channel_id=1, source_target_pairs={{0,4},{1,5},{2,6},{3,7},{4,0},{5,1},{6,2},{7,3},{8,12},{9,13},{10,... | collective-permute-start | bytes 196616 | tf_op jit(solution)/shard_map/ppermute | solution.py:340
  89.0 6.4 %collective-permute-start.1 = (f32[16,1024]{1,0:T(8,128)S(1)}, f32[16,1024]{1,0:T(8,128)S(1)}, u32[]{:S(2)}, u32[]{:S(2)}) collective-permute-start(f32[16,1024]{1,0:T(8,128)S(1)} %dynamic-slice_add_fusion), channel_id=1, source_target_pairs={{0,2},{1,3},{2,0},{3,1},{4,6},{5,7},{6,4},{7,5},{8,10},{9,11},{10,... | collective-permute-start | bytes 196616 | tf_op jit(solution)/shard_map/ppermute | solution.py:340
  95.5 11.0 %collective-permute-start.6 = (bf16[16,1024]{1,0:T(8,128)(2,1)S(1)}, bf16[16,1024]{1,0:T(8,128)(2,1)S(1)}, u32[]{:S(2)}, u32[]{:S(2)}) collective-permute-start(bf16[16,1024]{1,0:T(8,128)(2,1)S(1)} %add_convert_fusion), channel_id=1, source_target_pairs={{0,24},{1,25},{2,26},{3,27},{4,28},{5,29},{6,30},{7,31},{8,16},{9,... | collective-permute-start | bytes 98312 | tf_op jit(solution)/shard_map/ppermute | solution.py:340
  99.7 6.8 %collective-permute-start.5 = (bf16[16,1024]{1,0:T(8,128)(2,1)S(1)}, bf16[16,1024]{1,0:T(8,128)(2,1)S(1)}, u32[]{:S(2)}, u32[]{:S(2)}) collective-permute-start(bf16[16,1024]{1,0:T(8,128)(2,1)S(1)} %add_convert_fusion), channel_id=1, source_target_pairs={{0,16},{1,17},{2,18},{3,19},{4,20},{5,21},{6,22},{7,23},{8,24},{9,... | collective-permute-start | bytes 98312 | tf_op jit(solution)/shard_map/ppermute | solution.py:340
  99.7 6.8 %collective-permute-start.4 = (bf16[16,1024]{1,0:T(8,128)(2,1)S(1)}, bf16[16,1024]{1,0:T(8,128)(2,1)S(1)}, u32[]{:S(2)}, u32[]{:S(2)}) collective-permute-start(bf16[16,1024]{1,0:T(8,128)(2,1)S(1)} %add_convert_fusion), channel_id=1, source_target_pairs={{0,8},{1,9},{2,10},{3,11},{4,12},{5,13},{6,14},{7,15},{8,0},{9,1},... | collective-permute-start | bytes 98312 | tf_op jit(solution)/shard_map/ppermute | solution.py:340
  106.5 1.3 %collective-permute-start.7 = (f32[16,1024]{1,0:T(8,128)S(1)}, f32[16,1024]{1,0:T(8,128)S(1)}, u32[]{:S(2)}, u32[]{:S(2)}) collective-permute-start(f32[16,1024]{1,0:T(8,128)S(1)} %add_add_fusion), channel_id=1, source_target_pairs={{0,1},{1,0},{2,3},{3,2},{4,5},{5,4},{6,7},{7,6},{8,9},{9,8},{10,11... | collective-permute-start | bytes 196616 | tf_op jit(solution)/shard_map/ppermute | solution.py:340

commit v5 on v1

--- a/solution.py
+++ b/solution.py
@@ -12,6 +12,7 @@
 BF16 = jnp.bfloat16
 GROUP = 8
 VMEM_BYTES = 60 * 1024 * 1024
+SMALL_VMEM_BYTES = 24 * 1024 * 1024
 
 
 class Layout:
@@ -76,9 +77,9 @@
 class Order:
     def __init__(self, high, low, by_high):
         self.high, self.low, self.by_high = high, low, by_high
-        self.arrays = high if by_high else low
-        self.inside = low if by_high else high
-        self.rows = self.inside * GROUP
+        self.arrays = high if by_high else 1
+        self.blocks = high * low
+        self.rows = self.blocks // self.arrays * GROUP
 
     def position(self, block):
         if self.by_high:
@@ -210,13 +211,20 @@
 
 def repack_kernel(order, *refs):
     sources, outs = refs[: order.arrays], refs[order.arrays :]
-    for part, out_ref in enumerate(outs):
-        blocks = [ref[part * GROUP : (part + 1) * GROUP, :] for ref in sources]
-        out_ref[...] = jnp.concatenate(blocks, axis=0)
+    if order.by_high:
+        blocks = [
+            ref[part * GROUP : (part + 1) * GROUP, :] for part in range(order.low) for ref in sources
+        ]
+        outs[0][...] = jnp.concatenate(blocks, axis=0)
+    else:
+        for plane, out_ref in enumerate(outs):
+            starts = [(part * order.high + plane) * GROUP for part in range(order.low)]
+            blocks = [sources[0][start : start + GROUP, :] for start in starts]
+            out_ref[...] = jnp.concatenate(blocks, axis=0)
 
 
 def blocks_of(order, ids):
-    return order.position(ids ^ this_device())
+    return order.position(ids ^ (this_device() & -order.low))
 
 
 def send_tokens_kernel(lay, order, ids_ref, slots_ref, tokens_ref, *out_refs):
@@ -344,13 +352,13 @@
     out_ref[...] = (pick(lay, ranks, message) + back_ref[...]).astype(BF16)
 
 
-def call(kernel, out_shape, flops, args):
+def call(kernel, out_shape, flops, args, vmem_bytes=VMEM_BYTES):
     moved = sum(a.size * a.dtype.itemsize for a in args)
     moved += sum(o.size * o.dtype.itemsize for o in jax.tree.leaves(out_shape))
     return pl.pallas_call(
         kernel,
         out_shape=out_shape,
-        compiler_params=pltpu.CompilerParams(vmem_limit_bytes=VMEM_BYTES),
+        compiler_params=pltpu.CompilerParams(vmem_limit_bytes=vmem_bytes),
         cost_estimate=pl.CostEstimate(flops=flops, bytes_accessed=moved, transcendentals=0),
     )(*args)
 
@@ -362,7 +370,7 @@
 def expert_call(kernel, lay, order, out_order, message, hidden, in_weight, out_weight):
     ff = in_weight.shape[2]
     tile = min(512, ff)
-    rows = order.arrays * order.inside * lay.rows
+    rows = order.blocks * lay.rows
     win = pl.BlockSpec((1, lay.width, tile), lambda j: (0, 0, j))
     wout = pl.BlockSpec((1, tile, lay.width), lambda j: (0, j, 0))
     hid = pl.BlockSpec((rows, tile), lambda j: (0, j))
@@ -391,15 +399,27 @@
 def repack(lay, order, message):
     other = Order(order.high, order.low, not order.by_high)
     return call(
-        functools.partial(repack_kernel, order), messages_of(lay, other), 0, tuple(message)
-    )
-
-
-def step_of(order, message):
-    devices = order.high * order.low
-    unit = order.low if order.by_high else 1
+        functools.partial(repack_kernel, order),
+        messages_of(lay, other),
+        0,
+        tuple(message),
+        SMALL_VMEM_BYTES,
+    )
+
+
+def over_planes(order, message):
+    devices = order.blocks
     return [message[0]] + [
-        from_device(message[part], part * unit, devices) for part in range(1, order.arrays)
+        from_device(message[part], part * order.low, devices) for part in range(1, order.high)
+    ]
+
+
+def in_plane(order, message):
+    groups = [list(range(at, at + order.low)) for at in range(0, order.blocks, order.low)]
+    return [
+        lax.all_to_all(
+            message[0], AXES, split_axis=0, concat_axis=0, tiled=True, axis_index_groups=groups
+        )
     ]
 
 
@@ -410,6 +430,10 @@
 
 def from_device(x, bits, devices):
     return lax.ppermute(x, AXES, [(d, d ^ bits) for d in range(devices)])
+
+
+def sum_of_pairs(own, near, far, both):
+    return (own + near) + (far + both)
 
 
 def sum_over_devices(x, devices):
@@ -420,12 +444,11 @@
     own = own + from_device(other, 1, devices)
     bit = 2
     while bit < devices:
-        if 2 * bit < devices:
-            near = own + from_device(own, bit, devices)
-            far = from_device(own, 2 * bit, devices) + from_device(own, 3 * bit, devices)
-            own = near + far
-        else:
-            own = own + from_device(own, bit, devices)
+        sent = own if bit == 2 else own.astype(BF16)
+        steps = [1, 2, 3] if 2 * bit < devices else [1]
+        terms = [from_device(sent, step * bit, devices) for step in steps]
+        terms = [term.astype(F32) for term in [sent] + terms]
+        own = sum_of_pairs(*terms) if len(terms) == 4 else terms[0] + terms[1]
         bit *= 4
     other = from_device(own, 1, devices)
     first = core == 0
@@ -448,31 +471,31 @@
         place_flops,
         (ids, slots, tokens),
     )
-    token_half = step_of(by_high, sent_tokens)
+    token_half = over_planes(by_high, sent_tokens)
+    sent_tokens, (late_tokens,) = tied(sent_tokens, [tokens])
 
     gates, *sent_grads = call(
         functools.partial(send_grads_kernel, lay, by_low),
         [jax.ShapeDtypeStruct((2, tok_rows), F32)] + messages_of(lay, by_low),
         2 * place_flops,
-        (ids, slots, tokens, router, cotangent),
-    )
-    grad_half = repack(lay, by_low, step_of(by_low, sent_grads))
+        (ids, slots, late_tokens, router, cotangent),
+    )
+    grad_half = repack(lay, by_low, in_plane(by_low, sent_grads))
     token_half, grad_half = tied(token_half, grad_half)
-    grad_rows = step_of(by_high, grad_half)
-    arrived = step_of(by_low, repack(lay, by_high, token_half))
+    grad_rows = over_planes(by_high, grad_half)
+    arrived = in_plane(by_low, repack(lay, by_high, token_half))
 
     hidden, *produced = expert_call(
         forward_kernel, lay, by_low, by_high, arrived, None, in_weight, out_weight
     )
     produced, grad_rows = tied(produced, grad_rows)
-    produced_half = step_of(by_high, produced)
+    produced_half = over_planes(by_high, produced)
     returned = expert_call(
-        backward_kernel, lay, by_high, by_low, grad_rows, hidden, in_weight, out_weight
-    )
-    returned_half = repack(lay, by_low, step_of(by_low, returned))
-    produced_half, returned_half = tied(produced_half, returned_half)
-    returned_back = step_of(by_high, returned_half)
-    produced_back = step_of(by_low, repack(lay, by_high, produced_half))
+        backward_kernel, lay, by_high, by_high, grad_rows, hidden, in_weight, out_weight
+    )
+    returned, produced_half = tied(returned, produced_half)
+    returned_half = over_planes(by_high, returned)
+    produced_back = in_plane(by_low, repack(lay, by_high, produced_half))
 
     mixed, router_back, partial_grad = call(
         functools.partial(mix_kernel, lay, by_low),
@@ -483,13 +506,17 @@
         ],
         2 * place_flops,
         (ids, slots, gates, cotangent, tokens, router, *produced_back),
-    )
+        SMALL_VMEM_BYTES,
+    )
+    returned_half, produced_back = tied(returned_half, produced_back)
+    returned_back = in_plane(by_low, repack(lay, by_high, returned_half))
     grad_router = sum_over_devices(partial_grad, devices).T
     grad_tokens = call(
-        functools.partial(grad_kernel, lay, by_high),
+        functools.partial(grad_kernel, lay, by_low),
         jax.ShapeDtypeStruct((tok_rows, model_width), BF16),
         place_flops,
         (ids, slots, router_back, *returned_back),
+        SMALL_VMEM_BYTES,
     )
     return (mixed, grad_tokens, grad_router)
 

time: 163 us -> 143 us (0.88); the launches traced: 162 us -> 141 us
  starting transfers between devices: 59.5 us -> 48.9 us
  Pallas kernels: 48.7 us -> 40.6 us
  local copies, waits for them, and re-layouts: 6.36 us -> 3.48 us
    ppermute x48 -> x20, starting transfers between devices: 59.5 us -> 32.4 us  [from_device(): return lax.ppermute(x, AXES, [(d, d ^ bits) for d in range(devices)])]
    all_to_all x0 -> x4, waiting for transfers between devices: none -> 24.3 us  [in_plane(): lax.all_to_all(message[0], AXES, split_axis=0, concat_axis=0, tiled=True,...]
    ppermute x48 -> x20, waiting for transfers between devices: 45.4 us -> 21.9 us  [from_device(): return lax.ppermute(x, AXES, [(d, d ^ bits) for d in range(devices)])]
    all_to_all x0 -> x4, starting transfers between devices: none -> 16.5 us  [in_plane(): lax.all_to_all(message[0], AXES, split_axis=0, concat_axis=0, tiled=True,...]
    pallas_call x8, Pallas kernels: 19 us -> 10.8 us  [call(): pl.pallas_call(kernel, out_shape=out_shape, compiler_params=pltpu.Compile...]
    unnamed x86 -> x28, local copies, waits for them, and re-layouts: 5.52 us -> 3.47 us
  transfers between devices with their start and end apart: 48 -> 24, of which waited for: 21 -> 10; matrix products, arithmetic and copies ran while one was open for 0% -> 1% of each run, Pallas kernels for 15% -> 22%
where the time goes in v5:
time: 143 us; the launch traced here: 141 us
  starting transfers between devices  48.9 us (34%)
  waiting for transfers between devices  46.2 us (32%)
  Pallas kernels  40.6 us (28%)
  local copies, waits for them, and re-layouts  3.48 us (2%)
    ppermute x20, starting transfers between devices, from_device(): return lax.ppermute(x, AXES, [(d, d ^ bits) for d in range(devices)])  32.4 us
    pallas_call x2, Pallas kernels, expert_call(): pl.pallas_call(functools.partial(kernel, lay, order, out_order), grid=(ff...  29.8 us
    all_to_all x4, waiting for transfers between devices, in_plane(): lax.all_to_all(message[0], AXES, split_axis=0, concat_axis=0, tiled=True,...  24.3 us
    ppermute x20, waiting for transfers between devices, from_device(): return lax.ppermute(x, AXES, [(d, d ^ bits) for d in range(devices)])  21.9 us
    all_to_all x4, starting transfers between devices, in_plane(): lax.all_to_all(message[0], AXES, split_axis=0, concat_axis=0, tiled=True,...  16.5 us
    pallas_call x8, Pallas kernels, call(): pl.pallas_call(kernel, out_shape=out_shape, compiler_params=pltpu.Compile...  10.8 us
    unnamed x28, local copies, waits for them, and re-layouts  3.47 us
  transfers between devices with their start and end apart: 24, of which 10 were waited for; matrix products, arithmetic and copies ran while one was open for 1% of the time, Pallas kernels for 22%

profile of v5, /device:TPU:0, one launch (start us, length us, event | category | flops | bytes accessed | tf_op | source)
XLA Modules:
  0.0 140.7 jit_solution(41741147691611365)
XLA Ops:
  0.6 2.2 %shard_map.94 = (bf16[64,1536]{1,0:T(8,128)(2,1)}, bf16[64,1536]{1,0:T(8,128)(2,1)}, bf16[64,1536]{1,0:T(8,128)(2,1)}, bf16[64,1536]{1,0:T(8,128)(2,1)}) custom-call(s32[2,128]{1,0:T(2,128)} %bitcast.18, s32[2,128]{1,0:T(2,128)} %bitcast.22, bf16[128,1024]{1,0:T(8,128)(2,1)} %tokens_ref.4), custom_call_target="tpu_custom_call" | custom-call | flops 134217728 | bytes 1050624 | tf_op jit(solution)/shard_map/pallas_call | solution.py:358
  2.8 2.9 %shard_map.95 = (f32[2,128]{1,0:T(2,128)}, bf16[256,1536]{1,0:T(8,128)(2,1)}) custom-call(s32[2,128]{1,0:T(2,128)} %bitcast.19, s32[2,128]{1,0:T(2,128)} %bitcast.23, bf16[128,1024]{1,0:T(8,128)(2,1)} %tokens_ref.4, bf16[32,1024]{1,0:T(8,128)(2,1)} %bitcast.16, bf16[128,1024]{1,0:T(8,128)(2,1)} %cot_ref.3), custom_call_target="tpu_custom_call" | custom-call | flops 268435456 | bytes 1379328 | tf_op jit(solution)/shard_map/pallas_call | solution.py:358
  5.7 5.2 %all-to-all-start = ((bf16[8,32,1536]{2,1,0:T(8,128)(2,1)}), bf16[8,32,1536]{2,1,0:T(8,128)(2,1)S(1)}, u32[]{:S(2)}, u32[]{:S(2)}) async-start(bf16[8,32,1536]{2,1,0:T(8,128)(2,1)} %bitcast.27), calls=%async_computation | async-start | bytes 1572864 | tf_op jit(solution)/shard_map/all_to_all | solution.py:420
  10.8 1.6 %collective-permute-start = (bf16[64,1536]{1,0:T(8,128)(2,1)}, bf16[64,1536]{1,0:T(8,128)(2,1)S(1)}, u32[]{:S(2)}, u32[]{:S(2)}) collective-permute-start(bf16[64,1536]{1,0:T(8,128)(2,1)} %get-tuple-element.55), channel_id=1, source_target_pairs={{0,8},{1,9},{2,10},{3,11},{4,12},{5,13},{6,14},{7,15},{8,0},{9,1},... | collective-permute-start | bytes 589832 | tf_op jit(solution)/shard_map/ppermute | solution.py:432
  12.4 2.6 %collective-permute-start.1 = (bf16[64,1536]{1,0:T(8,128)(2,1)}, bf16[64,1536]{1,0:T(8,128)(2,1)S(1)}, u32[]{:S(2)}, u32[]{:S(2)}) collective-permute-start(bf16[64,1536]{1,0:T(8,128)(2,1)} %get-tuple-element.56), channel_id=1, source_target_pairs={{0,16},{1,17},{2,18},{3,19},{4,20},{5,21},{6,22},{7,23},{8,24},{9,... | collective-permute-start | bytes 589832 | tf_op jit(solution)/shard_map/ppermute | solution.py:432
  15.0 0.2 collective-permute-start.2
  15.2 7.3 %all-to-all-done = bf16[8,32,1536]{2,1,0:T(8,128)(2,1)S(1)} async-done(((bf16[8,32,1536]{2,1,0:T(8,128)(2,1)}), bf16[8,32,1536]{2,1,0:T(8,128)(2,1)S(1)}, u32[]{:S(2)}, u32[]{:S(2)}) %all-to-all-start) | async-done | bytes 786464 | tf_op jit(solution)/shard_map/all_to_all | solution.py:420
  22.5 0.1 shard_map.96
  22.6 0.7 copy-done.9
  23.3 6.4 %collective-permute-done.1.refs_2_ = bf16[64,1536]{1,0:T(8,128)(2,1)S(1)} collective-permute-done((bf16[64,1536]{1,0:T(8,128)(2,1)}, bf16[64,1536]{1,0:T(8,128)(2,1)S(1)}, u32[]{:S(2)}, u32[]{:S(2)}) %collective-permute-start.1) | collective-permute-done | bytes 196640 | tf_op jit(solution)/shard_map/ppermute | solution.py:432
  29.7 0.0 collective-permute-done.2.refs_3_
  29.7 0.9 copy-done.4
  30.7 1.0 shard_map.97
  31.7 4.2 %all-to-all-start.1 = ((bf16[8,32,1536]{2,1,0:T(8,128)(2,1)}), bf16[8,32,1536]{2,1,0:T(8,128)(2,1)S(1)}, u32[]{:S(2)}, u32[]{:S(2)}) async-start(bf16[8,32,1536]{2,1,0:T(8,128)(2,1)} %bitcast.5), calls=%async_computation.1 | async-start | bytes 1572864 | tf_op jit(solution)/shard_map/all_to_all | solution.py:420
  35.9 3.7 %collective-permute-start.3 = (bf16[64,1536]{1,0:T(8,128)(2,1)S(1)}, bf16[64,1536]{1,0:T(8,128)(2,1)S(1)}, u32[]{:S(2)}, u32[]{:S(2)}) collective-permute-start(bf16[64,1536]{1,0:T(8,128)(2,1)S(1)} %get-tuple-element.74), channel_id=1, source_target_pairs={{0,8},{1,9},{2,10},{3,11},{4,12},{5,13},{6,14},{7,15},{8,0},{9,1},... | collective-permute-start | bytes 589832 | tf_op jit(solution)/shard_map/ppermute | solution.py:432
  39.6 1.1 collective-permute-start.4
  40.7 1.4 collective-permute-start.5
  42.1 5.5 %all-to-all-done.1 = bf16[8,32,1536]{2,1,0:T(8,128)(2,1)S(1)} async-done(((bf16[8,32,1536]{2,1,0:T(8,128)(2,1)}), bf16[8,32,1536]{2,1,0:T(8,128)(2,1)S(1)}, u32[]{:S(2)}, u32[]{:S(2)}) %all-to-all-start.1) | async-done | bytes 786464 | tf_op jit(solution)/shard_map/all_to_all | solution.py:420
  47.5 0.9 copy-done.10
  48.4 14.7 %shard_map.98 = (bf16[384,4096]{1,0:T(8,128)(2,1)}, bf16[64,1536]{1,0:T(8,128)(2,1)}, bf16[64,1536]{1,0:T(8,128)(2,1)}, bf16[64,1536]{1,0:T(8,128)(2,1)}, bf16[64,1536]{1,0:T(8,128)(2,1)}) custom-call(bf16[256,1536]{1,0:T(8,128)(2,1)} %bitcast.26, bf16[1,1024,4096]{2,1,0:T(8,128)(2,1)} %refs_4_.1, bf16[1,4096,1024]{2,1,0:T(8,128)(2,1)} %refs_5_.1), custom_call_target="tpu_custom_call" | custom-call | flops 6442450944 | bytes 21495808 | tf_op jit(solution)/shard_map/pallas_call | solution.py:383
  63.1 0.0 collective-permute-done.3.refs_1_
  63.1 0.0 collective-permute-done.4.refs_2_
  63.1 0.0 collective-permute-done.5.refs_3_
  63.2 3.8 %collective-permute-start.6 = (bf16[64,1536]{1,0:T(8,128)(2,1)}, bf16[64,1536]{1,0:T(8,128)(2,1)S(1)}, u32[]{:S(2)}, u32[]{:S(2)}) collective-permute-start(bf16[64,1536]{1,0:T(8,128)(2,1)} %get-tuple-element.87), channel_id=1, source_target_pairs={{0,8},{1,9},{2,10},{3,11},{4,12},{5,13},{6,14},{7,15},{8,0},{9,1},... | collective-permute-start | bytes 589832 | tf_op jit(solution)/shard_map/ppermute | solution.py:432
  66.9 1.1 collective-permute-start.7
  68.0 1.4 collective-permute-start.8
  69.4 0.0 copy-start
  69.4 0.0 copy-start.1
  69.5 0.0 copy-start.5
  69.5 0.0 copy-start.6
  69.5 0.0 copy-start.7
  69.5 0.0 copy-start.8
  69.5 15.1 %shard_map.99 = (bf16[64,1536]{1,0:T(8,128)(2,1)}, bf16[64,1536]{1,0:T(8,128)(2,1)}, bf16[64,1536]{1,0:T(8,128)(2,1)}, bf16[64,1536]{1,0:T(8,128)(2,1)}) custom-call(bf16[64,1536]{1,0:T(8,128)(2,1)} %copy-done.9, bf16[64,1536]{1,0:T(8,128)(2,1)} %copy-done.11, bf16[64,1536]{1,0:T(8,128)(2,1)} %copy-done.12, bf16[64,1536]{1,0:T(8,128)(2,1)} %copy-done.13, ...), custom_call_target="tpu_custom_call" | custom-call | flops 6442450944 | bytes 21495808 | tf_op jit(solution)/shard_map/pallas_call | solution.py:383
  84.6 0.0 collective-permute-done.6.refs_1_
  84.6 0.0 collective-permute-done.7.refs_2_
  84.6 1.0 shard_map.100
  85.7 3.5 %all-to-all-start.2 = ((bf16[8,32,1536]{2,1,0:T(8,128)(2,1)}), bf16[8,32,1536]{2,1,0:T(8,128)(2,1)S(1)}, u32[]{:S(2)}, u32[]{:S(2)}) async-start(bf16[8,32,1536]{2,1,0:T(8,128)(2,1)} %bitcast.7), calls=%async_computation.2 | async-start | bytes 1572864 | tf_op jit(solution)/shard_map/all_to_all | solution.py:420
  89.2 11.6 %all-to-all-done.2 = bf16[8,32,1536]{2,1,0:T(8,128)(2,1)S(1)} async-done(((bf16[8,32,1536]{2,1,0:T(8,128)(2,1)}), bf16[8,32,1536]{2,1,0:T(8,128)(2,1)S(1)}, u32[]{:S(2)}, u32[]{:S(2)}) %all-to-all-start.2) | async-done | bytes 786464 | tf_op jit(solution)/shard_map/all_to_all | solution.py:420
  100.8 1.5 %shard_map.101 = (bf16[128,1024]{1,0:T(8,128)(2,1)}, f32[128,1024]{1,0:T(8,128)S(1)}, f32[32,1024]{1,0:T(8,128)S(1)}) custom-call(s32[2,128]{1,0:T(2,128)S(1)} %bitcast.20, s32[2,128]{1,0:T(2,128)S(1)} %bitcast.24, f32[2,128]{1,0:T(2,128)S(1)} %copy-done.8, bf16[128,1024]{1,0:T(8,128)(2,1)S(1)} %copy-done.1, bf16[128,1024]{1,0:T(8,128)(2,1)S(1)} %copy-done, ...), custom_call_target="tpu_custom_call" | custom-call | flops 268435456 | bytes 2296832 | tf_op jit(solution)/shard_map/pallas_call | solution.py:358
  102.3 0.0 collective-permute-start.12
  102.3 2.9 %collective-permute-start.9 = (bf16[64,1536]{1,0:T(8,128)(2,1)}, bf16[64,1536]{1,0:T(8,128)(2,1)S(1)}, u32[]{:S(2)}, u32[]{:S(2)}) collective-permute-start(bf16[64,1536]{1,0:T(8,128)(2,1)} %get-tuple-element.97), channel_id=1, source_target_pairs={{0,8},{1,9},{2,10},{3,11},{4,12},{5,13},{6,14},{7,15},{8,0},{9,1},... | collective-permute-start | bytes 589832 | tf_op jit(solution)/shard_map/ppermute | solution.py:432
  105.2 1.1 collective-permute-start.10
  106.3 1.4 collective-permute-start.11
  107.7 0.0 collective-permute-done.12
  107.7 1.5 %collective-permute-start.14 = (f32[16,1024]{1,0:T(8,128)S(1)}, f32[16,1024]{1,0:T(8,128)S(1)}, u32[]{:S(2)}, u32[]{:S(2)}) collective-permute-start(f32[16,1024]{1,0:T(8,128)S(1)} %dynamic-slice_add_fusion), channel_id=1, source_target_pairs={{0,4},{1,5},{2,6},{3,7},{4,0},{5,1},{6,2},{7,3},{8,12},{9,13},{10,... | collective-permute-start | bytes 196616 | tf_op jit(solution)/shard_map/ppermute | solution.py:432
  109.3 1.5 %collective-permute-start.15 = (f32[16,1024]{1,0:T(8,128)S(1)}, f32[16,1024]{1,0:T(8,128)S(1)}, u32[]{:S(2)}, u32[]{:S(2)}) collective-permute-start(f32[16,1024]{1,0:T(8,128)S(1)} %dynamic-slice_add_fusion), channel_id=1, source_target_pairs={{0,6},{1,7},{2,4},{3,5},{4,2},{5,3},{6,0},{7,1},{8,14},{9,15},{10,... | collective-permute-start | bytes 196616 | tf_op jit(solution)/shard_map/ppermute | solution.py:432
  110.7 4.0 %collective-permute-done.9.refs_1_ = bf16[64,1536]{1,0:T(8,128)(2,1)S(1)} collective-permute-done((bf16[64,1536]{1,0:T(8,128)(2,1)}, bf16[64,1536]{1,0:T(8,128)(2,1)S(1)}, u32[]{:S(2)}, u32[]{:S(2)}) %collective-permute-start.9) | collective-permute-done | bytes 196640 | tf_op jit(solution)/shard_map/ppermute | solution.py:432
  114.7 1.5 %collective-permute-start.13 = (f32[16,1024]{1,0:T(8,128)S(1)}, f32[16,1024]{1,0:T(8,128)S(1)}, u32[]{:S(2)}, u32[]{:S(2)}) collective-permute-start(f32[16,1024]{1,0:T(8,128)S(1)} %dynamic-slice_add_fusion), channel_id=1, source_target_pairs={{0,2},{1,3},{2,0},{3,1},{4,6},{5,7},{6,4},{7,5},{8,10},{9,11},{10,... | collective-permute-start | bytes 196616 | tf_op jit(solution)/shard_map/ppermute | solution.py:432
  116.2 6.4 %collective-permute-done.10.refs_2_ = bf16[64,1536]{1,0:T(8,128)(2,1)S(1)} collective-permute-done((bf16[64,1536]{1,0:T(8,128)(2,1)}, bf16[64,1536]{1,0:T(8,128)(2,1)S(1)}, u32[]{:S(2)}, u32[]{:S(2)}) %collective-permute-start.10) | collective-permute-done | bytes 196640 | tf_op jit(solution)/shard_map/ppermute | solution.py:432
  122.6 0.9 copy-done.2
  123.5 1.0 shard_map.102
  124.5 3.5 %all-to-all-start.3 = ((bf16[8,32,1536]{2,1,0:T(8,128)(2,1)}), bf16[8,32,1536]{2,1,0:T(8,128)(2,1)S(1)}, u32[]{:S(2)}, u32[]{:S(2)}) async-start(bf16[8,32,1536]{2,1,0:T(8,128)(2,1)} %bitcast.9), calls=%async_computation.3 | async-start | bytes 1572864 | tf_op jit(solution)/shard_map/all_to_all | solution.py:420
  128.1 0.0 collective-permute-done.14
  128.1 2.6 %collective-permute-start.18 = (bf16[16,1024]{1,0:T(8,128)(2,1)S(1)}, bf16[16,1024]{1,0:T(8,128)(2,1)S(1)}, u32[]{:S(2)}, u32[]{:S(2)}) collective-permute-start(bf16[16,1024]{1,0:T(8,128)(2,1)S(1)} %add_convert_fusion), channel_id=1, source_target_pairs={{0,24},{1,25},{2,26},{3,27},{4,28},{5,29},{6,30},{7,31},{8,16},{9,... | collective-permute-start | bytes 98312 | tf_op jit(solution)/shard_map/ppermute | solution.py:432
  130.7 3.0 %collective-permute-start.17 = (bf16[16,1024]{1,0:T(8,128)(2,1)S(1)}, bf16[16,1024]{1,0:T(8,128)(2,1)S(1)}, u32[]{:S(2)}, u32[]{:S(2)}) collective-permute-start(bf16[16,1024]{1,0:T(8,128)(2,1)S(1)} %add_convert_fusion), channel_id=1, source_target_pairs={{0,16},{1,17},{2,18},{3,19},{4,20},{5,21},{6,22},{7,23},{8,24},{9,... | collective-permute-start | bytes 98312 | tf_op jit(solution)/shard_map/ppermute | solution.py:432
  133.7 0.1 collective-permute-start.16
  133.8 0.1 collective-permute-done.18
  133.9 2.1 %collective-permute-done.17 = bf16[16,1024]{1,0:T(8,128)(2,1)S(1)} collective-permute-done((bf16[16,1024]{1,0:T(8,128)(2,1)S(1)}, bf16[16,1024]{1,0:T(8,128)(2,1)S(1)}, u32[]{:S(2)}, u32[]{:S(2)}) %collective-permute-start.17) | collective-permute-done | bytes 32800 | tf_op jit(solution)/shard_map/ppermute | solution.py:432
  136.0 1.6 %collective-permute-done.16 = bf16[16,1024]{1,0:T(8,128)(2,1)S(1)} collective-permute-done((bf16[16,1024]{1,0:T(8,128)(2,1)S(1)}, bf16[16,1024]{1,0:T(8,128)(2,1)S(1)}, u32[]{:S(2)}, u32[]{:S(2)}) %collective-permute-start.16) | collective-permute-done | bytes 32800 | tf_op jit(solution)/shard_map/ppermute | solution.py:432
  137.6 0.1 collective-permute-start.19
  137.7 1.2 collective-permute-done.19
  138.9 0.7 maximum_bitcast_fusion
  139.6 0.0 all-to-all-done.3
  139.6 1.1 shard_map.103
  (28 shorter events, 0.1 us)
Async XLA Ops:
  5.7 16.8 %all-to-all-start = ((bf16[8,32,1536]{2,1,0:T(8,128)(2,1)}), bf16[8,32,1536]{2,1,0:T(8,128)(2,1)S(1)}, u32[]{:S(2)}, u32[]{:S(2)}) async-start(bf16[8,32,1536]{2,1,0:T(8,128)(2,1)} %bitcast.27), calls=%async_computation | async-start | bytes 1572864 | tf_op jit(solution)/shard_map/all_to_all | solution.py:420
  10.8 12.5 %collective-permute-start = (bf16[64,1536]{1,0:T(8,128)(2,1)}, bf16[64,1536]{1,0:T(8,128)(2,1)S(1)}, u32[]{:S(2)}, u32[]{:S(2)}) collective-permute-start(bf16[64,1536]{1,0:T(8,128)(2,1)} %get-tuple-element.55), channel_id=1, source_target_pairs={{0,8},{1,9},{2,10},{3,11},{4,12},{5,13},{6,14},{7,15},{8,0},{9,1},... | collective-permute-start | bytes 589832 | tf_op jit(solution)/shard_map/ppermute | solution.py:432
  12.4 17.3 %collective-permute-start.1 = (bf16[64,1536]{1,0:T(8,128)(2,1)}, bf16[64,1536]{1,0:T(8,128)(2,1)S(1)}, u32[]{:S(2)}, u32[]{:S(2)}) collective-permute-start(bf16[64,1536]{1,0:T(8,128)(2,1)} %get-tuple-element.56), channel_id=1, source_target_pairs={{0,16},{1,17},{2,18},{3,19},{4,20},{5,21},{6,22},{7,23},{8,24},{9,... | collective-permute-start | bytes 589832 | tf_op jit(solution)/shard_map/ppermute | solution.py:432
  15.0 14.7 %collective-permute-start.2 = (bf16[64,1536]{1,0:T(8,128)(2,1)}, bf16[64,1536]{1,0:T(8,128)(2,1)S(1)}, u32[]{:S(2)}, u32[]{:S(2)}) collective-permute-start(bf16[64,1536]{1,0:T(8,128)(2,1)} %get-tuple-element.57), channel_id=1, source_target_pairs={{0,24},{1,25},{2,26},{3,27},{4,28},{5,29},{6,30},{7,31},{8,16},{9,... | collective-permute-start | bytes 589832 | tf_op jit(solution)/shard_map/ppermute | solution.py:432
  22.6 0.7 copy-start.9
  29.7 0.9 copy-start.4
  31.7 15.9 %all-to-all-start.1 = ((bf16[8,32,1536]{2,1,0:T(8,128)(2,1)}), bf16[8,32,1536]{2,1,0:T(8,128)(2,1)S(1)}, u32[]{:S(2)}, u32[]{:S(2)}) async-start(bf16[8,32,1536]{2,1,0:T(8,128)(2,1)} %bitcast.5), calls=%async_computation.1 | async-start | bytes 1572864 | tf_op jit(solution)/shard_map/all_to_all | solution.py:420
  35.9 27.2 %collective-permute-start.3 = (bf16[64,1536]{1,0:T(8,128)(2,1)S(1)}, bf16[64,1536]{1,0:T(8,128)(2,1)S(1)}, u32[]{:S(2)}, u32[]{:S(2)}) collective-permute-start(bf16[64,1536]{1,0:T(8,128)(2,1)S(1)} %get-tuple-element.74), channel_id=1, source_target_pairs={{0,8},{1,9},{2,10},{3,11},{4,12},{5,13},{6,14},{7,15},{8,0},{9,1},... | collective-permute-start | bytes 589832 | tf_op jit(solution)/shard_map/ppermute | solution.py:432
  39.6 23.5 %collective-permute-start.4 = (bf16[64,1536]{1,0:T(8,128)(2,1)S(1)}, bf16[64,1536]{1,0:T(8,128)(2,1)S(1)}, u32[]{:S(2)}, u32[]{:S(2)}) collective-permute-start(bf16[64,1536]{1,0:T(8,128)(2,1)S(1)} %get-tuple-element.75), channel_id=1, source_target_pairs={{0,16},{1,17},{2,18},{3,19},{4,20},{5,21},{6,22},{7,23},{8,24},{9,... | collective-permute-start | bytes 589832 | tf_op jit(solution)/shard_map/ppermute | solution.py:432
  40.7 22.5 %collective-permute-start.5 = (bf16[64,1536]{1,0:T(8,128)(2,1)S(1)}, bf16[64,1536]{1,0:T(8,128)(2,1)S(1)}, u32[]{:S(2)}, u32[]{:S(2)}) collective-permute-start(bf16[64,1536]{1,0:T(8,128)(2,1)S(1)} %get-tuple-element.76), channel_id=1, source_target_pairs={{0,24},{1,25},{2,26},{3,27},{4,28},{5,29},{6,30},{7,31},{8,16},{9,... | collective-permute-start | bytes 589832 | tf_op jit(solution)/shard_map/ppermute | solution.py:432
  47.5 0.9 copy-start.10
  63.1 6.3 %copy-start.11 = (bf16[64,1536]{1,0:T(8,128)(2,1)}, bf16[64,1536]{1,0:T(8,128)(2,1)S(1)}, u32[]{:S(2)}) copy-start(bf16[64,1536]{1,0:T(8,128)(2,1)S(1)} %collective-permute-done.3.refs_1_) | copy-start | bytes 589828
  63.1 6.3 %copy-start.12 = (bf16[64,1536]{1,0:T(8,128)(2,1)}, bf16[64,1536]{1,0:T(8,128)(2,1)S(1)}, u32[]{:S(2)}) copy-start(bf16[64,1536]{1,0:T(8,128)(2,1)S(1)} %collective-permute-done.4.refs_2_) | copy-start | bytes 589828
  63.2 6.3 %copy-start.13 = (bf16[64,1536]{1,0:T(8,128)(2,1)}, bf16[64,1536]{1,0:T(8,128)(2,1)S(1)}, u32[]{:S(2)}) copy-start(bf16[64,1536]{1,0:T(8,128)(2,1)S(1)} %collective-permute-done.5.refs_3_) | copy-start | bytes 589828
  63.2 21.5 %collective-permute-start.6 = (bf16[64,1536]{1,0:T(8,128)(2,1)}, bf16[64,1536]{1,0:T(8,128)(2,1)S(1)}, u32[]{:S(2)}, u32[]{:S(2)}) collective-permute-start(bf16[64,1536]{1,0:T(8,128)(2,1)} %get-tuple-element.87), channel_id=1, source_target_pairs={{0,8},{1,9},{2,10},{3,11},{4,12},{5,13},{6,14},{7,15},{8,0},{9,1},... | collective-permute-start | bytes 589832 | tf_op jit(solution)/shard_map/ppermute | solution.py:432
  66.9 17.7 %collective-permute-start.7 = (bf16[64,1536]{1,0:T(8,128)(2,1)}, bf16[64,1536]{1,0:T(8,128)(2,1)S(1)}, u32[]{:S(2)}, u32[]{:S(2)}) collective-permute-start(bf16[64,1536]{1,0:T(8,128)(2,1)} %get-tuple-element.88), channel_id=1, source_target_pairs={{0,16},{1,17},{2,18},{3,19},{4,20},{5,21},{6,22},{7,23},{8,24},{9,... | collective-permute-start | bytes 589832 | tf_op jit(solution)/shard_map/ppermute | solution.py:432
  68.0 16.6 %collective-permute-start.8 = (bf16[64,1536]{1,0:T(8,128)(2,1)}, bf16[64,1536]{1,0:T(8,128)(2,1)S(1)}, u32[]{:S(2)}, u32[]{:S(2)}) collective-permute-start(bf16[64,1536]{1,0:T(8,128)(2,1)} %get-tuple-element.89), channel_id=1, source_target_pairs={{0,24},{1,25},{2,26},{3,27},{4,28},{5,29},{6,30},{7,31},{8,16},{9,... | collective-permute-start | bytes 589832 | tf_op jit(solution)/shard_map/ppermute | solution.py:432
  69.4 15.2 %copy-start.3 = (bf16[64,1536]{1,0:T(8,128)(2,1)S(1)}, bf16[64,1536]{1,0:T(8,128)(2,1)}, u32[]{:S(2)}) copy-start(bf16[64,1536]{1,0:T(8,128)(2,1)} %get-tuple-element.90.refs_0_) | copy-start | bytes 589828
  69.4 31.4 %copy-start = (bf16[128,1024]{1,0:T(8,128)(2,1)S(1)}, bf16[128,1024]{1,0:T(8,128)(2,1)}, u32[]{:S(2)}) copy-start(bf16[128,1024]{1,0:T(8,128)(2,1)} %tokens_ref.4) | copy-start | bytes 786436
  69.4 31.3 %copy-start.1 = (bf16[128,1024]{1,0:T(8,128)(2,1)S(1)}, bf16[128,1024]{1,0:T(8,128)(2,1)}, u32[]{:S(2)}) copy-start(bf16[128,1024]{1,0:T(8,128)(2,1)} %cot_ref.3) | copy-start | bytes 786436
  69.5 31.3 %copy-start.5 = (bf16[1024,32]{0,1:T(8,128)(2,1)S(1)}, bf16[1024,32]{0,1:T(8,128)(2,1)}, u32[]{:S(2)}) copy-start(bf16[1024,32]{0,1:T(8,128)(2,1)} %param.8) | copy-start | bytes 196612
  69.5 31.3 %copy-start.6 = (s32[128,2]{0,1:T(2,128)S(1)}, s32[128,2]{0,1:T(2,128)}, u32[]{:S(2)}) copy-start(s32[128,2]{0,1:T(2,128)} %param.11) | copy-start | bytes 3076
  69.5 31.3 %copy-start.7 = (s32[128,2]{0,1:T(2,128)S(1)}, s32[128,2]{0,1:T(2,128)}, u32[]{:S(2)}) copy-start(s32[128,2]{0,1:T(2,128)} %param.12) | copy-start | bytes 3076
  69.5 31.3 %copy-start.8 = (f32[2,128]{1,0:T(2,128)S(1)}, f32[2,128]{1,0:T(2,128)}, u32[]{:S(2)}) copy-start(f32[2,128]{1,0:T(2,128)} %get-tuple-element.59.gates_ref) | copy-start | bytes 3076
  85.7 15.1 %all-to-all-start.2 = ((bf16[8,32,1536]{2,1,0:T(8,128)(2,1)}), bf16[8,32,1536]{2,1,0:T(8,128)(2,1)S(1)}, u32[]{:S(2)}, u32[]{:S(2)}) async-start(bf16[8,32,1536]{2,1,0:T(8,128)(2,1)} %bitcast.7), calls=%async_computation.2 | async-start | bytes 1572864 | tf_op jit(solution)/shard_map/all_to_all | solution.py:420
  102.3 5.4 %collective-permute-start.12 = (f32[16,1024]{1,0:T(8,128)S(1)}, f32[16,1024]{1,0:T(8,128)S(1)}, u32[]{:S(2)}, u32[]{:S(2)}) collective-permute-start(f32[16,1024]{1,0:T(8,128)S(1)} %constant_dynamic-slice_fusion), channel_id=1, source_target_pairs={{0,1},{1,0},{2,3},{3,2},{4,5},{5,4},{6,7},{7,6},{8,9},{9,8},{10,11... | collective-permute-start | bytes 196616 | tf_op jit(solution)/shard_map/ppermute | solution.py:432
  102.3 12.3 %collective-permute-start.9 = (bf16[64,1536]{1,0:T(8,128)(2,1)}, bf16[64,1536]{1,0:T(8,128)(2,1)S(1)}, u32[]{:S(2)}, u32[]{:S(2)}) collective-permute-start(bf16[64,1536]{1,0:T(8,128)(2,1)} %get-tuple-element.97), channel_id=1, source_target_pairs={{0,8},{1,9},{2,10},{3,11},{4,12},{5,13},{6,14},{7,15},{8,0},{9,1},... | collective-permute-start | bytes 589832 | tf_op jit(solution)/shard_map/ppermute | solution.py:432
  105.2 17.3 %collective-permute-start.10 = (bf16[64,1536]{1,0:T(8,128)(2,1)}, bf16[64,1536]{1,0:T(8,128)(2,1)S(1)}, u32[]{:S(2)}, u32[]{:S(2)}) collective-permute-start(bf16[64,1536]{1,0:T(8,128)(2,1)} %get-tuple-element.98), channel_id=1, source_target_pairs={{0,16},{1,17},{2,18},{3,19},{4,20},{5,21},{6,22},{7,23},{8,24},{9,... | collective-permute-start | bytes 589832 | tf_op jit(solution)/shard_map/ppermute | solution.py:432
  106.3 16.2 %collective-permute-start.11 = (bf16[64,1536]{1,0:T(8,128)(2,1)}, bf16[64,1536]{1,0:T(8,128)(2,1)S(1)}, u32[]{:S(2)}, u32[]{:S(2)}) collective-permute-start(bf16[64,1536]{1,0:T(8,128)(2,1)} %get-tuple-element.99), channel_id=1, source_target_pairs={{0,24},{1,25},{2,26},{3,27},{4,28},{5,29},{6,30},{7,31},{8,16},{9,... | collective-permute-start | bytes 589832 | tf_op jit(solution)/shard_map/ppermute | solution.py:432
  107.7 20.3 %collective-permute-start.14 = (f32[16,1024]{1,0:T(8,128)S(1)}, f32[16,1024]{1,0:T(8,128)S(1)}, u32[]{:S(2)}, u32[]{:S(2)}) collective-permute-start(f32[16,1024]{1,0:T(8,128)S(1)} %dynamic-slice_add_fusion), channel_id=1, source_target_pairs={{0,4},{1,5},{2,6},{3,7},{4,0},{5,1},{6,2},{7,3},{8,12},{9,13},{10,... | collective-permute-start | bytes 196616 | tf_op jit(solution)/shard_map/ppermute | solution.py:432
  109.3 18.8 %collective-permute-start.15 = (f32[16,1024]{1,0:T(8,128)S(1)}, f32[16,1024]{1,0:T(8,128)S(1)}, u32[]{:S(2)}, u32[]{:S(2)}) collective-permute-start(f32[16,1024]{1,0:T(8,128)S(1)} %dynamic-slice_add_fusion), channel_id=1, source_target_pairs={{0,6},{1,7},{2,4},{3,5},{4,2},{5,3},{6,0},{7,1},{8,14},{9,15},{10,... | collective-permute-start | bytes 196616 | tf_op jit(solution)/shard_map/ppermute | solution.py:432
  114.7 13.4 %collective-permute-start.13 = (f32[16,1024]{1,0:T(8,128)S(1)}, f32[16,1024]{1,0:T(8,128)S(1)}, u32[]{:S(2)}, u32[]{:S(2)}) collective-permute-start(f32[16,1024]{1,0:T(8,128)S(1)} %dynamic-slice_add_fusion), channel_id=1, source_target_pairs={{0,2},{1,3},{2,0},{3,1},{4,6},{5,7},{6,4},{7,5},{8,10},{9,11},{10,... | collective-permute-start | bytes 196616 | tf_op jit(solution)/shard_map/ppermute | solution.py:432
  122.6 0.9 copy-start.2
  124.5 15.1 %all-to-all-start.3 = ((bf16[8,32,1536]{2,1,0:T(8,128)(2,1)}), bf16[8,32,1536]{2,1,0:T(8,128)(2,1)S(1)}, u32[]{:S(2)}, u32[]{:S(2)}) async-start(bf16[8,32,1536]{2,1,0:T(8,128)(2,1)} %bitcast.9), calls=%async_computation.3 | async-start | bytes 1572864 | tf_op jit(solution)/shard_map/all_to_all | solution.py:420
  128.1 5.8 %collective-permute-start.18 = (bf16[16,1024]{1,0:T(8,128)(2,1)S(1)}, bf16[16,1024]{1,0:T(8,128)(2,1)S(1)}, u32[]{:S(2)}, u32[]{:S(2)}) collective-permute-start(bf16[16,1024]{1,0:T(8,128)(2,1)S(1)} %add_convert_fusion), channel_id=1, source_target_pairs={{0,24},{1,25},{2,26},{3,27},{4,28},{5,29},{6,30},{7,31},{8,16},{9,... | collective-permute-start | bytes 98312 | tf_op jit(solution)/shard_map/ppermute | solution.py:432
  130.7 5.3 %collective-permute-start.17 = (bf16[16,1024]{1,0:T(8,128)(2,1)S(1)}, bf16[16,1024]{1,0:T(8,128)(2,1)S(1)}, u32[]{:S(2)}, u32[]{:S(2)}) collective-permute-start(bf16[16,1024]{1,0:T(8,128)(2,1)S(1)} %add_convert_fusion), channel_id=1, source_target_pairs={{0,16},{1,17},{2,18},{3,19},{4,20},{5,21},{6,22},{7,23},{8,24},{9,... | collective-permute-start | bytes 98312 | tf_op jit(solution)/shard_map/ppermute | solution.py:432
  133.7 3.9 %collective-permute-start.16 = (bf16[16,1024]{1,0:T(8,128)(2,1)S(1)}, bf16[16,1024]{1,0:T(8,128)(2,1)S(1)}, u32[]{:S(2)}, u32[]{:S(2)}) collective-permute-start(bf16[16,1024]{1,0:T(8,128)(2,1)S(1)} %add_convert_fusion), channel_id=1, source_target_pairs={{0,8},{1,9},{2,10},{3,11},{4,12},{5,13},{6,14},{7,15},{8,0},{9,1},... | collective-permute-start | bytes 98312 | tf_op jit(solution)/shard_map/ppermute | solution.py:432
  137.6 1.3 collective-permute-start.19

commit v6 on v4

--- a/solution.py
+++ b/solution.py
@@ -167,7 +167,19 @@
         message_ref[:, lay.base :] = total.astype(BF16)
 
 
-def send_tokens_kernel(lay, ids_ref, slots_ref, tokens_ref, out_ref):
+def send_tokens_kernel(
+    lay, ids_hbm, slots_hbm, tokens_hbm, out_ref, ids_ref, slots_ref, tokens_ref, sems
+):
+    copies = [
+        pltpu.make_async_copy(source, target, sems.at[at])
+        for at, (source, target) in enumerate(
+            ((ids_hbm, ids_ref), (slots_hbm, slots_ref), (tokens_hbm, tokens_ref))
+        )
+    ]
+    for copy in copies:
+        copy.start()
+    for copy in copies:
+        copy.wait()
     first = targets(lay, ids_ref[0:1, :], slots_ref[0:1, :])
     second = targets(lay, ids_ref[1:2, :], slots_ref[1:2, :])
     place(lay, [[first, second]], [tokens_ref[...]], out_ref)
@@ -355,11 +367,10 @@
         sent = own if bit == 2 else own.astype(BF16)
         steps = [1, 2, 3] if 2 * bit < devices else [1]
         terms = [from_device(sent, step * bit, devices) for step in steps]
-        if bit * 4 >= devices:
-            beside, sent, *terms = lax.optimization_barrier((beside, sent, *terms))
         terms = [term.astype(F32) for term in [sent] + terms]
         own = sum_of_pairs(*terms) if len(terms) == 4 else terms[0] + terms[1]
         bit *= 4
+    beside, own = lax.optimization_barrier((beside, own))
     other = from_device(own, 1, devices)
     first = core == 0
     total = jnp.concatenate([jnp.where(first, own, other), jnp.where(first, other, own)], axis=0)
@@ -375,9 +386,21 @@
     ids, slots, router = expert_ids.T, slot_ids.T, router_weight.T
     place_flops = 4 * experts * GROUP * tok_rows * model_width
 
-    sent_tokens = call(
-        functools.partial(send_tokens_kernel, lay), message, place_flops, (ids, slots, tokens)
-    )
+    sent_tokens = pl.pallas_call(
+        functools.partial(send_tokens_kernel, lay),
+        out_shape=message,
+        in_specs=[pl.BlockSpec(memory_space=pltpu.HBM)] * 3,
+        scratch_shapes=[
+            pltpu.VMEM(ids.shape, jnp.int32),
+            pltpu.VMEM(slots.shape, jnp.int32),
+            pltpu.VMEM(tokens.shape, BF16),
+            pltpu.SemaphoreType.DMA((3,)),
+        ],
+        compiler_params=pltpu.CompilerParams(vmem_limit_bytes=SMALL_VMEM_BYTES),
+        cost_estimate=pl.CostEstimate(
+            flops=place_flops, bytes_accessed=2 * (tokens.size + message.size), transcendentals=0
+        ),
+    )(ids, slots, tokens)
     sent_grads, gates = call(
         functools.partial(send_grads_kernel, lay),
         [message, jax.ShapeDtypeStruct((2, tok_rows), F32)],
@@ -405,6 +428,7 @@
         (ids, slots, gates, produced_back, cotangent, tokens, router),
         SMALL_VMEM_BYTES,
     )
+    grad_router, returned_back = sum_over_devices(partial_grad, devices, returned_back)
     grad_tokens = call(
         functools.partial(grad_kernel, lay),
         jax.ShapeDtypeStruct((tok_rows, model_width), BF16),
@@ -412,7 +436,6 @@
         (ids, slots, returned_back, router_back),
         SMALL_VMEM_BYTES,
     )
-    grad_router, grad_tokens = sum_over_devices(partial_grad, devices, grad_tokens)
     return (mixed, grad_tokens, grad_router.T)
 
 

time: 109 us -> 111 us (1.018)
  local copies, waits for them, and re-layouts: 0.05 us -> 2.35 us
    all_to_all x4, waiting for transfers between devices: 34.1 us -> 29 us  [exchange(): return lax.all_to_all(x, AXES, split_axis=0, concat_axis=0, tiled=True)]
    ppermute x8, waiting for transfers between devices: 8.41 us -> 13.3 us  [from_device(): return lax.ppermute(x, AXES, [(d, d ^ bits) for d in range(devices)])]
    unnamed x16 -> x22, local copies, waits for them, and re-layouts: 0.05 us -> 2.35 us
    pallas_call x4 -> x3, Pallas kernels: 7.65 us -> 5.45 us  [call(): pl.pallas_call(kernel, out_shape=out_shape, compiler_params=pltpu.Compile...]
    pallas_call x0 -> x1, Pallas kernels: none -> 1.31 us  [on_device(): pl.pallas_call(functools.partial(send_tokens_kernel, lay), out_shape=mess...]
  transfers between devices with their start and end apart: 12 -> 12, of which waited for: 9 -> 10; matrix products, arithmetic and copies ran while one was open for 0% -> 0% of each run, Pallas kernels for 33% -> 32%
where the time goes in v6:
time: 111 us; the launch traced here: 110 us
  waiting for transfers between devices  42.3 us (38%)
  Pallas kernels  36.6 us (33%)
  starting transfers between devices  26.9 us (24%)
  local copies, waits for them, and re-layouts  2.35 us (2%)
    pallas_call x2, Pallas kernels, expert_call(): pl.pallas_call(functools.partial(kernel, lay), grid=(ff // tile,), in_spe...  29.9 us
    all_to_all x4, waiting for transfers between devices, exchange(): return lax.all_to_all(x, AXES, split_axis=0, concat_axis=0, tiled=True)  29 us
    all_to_all x4, starting transfers between devices, exchange(): return lax.all_to_all(x, AXES, split_axis=0, concat_axis=0, tiled=True)  18.2 us
    ppermute x8, waiting for transfers between devices, from_device(): return lax.ppermute(x, AXES, [(d, d ^ bits) for d in range(devices)])  13.3 us
    ppermute x8, starting transfers between devices, from_device(): return lax.ppermute(x, AXES, [(d, d ^ bits) for d in range(devices)])  8.76 us
    pallas_call x3, Pallas kernels, call(): pl.pallas_call(kernel, out_shape=out_shape, compiler_params=pltpu.Compile...  5.45 us
    unnamed x22, local copies, waits for them, and re-layouts  2.35 us
  transfers between devices with their start and end apart: 12, of which 10 were waited for; matrix products, arithmetic and copies ran while one was open for 0% of the time, Pallas kernels for 32%

profile of v6, /device:TPU:0, one launch (start us, length us, event | category | flops | bytes accessed | tf_op | source)
XLA Modules:
  0.0 109.8 jit_solution(17162923685762870367)
XLA Ops:
  0.6 0.0 copy-start
  0.6 0.9 copy-done
  1.6 0.0 copy-start.4
  1.6 0.7 copy-done.4
  2.3 0.0 copy-start.6
  2.3 0.7 copy-done.6
  2.9 1.3 %shard_map.95 = bf16[256,1536]{1,0:T(8,128)(2,1)} custom-call(s32[2,128]{1,0:T(2,128)S(1)} %bitcast.18, s32[2,128]{1,0:T(2,128)S(1)} %bitcast.22, bf16[128,1024]{1,0:T(8,128)(2,1)S(1)} %copy-done), custom_call_target="tpu_custom_call" | custom-call | flops 134217728 | bytes 1048576 | tf_op jit(solution)/shard_map/pallas_call | solution.py:389
  4.3 7.3 %all-to-all-start = ((bf16[32,8,1536]{2,1,0:T(8,128)(2,1)}), bf16[32,8,1536]{2,1,0:T(8,128)(2,1)S(1)}, u32[]{:S(2)}, u32[]{:S(2)}) async-start(bf16[32,8,1536]{2,1,0:T(8,128)(2,1)} %bitcast.3), calls=%async_computation | async-start | bytes 1572864 | tf_op jit(solution)/shard_map/all_to_all | solution.py:348
  11.6 2.9 %shard_map.94 = (bf16[256,1536]{1,0:T(8,128)(2,1)}, f32[2,128]{1,0:T(2,128)}) custom-call(s32[2,128]{1,0:T(2,128)} %bitcast.17, s32[2,128]{1,0:T(2,128)} %bitcast.21, bf16[128,1024]{1,0:T(8,128)(2,1)} %tokens_ref.3, bf16[32,1024]{1,0:T(8,128)(2,1)} %bitcast.15, bf16[128,1024]{1,0:T(8,128)(2,1)} %cot_ref.3), custom_call_target="tpu_custom_call" | custom-call | flops 268435456 | bytes 1379328 | tf_op jit(solution)/shard_map/pallas_call | solution.py:311
  14.5 17.7 %all-to-all-done = bf16[32,8,1536]{2,1,0:T(8,128)(2,1)S(1)} async-done(((bf16[32,8,1536]{2,1,0:T(8,128)(2,1)}), bf16[32,8,1536]{2,1,0:T(8,128)(2,1)S(1)}, u32[]{:S(2)}, u32[]{:S(2)}) %all-to-all-start) | async-done | bytes 786464 | tf_op jit(solution)/shard_map/all_to_all | solution.py:348
  32.2 0.0 copy-start.9
  32.2 3.6 %all-to-all-start.1 = ((bf16[32,8,1536]{2,1,0:T(8,128)(2,1)}), bf16[32,8,1536]{2,1,0:T(8,128)(2,1)S(1)}, u32[]{:S(2)}, u32[]{:S(2)}) async-start(bf16[32,8,1536]{2,1,0:T(8,128)(2,1)} %bitcast.28), calls=%async_computation.1 | async-start | bytes 1572864 | tf_op jit(solution)/shard_map/all_to_all | solution.py:348
  35.8 0.0 copy-done.9
  35.8 14.7 %shard_map.96 = (bf16[256,1536]{1,0:T(8,128)(2,1)}, bf16[384,4096]{1,0:T(8,128)(2,1)}) custom-call(bf16[256,1536]{1,0:T(8,128)(2,1)} %bitcast.26, bf16[1,1024,4096]{2,1,0:T(8,128)(2,1)} %win_ref.3, bf16[1,4096,1024]{2,1,0:T(8,128)(2,1)} %wout_ref.3), custom_call_target="tpu_custom_call" | custom-call | flops 6442450944 | bytes 21495808 | tf_op jit(solution)/shard_map/pallas_call | solution.py:331
  50.5 5.9 %all-to-all-done.1 = bf16[32,8,1536]{2,1,0:T(8,128)(2,1)S(1)} async-done(((bf16[32,8,1536]{2,1,0:T(8,128)(2,1)}), bf16[32,8,1536]{2,1,0:T(8,128)(2,1)S(1)}, u32[]{:S(2)}, u32[]{:S(2)}) %all-to-all-start.1) | async-done | bytes 786464 | tf_op jit(solution)/shard_map/all_to_all | solution.py:348
  56.4 0.0 copy-start.10
  56.4 3.6 %all-to-all-start.2 = ((bf16[32,8,1536]{2,1,0:T(8,128)(2,1)}), bf16[32,8,1536]{2,1,0:T(8,128)(2,1)S(1)}, u32[]{:S(2)}, u32[]{:S(2)}) async-start(bf16[32,8,1536]{2,1,0:T(8,128)(2,1)} %bitcast.29), calls=%async_computation.2 | async-start | bytes 1572864 | tf_op jit(solution)/shard_map/all_to_all | solution.py:348
  60.1 0.0 copy-done.10
  60.1 0.0 copy-start.1
  60.1 0.0 copy-start.2
  60.1 0.0 copy-start.3
  60.1 0.0 copy-start.5
  60.1 0.0 copy-start.7
  60.1 0.0 copy-start.8
  60.1 15.2 %shard_map.97 = bf16[256,1536]{1,0:T(8,128)(2,1)} custom-call(bf16[256,1536]{1,0:T(8,128)(2,1)} %bitcast.27, bf16[384,4096]{1,0:T(8,128)(2,1)} %get-tuple-element.24.hidden_ref, bf16[1,1024,4096]{2,1,0:T(8,128)(2,1)} %win_ref.3, bf16[1,4096,1024]{2,1,0:T(8,128)(2,1)} %wout_ref.3), custom_call_target="tpu_custom_call" | custom-call | flops 6442450944 | bytes 21495808 | tf_op jit(solution)/shard_map/pallas_call | solution.py:331
  75.3 5.4 %all-to-all-done.2 = bf16[32,8,1536]{2,1,0:T(8,128)(2,1)S(1)} async-done(((bf16[32,8,1536]{2,1,0:T(8,128)(2,1)}), bf16[32,8,1536]{2,1,0:T(8,128)(2,1)S(1)}, u32[]{:S(2)}, u32[]{:S(2)}) %all-to-all-start.2) | async-done | bytes 786464 | tf_op jit(solution)/shard_map/all_to_all | solution.py:348
  80.7 3.6 %all-to-all-start.3 = ((bf16[32,8,1536]{2,1,0:T(8,128)(2,1)}), bf16[32,8,1536]{2,1,0:T(8,128)(2,1)S(1)}, u32[]{:S(2)}, u32[]{:S(2)}) async-start(bf16[32,8,1536]{2,1,0:T(8,128)(2,1)} %bitcast.25), calls=%async_computation.3 | async-start | bytes 1572864 | tf_op jit(solution)/shard_map/all_to_all | solution.py:348
  84.3 0.0 copy-done.1
  84.3 0.0 copy-done.2
  84.3 0.0 copy-done.3
  84.4 0.0 copy-done.5
  84.4 0.0 copy-done.7
  84.4 0.0 copy-done.8
  84.4 1.5 %shard_map.98 = (bf16[128,1024]{1,0:T(8,128)(2,1)}, f32[128,1024]{1,0:T(8,128)S(1)}, f32[32,1024]{1,0:T(8,128)S(1)}) custom-call(s32[2,128]{1,0:T(2,128)S(1)} %bitcast.19, s32[2,128]{1,0:T(2,128)S(1)} %bitcast.23, f32[2,128]{1,0:T(2,128)S(1)} %copy-done.8, bf16[256,1536]{1,0:T(8,128)(2,1)S(1)} %bitcast.14, bf16[128,1024]{1,0:T(8,128)(2,1)S(1)} %copy-done.2, ...), custom_call_target="tpu_custom_call" | custom-call | flops 268435456 | bytes 2296832 | tf_op jit(solution)/shard_map/pallas_call | solution.py:311
  85.9 0.2 collective-permute-start
  86.1 1.0 collective-permute-done
  87.1 2.7 %collective-permute-start.3 = (f32[16,1024]{1,0:T(8,128)S(1)}, f32[16,1024]{1,0:T(8,128)S(1)}, u32[]{:S(2)}, u32[]{:S(2)}) collective-permute-start(f32[16,1024]{1,0:T(8,128)S(1)} %dynamic-slice_add_fusion), channel_id=1, source_target_pairs={{0,6},{1,7},{2,4},{3,5},{4,2},{5,3},{6,0},{7,1},{8,14},{9,15},{10,... | collective-permute-start | bytes 196616 | tf_op jit(solution)/shard_map/ppermute | solution.py:352
  89.9 0.6 collective-permute-start.2
  90.4 0.3 collective-permute-start.1
  90.7 4.2 %collective-permute-done.3 = f32[16,1024]{1,0:T(8,128)S(1)} collective-permute-done((f32[16,1024]{1,0:T(8,128)S(1)}, f32[16,1024]{1,0:T(8,128)S(1)}, u32[]{:S(2)}, u32[]{:S(2)}) %collective-permute-start.3) | collective-permute-done | bytes 65568 | tf_op jit(solution)/shard_map/ppermute | solution.py:352
  94.9 1.7 %collective-permute-done.2 = f32[16,1024]{1,0:T(8,128)S(1)} collective-permute-done((f32[16,1024]{1,0:T(8,128)S(1)}, f32[16,1024]{1,0:T(8,128)S(1)}, u32[]{:S(2)}, u32[]{:S(2)}) %collective-permute-start.2) | collective-permute-done | bytes 65568 | tf_op jit(solution)/shard_map/ppermute | solution.py:352
  96.6 0.2 collective-permute-done.1
  96.9 4.2 %collective-permute-start.6 = (bf16[16,1024]{1,0:T(8,128)(2,1)S(1)}, bf16[16,1024]{1,0:T(8,128)(2,1)S(1)}, u32[]{:S(2)}, u32[]{:S(2)}) collective-permute-start(bf16[16,1024]{1,0:T(8,128)(2,1)S(1)} %add_convert_fusion), channel_id=1, source_target_pairs={{0,24},{1,25},{2,26},{3,27},{4,28},{5,29},{6,30},{7,31},{8,16},{9,... | collective-permute-start | bytes 98312 | tf_op jit(solution)/shard_map/ppermute | solution.py:352
  101.1 0.0 collective-permute-start.5
  101.1 0.6 collective-permute-start.4
  101.8 1.4 %collective-permute-done.6 = bf16[16,1024]{1,0:T(8,128)(2,1)S(1)} collective-permute-done((bf16[16,1024]{1,0:T(8,128)(2,1)S(1)}, bf16[16,1024]{1,0:T(8,128)(2,1)S(1)}, u32[]{:S(2)}, u32[]{:S(2)}) %collective-permute-start.6) | collective-permute-done | bytes 32800 | tf_op jit(solution)/shard_map/ppermute | solution.py:352
  103.1 4.6 %collective-permute-done.5 = bf16[16,1024]{1,0:T(8,128)(2,1)S(1)} collective-permute-done((bf16[16,1024]{1,0:T(8,128)(2,1)S(1)}, bf16[16,1024]{1,0:T(8,128)(2,1)S(1)}, u32[]{:S(2)}, u32[]{:S(2)}) %collective-permute-start.5) | collective-permute-done | bytes 32800 | tf_op jit(solution)/shard_map/ppermute | solution.py:352
  107.7 0.0 collective-permute-done.4
  107.8 0.0 all-to-all-done.3
  107.8 0.1 collective-permute-start.7
  107.9 1.1 %shard_map.99 = bf16[128,1024]{1,0:T(8,128)(2,1)} custom-call(s32[2,128]{1,0:T(2,128)S(1)} %bitcast.20, s32[2,128]{1,0:T(2,128)S(1)} %bitcast.24, bf16[256,1536]{1,0:T(8,128)(2,1)S(1)} %bitcast.13, f32[128,1024]{1,0:T(8,128)S(1)} %get-tuple-element.31.back_ref), custom_call_target="tpu_custom_call" | custom-call | flops 134217728 | bytes 1574912 | tf_op jit(solution)/shard_map/pallas_call | solution.py:311
  109.0 0.1 collective-permute-done.7
  109.1 0.7 maximum_bitcast_fusion
  (5 shorter events, 0.1 us)
Async XLA Ops:
  0.6 1.0 copy-start
  1.6 0.7 copy-start.4
  2.3 0.7 copy-start.6
  4.3 27.9 %all-to-all-start = ((bf16[32,8,1536]{2,1,0:T(8,128)(2,1)}), bf16[32,8,1536]{2,1,0:T(8,128)(2,1)S(1)}, u32[]{:S(2)}, u32[]{:S(2)}) async-start(bf16[32,8,1536]{2,1,0:T(8,128)(2,1)} %bitcast.3), calls=%async_computation | async-start | bytes 1572864 | tf_op jit(solution)/shard_map/all_to_all | solution.py:348
  32.2 3.6 %copy-start.9 = (bf16[32,8,1536]{2,1,0:T(8,128)(2,1)}, bf16[32,8,1536]{2,1,0:T(8,128)(2,1)S(1)}, u32[]{:S(2)}) copy-start(bf16[32,8,1536]{2,1,0:T(8,128)(2,1)S(1)} %all-to-all-done) | copy-start | bytes 2359300
  32.2 24.2 %all-to-all-start.1 = ((bf16[32,8,1536]{2,1,0:T(8,128)(2,1)}), bf16[32,8,1536]{2,1,0:T(8,128)(2,1)S(1)}, u32[]{:S(2)}, u32[]{:S(2)}) async-start(bf16[32,8,1536]{2,1,0:T(8,128)(2,1)} %bitcast.28), calls=%async_computation.1 | async-start | bytes 1572864 | tf_op jit(solution)/shard_map/all_to_all | solution.py:348
  56.4 3.6 %copy-start.10 = (bf16[32,8,1536]{2,1,0:T(8,128)(2,1)}, bf16[32,8,1536]{2,1,0:T(8,128)(2,1)S(1)}, u32[]{:S(2)}) copy-start(bf16[32,8,1536]{2,1,0:T(8,128)(2,1)S(1)} %all-to-all-done.1) | copy-start | bytes 2359300
  56.4 24.2 %all-to-all-start.2 = ((bf16[32,8,1536]{2,1,0:T(8,128)(2,1)}), bf16[32,8,1536]{2,1,0:T(8,128)(2,1)S(1)}, u32[]{:S(2)}, u32[]{:S(2)}) async-start(bf16[32,8,1536]{2,1,0:T(8,128)(2,1)} %bitcast.29), calls=%async_computation.2 | async-start | bytes 1572864 | tf_op jit(solution)/shard_map/all_to_all | solution.py:348
  60.1 24.3 %copy-start.1 = (bf16[128,1024]{1,0:T(8,128)(2,1)S(1)}, bf16[128,1024]{1,0:T(8,128)(2,1)}, u32[]{:S(2)}) copy-start(bf16[128,1024]{1,0:T(8,128)(2,1)} %tokens_ref.3) | copy-start | bytes 786436
  60.1 24.3 %copy-start.2 = (bf16[128,1024]{1,0:T(8,128)(2,1)S(1)}, bf16[128,1024]{1,0:T(8,128)(2,1)}, u32[]{:S(2)}) copy-start(bf16[128,1024]{1,0:T(8,128)(2,1)} %cot_ref.3) | copy-start | bytes 786436
  60.1 24.3 %copy-start.3 = (bf16[1024,32]{0,1:T(8,128)(2,1)S(1)}, bf16[1024,32]{0,1:T(8,128)(2,1)}, u32[]{:S(2)}) copy-start(bf16[1024,32]{0,1:T(8,128)(2,1)} %param.8) | copy-start | bytes 196612
  60.1 24.2 %copy-start.5 = (s32[128,2]{0,1:T(2,128)S(1)}, s32[128,2]{0,1:T(2,128)}, u32[]{:S(2)}) copy-start(s32[128,2]{0,1:T(2,128)} %param.11) | copy-start | bytes 3076
  60.1 24.2 %copy-start.7 = (s32[128,2]{0,1:T(2,128)S(1)}, s32[128,2]{0,1:T(2,128)}, u32[]{:S(2)}) copy-start(s32[128,2]{0,1:T(2,128)} %param.12) | copy-start | bytes 3076
  60.1 24.2 %copy-start.8 = (f32[2,128]{1,0:T(2,128)S(1)}, f32[2,128]{1,0:T(2,128)}, u32[]{:S(2)}) copy-start(f32[2,128]{1,0:T(2,128)} %get-tuple-element.18.gates_ref) | copy-start | bytes 3076
  80.7 27.1 %all-to-all-start.3 = ((bf16[32,8,1536]{2,1,0:T(8,128)(2,1)}), bf16[32,8,1536]{2,1,0:T(8,128)(2,1)S(1)}, u32[]{:S(2)}, u32[]{:S(2)}) async-start(bf16[32,8,1536]{2,1,0:T(8,128)(2,1)} %bitcast.25), calls=%async_computation.3 | async-start | bytes 1572864 | tf_op jit(solution)/shard_map/all_to_all | solution.py:348
  85.9 1.3 %collective-permute-start = (f32[16,1024]{1,0:T(8,128)S(1)}, f32[16,1024]{1,0:T(8,128)S(1)}, u32[]{:S(2)}, u32[]{:S(2)}) collective-permute-start(f32[16,1024]{1,0:T(8,128)S(1)} %constant_dynamic-slice_fusion), channel_id=1, source_target_pairs={{0,1},{1,0},{2,3},{3,2},{4,5},{5,4},{6,7},{7,6},{8,9},{9,8},{10,11... | collective-permute-start | bytes 196616 | tf_op jit(solution)/shard_map/ppermute | solution.py:352
  87.1 7.8 %collective-permute-start.3 = (f32[16,1024]{1,0:T(8,128)S(1)}, f32[16,1024]{1,0:T(8,128)S(1)}, u32[]{:S(2)}, u32[]{:S(2)}) collective-permute-start(f32[16,1024]{1,0:T(8,128)S(1)} %dynamic-slice_add_fusion), channel_id=1, source_target_pairs={{0,6},{1,7},{2,4},{3,5},{4,2},{5,3},{6,0},{7,1},{8,14},{9,15},{10,... | collective-permute-start | bytes 196616 | tf_op jit(solution)/shard_map/ppermute | solution.py:352
  89.9 6.7 %collective-permute-start.2 = (f32[16,1024]{1,0:T(8,128)S(1)}, f32[16,1024]{1,0:T(8,128)S(1)}, u32[]{:S(2)}, u32[]{:S(2)}) collective-permute-start(f32[16,1024]{1,0:T(8,128)S(1)} %dynamic-slice_add_fusion), channel_id=1, source_target_pairs={{0,4},{1,5},{2,6},{3,7},{4,0},{5,1},{6,2},{7,3},{8,12},{9,13},{10,... | collective-permute-start | bytes 196616 | tf_op jit(solution)/shard_map/ppermute | solution.py:352
  90.4 6.4 %collective-permute-start.1 = (f32[16,1024]{1,0:T(8,128)S(1)}, f32[16,1024]{1,0:T(8,128)S(1)}, u32[]{:S(2)}, u32[]{:S(2)}) collective-permute-start(f32[16,1024]{1,0:T(8,128)S(1)} %dynamic-slice_add_fusion), channel_id=1, source_target_pairs={{0,2},{1,3},{2,0},{3,1},{4,6},{5,7},{6,4},{7,5},{8,10},{9,11},{10,... | collective-permute-start | bytes 196616 | tf_op jit(solution)/shard_map/ppermute | solution.py:352
  96.9 6.3 %collective-permute-start.6 = (bf16[16,1024]{1,0:T(8,128)(2,1)S(1)}, bf16[16,1024]{1,0:T(8,128)(2,1)S(1)}, u32[]{:S(2)}, u32[]{:S(2)}) collective-permute-start(bf16[16,1024]{1,0:T(8,128)(2,1)S(1)} %add_convert_fusion), channel_id=1, source_target_pairs={{0,24},{1,25},{2,26},{3,27},{4,28},{5,29},{6,30},{7,31},{8,16},{9,... | collective-permute-start | bytes 98312 | tf_op jit(solution)/shard_map/ppermute | solution.py:352
  101.1 6.6 %collective-permute-start.5 = (bf16[16,1024]{1,0:T(8,128)(2,1)S(1)}, bf16[16,1024]{1,0:T(8,128)(2,1)S(1)}, u32[]{:S(2)}, u32[]{:S(2)}) collective-permute-start(bf16[16,1024]{1,0:T(8,128)(2,1)S(1)} %add_convert_fusion), channel_id=1, source_target_pairs={{0,16},{1,17},{2,18},{3,19},{4,20},{5,21},{6,22},{7,23},{8,24},{9,... | collective-permute-start | bytes 98312 | tf_op jit(solution)/shard_map/ppermute | solution.py:352
  101.1 6.6 %collective-permute-start.4 = (bf16[16,1024]{1,0:T(8,128)(2,1)S(1)}, bf16[16,1024]{1,0:T(8,128)(2,1)S(1)}, u32[]{:S(2)}, u32[]{:S(2)}) collective-permute-start(bf16[16,1024]{1,0:T(8,128)(2,1)S(1)} %add_convert_fusion), channel_id=1, source_target_pairs={{0,8},{1,9},{2,10},{3,11},{4,12},{5,13},{6,14},{7,15},{8,0},{9,1},... | collective-permute-start | bytes 98312 | tf_op jit(solution)/shard_map/ppermute | solution.py:352
  107.8 1.3 %collective-permute-start.7 = (f32[16,1024]{1,0:T(8,128)S(1)}, f32[16,1024]{1,0:T(8,128)S(1)}, u32[]{:S(2)}, u32[]{:S(2)}) collective-permute-start(f32[16,1024]{1,0:T(8,128)S(1)} %add_add_fusion), channel_id=1, source_target_pairs={{0,1},{1,0},{2,3},{3,2},{4,5},{5,4},{6,7},{7,6},{8,9},{9,8},{10,11... | collective-permute-start | bytes 196616 | tf_op jit(solution)/shard_map/ppermute | solution.py:352

commit v7 on v4

--- a/solution.py
+++ b/solution.py
@@ -11,6 +11,7 @@
 F32 = jnp.float32
 BF16 = jnp.bfloat16
 GROUP = 8
+PLANE = 8
 VMEM_BYTES = 60 * 1024 * 1024
 SMALL_VMEM_BYTES = 24 * 1024 * 1024
 
@@ -350,16 +351,14 @@
     own = lax.dynamic_slice_in_dim(x, core * half, half, 0)
     other = lax.dynamic_slice_in_dim(x, (1 - core) * half, half, 0)
     own = own + from_device(other, 1, devices)
-    bit = 2
+    terms = [own] + [from_device(own, bits, devices) for bits in (2, 4, 6)]
+    own = sum_of_pairs(*terms)
+    bit = PLANE
     while bit < devices:
-        sent = own if bit == 2 else own.astype(BF16)
-        steps = [1, 2, 3] if 2 * bit < devices else [1]
-        terms = [from_device(sent, step * bit, devices) for step in steps]
-        if bit * 4 >= devices:
-            beside, sent, *terms = lax.optimization_barrier((beside, sent, *terms))
-        terms = [term.astype(F32) for term in [sent] + terms]
-        own = sum_of_pairs(*terms) if len(terms) == 4 else terms[0] + terms[1]
-        bit *= 4
+        sent = own.astype(BF16)
+        own = sent.astype(F32) + from_device(sent, bit, devices).astype(F32)
+        bit *= 2
+    beside, own = lax.optimization_barrier((beside, own))
     other = from_device(own, 1, devices)
     first = core == 0
     total = jnp.concatenate([jnp.where(first, own, other), jnp.where(first, other, own)], axis=0)
@@ -385,7 +384,6 @@
         (ids, slots, tokens, router, cotangent),
     )
     arrived = exchange(sent_tokens)
-    arrived, sent_grads = lax.optimization_barrier((arrived, sent_grads))
     grad_rows = exchange(sent_grads)
     produced, hidden = expert_call(forward_kernel, lay, arrived, None, in_weight, out_weight)
     produced, grad_rows = lax.optimization_barrier((produced, grad_rows))
@@ -405,6 +403,7 @@
         (ids, slots, gates, produced_back, cotangent, tokens, router),
         SMALL_VMEM_BYTES,
     )
+    grad_router, returned_back = sum_over_devices(partial_grad, devices, returned_back)
     grad_tokens = call(
         functools.partial(grad_kernel, lay),
         jax.ShapeDtypeStruct((tok_rows, model_width), BF16),
@@ -412,7 +411,6 @@
         (ids, slots, returned_back, router_back),
         SMALL_VMEM_BYTES,
     )
-    grad_router, grad_tokens = sum_over_devices(partial_grad, devices, grad_tokens)
     return (mixed, grad_tokens, grad_router.T)
 
 

time: 109 us -> 107 us (0.982)
  waiting for transfers between devices: 42.5 us -> 40.9 us
    all_to_all x4, waiting for transfers between devices: 34.1 us -> 29 us  [exchange(): return lax.all_to_all(x, AXES, split_axis=0, concat_axis=0, tiled=True)]
    ppermute x8 -> x7, waiting for transfers between devices: 8.41 us -> 11.8 us  [from_device(): return lax.ppermute(x, AXES, [(d, d ^ bits) for d in range(devices)])]
    ppermute x8 -> x7, starting transfers between devices: 8.76 us -> 8.45 us  [from_device(): return lax.ppermute(x, AXES, [(d, d ^ bits) for d in range(devices)])]
  transfers between devices with their start and end apart: 12 -> 11, of which waited for: 9 -> 9; matrix products, arithmetic and copies ran while one was open for 0% -> 0% of each run, Pallas kernels for 33% -> 33%
where the time goes in v7:
time: 107 us
  waiting for transfers between devices  40.9 us (38%)
  Pallas kernels  37.5 us (35%)
  starting transfers between devices  26.6 us (25%)
    pallas_call x2, Pallas kernels, expert_call(): pl.pallas_call(functools.partial(kernel, lay), grid=(ff // tile,), in_spe...  29.9 us
    all_to_all x4, waiting for transfers between devices, exchange(): return lax.all_to_all(x, AXES, split_axis=0, concat_axis=0, tiled=True)  29 us
    all_to_all x4, starting transfers between devices, exchange(): return lax.all_to_all(x, AXES, split_axis=0, concat_axis=0, tiled=True)  18.2 us
    ppermute x7, waiting for transfers between devices, from_device(): return lax.ppermute(x, AXES, [(d, d ^ bits) for d in range(devices)])  11.8 us
    ppermute x7, starting transfers between devices, from_device(): return lax.ppermute(x, AXES, [(d, d ^ bits) for d in range(devices)])  8.45 us
    pallas_call x4, Pallas kernels, call(): pl.pallas_call(kernel, out_shape=out_shape, compiler_params=pltpu.Compile...  7.66 us
  transfers between devices with their start and end apart: 11, of which 9 were waited for; matrix products, arithmetic and copies ran while one was open for 0% of the time, Pallas kernels for 33%

profile of v7, /device:TPU:0, one launch (start us, length us, event | category | flops | bytes accessed | tf_op | source)
XLA Modules:
  0.0 106.6 jit_solution(3967874436649193643)
XLA Ops:
  0.6 2.2 %shard_map.95 = bf16[256,1536]{1,0:T(8,128)(2,1)} custom-call(s32[2,128]{1,0:T(2,128)} %bitcast.17, s32[2,128]{1,0:T(2,128)} %bitcast.21, bf16[128,1024]{1,0:T(8,128)(2,1)} %tokens_ref.5), custom_call_target="tpu_custom_call" | custom-call | flops 134217728 | bytes 1050624 | tf_op jit(solution)/shard_map/pallas_call | solution.py:300
  2.9 7.3 %all-to-all-start = ((bf16[32,8,1536]{2,1,0:T(8,128)(2,1)}), bf16[32,8,1536]{2,1,0:T(8,128)(2,1)S(1)}, u32[]{:S(2)}, u32[]{:S(2)}) async-start(bf16[32,8,1536]{2,1,0:T(8,128)(2,1)} %bitcast.25), calls=%async_computation | async-start | bytes 1572864 | tf_op jit(solution)/shard_map/all_to_all | solution.py:337
  10.2 2.9 %shard_map.94 = (bf16[256,1536]{1,0:T(8,128)(2,1)}, f32[2,128]{1,0:T(2,128)}) custom-call(s32[2,128]{1,0:T(2,128)} %bitcast.18, s32[2,128]{1,0:T(2,128)} %bitcast.22, bf16[128,1024]{1,0:T(8,128)(2,1)} %tokens_ref.5, bf16[32,1024]{1,0:T(8,128)(2,1)} %bitcast.15, bf16[128,1024]{1,0:T(8,128)(2,1)} %cot_ref.3), custom_call_target="tpu_custom_call" | custom-call | flops 268435456 | bytes 1379328 | tf_op jit(solution)/shard_map/pallas_call | solution.py:300
  13.0 17.8 %all-to-all-done = bf16[32,8,1536]{2,1,0:T(8,128)(2,1)S(1)} async-done(((bf16[32,8,1536]{2,1,0:T(8,128)(2,1)}), bf16[32,8,1536]{2,1,0:T(8,128)(2,1)S(1)}, u32[]{:S(2)}, u32[]{:S(2)}) %all-to-all-start) | async-done | bytes 786464 | tf_op jit(solution)/shard_map/all_to_all | solution.py:337
  30.8 0.0 copy-start.6
  30.8 3.6 %all-to-all-start.1 = ((bf16[32,8,1536]{2,1,0:T(8,128)(2,1)}), bf16[32,8,1536]{2,1,0:T(8,128)(2,1)S(1)}, u32[]{:S(2)}, u32[]{:S(2)}) async-start(bf16[32,8,1536]{2,1,0:T(8,128)(2,1)} %bitcast.29), calls=%async_computation.1 | async-start | bytes 1572864 | tf_op jit(solution)/shard_map/all_to_all | solution.py:337
  34.4 0.0 copy-done.6
  34.4 14.7 %shard_map.96 = (bf16[256,1536]{1,0:T(8,128)(2,1)}, bf16[384,4096]{1,0:T(8,128)(2,1)}) custom-call(bf16[256,1536]{1,0:T(8,128)(2,1)} %bitcast.27, bf16[1,1024,4096]{2,1,0:T(8,128)(2,1)} %win_ref.3, bf16[1,4096,1024]{2,1,0:T(8,128)(2,1)} %wout_ref.3), custom_call_target="tpu_custom_call" | custom-call | flops 6442450944 | bytes 21495808 | tf_op jit(solution)/shard_map/pallas_call | solution.py:320
  49.1 5.9 %all-to-all-done.1 = bf16[32,8,1536]{2,1,0:T(8,128)(2,1)S(1)} async-done(((bf16[32,8,1536]{2,1,0:T(8,128)(2,1)}), bf16[32,8,1536]{2,1,0:T(8,128)(2,1)S(1)}, u32[]{:S(2)}, u32[]{:S(2)}) %all-to-all-start.1) | async-done | bytes 786464 | tf_op jit(solution)/shard_map/all_to_all | solution.py:337
  55.0 0.0 copy-start.7
  55.0 3.6 %all-to-all-start.2 = ((bf16[32,8,1536]{2,1,0:T(8,128)(2,1)}), bf16[32,8,1536]{2,1,0:T(8,128)(2,1)S(1)}, u32[]{:S(2)}, u32[]{:S(2)}) async-start(bf16[32,8,1536]{2,1,0:T(8,128)(2,1)} %bitcast.30), calls=%async_computation.2 | async-start | bytes 1572864 | tf_op jit(solution)/shard_map/all_to_all | solution.py:337
  58.7 0.0 copy-done.7
  58.7 0.0 copy-start
  58.7 0.0 copy-start.1
  58.7 0.0 copy-start.2
  58.7 0.0 copy-start.3
  58.7 0.0 copy-start.4
  58.7 0.0 copy-start.5
  58.7 15.1 %shard_map.97 = bf16[256,1536]{1,0:T(8,128)(2,1)} custom-call(bf16[256,1536]{1,0:T(8,128)(2,1)} %bitcast.28, bf16[384,4096]{1,0:T(8,128)(2,1)} %get-tuple-element.20.hidden_ref, bf16[1,1024,4096]{2,1,0:T(8,128)(2,1)} %win_ref.3, bf16[1,4096,1024]{2,1,0:T(8,128)(2,1)} %wout_ref.3), custom_call_target="tpu_custom_call" | custom-call | flops 6442450944 | bytes 21495808 | tf_op jit(solution)/shard_map/pallas_call | solution.py:320
  73.9 5.4 %all-to-all-done.2 = bf16[32,8,1536]{2,1,0:T(8,128)(2,1)S(1)} async-done(((bf16[32,8,1536]{2,1,0:T(8,128)(2,1)}), bf16[32,8,1536]{2,1,0:T(8,128)(2,1)S(1)}, u32[]{:S(2)}, u32[]{:S(2)}) %all-to-all-start.2) | async-done | bytes 786464 | tf_op jit(solution)/shard_map/all_to_all | solution.py:337
  79.3 3.6 %all-to-all-start.3 = ((bf16[32,8,1536]{2,1,0:T(8,128)(2,1)}), bf16[32,8,1536]{2,1,0:T(8,128)(2,1)S(1)}, u32[]{:S(2)}, u32[]{:S(2)}) async-start(bf16[32,8,1536]{2,1,0:T(8,128)(2,1)} %bitcast.26), calls=%async_computation.3 | async-start | bytes 1572864 | tf_op jit(solution)/shard_map/all_to_all | solution.py:337
  82.9 0.0 copy-done
  82.9 0.0 copy-done.1
  82.9 0.0 copy-done.2
  83.0 0.0 copy-done.3
  83.0 0.0 copy-done.4
  83.0 0.0 copy-done.5
  83.0 1.5 %shard_map.98 = (bf16[128,1024]{1,0:T(8,128)(2,1)}, f32[128,1024]{1,0:T(8,128)S(1)}, f32[32,1024]{1,0:T(8,128)S(1)}) custom-call(s32[2,128]{1,0:T(2,128)S(1)} %bitcast.19, s32[2,128]{1,0:T(2,128)S(1)} %bitcast.23, f32[2,128]{1,0:T(2,128)S(1)} %copy-done.5, bf16[256,1536]{1,0:T(8,128)(2,1)S(1)} %bitcast.14, bf16[128,1024]{1,0:T(8,128)(2,1)S(1)} %copy-done.1, ...), custom_call_target="tpu_custom_call" | custom-call | flops 268435456 | bytes 2296832 | tf_op jit(solution)/shard_map/pallas_call | solution.py:300
  84.5 0.3 collective-permute-start
  84.7 1.0 collective-permute-done
  85.7 1.8 %collective-permute-start.1 = (f32[16,1024]{1,0:T(8,128)S(1)}, f32[16,1024]{1,0:T(8,128)S(1)}, u32[]{:S(2)}, u32[]{:S(2)}) collective-permute-start(f32[16,1024]{1,0:T(8,128)S(1)} %dynamic-slice_add_fusion), channel_id=1, source_target_pairs={{0,2},{1,3},{2,0},{3,1},{4,6},{5,7},{6,4},{7,5},{8,10},{9,11},{10,... | collective-permute-start | bytes 196616 | tf_op jit(solution)/shard_map/ppermute | solution.py:341
  87.6 1.5 %collective-permute-start.2 = (f32[16,1024]{1,0:T(8,128)S(1)}, f32[16,1024]{1,0:T(8,128)S(1)}, u32[]{:S(2)}, u32[]{:S(2)}) collective-permute-start(f32[16,1024]{1,0:T(8,128)S(1)} %dynamic-slice_add_fusion), channel_id=1, source_target_pairs={{0,4},{1,5},{2,6},{3,7},{4,0},{5,1},{6,2},{7,3},{8,12},{9,13},{10,... | collective-permute-start | bytes 196616 | tf_op jit(solution)/shard_map/ppermute | solution.py:341
  89.0 0.3 collective-permute-start.3
  89.3 5.4 %collective-permute-done.1 = f32[16,1024]{1,0:T(8,128)S(1)} collective-permute-done((f32[16,1024]{1,0:T(8,128)S(1)}, f32[16,1024]{1,0:T(8,128)S(1)}, u32[]{:S(2)}, u32[]{:S(2)}) %collective-permute-start.1) | collective-permute-done | bytes 65568 | tf_op jit(solution)/shard_map/ppermute | solution.py:341
  94.7 0.0 collective-permute-done.2
  94.7 0.6 collective-permute-done.3
  95.3 1.8 %collective-permute-start.4 = (bf16[16,1024]{1,0:T(8,128)(2,1)S(1)}, bf16[16,1024]{1,0:T(8,128)(2,1)S(1)}, u32[]{:S(2)}, u32[]{:S(2)}) collective-permute-start(bf16[16,1024]{1,0:T(8,128)(2,1)S(1)} %add_convert_fusion.1), channel_id=1, source_target_pairs={{0,8},{1,9},{2,10},{3,11},{4,12},{5,13},{6,14},{7,15},{8,0},{9,1},... | collective-permute-start | bytes 98312 | tf_op jit(solution)/shard_map/ppermute | solution.py:341
  97.1 2.4 %collective-permute-done.4 = bf16[16,1024]{1,0:T(8,128)(2,1)S(1)} collective-permute-done((bf16[16,1024]{1,0:T(8,128)(2,1)S(1)}, bf16[16,1024]{1,0:T(8,128)(2,1)S(1)}, u32[]{:S(2)}, u32[]{:S(2)}) %collective-permute-start.4) | collective-permute-done | bytes 32800 | tf_op jit(solution)/shard_map/ppermute | solution.py:341
  99.5 2.8 %collective-permute-start.5 = (bf16[16,1024]{1,0:T(8,128)(2,1)S(1)}, bf16[16,1024]{1,0:T(8,128)(2,1)S(1)}, u32[]{:S(2)}, u32[]{:S(2)}) collective-permute-start(bf16[16,1024]{1,0:T(8,128)(2,1)S(1)} %add_convert_fusion), channel_id=1, source_target_pairs={{0,16},{1,17},{2,18},{3,19},{4,20},{5,21},{6,22},{7,23},{8,24},{9,... | collective-permute-start | bytes 98312 | tf_op jit(solution)/shard_map/ppermute | solution.py:341
  102.3 2.3 %collective-permute-done.5 = bf16[16,1024]{1,0:T(8,128)(2,1)S(1)} collective-permute-done((bf16[16,1024]{1,0:T(8,128)(2,1)S(1)}, bf16[16,1024]{1,0:T(8,128)(2,1)S(1)}, u32[]{:S(2)}, u32[]{:S(2)}) %collective-permute-start.5) | collective-permute-done | bytes 32800 | tf_op jit(solution)/shard_map/ppermute | solution.py:341
  104.6 0.0 all-to-all-done.3
  104.6 0.1 collective-permute-start.6
  104.7 1.1 %shard_map.99 = bf16[128,1024]{1,0:T(8,128)(2,1)} custom-call(s32[2,128]{1,0:T(2,128)S(1)} %bitcast.20, s32[2,128]{1,0:T(2,128)S(1)} %bitcast.24, bf16[256,1536]{1,0:T(8,128)(2,1)S(1)} %bitcast.13, f32[128,1024]{1,0:T(8,128)S(1)} %get-tuple-element.27.back_ref), custom_call_target="tpu_custom_call" | custom-call | flops 134217728 | bytes 1574912 | tf_op jit(solution)/shard_map/pallas_call | solution.py:300
  105.8 0.1 collective-permute-done.6
  105.9 0.7 maximum_bitcast_fusion
  (6 shorter events, 0.1 us)
Async XLA Ops:
  2.9 27.9 %all-to-all-start = ((bf16[32,8,1536]{2,1,0:T(8,128)(2,1)}), bf16[32,8,1536]{2,1,0:T(8,128)(2,1)S(1)}, u32[]{:S(2)}, u32[]{:S(2)}) async-start(bf16[32,8,1536]{2,1,0:T(8,128)(2,1)} %bitcast.25), calls=%async_computation | async-start | bytes 1572864 | tf_op jit(solution)/shard_map/all_to_all | solution.py:337
  30.8 3.6 %copy-start.6 = (bf16[32,8,1536]{2,1,0:T(8,128)(2,1)}, bf16[32,8,1536]{2,1,0:T(8,128)(2,1)S(1)}, u32[]{:S(2)}) copy-start(bf16[32,8,1536]{2,1,0:T(8,128)(2,1)S(1)} %all-to-all-done) | copy-start | bytes 2359300
  30.8 24.2 %all-to-all-start.1 = ((bf16[32,8,1536]{2,1,0:T(8,128)(2,1)}), bf16[32,8,1536]{2,1,0:T(8,128)(2,1)S(1)}, u32[]{:S(2)}, u32[]{:S(2)}) async-start(bf16[32,8,1536]{2,1,0:T(8,128)(2,1)} %bitcast.29), calls=%async_computation.1 | async-start | bytes 1572864 | tf_op jit(solution)/shard_map/all_to_all | solution.py:337
  55.0 3.6 %copy-start.7 = (bf16[32,8,1536]{2,1,0:T(8,128)(2,1)}, bf16[32,8,1536]{2,1,0:T(8,128)(2,1)S(1)}, u32[]{:S(2)}) copy-start(bf16[32,8,1536]{2,1,0:T(8,128)(2,1)S(1)} %all-to-all-done.1) | copy-start | bytes 2359300
  55.0 24.2 %all-to-all-start.2 = ((bf16[32,8,1536]{2,1,0:T(8,128)(2,1)}), bf16[32,8,1536]{2,1,0:T(8,128)(2,1)S(1)}, u32[]{:S(2)}, u32[]{:S(2)}) async-start(bf16[32,8,1536]{2,1,0:T(8,128)(2,1)} %bitcast.30), calls=%async_computation.2 | async-start | bytes 1572864 | tf_op jit(solution)/shard_map/all_to_all | solution.py:337
  58.7 24.3 %copy-start = (bf16[128,1024]{1,0:T(8,128)(2,1)S(1)}, bf16[128,1024]{1,0:T(8,128)(2,1)}, u32[]{:S(2)}) copy-start(bf16[128,1024]{1,0:T(8,128)(2,1)} %tokens_ref.5) | copy-start | bytes 786436
  58.7 24.3 %copy-start.1 = (bf16[128,1024]{1,0:T(8,128)(2,1)S(1)}, bf16[128,1024]{1,0:T(8,128)(2,1)}, u32[]{:S(2)}) copy-start(bf16[128,1024]{1,0:T(8,128)(2,1)} %cot_ref.3) | copy-start | bytes 786436
  58.7 24.3 %copy-start.2 = (bf16[1024,32]{0,1:T(8,128)(2,1)S(1)}, bf16[1024,32]{0,1:T(8,128)(2,1)}, u32[]{:S(2)}) copy-start(bf16[1024,32]{0,1:T(8,128)(2,1)} %param.8) | copy-start | bytes 196612
  58.7 24.2 %copy-start.3 = (s32[128,2]{0,1:T(2,128)S(1)}, s32[128,2]{0,1:T(2,128)}, u32[]{:S(2)}) copy-start(s32[128,2]{0,1:T(2,128)} %param.11) | copy-start | bytes 3076
  58.7 24.2 %copy-start.4 = (s32[128,2]{0,1:T(2,128)S(1)}, s32[128,2]{0,1:T(2,128)}, u32[]{:S(2)}) copy-start(s32[128,2]{0,1:T(2,128)} %param.12) | copy-start | bytes 3076
  58.7 24.2 %copy-start.5 = (f32[2,128]{1,0:T(2,128)S(1)}, f32[2,128]{1,0:T(2,128)}, u32[]{:S(2)}) copy-start(f32[2,128]{1,0:T(2,128)} %get-tuple-element.16.gates_ref) | copy-start | bytes 3076
  79.3 25.3 %all-to-all-start.3 = ((bf16[32,8,1536]{2,1,0:T(8,128)(2,1)}), bf16[32,8,1536]{2,1,0:T(8,128)(2,1)S(1)}, u32[]{:S(2)}, u32[]{:S(2)}) async-start(bf16[32,8,1536]{2,1,0:T(8,128)(2,1)} %bitcast.26), calls=%async_computation.3 | async-start | bytes 1572864 | tf_op jit(solution)/shard_map/all_to_all | solution.py:337
  84.5 1.3 %collective-permute-start = (f32[16,1024]{1,0:T(8,128)S(1)}, f32[16,1024]{1,0:T(8,128)S(1)}, u32[]{:S(2)}, u32[]{:S(2)}) collective-permute-start(f32[16,1024]{1,0:T(8,128)S(1)} %constant_dynamic-slice_fusion), channel_id=1, source_target_pairs={{0,1},{1,0},{2,3},{3,2},{4,5},{5,4},{6,7},{7,6},{8,9},{9,8},{10,11... | collective-permute-start | bytes 196616 | tf_op jit(solution)/shard_map/ppermute | solution.py:341
  85.7 9.0 %collective-permute-start.1 = (f32[16,1024]{1,0:T(8,128)S(1)}, f32[16,1024]{1,0:T(8,128)S(1)}, u32[]{:S(2)}, u32[]{:S(2)}) collective-permute-start(f32[16,1024]{1,0:T(8,128)S(1)} %dynamic-slice_add_fusion), channel_id=1, source_target_pairs={{0,2},{1,3},{2,0},{3,1},{4,6},{5,7},{6,4},{7,5},{8,10},{9,11},{10,... | collective-permute-start | bytes 196616 | tf_op jit(solution)/shard_map/ppermute | solution.py:341
  87.6 7.1 %collective-permute-start.2 = (f32[16,1024]{1,0:T(8,128)S(1)}, f32[16,1024]{1,0:T(8,128)S(1)}, u32[]{:S(2)}, u32[]{:S(2)}) collective-permute-start(f32[16,1024]{1,0:T(8,128)S(1)} %dynamic-slice_add_fusion), channel_id=1, source_target_pairs={{0,4},{1,5},{2,6},{3,7},{4,0},{5,1},{6,2},{7,3},{8,12},{9,13},{10,... | collective-permute-start | bytes 196616 | tf_op jit(solution)/shard_map/ppermute | solution.py:341
  89.0 6.3 %collective-permute-start.3 = (f32[16,1024]{1,0:T(8,128)S(1)}, f32[16,1024]{1,0:T(8,128)S(1)}, u32[]{:S(2)}, u32[]{:S(2)}) collective-permute-start(f32[16,1024]{1,0:T(8,128)S(1)} %dynamic-slice_add_fusion), channel_id=1, source_target_pairs={{0,6},{1,7},{2,4},{3,5},{4,2},{5,3},{6,0},{7,1},{8,14},{9,15},{10,... | collective-permute-start | bytes 196616 | tf_op jit(solution)/shard_map/ppermute | solution.py:341
  95.3 4.2 %collective-permute-start.4 = (bf16[16,1024]{1,0:T(8,128)(2,1)S(1)}, bf16[16,1024]{1,0:T(8,128)(2,1)S(1)}, u32[]{:S(2)}, u32[]{:S(2)}) collective-permute-start(bf16[16,1024]{1,0:T(8,128)(2,1)S(1)} %add_convert_fusion.1), channel_id=1, source_target_pairs={{0,8},{1,9},{2,10},{3,11},{4,12},{5,13},{6,14},{7,15},{8,0},{9,1},... | collective-permute-start | bytes 98312 | tf_op jit(solution)/shard_map/ppermute | solution.py:341
  99.5 5.1 %collective-permute-start.5 = (bf16[16,1024]{1,0:T(8,128)(2,1)S(1)}, bf16[16,1024]{1,0:T(8,128)(2,1)S(1)}, u32[]{:S(2)}, u32[]{:S(2)}) collective-permute-start(bf16[16,1024]{1,0:T(8,128)(2,1)S(1)} %add_convert_fusion), channel_id=1, source_target_pairs={{0,16},{1,17},{2,18},{3,19},{4,20},{5,21},{6,22},{7,23},{8,24},{9,... | collective-permute-start | bytes 98312 | tf_op jit(solution)/shard_map/ppermute | solution.py:341
  104.6 1.3 %collective-permute-start.6 = (f32[16,1024]{1,0:T(8,128)S(1)}, f32[16,1024]{1,0:T(8,128)S(1)}, u32[]{:S(2)}, u32[]{:S(2)}) collective-permute-start(f32[16,1024]{1,0:T(8,128)S(1)} %convert_add_fusion), channel_id=1, source_target_pairs={{0,1},{1,0},{2,3},{3,2},{4,5},{5,4},{6,7},{7,6},{8,9},{9,8},{10,11... | collective-permute-start | bytes 196616 | tf_op jit(solution)/shard_map/ppermute | solution.py:341

commit v8 on v7

--- a/solution.py
+++ b/solution.py
@@ -14,6 +14,7 @@
 PLANE = 8
 VMEM_BYTES = 60 * 1024 * 1024
 SMALL_VMEM_BYTES = 24 * 1024 * 1024
+EXPERT_VMEM_BYTES = 56 * 1024 * 1024 + 512 * 1024
 
 
 class Layout:
@@ -324,7 +325,7 @@
         out_specs=[whole, hid] if forward else whole,
         out_shape=[message_out, jax.ShapeDtypeStruct((rows, ff), BF16)] if forward else message_out,
         scratch_shapes=[pltpu.VMEM((rows, lay.width), BF16), pltpu.VMEM((rows, lay.width), F32)],
-        compiler_params=pltpu.CompilerParams(vmem_limit_bytes=VMEM_BYTES),
+        compiler_params=pltpu.CompilerParams(vmem_limit_bytes=EXPERT_VMEM_BYTES),
         cost_estimate=pl.CostEstimate(
             flops=4 * rows * lay.width * ff,
             bytes_accessed=4 * lay.width * ff + 2 * rows * ff + 4 * message.size,
@@ -382,6 +383,7 @@
         [message, jax.ShapeDtypeStruct((2, tok_rows), F32)],
         2 * place_flops,
         (ids, slots, tokens, router, cotangent),
+        EXPERT_VMEM_BYTES,
     )
     arrived = exchange(sent_tokens)
     grad_rows = exchange(sent_grads)

time: 107 us -> 107 us (level)
  no operation moved by 1% of the time
where the time goes in v8:
time: 107 us
  waiting for transfers between devices  40.9 us (38%)
  Pallas kernels  37.5 us (35%)
  starting transfers between devices  26.6 us (25%)
    pallas_call x2, Pallas kernels, expert_call(): pl.pallas_call(functools.partial(kernel, lay), grid=(ff // tile,), in_spe...  29.9 us
    all_to_all x4, waiting for transfers between devices, exchange(): return lax.all_to_all(x, AXES, split_axis=0, concat_axis=0, tiled=True)  29 us
    all_to_all x4, starting transfers between devices, exchange(): return lax.all_to_all(x, AXES, split_axis=0, concat_axis=0, tiled=True)  18.2 us
    ppermute x7, waiting for transfers between devices, from_device(): return lax.ppermute(x, AXES, [(d, d ^ bits) for d in range(devices)])  11.8 us
    ppermute x7, starting transfers between devices, from_device(): return lax.ppermute(x, AXES, [(d, d ^ bits) for d in range(devices)])  8.45 us
    pallas_call x4, Pallas kernels, call(): pl.pallas_call(kernel, out_shape=out_shape, compiler_params=pltpu.Compile...  7.66 us
  transfers between devices with their start and end apart: 11, of which 9 were waited for; matrix products, arithmetic and copies ran while one was open for 0% of the time, Pallas kernels for 33%

profile of v8, /device:TPU:0, one launch (start us, length us, event | category | flops | bytes accessed | tf_op | source)
XLA Modules:
  0.0 106.6 jit_solution(3967874436649193643)
XLA Ops:
  0.6 2.2 %shard_map.95 = bf16[256,1536]{1,0:T(8,128)(2,1)} custom-call(s32[2,128]{1,0:T(2,128)} %bitcast.17, s32[2,128]{1,0:T(2,128)} %bitcast.21, bf16[128,1024]{1,0:T(8,128)(2,1)} %tokens_ref.5), custom_call_target="tpu_custom_call" | custom-call | flops 134217728 | bytes 1050624 | tf_op jit(solution)/shard_map/pallas_call | solution.py:301
  2.9 7.3 %all-to-all-start = ((bf16[32,8,1536]{2,1,0:T(8,128)(2,1)}), bf16[32,8,1536]{2,1,0:T(8,128)(2,1)S(1)}, u32[]{:S(2)}, u32[]{:S(2)}) async-start(bf16[32,8,1536]{2,1,0:T(8,128)(2,1)} %bitcast.25), calls=%async_computation | async-start | bytes 1572864 | tf_op jit(solution)/shard_map/all_to_all | solution.py:338
  10.2 2.9 %shard_map.94 = (bf16[256,1536]{1,0:T(8,128)(2,1)}, f32[2,128]{1,0:T(2,128)}) custom-call(s32[2,128]{1,0:T(2,128)} %bitcast.18, s32[2,128]{1,0:T(2,128)} %bitcast.22, bf16[128,1024]{1,0:T(8,128)(2,1)} %tokens_ref.5, bf16[32,1024]{1,0:T(8,128)(2,1)} %bitcast.15, bf16[128,1024]{1,0:T(8,128)(2,1)} %cot_ref.3), custom_call_target="tpu_custom_call" | custom-call | flops 268435456 | bytes 1379328 | tf_op jit(solution)/shard_map/pallas_call | solution.py:301
  13.0 17.8 %all-to-all-done = bf16[32,8,1536]{2,1,0:T(8,128)(2,1)S(1)} async-done(((bf16[32,8,1536]{2,1,0:T(8,128)(2,1)}), bf16[32,8,1536]{2,1,0:T(8,128)(2,1)S(1)}, u32[]{:S(2)}, u32[]{:S(2)}) %all-to-all-start) | async-done | bytes 786464 | tf_op jit(solution)/shard_map/all_to_all | solution.py:338
  30.8 0.0 copy-start.6
  30.8 3.6 %all-to-all-start.1 = ((bf16[32,8,1536]{2,1,0:T(8,128)(2,1)}), bf16[32,8,1536]{2,1,0:T(8,128)(2,1)S(1)}, u32[]{:S(2)}, u32[]{:S(2)}) async-start(bf16[32,8,1536]{2,1,0:T(8,128)(2,1)} %bitcast.29), calls=%async_computation.1 | async-start | bytes 1572864 | tf_op jit(solution)/shard_map/all_to_all | solution.py:338
  34.4 0.0 copy-done.6
  34.4 14.7 %shard_map.96 = (bf16[256,1536]{1,0:T(8,128)(2,1)}, bf16[384,4096]{1,0:T(8,128)(2,1)}) custom-call(bf16[256,1536]{1,0:T(8,128)(2,1)} %bitcast.27, bf16[1,1024,4096]{2,1,0:T(8,128)(2,1)} %win_ref.3, bf16[1,4096,1024]{2,1,0:T(8,128)(2,1)} %wout_ref.3), custom_call_target="tpu_custom_call" | custom-call | flops 6442450944 | bytes 21495808 | tf_op jit(solution)/shard_map/pallas_call | solution.py:321
  49.1 5.9 %all-to-all-done.1 = bf16[32,8,1536]{2,1,0:T(8,128)(2,1)S(1)} async-done(((bf16[32,8,1536]{2,1,0:T(8,128)(2,1)}), bf16[32,8,1536]{2,1,0:T(8,128)(2,1)S(1)}, u32[]{:S(2)}, u32[]{:S(2)}) %all-to-all-start.1) | async-done | bytes 786464 | tf_op jit(solution)/shard_map/all_to_all | solution.py:338
  55.0 0.0 copy-start.7
  55.0 3.6 %all-to-all-start.2 = ((bf16[32,8,1536]{2,1,0:T(8,128)(2,1)}), bf16[32,8,1536]{2,1,0:T(8,128)(2,1)S(1)}, u32[]{:S(2)}, u32[]{:S(2)}) async-start(bf16[32,8,1536]{2,1,0:T(8,128)(2,1)} %bitcast.30), calls=%async_computation.2 | async-start | bytes 1572864 | tf_op jit(solution)/shard_map/all_to_all | solution.py:338
  58.7 0.0 copy-done.7
  58.7 0.0 copy-start
  58.7 0.0 copy-start.1
  58.7 0.0 copy-start.2
  58.7 0.0 copy-start.3
  58.7 0.0 copy-start.4
  58.7 0.0 copy-start.5
  58.7 15.1 %shard_map.97 = bf16[256,1536]{1,0:T(8,128)(2,1)} custom-call(bf16[256,1536]{1,0:T(8,128)(2,1)} %bitcast.28, bf16[384,4096]{1,0:T(8,128)(2,1)} %get-tuple-element.20.hidden_ref, bf16[1,1024,4096]{2,1,0:T(8,128)(2,1)} %win_ref.3, bf16[1,4096,1024]{2,1,0:T(8,128)(2,1)} %wout_ref.3), custom_call_target="tpu_custom_call" | custom-call | flops 6442450944 | bytes 21495808 | tf_op jit(solution)/shard_map/pallas_call | solution.py:321
  73.9 5.4 %all-to-all-done.2 = bf16[32,8,1536]{2,1,0:T(8,128)(2,1)S(1)} async-done(((bf16[32,8,1536]{2,1,0:T(8,128)(2,1)}), bf16[32,8,1536]{2,1,0:T(8,128)(2,1)S(1)}, u32[]{:S(2)}, u32[]{:S(2)}) %all-to-all-start.2) | async-done | bytes 786464 | tf_op jit(solution)/shard_map/all_to_all | solution.py:338
  79.3 3.6 %all-to-all-start.3 = ((bf16[32,8,1536]{2,1,0:T(8,128)(2,1)}), bf16[32,8,1536]{2,1,0:T(8,128)(2,1)S(1)}, u32[]{:S(2)}, u32[]{:S(2)}) async-start(bf16[32,8,1536]{2,1,0:T(8,128)(2,1)} %bitcast.26), calls=%async_computation.3 | async-start | bytes 1572864 | tf_op jit(solution)/shard_map/all_to_all | solution.py:338
  82.9 0.0 copy-done
  82.9 0.0 copy-done.1
  82.9 0.0 copy-done.2
  83.0 0.0 copy-done.3
  83.0 0.0 copy-done.4
  83.0 0.0 copy-done.5
  83.0 1.5 %shard_map.98 = (bf16[128,1024]{1,0:T(8,128)(2,1)}, f32[128,1024]{1,0:T(8,128)S(1)}, f32[32,1024]{1,0:T(8,128)S(1)}) custom-call(s32[2,128]{1,0:T(2,128)S(1)} %bitcast.19, s32[2,128]{1,0:T(2,128)S(1)} %bitcast.23, f32[2,128]{1,0:T(2,128)S(1)} %copy-done.5, bf16[256,1536]{1,0:T(8,128)(2,1)S(1)} %bitcast.14, bf16[128,1024]{1,0:T(8,128)(2,1)S(1)} %copy-done.1, ...), custom_call_target="tpu_custom_call" | custom-call | flops 268435456 | bytes 2296832 | tf_op jit(solution)/shard_map/pallas_call | solution.py:301
  84.5 0.3 collective-permute-start
  84.7 1.0 collective-permute-done
  85.7 1.8 %collective-permute-start.1 = (f32[16,1024]{1,0:T(8,128)S(1)}, f32[16,1024]{1,0:T(8,128)S(1)}, u32[]{:S(2)}, u32[]{:S(2)}) collective-permute-start(f32[16,1024]{1,0:T(8,128)S(1)} %dynamic-slice_add_fusion), channel_id=1, source_target_pairs={{0,2},{1,3},{2,0},{3,1},{4,6},{5,7},{6,4},{7,5},{8,10},{9,11},{10,... | collective-permute-start | bytes 196616 | tf_op jit(solution)/shard_map/ppermute | solution.py:342
  87.6 1.5 %collective-permute-start.2 = (f32[16,1024]{1,0:T(8,128)S(1)}, f32[16,1024]{1,0:T(8,128)S(1)}, u32[]{:S(2)}, u32[]{:S(2)}) collective-permute-start(f32[16,1024]{1,0:T(8,128)S(1)} %dynamic-slice_add_fusion), channel_id=1, source_target_pairs={{0,4},{1,5},{2,6},{3,7},{4,0},{5,1},{6,2},{7,3},{8,12},{9,13},{10,... | collective-permute-start | bytes 196616 | tf_op jit(solution)/shard_map/ppermute | solution.py:342
  89.0 0.3 collective-permute-start.3
  89.3 5.4 %collective-permute-done.1 = f32[16,1024]{1,0:T(8,128)S(1)} collective-permute-done((f32[16,1024]{1,0:T(8,128)S(1)}, f32[16,1024]{1,0:T(8,128)S(1)}, u32[]{:S(2)}, u32[]{:S(2)}) %collective-permute-start.1) | collective-permute-done | bytes 65568 | tf_op jit(solution)/shard_map/ppermute | solution.py:342
  94.7 0.0 collective-permute-done.2
  94.7 0.6 collective-permute-done.3
  95.3 1.8 %collective-permute-start.4 = (bf16[16,1024]{1,0:T(8,128)(2,1)S(1)}, bf16[16,1024]{1,0:T(8,128)(2,1)S(1)}, u32[]{:S(2)}, u32[]{:S(2)}) collective-permute-start(bf16[16,1024]{1,0:T(8,128)(2,1)S(1)} %add_convert_fusion.1), channel_id=1, source_target_pairs={{0,8},{1,9},{2,10},{3,11},{4,12},{5,13},{6,14},{7,15},{8,0},{9,1},... | collective-permute-start | bytes 98312 | tf_op jit(solution)/shard_map/ppermute | solution.py:342
  97.1 2.4 %collective-permute-done.4 = bf16[16,1024]{1,0:T(8,128)(2,1)S(1)} collective-permute-done((bf16[16,1024]{1,0:T(8,128)(2,1)S(1)}, bf16[16,1024]{1,0:T(8,128)(2,1)S(1)}, u32[]{:S(2)}, u32[]{:S(2)}) %collective-permute-start.4) | collective-permute-done | bytes 32800 | tf_op jit(solution)/shard_map/ppermute | solution.py:342
  99.5 2.8 %collective-permute-start.5 = (bf16[16,1024]{1,0:T(8,128)(2,1)S(1)}, bf16[16,1024]{1,0:T(8,128)(2,1)S(1)}, u32[]{:S(2)}, u32[]{:S(2)}) collective-permute-start(bf16[16,1024]{1,0:T(8,128)(2,1)S(1)} %add_convert_fusion), channel_id=1, source_target_pairs={{0,16},{1,17},{2,18},{3,19},{4,20},{5,21},{6,22},{7,23},{8,24},{9,... | collective-permute-start | bytes 98312 | tf_op jit(solution)/shard_map/ppermute | solution.py:342
  102.3 2.3 %collective-permute-done.5 = bf16[16,1024]{1,0:T(8,128)(2,1)S(1)} collective-permute-done((bf16[16,1024]{1,0:T(8,128)(2,1)S(1)}, bf16[16,1024]{1,0:T(8,128)(2,1)S(1)}, u32[]{:S(2)}, u32[]{:S(2)}) %collective-permute-start.5) | collective-permute-done | bytes 32800 | tf_op jit(solution)/shard_map/ppermute | solution.py:342
  104.6 0.0 all-to-all-done.3
  104.6 0.1 collective-permute-start.6
  104.7 1.1 %shard_map.99 = bf16[128,1024]{1,0:T(8,128)(2,1)} custom-call(s32[2,128]{1,0:T(2,128)S(1)} %bitcast.20, s32[2,128]{1,0:T(2,128)S(1)} %bitcast.24, bf16[256,1536]{1,0:T(8,128)(2,1)S(1)} %bitcast.13, f32[128,1024]{1,0:T(8,128)S(1)} %get-tuple-element.27.back_ref), custom_call_target="tpu_custom_call" | custom-call | flops 134217728 | bytes 1574912 | tf_op jit(solution)/shard_map/pallas_call | solution.py:301
  105.8 0.1 collective-permute-done.6
  105.9 0.7 maximum_bitcast_fusion
  (6 shorter events, 0.1 us)
Async XLA Ops:
  2.9 27.9 %all-to-all-start = ((bf16[32,8,1536]{2,1,0:T(8,128)(2,1)}), bf16[32,8,1536]{2,1,0:T(8,128)(2,1)S(1)}, u32[]{:S(2)}, u32[]{:S(2)}) async-start(bf16[32,8,1536]{2,1,0:T(8,128)(2,1)} %bitcast.25), calls=%async_computation | async-start | bytes 1572864 | tf_op jit(solution)/shard_map/all_to_all | solution.py:338
  30.8 3.6 %copy-start.6 = (bf16[32,8,1536]{2,1,0:T(8,128)(2,1)}, bf16[32,8,1536]{2,1,0:T(8,128)(2,1)S(1)}, u32[]{:S(2)}) copy-start(bf16[32,8,1536]{2,1,0:T(8,128)(2,1)S(1)} %all-to-all-done) | copy-start | bytes 2359300
  30.8 24.2 %all-to-all-start.1 = ((bf16[32,8,1536]{2,1,0:T(8,128)(2,1)}), bf16[32,8,1536]{2,1,0:T(8,128)(2,1)S(1)}, u32[]{:S(2)}, u32[]{:S(2)}) async-start(bf16[32,8,1536]{2,1,0:T(8,128)(2,1)} %bitcast.29), calls=%async_computation.1 | async-start | bytes 1572864 | tf_op jit(solution)/shard_map/all_to_all | solution.py:338
  55.0 3.6 %copy-start.7 = (bf16[32,8,1536]{2,1,0:T(8,128)(2,1)}, bf16[32,8,1536]{2,1,0:T(8,128)(2,1)S(1)}, u32[]{:S(2)}) copy-start(bf16[32,8,1536]{2,1,0:T(8,128)(2,1)S(1)} %all-to-all-done.1) | copy-start | bytes 2359300
  55.0 24.2 %all-to-all-start.2 = ((bf16[32,8,1536]{2,1,0:T(8,128)(2,1)}), bf16[32,8,1536]{2,1,0:T(8,128)(2,1)S(1)}, u32[]{:S(2)}, u32[]{:S(2)}) async-start(bf16[32,8,1536]{2,1,0:T(8,128)(2,1)} %bitcast.30), calls=%async_computation.2 | async-start | bytes 1572864 | tf_op jit(solution)/shard_map/all_to_all | solution.py:338
  58.7 24.3 %copy-start = (bf16[128,1024]{1,0:T(8,128)(2,1)S(1)}, bf16[128,1024]{1,0:T(8,128)(2,1)}, u32[]{:S(2)}) copy-start(bf16[128,1024]{1,0:T(8,128)(2,1)} %tokens_ref.5) | copy-start | bytes 786436
  58.7 24.3 %copy-start.1 = (bf16[128,1024]{1,0:T(8,128)(2,1)S(1)}, bf16[128,1024]{1,0:T(8,128)(2,1)}, u32[]{:S(2)}) copy-start(bf16[128,1024]{1,0:T(8,128)(2,1)} %cot_ref.3) | copy-start | bytes 786436
  58.7 24.3 %copy-start.2 = (bf16[1024,32]{0,1:T(8,128)(2,1)S(1)}, bf16[1024,32]{0,1:T(8,128)(2,1)}, u32[]{:S(2)}) copy-start(bf16[1024,32]{0,1:T(8,128)(2,1)} %param.8) | copy-start | bytes 196612
  58.7 24.2 %copy-start.3 = (s32[128,2]{0,1:T(2,128)S(1)}, s32[128,2]{0,1:T(2,128)}, u32[]{:S(2)}) copy-start(s32[128,2]{0,1:T(2,128)} %param.11) | copy-start | bytes 3076
  58.7 24.2 %copy-start.4 = (s32[128,2]{0,1:T(2,128)S(1)}, s32[128,2]{0,1:T(2,128)}, u32[]{:S(2)}) copy-start(s32[128,2]{0,1:T(2,128)} %param.12) | copy-start | bytes 3076
  58.7 24.2 %copy-start.5 = (f32[2,128]{1,0:T(2,128)S(1)}, f32[2,128]{1,0:T(2,128)}, u32[]{:S(2)}) copy-start(f32[2,128]{1,0:T(2,128)} %get-tuple-element.16.gates_ref) | copy-start | bytes 3076
  79.3 25.3 %all-to-all-start.3 = ((bf16[32,8,1536]{2,1,0:T(8,128)(2,1)}), bf16[32,8,1536]{2,1,0:T(8,128)(2,1)S(1)}, u32[]{:S(2)}, u32[]{:S(2)}) async-start(bf16[32,8,1536]{2,1,0:T(8,128)(2,1)} %bitcast.26), calls=%async_computation.3 | async-start | bytes 1572864 | tf_op jit(solution)/shard_map/all_to_all | solution.py:338
  84.5 1.3 %collective-permute-start = (f32[16,1024]{1,0:T(8,128)S(1)}, f32[16,1024]{1,0:T(8,128)S(1)}, u32[]{:S(2)}, u32[]{:S(2)}) collective-permute-start(f32[16,1024]{1,0:T(8,128)S(1)} %constant_dynamic-slice_fusion), channel_id=1, source_target_pairs={{0,1},{1,0},{2,3},{3,2},{4,5},{5,4},{6,7},{7,6},{8,9},{9,8},{10,11... | collective-permute-start | bytes 196616 | tf_op jit(solution)/shard_map/ppermute | solution.py:342
  85.7 9.0 %collective-permute-start.1 = (f32[16,1024]{1,0:T(8,128)S(1)}, f32[16,1024]{1,0:T(8,128)S(1)}, u32[]{:S(2)}, u32[]{:S(2)}) collective-permute-start(f32[16,1024]{1,0:T(8,128)S(1)} %dynamic-slice_add_fusion), channel_id=1, source_target_pairs={{0,2},{1,3},{2,0},{3,1},{4,6},{5,7},{6,4},{7,5},{8,10},{9,11},{10,... | collective-permute-start | bytes 196616 | tf_op jit(solution)/shard_map/ppermute | solution.py:342
  87.6 7.1 %collective-permute-start.2 = (f32[16,1024]{1,0:T(8,128)S(1)}, f32[16,1024]{1,0:T(8,128)S(1)}, u32[]{:S(2)}, u32[]{:S(2)}) collective-permute-start(f32[16,1024]{1,0:T(8,128)S(1)} %dynamic-slice_add_fusion), channel_id=1, source_target_pairs={{0,4},{1,5},{2,6},{3,7},{4,0},{5,1},{6,2},{7,3},{8,12},{9,13},{10,... | collective-permute-start | bytes 196616 | tf_op jit(solution)/shard_map/ppermute | solution.py:342
  89.0 6.3 %collective-permute-start.3 = (f32[16,1024]{1,0:T(8,128)S(1)}, f32[16,1024]{1,0:T(8,128)S(1)}, u32[]{:S(2)}, u32[]{:S(2)}) collective-permute-start(f32[16,1024]{1,0:T(8,128)S(1)} %dynamic-slice_add_fusion), channel_id=1, source_target_pairs={{0,6},{1,7},{2,4},{3,5},{4,2},{5,3},{6,0},{7,1},{8,14},{9,15},{10,... | collective-permute-start | bytes 196616 | tf_op jit(solution)/shard_map/ppermute | solution.py:342
  95.3 4.2 %collective-permute-start.4 = (bf16[16,1024]{1,0:T(8,128)(2,1)S(1)}, bf16[16,1024]{1,0:T(8,128)(2,1)S(1)}, u32[]{:S(2)}, u32[]{:S(2)}) collective-permute-start(bf16[16,1024]{1,0:T(8,128)(2,1)S(1)} %add_convert_fusion.1), channel_id=1, source_target_pairs={{0,8},{1,9},{2,10},{3,11},{4,12},{5,13},{6,14},{7,15},{8,0},{9,1},... | collective-permute-start | bytes 98312 | tf_op jit(solution)/shard_map/ppermute | solution.py:342
  99.5 5.1 %collective-permute-start.5 = (bf16[16,1024]{1,0:T(8,128)(2,1)S(1)}, bf16[16,1024]{1,0:T(8,128)(2,1)S(1)}, u32[]{:S(2)}, u32[]{:S(2)}) collective-permute-start(bf16[16,1024]{1,0:T(8,128)(2,1)S(1)} %add_convert_fusion), channel_id=1, source_target_pairs={{0,16},{1,17},{2,18},{3,19},{4,20},{5,21},{6,22},{7,23},{8,24},{9,... | collective-permute-start | bytes 98312 | tf_op jit(solution)/shard_map/ppermute | solution.py:342
  104.6 1.3 %collective-permute-start.6 = (f32[16,1024]{1,0:T(8,128)S(1)}, f32[16,1024]{1,0:T(8,128)S(1)}, u32[]{:S(2)}, u32[]{:S(2)}) collective-permute-start(f32[16,1024]{1,0:T(8,128)S(1)} %convert_add_fusion), channel_id=1, source_target_pairs={{0,1},{1,0},{2,3},{3,2},{4,5},{5,4},{6,7},{7,6},{8,9},{9,8},{10,11... | collective-permute-start | bytes 196616 | tf_op jit(solution)/shard_map/ppermute | solution.py:342

commit v9 on v7

--- a/solution.py
+++ b/solution.py
@@ -59,7 +59,8 @@
     return jnp.sum(jnp.where(eye, column, 0.0), axis=0, keepdims=True)
 
 
-def targets(lay, ids, slots):
+def targets(lay, experts, ids, slots):
+    ids = rank_of(ids, experts)
     found = []
     kept = slots < lay.capacity
     for group in range(lay.full):
@@ -169,8 +170,8 @@
 
 
 def send_tokens_kernel(lay, ids_ref, slots_ref, tokens_ref, out_ref):
-    first = targets(lay, ids_ref[0:1, :], slots_ref[0:1, :])
-    second = targets(lay, ids_ref[1:2, :], slots_ref[1:2, :])
+    first = targets(lay, out_ref.shape[0] // GROUP, ids_ref[0:1, :], slots_ref[0:1, :])
+    second = targets(lay, out_ref.shape[0] // GROUP, ids_ref[1:2, :], slots_ref[1:2, :])
     place(lay, [[first, second]], [tokens_ref[...]], out_ref)
 
 
@@ -188,7 +189,10 @@
     gates_ref[1:2, :] = gates[1]
     cot = cot_ref[...].astype(F32)
     scaled = [(as_column(gate) * cot).astype(BF16) for gate in gates]
-    ranks = [[targets(lay, ids_ref[k : k + 1, :], slots_ref[k : k + 1, :])] for k in range(2)]
+    experts = out_ref.shape[0] // GROUP
+    ranks = [
+        [targets(lay, experts, ids_ref[k : k + 1, :], slots_ref[k : k + 1, :])] for k in range(2)
+    ]
     place(lay, ranks, scaled, out_ref)
 
 
@@ -240,10 +244,10 @@
         pack(lay, total_ref, out_ref)
 
 
-def column_targets(lay, ids_ref, slots_ref):
+def column_targets(lay, experts, ids_ref, slots_ref):
     ids = [as_column(ids_ref[k : k + 1, :].astype(F32)).astype(jnp.int32) for k in range(2)]
     slots = [as_column(slots_ref[k : k + 1, :].astype(F32)).astype(jnp.int32) for k in range(2)]
-    return ids, [targets(lay, ids[k], slots[k]) for k in range(2)]
+    return ids, [targets(lay, experts, ids[k], slots[k]) for k in range(2)]
 
 
 def split_in_two(x):
@@ -266,7 +270,7 @@
 ):
     experts = router_ref.shape[0]
     toks = tokens_ref.shape[0]
-    ids, ranks = column_targets(lay, ids_ref, slots_ref)
+    ids, ranks = column_targets(lay, experts, ids_ref, slots_ref)
     gates = [as_column(gates_ref[k : k + 1, :]) for k in range(2)]
     cot = cot_ref[...].astype(F32)
     choice = [pick(lay, [ranks[k]], message_ref) for k in range(2)]
@@ -290,7 +294,7 @@
 
 
 def grad_kernel(lay, ids_ref, slots_ref, message_ref, back_ref, out_ref):
-    _, ranks = column_targets(lay, ids_ref, slots_ref)
+    _, ranks = column_targets(lay, message_ref.shape[0] // GROUP, ids_ref, slots_ref)
     out_ref[...] = (pick(lay, ranks, message_ref) + back_ref[...]).astype(BF16)
 
 
@@ -333,8 +337,16 @@
     )(*operands)
 
 
-def exchange(x):
-    return lax.all_to_all(x, AXES, split_axis=0, concat_axis=0, tiled=True)
+def rank_of(device, devices):
+    half = devices // 2
+    return (device & (half - 1)) * 2 + jnp.where(device >= half, 1, 0)
+
+
+def exchange(x, devices):
+    order = [rank // 2 + rank % 2 * (devices // 2) for rank in range(devices)]
+    return lax.all_to_all(
+        x, AXES, split_axis=0, concat_axis=0, tiled=True, axis_index_groups=[order]
+    )
 
 
 def from_device(x, bits, devices):
@@ -383,14 +395,14 @@
         2 * place_flops,
         (ids, slots, tokens, router, cotangent),
     )
-    arrived = exchange(sent_tokens)
-    grad_rows = exchange(sent_grads)
+    arrived = exchange(sent_tokens, devices)
+    grad_rows = exchange(sent_grads, devices)
     produced, hidden = expert_call(forward_kernel, lay, arrived, None, in_weight, out_weight)
     produced, grad_rows = lax.optimization_barrier((produced, grad_rows))
-    produced_back = exchange(produced)
+    produced_back = exchange(produced, devices)
     returned = expert_call(backward_kernel, lay, grad_rows, hidden, in_weight, out_weight)
     returned, produced_back = lax.optimization_barrier((returned, produced_back))
-    returned_back = exchange(returned)
+    returned_back = exchange(returned, devices)
 
     mixed, router_back, partial_grad = call(
         functools.partial(mix_kernel, lay),

time: 107 us -> 108 us (level)
  waiting for transfers between devices: 40.9 us -> 43.4 us
  starting transfers between devices: 26.6 us -> 25 us
    ppermute x7, waiting for transfers between devices: 11.8 us -> 14.7 us  [from_device(): return lax.ppermute(x, AXES, [(d, d ^ bits) for d in range(devices)])]
    ppermute x7, starting transfers between devices: 8.45 us -> 6.72 us  [from_device(): return lax.ppermute(x, AXES, [(d, d ^ bits) for d in range(devices)])]
  transfers between devices with their start and end apart: 11 -> 11, of which waited for: 9 -> 8; matrix products, arithmetic and copies ran while one was open for 0% -> 0% of each run, Pallas kernels for 33% -> 33%
where the time goes in v9:
time: 108 us
  waiting for transfers between devices  43.4 us (40%)
  Pallas kernels  37.6 us (35%)
  starting transfers between devices  25 us (23%)
    pallas_call x2, Pallas kernels, expert_call(): pl.pallas_call(functools.partial(kernel, lay), grid=(ff // tile,), in_spe...  29.9 us
    all_to_all x4, waiting for transfers between devices, exchange(): lax.all_to_all(x, AXES, split_axis=0, concat_axis=0, tiled=True, axis_ind...  28.7 us
    all_to_all x4, starting transfers between devices, exchange(): lax.all_to_all(x, AXES, split_axis=0, concat_axis=0, tiled=True, axis_ind...  18.3 us
    ppermute x7, waiting for transfers between devices, from_device(): return lax.ppermute(x, AXES, [(d, d ^ bits) for d in range(devices)])  14.7 us
    pallas_call x4, Pallas kernels, call(): pl.pallas_call(kernel, out_shape=out_shape, compiler_params=pltpu.Compile...  7.7 us
    ppermute x7, starting transfers between devices, from_device(): return lax.ppermute(x, AXES, [(d, d ^ bits) for d in range(devices)])  6.72 us
  transfers between devices with their start and end apart: 11, of which 8 were waited for; matrix products, arithmetic and copies ran while one was open for 0% of the time, Pallas kernels for 33%

profile of v9, /device:TPU:0, one launch (start us, length us, event | category | flops | bytes accessed | tf_op | source)
XLA Modules:
  0.0 107.6 jit_solution(3560699444687065547)
XLA Ops:
  0.6 2.2 %shard_map.95 = bf16[256,1536]{1,0:T(8,128)(2,1)} custom-call(s32[2,128]{1,0:T(2,128)} %bitcast.17, s32[2,128]{1,0:T(2,128)} %bitcast.21, bf16[128,1024]{1,0:T(8,128)(2,1)} %tokens_ref.5), custom_call_target="tpu_custom_call" | custom-call | flops 134217728 | bytes 1050624 | tf_op jit(solution)/shard_map/pallas_call | solution.py:304
  2.9 7.3 %all-to-all-start = ((bf16[32,8,1536]{2,1,0:T(8,128)(2,1)}), bf16[32,8,1536]{2,1,0:T(8,128)(2,1)S(1)}, u32[]{:S(2)}, u32[]{:S(2)}) async-start(bf16[32,8,1536]{2,1,0:T(8,128)(2,1)} %bitcast.25), calls=%async_computation | async-start | bytes 1572864 | tf_op jit(solution)/shard_map/all_to_all | solution.py:347
  10.2 2.9 %shard_map.94 = (bf16[256,1536]{1,0:T(8,128)(2,1)}, f32[2,128]{1,0:T(2,128)}) custom-call(s32[2,128]{1,0:T(2,128)} %bitcast.18, s32[2,128]{1,0:T(2,128)} %bitcast.22, bf16[128,1024]{1,0:T(8,128)(2,1)} %tokens_ref.5, bf16[32,1024]{1,0:T(8,128)(2,1)} %bitcast.15, bf16[128,1024]{1,0:T(8,128)(2,1)} %cot_ref.3), custom_call_target="tpu_custom_call" | custom-call | flops 268435456 | bytes 1379328 | tf_op jit(solution)/shard_map/pallas_call | solution.py:304
  13.0 17.6 %all-to-all-done = bf16[32,8,1536]{2,1,0:T(8,128)(2,1)S(1)} async-done(((bf16[32,8,1536]{2,1,0:T(8,128)(2,1)}), bf16[32,8,1536]{2,1,0:T(8,128)(2,1)S(1)}, u32[]{:S(2)}, u32[]{:S(2)}) %all-to-all-start) | async-done | bytes 786464 | tf_op jit(solution)/shard_map/all_to_all | solution.py:347
  30.7 0.0 copy-start.6
  30.7 3.7 %all-to-all-start.1 = ((bf16[32,8,1536]{2,1,0:T(8,128)(2,1)}), bf16[32,8,1536]{2,1,0:T(8,128)(2,1)S(1)}, u32[]{:S(2)}, u32[]{:S(2)}) async-start(bf16[32,8,1536]{2,1,0:T(8,128)(2,1)} %bitcast.29), calls=%async_computation.1 | async-start | bytes 1572864 | tf_op jit(solution)/shard_map/all_to_all | solution.py:347
  34.4 0.0 copy-done.6
  34.4 14.7 %shard_map.96 = (bf16[256,1536]{1,0:T(8,128)(2,1)}, bf16[384,4096]{1,0:T(8,128)(2,1)}) custom-call(bf16[256,1536]{1,0:T(8,128)(2,1)} %bitcast.27, bf16[1,1024,4096]{2,1,0:T(8,128)(2,1)} %win_ref.3, bf16[1,4096,1024]{2,1,0:T(8,128)(2,1)} %wout_ref.3), custom_call_target="tpu_custom_call" | custom-call | flops 6442450944 | bytes 21495808 | tf_op jit(solution)/shard_map/pallas_call | solution.py:324
  49.1 5.8 %all-to-all-done.1 = bf16[32,8,1536]{2,1,0:T(8,128)(2,1)S(1)} async-done(((bf16[32,8,1536]{2,1,0:T(8,128)(2,1)}), bf16[32,8,1536]{2,1,0:T(8,128)(2,1)S(1)}, u32[]{:S(2)}, u32[]{:S(2)}) %all-to-all-start.1) | async-done | bytes 786464 | tf_op jit(solution)/shard_map/all_to_all | solution.py:347
  54.9 0.0 copy-start.7
  54.9 3.7 %all-to-all-start.2 = ((bf16[32,8,1536]{2,1,0:T(8,128)(2,1)}), bf16[32,8,1536]{2,1,0:T(8,128)(2,1)S(1)}, u32[]{:S(2)}, u32[]{:S(2)}) async-start(bf16[32,8,1536]{2,1,0:T(8,128)(2,1)} %bitcast.30), calls=%async_computation.2 | async-start | bytes 1572864 | tf_op jit(solution)/shard_map/all_to_all | solution.py:347
  58.6 0.0 copy-done.7
  58.6 0.0 copy-start
  58.6 0.0 copy-start.1
  58.6 0.0 copy-start.2
  58.6 0.0 copy-start.3
  58.6 0.0 copy-start.4
  58.6 0.0 copy-start.5
  58.6 15.1 %shard_map.97 = bf16[256,1536]{1,0:T(8,128)(2,1)} custom-call(bf16[256,1536]{1,0:T(8,128)(2,1)} %bitcast.28, bf16[384,4096]{1,0:T(8,128)(2,1)} %get-tuple-element.20.hidden_ref, bf16[1,1024,4096]{2,1,0:T(8,128)(2,1)} %win_ref.3, bf16[1,4096,1024]{2,1,0:T(8,128)(2,1)} %wout_ref.3), custom_call_target="tpu_custom_call" | custom-call | flops 6442450944 | bytes 21495808 | tf_op jit(solution)/shard_map/pallas_call | solution.py:324
  73.8 5.3 %all-to-all-done.2 = bf16[32,8,1536]{2,1,0:T(8,128)(2,1)S(1)} async-done(((bf16[32,8,1536]{2,1,0:T(8,128)(2,1)}), bf16[32,8,1536]{2,1,0:T(8,128)(2,1)S(1)}, u32[]{:S(2)}, u32[]{:S(2)}) %all-to-all-start.2) | async-done | bytes 786464 | tf_op jit(solution)/shard_map/all_to_all | solution.py:347
  79.1 3.7 %all-to-all-start.3 = ((bf16[32,8,1536]{2,1,0:T(8,128)(2,1)}), bf16[32,8,1536]{2,1,0:T(8,128)(2,1)S(1)}, u32[]{:S(2)}, u32[]{:S(2)}) async-start(bf16[32,8,1536]{2,1,0:T(8,128)(2,1)} %bitcast.26), calls=%async_computation.3 | async-start | bytes 1572864 | tf_op jit(solution)/shard_map/all_to_all | solution.py:347
  82.8 0.0 copy-done
  82.8 0.0 copy-done.1
  82.8 0.0 copy-done.2
  82.8 0.0 copy-done.3
  82.8 0.0 copy-done.4
  82.8 0.0 copy-done.5
  82.8 1.5 %shard_map.98 = (bf16[128,1024]{1,0:T(8,128)(2,1)}, f32[128,1024]{1,0:T(8,128)S(1)}, f32[32,1024]{1,0:T(8,128)S(1)}) custom-call(s32[2,128]{1,0:T(2,128)S(1)} %bitcast.19, s32[2,128]{1,0:T(2,128)S(1)} %bitcast.23, f32[2,128]{1,0:T(2,128)S(1)} %copy-done.5, bf16[256,1536]{1,0:T(8,128)(2,1)S(1)} %bitcast.14, bf16[128,1024]{1,0:T(8,128)(2,1)S(1)} %copy-done.1, ...), custom_call_target="tpu_custom_call" | custom-call | flops 268435456 | bytes 2296832 | tf_op jit(solution)/shard_map/pallas_call | solution.py:304
  84.3 0.3 collective-permute-start
  84.6 1.0 collective-permute-done
  85.6 1.8 %collective-permute-start.1 = (f32[16,1024]{1,0:T(8,128)S(1)}, f32[16,1024]{1,0:T(8,128)S(1)}, u32[]{:S(2)}, u32[]{:S(2)}) collective-permute-start(f32[16,1024]{1,0:T(8,128)S(1)} %dynamic-slice_add_fusion), channel_id=1, source_target_pairs={{0,2},{1,3},{2,0},{3,1},{4,6},{5,7},{6,4},{7,5},{8,10},{9,11},{10,... | collective-permute-start | bytes 196616 | tf_op jit(solution)/shard_map/ppermute | solution.py:353
  87.4 1.5 %collective-permute-start.2 = (f32[16,1024]{1,0:T(8,128)S(1)}, f32[16,1024]{1,0:T(8,128)S(1)}, u32[]{:S(2)}, u32[]{:S(2)}) collective-permute-start(f32[16,1024]{1,0:T(8,128)S(1)} %dynamic-slice_add_fusion), channel_id=1, source_target_pairs={{0,4},{1,5},{2,6},{3,7},{4,0},{5,1},{6,2},{7,3},{8,12},{9,13},{10,... | collective-permute-start | bytes 196616 | tf_op jit(solution)/shard_map/ppermute | solution.py:353
  88.9 0.3 collective-permute-start.3
  89.1 7.3 %collective-permute-done.1 = f32[16,1024]{1,0:T(8,128)S(1)} collective-permute-done((f32[16,1024]{1,0:T(8,128)S(1)}, f32[16,1024]{1,0:T(8,128)S(1)}, u32[]{:S(2)}, u32[]{:S(2)}) %collective-permute-start.1) | collective-permute-done | bytes 65568 | tf_op jit(solution)/shard_map/ppermute | solution.py:353
  96.4 0.0 collective-permute-done.2
  96.4 0.0 collective-permute-done.3
  96.5 1.2 %collective-permute-start.4 = (bf16[16,1024]{1,0:T(8,128)(2,1)S(1)}, bf16[16,1024]{1,0:T(8,128)(2,1)S(1)}, u32[]{:S(2)}, u32[]{:S(2)}) collective-permute-start(bf16[16,1024]{1,0:T(8,128)(2,1)S(1)} %add_convert_fusion.1), channel_id=1, source_target_pairs={{0,8},{1,9},{2,10},{3,11},{4,12},{5,13},{6,14},{7,15},{8,0},{9,1},... | collective-permute-start | bytes 98312 | tf_op jit(solution)/shard_map/ppermute | solution.py:353
  97.7 3.0 %collective-permute-done.4 = bf16[16,1024]{1,0:T(8,128)(2,1)S(1)} collective-permute-done((bf16[16,1024]{1,0:T(8,128)(2,1)S(1)}, bf16[16,1024]{1,0:T(8,128)(2,1)S(1)}, u32[]{:S(2)}, u32[]{:S(2)}) %collective-permute-start.4) | collective-permute-done | bytes 32800 | tf_op jit(solution)/shard_map/ppermute | solution.py:353
  100.7 1.6 %collective-permute-start.5 = (bf16[16,1024]{1,0:T(8,128)(2,1)S(1)}, bf16[16,1024]{1,0:T(8,128)(2,1)S(1)}, u32[]{:S(2)}, u32[]{:S(2)}) collective-permute-start(bf16[16,1024]{1,0:T(8,128)(2,1)S(1)} %add_convert_fusion), channel_id=1, source_target_pairs={{0,16},{1,17},{2,18},{3,19},{4,20},{5,21},{6,22},{7,23},{8,24},{9,... | collective-permute-start | bytes 98312 | tf_op jit(solution)/shard_map/ppermute | solution.py:353
  102.3 3.3 %collective-permute-done.5 = bf16[16,1024]{1,0:T(8,128)(2,1)S(1)} collective-permute-done((bf16[16,1024]{1,0:T(8,128)(2,1)S(1)}, bf16[16,1024]{1,0:T(8,128)(2,1)S(1)}, u32[]{:S(2)}, u32[]{:S(2)}) %collective-permute-start.5) | collective-permute-done | bytes 32800 | tf_op jit(solution)/shard_map/ppermute | solution.py:353
  105.6 0.0 all-to-all-done.3
  105.6 0.1 collective-permute-start.6
  105.7 1.1 %shard_map.99 = bf16[128,1024]{1,0:T(8,128)(2,1)} custom-call(s32[2,128]{1,0:T(2,128)S(1)} %bitcast.20, s32[2,128]{1,0:T(2,128)S(1)} %bitcast.24, bf16[256,1536]{1,0:T(8,128)(2,1)S(1)} %bitcast.13, f32[128,1024]{1,0:T(8,128)S(1)} %get-tuple-element.27.back_ref), custom_call_target="tpu_custom_call" | custom-call | flops 134217728 | bytes 1574912 | tf_op jit(solution)/shard_map/pallas_call | solution.py:304
  106.8 0.1 collective-permute-done.6
  106.9 0.7 maximum_bitcast_fusion
  (6 shorter events, 0.1 us)
Async XLA Ops:
  2.9 27.8 %all-to-all-start = ((bf16[32,8,1536]{2,1,0:T(8,128)(2,1)}), bf16[32,8,1536]{2,1,0:T(8,128)(2,1)S(1)}, u32[]{:S(2)}, u32[]{:S(2)}) async-start(bf16[32,8,1536]{2,1,0:T(8,128)(2,1)} %bitcast.25), calls=%async_computation | async-start | bytes 1572864 | tf_op jit(solution)/shard_map/all_to_all | solution.py:347
  30.7 3.7 %copy-start.6 = (bf16[32,8,1536]{2,1,0:T(8,128)(2,1)}, bf16[32,8,1536]{2,1,0:T(8,128)(2,1)S(1)}, u32[]{:S(2)}) copy-start(bf16[32,8,1536]{2,1,0:T(8,128)(2,1)S(1)} %all-to-all-done) | copy-start | bytes 2359300
  30.7 24.2 %all-to-all-start.1 = ((bf16[32,8,1536]{2,1,0:T(8,128)(2,1)}), bf16[32,8,1536]{2,1,0:T(8,128)(2,1)S(1)}, u32[]{:S(2)}, u32[]{:S(2)}) async-start(bf16[32,8,1536]{2,1,0:T(8,128)(2,1)} %bitcast.29), calls=%async_computation.1 | async-start | bytes 1572864 | tf_op jit(solution)/shard_map/all_to_all | solution.py:347
  54.9 3.7 %copy-start.7 = (bf16[32,8,1536]{2,1,0:T(8,128)(2,1)}, bf16[32,8,1536]{2,1,0:T(8,128)(2,1)S(1)}, u32[]{:S(2)}) copy-start(bf16[32,8,1536]{2,1,0:T(8,128)(2,1)S(1)} %all-to-all-done.1) | copy-start | bytes 2359300
  54.9 24.2 %all-to-all-start.2 = ((bf16[32,8,1536]{2,1,0:T(8,128)(2,1)}), bf16[32,8,1536]{2,1,0:T(8,128)(2,1)S(1)}, u32[]{:S(2)}, u32[]{:S(2)}) async-start(bf16[32,8,1536]{2,1,0:T(8,128)(2,1)} %bitcast.30), calls=%async_computation.2 | async-start | bytes 1572864 | tf_op jit(solution)/shard_map/all_to_all | solution.py:347
  58.6 24.2 %copy-start = (bf16[128,1024]{1,0:T(8,128)(2,1)S(1)}, bf16[128,1024]{1,0:T(8,128)(2,1)}, u32[]{:S(2)}) copy-start(bf16[128,1024]{1,0:T(8,128)(2,1)} %tokens_ref.5) | copy-start | bytes 786436
  58.6 24.2 %copy-start.1 = (bf16[128,1024]{1,0:T(8,128)(2,1)S(1)}, bf16[128,1024]{1,0:T(8,128)(2,1)}, u32[]{:S(2)}) copy-start(bf16[128,1024]{1,0:T(8,128)(2,1)} %cot_ref.3) | copy-start | bytes 786436
  58.6 24.2 %copy-start.2 = (bf16[1024,32]{0,1:T(8,128)(2,1)S(1)}, bf16[1024,32]{0,1:T(8,128)(2,1)}, u32[]{:S(2)}) copy-start(bf16[1024,32]{0,1:T(8,128)(2,1)} %param.8) | copy-start | bytes 196612
  58.6 24.2 %copy-start.3 = (s32[128,2]{0,1:T(2,128)S(1)}, s32[128,2]{0,1:T(2,128)}, u32[]{:S(2)}) copy-start(s32[128,2]{0,1:T(2,128)} %param.11) | copy-start | bytes 3076
  58.6 24.2 %copy-start.4 = (s32[128,2]{0,1:T(2,128)S(1)}, s32[128,2]{0,1:T(2,128)}, u32[]{:S(2)}) copy-start(s32[128,2]{0,1:T(2,128)} %param.12) | copy-start | bytes 3076
  58.6 24.2 %copy-start.5 = (f32[2,128]{1,0:T(2,128)S(1)}, f32[2,128]{1,0:T(2,128)}, u32[]{:S(2)}) copy-start(f32[2,128]{1,0:T(2,128)} %get-tuple-element.16.gates_ref) | copy-start | bytes 3076
  79.1 26.5 %all-to-all-start.3 = ((bf16[32,8,1536]{2,1,0:T(8,128)(2,1)}), bf16[32,8,1536]{2,1,0:T(8,128)(2,1)S(1)}, u32[]{:S(2)}, u32[]{:S(2)}) async-start(bf16[32,8,1536]{2,1,0:T(8,128)(2,1)} %bitcast.26), calls=%async_computation.3 | async-start | bytes 1572864 | tf_op jit(solution)/shard_map/all_to_all | solution.py:347
  84.3 1.3 %collective-permute-start = (f32[16,1024]{1,0:T(8,128)S(1)}, f32[16,1024]{1,0:T(8,128)S(1)}, u32[]{:S(2)}, u32[]{:S(2)}) collective-permute-start(f32[16,1024]{1,0:T(8,128)S(1)} %constant_dynamic-slice_fusion), channel_id=1, source_target_pairs={{0,1},{1,0},{2,3},{3,2},{4,5},{5,4},{6,7},{7,6},{8,9},{9,8},{10,11... | collective-permute-start | bytes 196616 | tf_op jit(solution)/shard_map/ppermute | solution.py:353
  85.6 10.8 %collective-permute-start.1 = (f32[16,1024]{1,0:T(8,128)S(1)}, f32[16,1024]{1,0:T(8,128)S(1)}, u32[]{:S(2)}, u32[]{:S(2)}) collective-permute-start(f32[16,1024]{1,0:T(8,128)S(1)} %dynamic-slice_add_fusion), channel_id=1, source_target_pairs={{0,2},{1,3},{2,0},{3,1},{4,6},{5,7},{6,4},{7,5},{8,10},{9,11},{10,... | collective-permute-start | bytes 196616 | tf_op jit(solution)/shard_map/ppermute | solution.py:353
  87.4 9.0 %collective-permute-start.2 = (f32[16,1024]{1,0:T(8,128)S(1)}, f32[16,1024]{1,0:T(8,128)S(1)}, u32[]{:S(2)}, u32[]{:S(2)}) collective-permute-start(f32[16,1024]{1,0:T(8,128)S(1)} %dynamic-slice_add_fusion), channel_id=1, source_target_pairs={{0,4},{1,5},{2,6},{3,7},{4,0},{5,1},{6,2},{7,3},{8,12},{9,13},{10,... | collective-permute-start | bytes 196616 | tf_op jit(solution)/shard_map/ppermute | solution.py:353
  88.9 7.6 %collective-permute-start.3 = (f32[16,1024]{1,0:T(8,128)S(1)}, f32[16,1024]{1,0:T(8,128)S(1)}, u32[]{:S(2)}, u32[]{:S(2)}) collective-permute-start(f32[16,1024]{1,0:T(8,128)S(1)} %dynamic-slice_add_fusion), channel_id=1, source_target_pairs={{0,6},{1,7},{2,4},{3,5},{4,2},{5,3},{6,0},{7,1},{8,14},{9,15},{10,... | collective-permute-start | bytes 196616 | tf_op jit(solution)/shard_map/ppermute | solution.py:353
  96.5 4.2 %collective-permute-start.4 = (bf16[16,1024]{1,0:T(8,128)(2,1)S(1)}, bf16[16,1024]{1,0:T(8,128)(2,1)S(1)}, u32[]{:S(2)}, u32[]{:S(2)}) collective-permute-start(bf16[16,1024]{1,0:T(8,128)(2,1)S(1)} %add_convert_fusion.1), channel_id=1, source_target_pairs={{0,8},{1,9},{2,10},{3,11},{4,12},{5,13},{6,14},{7,15},{8,0},{9,1},... | collective-permute-start | bytes 98312 | tf_op jit(solution)/shard_map/ppermute | solution.py:353
  100.7 4.9 %collective-permute-start.5 = (bf16[16,1024]{1,0:T(8,128)(2,1)S(1)}, bf16[16,1024]{1,0:T(8,128)(2,1)S(1)}, u32[]{:S(2)}, u32[]{:S(2)}) collective-permute-start(bf16[16,1024]{1,0:T(8,128)(2,1)S(1)} %add_convert_fusion), channel_id=1, source_target_pairs={{0,16},{1,17},{2,18},{3,19},{4,20},{5,21},{6,22},{7,23},{8,24},{9,... | collective-permute-start | bytes 98312 | tf_op jit(solution)/shard_map/ppermute | solution.py:353
  105.6 1.3 %collective-permute-start.6 = (f32[16,1024]{1,0:T(8,128)S(1)}, f32[16,1024]{1,0:T(8,128)S(1)}, u32[]{:S(2)}, u32[]{:S(2)}) collective-permute-start(f32[16,1024]{1,0:T(8,128)S(1)} %convert_add_fusion), channel_id=1, source_target_pairs={{0,1},{1,0},{2,3},{3,2},{4,5},{5,4},{6,7},{7,6},{8,9},{9,8},{10,11... | collective-permute-start | bytes 196616 | tf_op jit(solution)/shard_map/ppermute | solution.py:353

commit v10 on v6

--- a/solution.py
+++ b/solution.py
@@ -11,6 +11,7 @@
 F32 = jnp.float32
 BF16 = jnp.bfloat16
 GROUP = 8
+PLANE = 8
 VMEM_BYTES = 60 * 1024 * 1024
 SMALL_VMEM_BYTES = 24 * 1024 * 1024
 
@@ -168,21 +169,55 @@
 
 
 def send_tokens_kernel(
-    lay, ids_hbm, slots_hbm, tokens_hbm, out_ref, ids_ref, slots_ref, tokens_ref, sems
+    lay, ids_hbm, slots_hbm, tokens_hbm, out_hbm, ids_ref, slots_ref, tokens_ref, rows_ref, sems, out_sems
 ):
+    pairs = ((ids_hbm, ids_ref), (slots_hbm, slots_ref), (tokens_hbm, tokens_ref))
     copies = [
-        pltpu.make_async_copy(source, target, sems.at[at])
-        for at, (source, target) in enumerate(
-            ((ids_hbm, ids_ref), (slots_hbm, slots_ref), (tokens_hbm, tokens_ref))
-        )
+        pltpu.make_async_copy(source, target, sems.at[at]) for at, (source, target) in enumerate(pairs)
     ]
     for copy in copies:
         copy.start()
-    for copy in copies:
+    for copy in copies[:2]:
         copy.wait()
-    first = targets(lay, ids_ref[0:1, :], slots_ref[0:1, :])
-    second = targets(lay, ids_ref[1:2, :], slots_ref[1:2, :])
-    place(lay, [[first, second]], [tokens_ref[...]], out_ref)
+    count, toks = rows_ref.shape[0], tokens_ref.shape[0]
+    row_at = iota((count, toks), 0)
+    first, second = [
+        targets(lay, ids_ref[k : k + 1, :], slots_ref[k : k + 1, :]) for k in range(2)
+    ]
+
+    def onehot(at, by):
+        hit = (row_at == shifted(first[at], by)) | (row_at == shifted(second[at], by))
+        return jnp.where(hit, 1.0, 0.0).astype(BF16)
+
+    whole = [onehot(group, 0) for group in range(lay.full)]
+    cut = [onehot(lay.full, at * lay.rest) for at in range(lay.cuts)] if lay.rest else []
+    copies[2].wait()
+
+    sent = []
+
+    def send(start, width, values):
+        rows_ref[:, start : start + width] = values.astype(BF16)
+        copy = pltpu.make_async_copy(
+            rows_ref.at[:, start : start + width],
+            out_hbm.at[:, start : start + width],
+            out_sems.at[len(sent)],
+        )
+        copy.start()
+        sent.append(copy)
+
+    half = lay.width // 2
+    for group, hot in enumerate(whole):
+        for at in (0, half):
+            send(group * lay.width + at, half, dot(hot, tokens_ref[:, at : at + half]))
+    if lay.rest:
+        pieces = [tokens_ref[:, at * lay.piece : (at + 1) * lay.piece] for at in range(lay.cuts)]
+        send(
+            lay.base,
+            lay.piece,
+            dot(jnp.concatenate(cut, axis=1), jnp.concatenate(pieces, axis=0)),
+        )
+    for copy in sent:
+        copy.wait()
 
 
 def send_grads_kernel(
@@ -362,14 +397,14 @@
     own = lax.dynamic_slice_in_dim(x, core * half, half, 0)
     other = lax.dynamic_slice_in_dim(x, (1 - core) * half, half, 0)
     own = own + from_device(other, 1, devices)
-    bit = 2
+    sent = own.astype(BF16)
+    terms = [sent] + [from_device(sent, bits, devices) for bits in (2, 4, 6)]
+    own = sum_of_pairs(*[term.astype(F32) for term in terms])
+    bit = PLANE
     while bit < devices:
-        sent = own if bit == 2 else own.astype(BF16)
-        steps = [1, 2, 3] if 2 * bit < devices else [1]
-        terms = [from_device(sent, step * bit, devices) for step in steps]
-        terms = [term.astype(F32) for term in [sent] + terms]
-        own = sum_of_pairs(*terms) if len(terms) == 4 else terms[0] + terms[1]
-        bit *= 4
+        sent = own.astype(BF16)
+        own = sent.astype(F32) + from_device(sent, bit, devices).astype(F32)
+        bit *= 2
     beside, own = lax.optimization_barrier((beside, own))
     other = from_device(own, 1, devices)
     first = core == 0
@@ -389,14 +424,17 @@
     sent_tokens = pl.pallas_call(
         functools.partial(send_tokens_kernel, lay),
         out_shape=message,
-        in_specs=[pl.BlockSpec(memory_space=pltpu.HBM)] * 3,
+        in_specs=[pl.BlockSpec(memory_space=pl.ANY)] * 3,
+        out_specs=pl.BlockSpec(memory_space=pl.ANY),
         scratch_shapes=[
             pltpu.VMEM(ids.shape, jnp.int32),
             pltpu.VMEM(slots.shape, jnp.int32),
             pltpu.VMEM(tokens.shape, BF16),
+            pltpu.VMEM(message.shape, BF16),
             pltpu.SemaphoreType.DMA((3,)),
+            pltpu.SemaphoreType.DMA((2 * lay.full + 1,)),
         ],
-        compiler_params=pltpu.CompilerParams(vmem_limit_bytes=SMALL_VMEM_BYTES),
+        compiler_params=pltpu.CompilerParams(vmem_limit_bytes=VMEM_BYTES),
         cost_estimate=pl.CostEstimate(
             flops=place_flops, bytes_accessed=2 * (tokens.size + message.size), transcendentals=0
         ),
@@ -408,7 +446,6 @@
         (ids, slots, tokens, router, cotangent),
     )
     arrived = exchange(sent_tokens)
-    arrived, sent_grads = lax.optimization_barrier((arrived, sent_grads))
     grad_rows = exchange(sent_grads)
     produced, hidden = expert_call(forward_kernel, lay, arrived, None, in_weight, out_weight)
     produced, grad_rows = lax.optimization_barrier((produced, grad_rows))

time: 111 us -> 107 us (0.964)
  local copies, waits for them, and re-layouts: 2.35 us -> 0.05 us
  waiting for transfers between devices: 42.3 us -> 41.1 us
    unnamed x22 -> x16, local copies, waits for them, and re-layouts: 2.35 us -> 0.05 us
    ppermute x8 -> x7, waiting for transfers between devices: 13.3 us -> 12.1 us  [from_device(): return lax.ppermute(x, AXES, [(d, d ^ bits) for d in range(devices)])]
    ppermute x8 -> x7, starting transfers between devices: 8.76 us -> 8.21 us  [from_device(): return lax.ppermute(x, AXES, [(d, d ^ bits) for d in range(devices)])]
  transfers between devices with their start and end apart: 12 -> 11, of which waited for: 10 -> 10; matrix products, arithmetic and copies ran while one was open for 0% -> 0% of each run, Pallas kernels for 32% -> 33%
where the time goes in v10:
time: 107 us
  waiting for transfers between devices  41.1 us (38%)
  Pallas kernels  37.5 us (35%)
  starting transfers between devices  26.4 us (25%)
    pallas_call x2, Pallas kernels, expert_call(): pl.pallas_call(functools.partial(kernel, lay), grid=(ff // tile,), in_spe...  29.9 us
    all_to_all x4, waiting for transfers between devices, exchange(): return lax.all_to_all(x, AXES, split_axis=0, concat_axis=0, tiled=True)  29 us
    all_to_all x4, starting transfers between devices, exchange(): return lax.all_to_all(x, AXES, split_axis=0, concat_axis=0, tiled=True)  18.2 us
    ppermute x7, waiting for transfers between devices, from_device(): return lax.ppermute(x, AXES, [(d, d ^ bits) for d in range(devices)])  12.1 us
    ppermute x7, starting transfers between devices, from_device(): return lax.ppermute(x, AXES, [(d, d ^ bits) for d in range(devices)])  8.21 us
    pallas_call x3, Pallas kernels, call(): pl.pallas_call(kernel, out_shape=out_shape, compiler_params=pltpu.Compile...  5.43 us
    pallas_call x1, Pallas kernels, on_device(): pl.pallas_call(functools.partial(send_tokens_kernel, lay), out_shape=mess...  2.16 us
  transfers between devices with their start and end apart: 11, of which 10 were waited for; matrix products, arithmetic and copies ran while one was open for 0% of the time, Pallas kernels for 33%

profile of v10, /device:TPU:0, one launch (start us, length us, event | category | flops | bytes accessed | tf_op | source)
XLA Modules:
  0.0 106.6 jit_solution(16703758538660737586)
XLA Ops:
  0.6 2.2 %shard_map.95 = bf16[256,1536]{1,0:T(8,128)(2,1)} custom-call(s32[2,128]{1,0:T(2,128)} %bitcast.17, s32[2,128]{1,0:T(2,128)} %bitcast.21, bf16[128,1024]{1,0:T(8,128)(2,1)} %tokens_ref.3), custom_call_target="tpu_custom_call" | custom-call | flops 134217728 | bytes 1048576 | tf_op jit(solution)/shard_map/pallas_call | solution.py:424
  2.8 7.3 %all-to-all-start = ((bf16[32,8,1536]{2,1,0:T(8,128)(2,1)}), bf16[32,8,1536]{2,1,0:T(8,128)(2,1)S(1)}, u32[]{:S(2)}, u32[]{:S(2)}) async-start(bf16[32,8,1536]{2,1,0:T(8,128)(2,1)} %bitcast.25), calls=%async_computation | async-start | bytes 1572864 | tf_op jit(solution)/shard_map/all_to_all | solution.py:383
  10.1 2.9 %shard_map.94 = (bf16[256,1536]{1,0:T(8,128)(2,1)}, f32[2,128]{1,0:T(2,128)}) custom-call(s32[2,128]{1,0:T(2,128)} %bitcast.18, s32[2,128]{1,0:T(2,128)} %bitcast.22, bf16[128,1024]{1,0:T(8,128)(2,1)} %tokens_ref.3, bf16[32,1024]{1,0:T(8,128)(2,1)} %bitcast.15, bf16[128,1024]{1,0:T(8,128)(2,1)} %cot_ref.3), custom_call_target="tpu_custom_call" | custom-call | flops 268435456 | bytes 1379328 | tf_op jit(solution)/shard_map/pallas_call | solution.py:346
  13.0 17.8 %all-to-all-done = bf16[32,8,1536]{2,1,0:T(8,128)(2,1)S(1)} async-done(((bf16[32,8,1536]{2,1,0:T(8,128)(2,1)}), bf16[32,8,1536]{2,1,0:T(8,128)(2,1)S(1)}, u32[]{:S(2)}, u32[]{:S(2)}) %all-to-all-start) | async-done | bytes 786464 | tf_op jit(solution)/shard_map/all_to_all | solution.py:383
  30.7 0.0 copy-start.6
  30.7 3.6 %all-to-all-start.1 = ((bf16[32,8,1536]{2,1,0:T(8,128)(2,1)}), bf16[32,8,1536]{2,1,0:T(8,128)(2,1)S(1)}, u32[]{:S(2)}, u32[]{:S(2)}) async-start(bf16[32,8,1536]{2,1,0:T(8,128)(2,1)} %bitcast.29), calls=%async_computation.1 | async-start | bytes 1572864 | tf_op jit(solution)/shard_map/all_to_all | solution.py:383
  34.4 0.0 copy-done.6
  34.4 14.7 %shard_map.96 = (bf16[256,1536]{1,0:T(8,128)(2,1)}, bf16[384,4096]{1,0:T(8,128)(2,1)}) custom-call(bf16[256,1536]{1,0:T(8,128)(2,1)} %bitcast.27, bf16[1,1024,4096]{2,1,0:T(8,128)(2,1)} %win_ref.3, bf16[1,4096,1024]{2,1,0:T(8,128)(2,1)} %wout_ref.3), custom_call_target="tpu_custom_call" | custom-call | flops 6442450944 | bytes 21495808 | tf_op jit(solution)/shard_map/pallas_call | solution.py:366
  49.1 5.9 %all-to-all-done.1 = bf16[32,8,1536]{2,1,0:T(8,128)(2,1)S(1)} async-done(((bf16[32,8,1536]{2,1,0:T(8,128)(2,1)}), bf16[32,8,1536]{2,1,0:T(8,128)(2,1)S(1)}, u32[]{:S(2)}, u32[]{:S(2)}) %all-to-all-start.1) | async-done | bytes 786464 | tf_op jit(solution)/shard_map/all_to_all | solution.py:383
  55.0 0.0 copy-start.7
  55.0 3.6 %all-to-all-start.2 = ((bf16[32,8,1536]{2,1,0:T(8,128)(2,1)}), bf16[32,8,1536]{2,1,0:T(8,128)(2,1)S(1)}, u32[]{:S(2)}, u32[]{:S(2)}) async-start(bf16[32,8,1536]{2,1,0:T(8,128)(2,1)} %bitcast.30), calls=%async_computation.2 | async-start | bytes 1572864 | tf_op jit(solution)/shard_map/all_to_all | solution.py:383
  58.6 0.0 copy-done.7
  58.6 0.0 copy-start
  58.6 0.0 copy-start.1
  58.6 0.0 copy-start.2
  58.7 0.0 copy-start.3
  58.7 0.0 copy-start.4
  58.7 0.0 copy-start.5
  58.7 15.1 %shard_map.97 = bf16[256,1536]{1,0:T(8,128)(2,1)} custom-call(bf16[256,1536]{1,0:T(8,128)(2,1)} %bitcast.28, bf16[384,4096]{1,0:T(8,128)(2,1)} %get-tuple-element.20.hidden_ref, bf16[1,1024,4096]{2,1,0:T(8,128)(2,1)} %win_ref.3, bf16[1,4096,1024]{2,1,0:T(8,128)(2,1)} %wout_ref.3), custom_call_target="tpu_custom_call" | custom-call | flops 6442450944 | bytes 21495808 | tf_op jit(solution)/shard_map/pallas_call | solution.py:366
  73.8 5.4 %all-to-all-done.2 = bf16[32,8,1536]{2,1,0:T(8,128)(2,1)S(1)} async-done(((bf16[32,8,1536]{2,1,0:T(8,128)(2,1)}), bf16[32,8,1536]{2,1,0:T(8,128)(2,1)S(1)}, u32[]{:S(2)}, u32[]{:S(2)}) %all-to-all-start.2) | async-done | bytes 786464 | tf_op jit(solution)/shard_map/all_to_all | solution.py:383
  79.2 3.6 %all-to-all-start.3 = ((bf16[32,8,1536]{2,1,0:T(8,128)(2,1)}), bf16[32,8,1536]{2,1,0:T(8,128)(2,1)S(1)}, u32[]{:S(2)}, u32[]{:S(2)}) async-start(bf16[32,8,1536]{2,1,0:T(8,128)(2,1)} %bitcast.26), calls=%async_computation.3 | async-start | bytes 1572864 | tf_op jit(solution)/shard_map/all_to_all | solution.py:383
  82.9 0.0 copy-done
  82.9 0.0 copy-done.1
  82.9 0.0 copy-done.2
  82.9 0.0 copy-done.3
  82.9 0.0 copy-done.4
  82.9 0.0 copy-done.5
  82.9 1.5 %shard_map.98 = (bf16[128,1024]{1,0:T(8,128)(2,1)}, f32[128,1024]{1,0:T(8,128)S(1)}, f32[32,1024]{1,0:T(8,128)S(1)}) custom-call(s32[2,128]{1,0:T(2,128)S(1)} %bitcast.19, s32[2,128]{1,0:T(2,128)S(1)} %bitcast.23, f32[2,128]{1,0:T(2,128)S(1)} %copy-done.5, bf16[256,1536]{1,0:T(8,128)(2,1)S(1)} %bitcast.14, bf16[128,1024]{1,0:T(8,128)(2,1)S(1)} %copy-done.1, ...), custom_call_target="tpu_custom_call" | custom-call | flops 268435456 | bytes 2296832 | tf_op jit(solution)/shard_map/pallas_call | solution.py:346
  84.4 0.3 collective-permute-start
  84.7 1.0 collective-permute-done
  85.7 1.8 %collective-permute-start.1 = (bf16[16,1024]{1,0:T(8,128)(2,1)S(1)}, bf16[16,1024]{1,0:T(8,128)(2,1)S(1)}, u32[]{:S(2)}, u32[]{:S(2)}) collective-permute-start(bf16[16,1024]{1,0:T(8,128)(2,1)S(1)} %add_convert_fusion.2), channel_id=1, source_target_pairs={{0,2},{1,3},{2,0},{3,1},{4,6},{5,7},{6,4},{7,5},{8,10},{9,11},{10,... | collective-permute-start | bytes 98312 | tf_op jit(solution)/shard_map/ppermute | solution.py:387
  87.5 1.5 %collective-permute-start.2 = (bf16[16,1024]{1,0:T(8,128)(2,1)S(1)}, bf16[16,1024]{1,0:T(8,128)(2,1)S(1)}, u32[]{:S(2)}, u32[]{:S(2)}) collective-permute-start(bf16[16,1024]{1,0:T(8,128)(2,1)S(1)} %add_convert_fusion.2), channel_id=1, source_target_pairs={{0,4},{1,5},{2,6},{3,7},{4,0},{5,1},{6,2},{7,3},{8,12},{9,13},{10,... | collective-permute-start | bytes 98312 | tf_op jit(solution)/shard_map/ppermute | solution.py:387
  89.0 0.3 collective-permute-start.3
  89.2 2.4 %collective-permute-done.1 = bf16[16,1024]{1,0:T(8,128)(2,1)S(1)} collective-permute-done((bf16[16,1024]{1,0:T(8,128)(2,1)S(1)}, bf16[16,1024]{1,0:T(8,128)(2,1)S(1)}, u32[]{:S(2)}, u32[]{:S(2)}) %collective-permute-start.1) | collective-permute-done | bytes 32800 | tf_op jit(solution)/shard_map/ppermute | solution.py:387
  91.6 0.9 collective-permute-done.2
  92.5 2.2 %collective-permute-done.3 = bf16[16,1024]{1,0:T(8,128)(2,1)S(1)} collective-permute-done((bf16[16,1024]{1,0:T(8,128)(2,1)S(1)}, bf16[16,1024]{1,0:T(8,128)(2,1)S(1)}, u32[]{:S(2)}, u32[]{:S(2)}) %collective-permute-start.3) | collective-permute-done | bytes 32800 | tf_op jit(solution)/shard_map/ppermute | solution.py:387
  94.7 1.9 %collective-permute-start.4 = (bf16[16,1024]{1,0:T(8,128)(2,1)S(1)}, bf16[16,1024]{1,0:T(8,128)(2,1)S(1)}, u32[]{:S(2)}, u32[]{:S(2)}) collective-permute-start(bf16[16,1024]{1,0:T(8,128)(2,1)S(1)} %add_convert_fusion.1), channel_id=1, source_target_pairs={{0,8},{1,9},{2,10},{3,11},{4,12},{5,13},{6,14},{7,15},{8,0},{9,1},... | collective-permute-start | bytes 98312 | tf_op jit(solution)/shard_map/ppermute | solution.py:387
  96.6 2.5 %collective-permute-done.4 = bf16[16,1024]{1,0:T(8,128)(2,1)S(1)} collective-permute-done((bf16[16,1024]{1,0:T(8,128)(2,1)S(1)}, bf16[16,1024]{1,0:T(8,128)(2,1)S(1)}, u32[]{:S(2)}, u32[]{:S(2)}) %collective-permute-start.4) | collective-permute-done | bytes 32800 | tf_op jit(solution)/shard_map/ppermute | solution.py:387
  99.1 2.4 %collective-permute-start.5 = (bf16[16,1024]{1,0:T(8,128)(2,1)S(1)}, bf16[16,1024]{1,0:T(8,128)(2,1)S(1)}, u32[]{:S(2)}, u32[]{:S(2)}) collective-permute-start(bf16[16,1024]{1,0:T(8,128)(2,1)S(1)} %add_convert_fusion), channel_id=1, source_target_pairs={{0,16},{1,17},{2,18},{3,19},{4,20},{5,21},{6,22},{7,23},{8,24},{9,... | collective-permute-start | bytes 98312 | tf_op jit(solution)/shard_map/ppermute | solution.py:387
  101.6 3.0 %collective-permute-done.5 = bf16[16,1024]{1,0:T(8,128)(2,1)S(1)} collective-permute-done((bf16[16,1024]{1,0:T(8,128)(2,1)S(1)}, bf16[16,1024]{1,0:T(8,128)(2,1)S(1)}, u32[]{:S(2)}, u32[]{:S(2)}) %collective-permute-start.5) | collective-permute-done | bytes 32800 | tf_op jit(solution)/shard_map/ppermute | solution.py:387
  104.5 0.0 all-to-all-done.3
  104.6 0.1 collective-permute-start.6
  104.6 1.1 %shard_map.99 = bf16[128,1024]{1,0:T(8,128)(2,1)} custom-call(s32[2,128]{1,0:T(2,128)S(1)} %bitcast.20, s32[2,128]{1,0:T(2,128)S(1)} %bitcast.24, bf16[256,1536]{1,0:T(8,128)(2,1)S(1)} %bitcast.13, f32[128,1024]{1,0:T(8,128)S(1)} %get-tuple-element.27.back_ref), custom_call_target="tpu_custom_call" | custom-call | flops 134217728 | bytes 1574912 | tf_op jit(solution)/shard_map/pallas_call | solution.py:346
  105.7 0.1 collective-permute-done.6
  105.9 0.7 maximum_bitcast_fusion
  (6 shorter events, 0.1 us)
Async XLA Ops:
  2.8 27.9 %all-to-all-start = ((bf16[32,8,1536]{2,1,0:T(8,128)(2,1)}), bf16[32,8,1536]{2,1,0:T(8,128)(2,1)S(1)}, u32[]{:S(2)}, u32[]{:S(2)}) async-start(bf16[32,8,1536]{2,1,0:T(8,128)(2,1)} %bitcast.25), calls=%async_computation | async-start | bytes 1572864 | tf_op jit(solution)/shard_map/all_to_all | solution.py:383
  30.7 3.6 %copy-start.6 = (bf16[32,8,1536]{2,1,0:T(8,128)(2,1)}, bf16[32,8,1536]{2,1,0:T(8,128)(2,1)S(1)}, u32[]{:S(2)}) copy-start(bf16[32,8,1536]{2,1,0:T(8,128)(2,1)S(1)} %all-to-all-done) | copy-start | bytes 2359300
  30.7 24.2 %all-to-all-start.1 = ((bf16[32,8,1536]{2,1,0:T(8,128)(2,1)}), bf16[32,8,1536]{2,1,0:T(8,128)(2,1)S(1)}, u32[]{:S(2)}, u32[]{:S(2)}) async-start(bf16[32,8,1536]{2,1,0:T(8,128)(2,1)} %bitcast.29), calls=%async_computation.1 | async-start | bytes 1572864 | tf_op jit(solution)/shard_map/all_to_all | solution.py:383
  55.0 3.6 %copy-start.7 = (bf16[32,8,1536]{2,1,0:T(8,128)(2,1)}, bf16[32,8,1536]{2,1,0:T(8,128)(2,1)S(1)}, u32[]{:S(2)}) copy-start(bf16[32,8,1536]{2,1,0:T(8,128)(2,1)S(1)} %all-to-all-done.1) | copy-start | bytes 2359300
  55.0 24.2 %all-to-all-start.2 = ((bf16[32,8,1536]{2,1,0:T(8,128)(2,1)}), bf16[32,8,1536]{2,1,0:T(8,128)(2,1)S(1)}, u32[]{:S(2)}, u32[]{:S(2)}) async-start(bf16[32,8,1536]{2,1,0:T(8,128)(2,1)} %bitcast.30), calls=%async_computation.2 | async-start | bytes 1572864 | tf_op jit(solution)/shard_map/all_to_all | solution.py:383
  58.6 24.3 %copy-start = (bf16[128,1024]{1,0:T(8,128)(2,1)S(1)}, bf16[128,1024]{1,0:T(8,128)(2,1)}, u32[]{:S(2)}) copy-start(bf16[128,1024]{1,0:T(8,128)(2,1)} %tokens_ref.3) | copy-start | bytes 786436
  58.6 24.3 %copy-start.1 = (bf16[128,1024]{1,0:T(8,128)(2,1)S(1)}, bf16[128,1024]{1,0:T(8,128)(2,1)}, u32[]{:S(2)}) copy-start(bf16[128,1024]{1,0:T(8,128)(2,1)} %cot_ref.3) | copy-start | bytes 786436
  58.6 24.3 %copy-start.2 = (bf16[1024,32]{0,1:T(8,128)(2,1)S(1)}, bf16[1024,32]{0,1:T(8,128)(2,1)}, u32[]{:S(2)}) copy-start(bf16[1024,32]{0,1:T(8,128)(2,1)} %param.8) | copy-start | bytes 196612
  58.7 24.2 %copy-start.3 = (s32[128,2]{0,1:T(2,128)S(1)}, s32[128,2]{0,1:T(2,128)}, u32[]{:S(2)}) copy-start(s32[128,2]{0,1:T(2,128)} %param.11) | copy-start | bytes 3076
  58.7 24.2 %copy-start.4 = (s32[128,2]{0,1:T(2,128)S(1)}, s32[128,2]{0,1:T(2,128)}, u32[]{:S(2)}) copy-start(s32[128,2]{0,1:T(2,128)} %param.12) | copy-start | bytes 3076
  58.7 24.2 %copy-start.5 = (f32[2,128]{1,0:T(2,128)S(1)}, f32[2,128]{1,0:T(2,128)}, u32[]{:S(2)}) copy-start(f32[2,128]{1,0:T(2,128)} %get-tuple-element.16.gates_ref) | copy-start | bytes 3076
  79.2 25.3 %all-to-all-start.3 = ((bf16[32,8,1536]{2,1,0:T(8,128)(2,1)}), bf16[32,8,1536]{2,1,0:T(8,128)(2,1)S(1)}, u32[]{:S(2)}, u32[]{:S(2)}) async-start(bf16[32,8,1536]{2,1,0:T(8,128)(2,1)} %bitcast.26), calls=%async_computation.3 | async-start | bytes 1572864 | tf_op jit(solution)/shard_map/all_to_all | solution.py:383
  84.4 1.3 %collective-permute-start = (f32[16,1024]{1,0:T(8,128)S(1)}, f32[16,1024]{1,0:T(8,128)S(1)}, u32[]{:S(2)}, u32[]{:S(2)}) collective-permute-start(f32[16,1024]{1,0:T(8,128)S(1)} %constant_dynamic-slice_fusion), channel_id=1, source_target_pairs={{0,1},{1,0},{2,3},{3,2},{4,5},{5,4},{6,7},{7,6},{8,9},{9,8},{10,11... | collective-permute-start | bytes 196616 | tf_op jit(solution)/shard_map/ppermute | solution.py:387
  85.7 6.0 %collective-permute-start.1 = (bf16[16,1024]{1,0:T(8,128)(2,1)S(1)}, bf16[16,1024]{1,0:T(8,128)(2,1)S(1)}, u32[]{:S(2)}, u32[]{:S(2)}) collective-permute-start(bf16[16,1024]{1,0:T(8,128)(2,1)S(1)} %add_convert_fusion.2), channel_id=1, source_target_pairs={{0,2},{1,3},{2,0},{3,1},{4,6},{5,7},{6,4},{7,5},{8,10},{9,11},{10,... | collective-permute-start | bytes 98312 | tf_op jit(solution)/shard_map/ppermute | solution.py:387
  87.5 5.0 %collective-permute-start.2 = (bf16[16,1024]{1,0:T(8,128)(2,1)S(1)}, bf16[16,1024]{1,0:T(8,128)(2,1)S(1)}, u32[]{:S(2)}, u32[]{:S(2)}) collective-permute-start(bf16[16,1024]{1,0:T(8,128)(2,1)S(1)} %add_convert_fusion.2), channel_id=1, source_target_pairs={{0,4},{1,5},{2,6},{3,7},{4,0},{5,1},{6,2},{7,3},{8,12},{9,13},{10,... | collective-permute-start | bytes 98312 | tf_op jit(solution)/shard_map/ppermute | solution.py:387
  89.0 5.7 %collective-permute-start.3 = (bf16[16,1024]{1,0:T(8,128)(2,1)S(1)}, bf16[16,1024]{1,0:T(8,128)(2,1)S(1)}, u32[]{:S(2)}, u32[]{:S(2)}) collective-permute-start(bf16[16,1024]{1,0:T(8,128)(2,1)S(1)} %add_convert_fusion.2), channel_id=1, source_target_pairs={{0,6},{1,7},{2,4},{3,5},{4,2},{5,3},{6,0},{7,1},{8,14},{9,15},{10,... | collective-permute-start | bytes 98312 | tf_op jit(solution)/shard_map/ppermute | solution.py:387
  94.7 4.4 %collective-permute-start.4 = (bf16[16,1024]{1,0:T(8,128)(2,1)S(1)}, bf16[16,1024]{1,0:T(8,128)(2,1)S(1)}, u32[]{:S(2)}, u32[]{:S(2)}) collective-permute-start(bf16[16,1024]{1,0:T(8,128)(2,1)S(1)} %add_convert_fusion.1), channel_id=1, source_target_pairs={{0,8},{1,9},{2,10},{3,11},{4,12},{5,13},{6,14},{7,15},{8,0},{9,1},... | collective-permute-start | bytes 98312 | tf_op jit(solution)/shard_map/ppermute | solution.py:387
  99.1 5.4 %collective-permute-start.5 = (bf16[16,1024]{1,0:T(8,128)(2,1)S(1)}, bf16[16,1024]{1,0:T(8,128)(2,1)S(1)}, u32[]{:S(2)}, u32[]{:S(2)}) collective-permute-start(bf16[16,1024]{1,0:T(8,128)(2,1)S(1)} %add_convert_fusion), channel_id=1, source_target_pairs={{0,16},{1,17},{2,18},{3,19},{4,20},{5,21},{6,22},{7,23},{8,24},{9,... | collective-permute-start | bytes 98312 | tf_op jit(solution)/shard_map/ppermute | solution.py:387
  104.6 1.3 %collective-permute-start.6 = (f32[16,1024]{1,0:T(8,128)S(1)}, f32[16,1024]{1,0:T(8,128)S(1)}, u32[]{:S(2)}, u32[]{:S(2)}) collective-permute-start(f32[16,1024]{1,0:T(8,128)S(1)} %convert_add_fusion), channel_id=1, source_target_pairs={{0,1},{1,0},{2,3},{3,2},{4,5},{5,4},{6,7},{7,6},{8,9},{9,8},{10,11... | collective-permute-start | bytes 196616 | tf_op jit(solution)/shard_map/ppermute | solution.py:387

commit v11 on v10

--- a/solution.py
+++ b/solution.py
@@ -335,9 +335,12 @@
     partial_ref[...] = (dot(high, tokens) + dot(low, tokens)) * (1.0 / toks)
 
 
-def grad_kernel(lay, ids_ref, slots_ref, message_ref, back_ref, out_ref):
+def last_kernel(
+    lay, ids_ref, slots_ref, message_ref, back_ref, near_ref, far_ref, out_ref, router_ref
+):
     _, ranks = column_targets(lay, ids_ref, slots_ref)
     out_ref[...] = (pick(lay, ranks, message_ref) + back_ref[...]).astype(BF16)
+    router_ref[...] = near_ref[...].astype(F32) + far_ref[...].astype(F32)
 
 
 def call(kernel, out_shape, flops, args, vmem_bytes=VMEM_BYTES):
@@ -391,7 +394,7 @@
     return (own + near) + (far + both)
 
 
-def sum_over_devices(x, devices, beside):
+def sum_over_devices(x, devices):
     half = x.shape[0] // 2
     core = lax.axis_index("inner") % 2
     own = lax.dynamic_slice_in_dim(x, core * half, half, 0)
@@ -401,15 +404,15 @@
     terms = [sent] + [from_device(sent, bits, devices) for bits in (2, 4, 6)]
     own = sum_of_pairs(*[term.astype(F32) for term in terms])
     bit = PLANE
-    while bit < devices:
+    while 2 * bit < devices:
         sent = own.astype(BF16)
         own = sent.astype(F32) + from_device(sent, bit, devices).astype(F32)
         bit *= 2
-    beside, own = lax.optimization_barrier((beside, own))
-    other = from_device(own, 1, devices)
+    sent = own.astype(BF16)
+    other = from_device(sent, 1, devices)
     first = core == 0
-    total = jnp.concatenate([jnp.where(first, own, other), jnp.where(first, other, own)], axis=0)
-    return total, beside
+    sent = jnp.concatenate([jnp.where(first, sent, other), jnp.where(first, other, sent)], axis=0)
+    return sent, from_device(sent, bit, devices)
 
 
 def on_device(tokens, router_weight, in_weight, out_weight, expert_ids, slot_ids, cotangent):
@@ -465,12 +468,15 @@
         (ids, slots, gates, produced_back, cotangent, tokens, router),
         SMALL_VMEM_BYTES,
     )
-    grad_router, returned_back = sum_over_devices(partial_grad, devices, returned_back)
-    grad_tokens = call(
-        functools.partial(grad_kernel, lay),
-        jax.ShapeDtypeStruct((tok_rows, model_width), BF16),
+    near, far = sum_over_devices(partial_grad, devices)
+    grad_tokens, grad_router = call(
+        functools.partial(last_kernel, lay),
+        [
+            jax.ShapeDtypeStruct((tok_rows, model_width), BF16),
+            jax.ShapeDtypeStruct((experts, model_width), F32),
+        ],
         place_flops,
-        (ids, slots, returned_back, router_back),
+        (ids, slots, returned_back, router_back, near, far),
         SMALL_VMEM_BYTES,
     )
     return (mixed, grad_tokens, grad_router.T)

time: 107 us -> 109 us (1.019)
  waiting for transfers between devices: 41.1 us -> 43.4 us
    ppermute x7, waiting for transfers between devices: 12.1 us -> 14.4 us  [from_device(): return lax.ppermute(x, AXES, [(d, d ^ bits) for d in range(devices)])]
  transfers between devices with their start and end apart: 11 -> 11, of which waited for: 10 -> 10; matrix products, arithmetic and copies ran while one was open for 0% -> 0% of each run, Pallas kernels for 33% -> 32%
where the time goes in v11:
time: 109 us; the launch traced here: 108 us
  waiting for transfers between devices  43.4 us (40%)
  Pallas kernels  37.4 us (34%)
  starting transfers between devices  26.4 us (24%)
    pallas_call x2, Pallas kernels, expert_call(): pl.pallas_call(functools.partial(kernel, lay), grid=(ff // tile,), in_spe...  29.8 us
    all_to_all x4, waiting for transfers between devices, exchange(): return lax.all_to_all(x, AXES, split_axis=0, concat_axis=0, tiled=True)  29.1 us
    all_to_all x4, starting transfers between devices, exchange(): return lax.all_to_all(x, AXES, split_axis=0, concat_axis=0, tiled=True)  18.2 us
    ppermute x7, waiting for transfers between devices, from_device(): return lax.ppermute(x, AXES, [(d, d ^ bits) for d in range(devices)])  14.4 us
    ppermute x7, starting transfers between devices, from_device(): return lax.ppermute(x, AXES, [(d, d ^ bits) for d in range(devices)])  8.22 us
    pallas_call x3, Pallas kernels, call(): pl.pallas_call(kernel, out_shape=out_shape, compiler_params=pltpu.Compile...  5.43 us
  transfers between devices with their start and end apart: 11, of which 10 were waited for; matrix products, arithmetic and copies ran while one was open for 0% of the time, Pallas kernels for 32%

profile of v11, /device:TPU:0, one launch (start us, length us, event | category | flops | bytes accessed | tf_op | source)
XLA Modules:
  0.0 108.2 jit_solution(14937781820118409247)
XLA Ops:
  0.6 2.2 %shard_map.95 = bf16[256,1536]{1,0:T(8,128)(2,1)} custom-call(s32[2,128]{1,0:T(2,128)} %bitcast.16, s32[2,128]{1,0:T(2,128)} %bitcast.20, bf16[128,1024]{1,0:T(8,128)(2,1)} %tokens_ref.3), custom_call_target="tpu_custom_call" | custom-call | flops 134217728 | bytes 1048576 | tf_op jit(solution)/shard_map/pallas_call | solution.py:427
  2.8 7.3 %all-to-all-start = ((bf16[32,8,1536]{2,1,0:T(8,128)(2,1)}), bf16[32,8,1536]{2,1,0:T(8,128)(2,1)S(1)}, u32[]{:S(2)}, u32[]{:S(2)}) async-start(bf16[32,8,1536]{2,1,0:T(8,128)(2,1)} %bitcast.24), calls=%async_computation | async-start | bytes 1572864 | tf_op jit(solution)/shard_map/all_to_all | solution.py:386
  10.1 2.9 %shard_map.94 = (bf16[256,1536]{1,0:T(8,128)(2,1)}, f32[2,128]{1,0:T(2,128)}) custom-call(s32[2,128]{1,0:T(2,128)} %bitcast.17, s32[2,128]{1,0:T(2,128)} %bitcast.21, bf16[128,1024]{1,0:T(8,128)(2,1)} %tokens_ref.3, bf16[32,1024]{1,0:T(8,128)(2,1)} %bitcast.14, bf16[128,1024]{1,0:T(8,128)(2,1)} %cot_ref.3), custom_call_target="tpu_custom_call" | custom-call | flops 268435456 | bytes 1379328 | tf_op jit(solution)/shard_map/pallas_call | solution.py:349
  13.0 17.8 %all-to-all-done = bf16[32,8,1536]{2,1,0:T(8,128)(2,1)S(1)} async-done(((bf16[32,8,1536]{2,1,0:T(8,128)(2,1)}), bf16[32,8,1536]{2,1,0:T(8,128)(2,1)S(1)}, u32[]{:S(2)}, u32[]{:S(2)}) %all-to-all-start) | async-done | bytes 786464 | tf_op jit(solution)/shard_map/all_to_all | solution.py:386
  30.7 0.0 copy-start.6
  30.7 3.6 %all-to-all-start.1 = ((bf16[32,8,1536]{2,1,0:T(8,128)(2,1)}), bf16[32,8,1536]{2,1,0:T(8,128)(2,1)S(1)}, u32[]{:S(2)}, u32[]{:S(2)}) async-start(bf16[32,8,1536]{2,1,0:T(8,128)(2,1)} %bitcast.28), calls=%async_computation.1 | async-start | bytes 1572864 | tf_op jit(solution)/shard_map/all_to_all | solution.py:386
  34.4 0.0 copy-done.6
  34.4 14.7 %shard_map.96 = (bf16[256,1536]{1,0:T(8,128)(2,1)}, bf16[384,4096]{1,0:T(8,128)(2,1)}) custom-call(bf16[256,1536]{1,0:T(8,128)(2,1)} %bitcast.26, bf16[1,1024,4096]{2,1,0:T(8,128)(2,1)} %win_ref.3, bf16[1,4096,1024]{2,1,0:T(8,128)(2,1)} %wout_ref.3), custom_call_target="tpu_custom_call" | custom-call | flops 6442450944 | bytes 21495808 | tf_op jit(solution)/shard_map/pallas_call | solution.py:369
  49.1 5.9 %all-to-all-done.1 = bf16[32,8,1536]{2,1,0:T(8,128)(2,1)S(1)} async-done(((bf16[32,8,1536]{2,1,0:T(8,128)(2,1)}), bf16[32,8,1536]{2,1,0:T(8,128)(2,1)S(1)}, u32[]{:S(2)}, u32[]{:S(2)}) %all-to-all-start.1) | async-done | bytes 786464 | tf_op jit(solution)/shard_map/all_to_all | solution.py:386
  55.0 0.0 copy-start.7
  55.0 3.6 %all-to-all-start.2 = ((bf16[32,8,1536]{2,1,0:T(8,128)(2,1)}), bf16[32,8,1536]{2,1,0:T(8,128)(2,1)S(1)}, u32[]{:S(2)}, u32[]{:S(2)}) async-start(bf16[32,8,1536]{2,1,0:T(8,128)(2,1)} %bitcast.29), calls=%async_computation.2 | async-start | bytes 1572864 | tf_op jit(solution)/shard_map/all_to_all | solution.py:386
  58.6 0.0 copy-done.7
  58.6 0.0 copy-start
  58.6 0.0 copy-start.1
  58.6 0.0 copy-start.2
  58.6 0.0 copy-start.3
  58.7 0.0 copy-start.4
  58.7 0.0 copy-start.5
  58.7 15.1 %shard_map.97 = bf16[256,1536]{1,0:T(8,128)(2,1)} custom-call(bf16[256,1536]{1,0:T(8,128)(2,1)} %bitcast.27, bf16[384,4096]{1,0:T(8,128)(2,1)} %get-tuple-element.20.hidden_ref, bf16[1,1024,4096]{2,1,0:T(8,128)(2,1)} %win_ref.3, bf16[1,4096,1024]{2,1,0:T(8,128)(2,1)} %wout_ref.3), custom_call_target="tpu_custom_call" | custom-call | flops 6442450944 | bytes 21495808 | tf_op jit(solution)/shard_map/pallas_call | solution.py:369
  73.8 5.4 %all-to-all-done.2 = bf16[32,8,1536]{2,1,0:T(8,128)(2,1)S(1)} async-done(((bf16[32,8,1536]{2,1,0:T(8,128)(2,1)}), bf16[32,8,1536]{2,1,0:T(8,128)(2,1)S(1)}, u32[]{:S(2)}, u32[]{:S(2)}) %all-to-all-start.2) | async-done | bytes 786464 | tf_op jit(solution)/shard_map/all_to_all | solution.py:386
  79.2 3.6 %all-to-all-start.3 = ((bf16[32,8,1536]{2,1,0:T(8,128)(2,1)}), bf16[32,8,1536]{2,1,0:T(8,128)(2,1)S(1)}, u32[]{:S(2)}, u32[]{:S(2)}) async-start(bf16[32,8,1536]{2,1,0:T(8,128)(2,1)} %bitcast.25), calls=%async_computation.3 | async-start | bytes 1572864 | tf_op jit(solution)/shard_map/all_to_all | solution.py:386
  82.9 0.0 copy-done
  82.9 0.0 copy-done.1
  82.9 0.0 copy-done.2
  82.9 0.0 copy-done.3
  82.9 0.0 copy-done.4
  82.9 0.0 copy-done.5
  82.9 1.5 %shard_map.98 = (bf16[128,1024]{1,0:T(8,128)(2,1)}, f32[128,1024]{1,0:T(8,128)S(1)}, f32[32,1024]{1,0:T(8,128)S(1)}) custom-call(s32[2,128]{1,0:T(2,128)S(1)} %bitcast.18, s32[2,128]{1,0:T(2,128)S(1)} %bitcast.22, f32[2,128]{1,0:T(2,128)S(1)} %copy-done.5, bf16[256,1536]{1,0:T(8,128)(2,1)S(1)} %bitcast.12, bf16[128,1024]{1,0:T(8,128)(2,1)S(1)} %copy-done.1, ...), custom_call_target="tpu_custom_call" | custom-call | flops 268435456 | bytes 2296832 | tf_op jit(solution)/shard_map/pallas_call | solution.py:349
  84.4 0.3 collective-permute-start
  84.6 1.0 collective-permute-done
  85.7 1.8 %collective-permute-start.1 = (bf16[16,1024]{1,0:T(8,128)(2,1)S(1)}, bf16[16,1024]{1,0:T(8,128)(2,1)S(1)}, u32[]{:S(2)}, u32[]{:S(2)}) collective-permute-start(bf16[16,1024]{1,0:T(8,128)(2,1)S(1)} %add_convert_fusion.2), channel_id=1, source_target_pairs={{0,2},{1,3},{2,0},{3,1},{4,6},{5,7},{6,4},{7,5},{8,10},{9,11},{10,... | collective-permute-start | bytes 98312 | tf_op jit(solution)/shard_map/ppermute | solution.py:390
  87.5 1.5 %collective-permute-start.2 = (bf16[16,1024]{1,0:T(8,128)(2,1)S(1)}, bf16[16,1024]{1,0:T(8,128)(2,1)S(1)}, u32[]{:S(2)}, u32[]{:S(2)}) collective-permute-start(bf16[16,1024]{1,0:T(8,128)(2,1)S(1)} %add_convert_fusion.2), channel_id=1, source_target_pairs={{0,4},{1,5},{2,6},{3,7},{4,0},{5,1},{6,2},{7,3},{8,12},{9,13},{10,... | collective-permute-start | bytes 98312 | tf_op jit(solution)/shard_map/ppermute | solution.py:390
  89.0 0.3 collective-permute-start.3
  89.2 2.4 %collective-permute-done.1 = bf16[16,1024]{1,0:T(8,128)(2,1)S(1)} collective-permute-done((bf16[16,1024]{1,0:T(8,128)(2,1)S(1)}, bf16[16,1024]{1,0:T(8,128)(2,1)S(1)}, u32[]{:S(2)}, u32[]{:S(2)}) %collective-permute-start.1) | collective-permute-done | bytes 32800 | tf_op jit(solution)/shard_map/ppermute | solution.py:390
  91.6 0.9 collective-permute-done.2
  92.5 2.2 %collective-permute-done.3 = bf16[16,1024]{1,0:T(8,128)(2,1)S(1)} collective-permute-done((bf16[16,1024]{1,0:T(8,128)(2,1)S(1)}, bf16[16,1024]{1,0:T(8,128)(2,1)S(1)}, u32[]{:S(2)}, u32[]{:S(2)}) %collective-permute-start.3) | collective-permute-done | bytes 32800 | tf_op jit(solution)/shard_map/ppermute | solution.py:390
  94.7 1.9 %collective-permute-start.4 = (bf16[16,1024]{1,0:T(8,128)(2,1)S(1)}, bf16[16,1024]{1,0:T(8,128)(2,1)S(1)}, u32[]{:S(2)}, u32[]{:S(2)}) collective-permute-start(bf16[16,1024]{1,0:T(8,128)(2,1)S(1)} %add_convert_fusion.1), channel_id=1, source_target_pairs={{0,8},{1,9},{2,10},{3,11},{4,12},{5,13},{6,14},{7,15},{8,0},{9,1},... | collective-permute-start | bytes 98312 | tf_op jit(solution)/shard_map/ppermute | solution.py:390
  96.6 2.5 %collective-permute-done.4 = bf16[16,1024]{1,0:T(8,128)(2,1)S(1)} collective-permute-done((bf16[16,1024]{1,0:T(8,128)(2,1)S(1)}, bf16[16,1024]{1,0:T(8,128)(2,1)S(1)}, u32[]{:S(2)}, u32[]{:S(2)}) %collective-permute-start.4) | collective-permute-done | bytes 32800 | tf_op jit(solution)/shard_map/ppermute | solution.py:390
  99.1 0.1 collective-permute-start.5
  99.2 1.2 %collective-permute-done.5 = bf16[16,1024]{1,0:T(8,128)(2,1)S(1)} collective-permute-done((bf16[16,1024]{1,0:T(8,128)(2,1)S(1)}, bf16[16,1024]{1,0:T(8,128)(2,1)S(1)}, u32[]{:S(2)}, u32[]{:S(2)}) %collective-permute-start.5) | collective-permute-done | bytes 32800 | tf_op jit(solution)/shard_map/ppermute | solution.py:390
  100.4 2.4 %collective-permute-start.6 = (bf16[32,1024]{1,0:T(8,128)(2,1)S(1)}, bf16[32,1024]{1,0:T(8,128)(2,1)S(1)}, u32[]{:S(2)}, u32[]{:S(2)}) collective-permute-start(bf16[32,1024]{1,0:T(8,128)(2,1)S(1)} %pad_maximum_fusion.near_ref), channel_id=1, source_target_pairs={{0,16},{1,17},{2,18},{3,19},{4,20},{5,21},{6,22},{7,23},{8,24},{9,... | collective-permute-start | bytes 196616 | tf_op jit(solution)/shard_map/ppermute | solution.py:390
  102.8 4.2 %collective-permute-done.6.far_ref = bf16[32,1024]{1,0:T(8,128)(2,1)S(1)} collective-permute-done((bf16[32,1024]{1,0:T(8,128)(2,1)S(1)}, bf16[32,1024]{1,0:T(8,128)(2,1)S(1)}, u32[]{:S(2)}, u32[]{:S(2)}) %collective-permute-start.6) | collective-permute-done | bytes 65568 | tf_op jit(solution)/shard_map/ppermute | solution.py:390
  107.1 0.0 all-to-all-done.3
  107.1 1.1 %shard_map.99 = (bf16[128,1024]{1,0:T(8,128)(2,1)}, f32[32,1024]{1,0:T(8,128)}) custom-call(s32[2,128]{1,0:T(2,128)S(1)} %bitcast.19, s32[2,128]{1,0:T(2,128)S(1)} %bitcast.23, bf16[256,1536]{1,0:T(8,128)(2,1)S(1)} %bitcast.13, f32[128,1024]{1,0:T(8,128)S(1)} %get-tuple-element.25.back_ref, bf16[32,1024]{1,0:T(8,128)(2,1)S(1)} %pad_maximum_fusion.near_ref, ...), custom_call_target="tpu_custom_call" | custom-call | flops 134217728 | bytes 1837056 | tf_op jit(solution)/shard_map/pallas_call | solution.py:349
  (6 shorter events, 0.1 us)
Async XLA Ops:
  2.8 27.9 %all-to-all-start = ((bf16[32,8,1536]{2,1,0:T(8,128)(2,1)}), bf16[32,8,1536]{2,1,0:T(8,128)(2,1)S(1)}, u32[]{:S(2)}, u32[]{:S(2)}) async-start(bf16[32,8,1536]{2,1,0:T(8,128)(2,1)} %bitcast.24), calls=%async_computation | async-start | bytes 1572864 | tf_op jit(solution)/shard_map/all_to_all | solution.py:386
  30.7 3.6 %copy-start.6 = (bf16[32,8,1536]{2,1,0:T(8,128)(2,1)}, bf16[32,8,1536]{2,1,0:T(8,128)(2,1)S(1)}, u32[]{:S(2)}) copy-start(bf16[32,8,1536]{2,1,0:T(8,128)(2,1)S(1)} %all-to-all-done) | copy-start | bytes 2359300
  30.7 24.2 %all-to-all-start.1 = ((bf16[32,8,1536]{2,1,0:T(8,128)(2,1)}), bf16[32,8,1536]{2,1,0:T(8,128)(2,1)S(1)}, u32[]{:S(2)}, u32[]{:S(2)}) async-start(bf16[32,8,1536]{2,1,0:T(8,128)(2,1)} %bitcast.28), calls=%async_computation.1 | async-start | bytes 1572864 | tf_op jit(solution)/shard_map/all_to_all | solution.py:386
  55.0 3.6 %copy-start.7 = (bf16[32,8,1536]{2,1,0:T(8,128)(2,1)}, bf16[32,8,1536]{2,1,0:T(8,128)(2,1)S(1)}, u32[]{:S(2)}) copy-start(bf16[32,8,1536]{2,1,0:T(8,128)(2,1)S(1)} %all-to-all-done.1) | copy-start | bytes 2359300
  55.0 24.2 %all-to-all-start.2 = ((bf16[32,8,1536]{2,1,0:T(8,128)(2,1)}), bf16[32,8,1536]{2,1,0:T(8,128)(2,1)S(1)}, u32[]{:S(2)}, u32[]{:S(2)}) async-start(bf16[32,8,1536]{2,1,0:T(8,128)(2,1)} %bitcast.29), calls=%async_computation.2 | async-start | bytes 1572864 | tf_op jit(solution)/shard_map/all_to_all | solution.py:386
  58.6 24.3 %copy-start = (bf16[128,1024]{1,0:T(8,128)(2,1)S(1)}, bf16[128,1024]{1,0:T(8,128)(2,1)}, u32[]{:S(2)}) copy-start(bf16[128,1024]{1,0:T(8,128)(2,1)} %tokens_ref.3) | copy-start | bytes 786436
  58.6 24.3 %copy-start.1 = (bf16[128,1024]{1,0:T(8,128)(2,1)S(1)}, bf16[128,1024]{1,0:T(8,128)(2,1)}, u32[]{:S(2)}) copy-start(bf16[128,1024]{1,0:T(8,128)(2,1)} %cot_ref.3) | copy-start | bytes 786436
  58.6 24.3 %copy-start.2 = (bf16[1024,32]{0,1:T(8,128)(2,1)S(1)}, bf16[1024,32]{0,1:T(8,128)(2,1)}, u32[]{:S(2)}) copy-start(bf16[1024,32]{0,1:T(8,128)(2,1)} %param.8) | copy-start | bytes 196612
  58.6 24.2 %copy-start.3 = (s32[128,2]{0,1:T(2,128)S(1)}, s32[128,2]{0,1:T(2,128)}, u32[]{:S(2)}) copy-start(s32[128,2]{0,1:T(2,128)} %param.11) | copy-start | bytes 3076
  58.7 24.2 %copy-start.4 = (s32[128,2]{0,1:T(2,128)S(1)}, s32[128,2]{0,1:T(2,128)}, u32[]{:S(2)}) copy-start(s32[128,2]{0,1:T(2,128)} %param.12) | copy-start | bytes 3076
  58.7 24.2 %copy-start.5 = (f32[2,128]{1,0:T(2,128)S(1)}, f32[2,128]{1,0:T(2,128)}, u32[]{:S(2)}) copy-start(f32[2,128]{1,0:T(2,128)} %get-tuple-element.16.gates_ref) | copy-start | bytes 3076
  79.2 27.8 %all-to-all-start.3 = ((bf16[32,8,1536]{2,1,0:T(8,128)(2,1)}), bf16[32,8,1536]{2,1,0:T(8,128)(2,1)S(1)}, u32[]{:S(2)}, u32[]{:S(2)}) async-start(bf16[32,8,1536]{2,1,0:T(8,128)(2,1)} %bitcast.25), calls=%async_computation.3 | async-start | bytes 1572864 | tf_op jit(solution)/shard_map/all_to_all | solution.py:386
  84.4 1.3 %collective-permute-start = (f32[16,1024]{1,0:T(8,128)S(1)}, f32[16,1024]{1,0:T(8,128)S(1)}, u32[]{:S(2)}, u32[]{:S(2)}) collective-permute-start(f32[16,1024]{1,0:T(8,128)S(1)} %constant_dynamic-slice_fusion), channel_id=1, source_target_pairs={{0,1},{1,0},{2,3},{3,2},{4,5},{5,4},{6,7},{7,6},{8,9},{9,8},{10,11... | collective-permute-start | bytes 196616 | tf_op jit(solution)/shard_map/ppermute | solution.py:390
  85.7 6.0 %collective-permute-start.1 = (bf16[16,1024]{1,0:T(8,128)(2,1)S(1)}, bf16[16,1024]{1,0:T(8,128)(2,1)S(1)}, u32[]{:S(2)}, u32[]{:S(2)}) collective-permute-start(bf16[16,1024]{1,0:T(8,128)(2,1)S(1)} %add_convert_fusion.2), channel_id=1, source_target_pairs={{0,2},{1,3},{2,0},{3,1},{4,6},{5,7},{6,4},{7,5},{8,10},{9,11},{10,... | collective-permute-start | bytes 98312 | tf_op jit(solution)/shard_map/ppermute | solution.py:390
  87.5 5.0 %collective-permute-start.2 = (bf16[16,1024]{1,0:T(8,128)(2,1)S(1)}, bf16[16,1024]{1,0:T(8,128)(2,1)S(1)}, u32[]{:S(2)}, u32[]{:S(2)}) collective-permute-start(bf16[16,1024]{1,0:T(8,128)(2,1)S(1)} %add_convert_fusion.2), channel_id=1, source_target_pairs={{0,4},{1,5},{2,6},{3,7},{4,0},{5,1},{6,2},{7,3},{8,12},{9,13},{10,... | collective-permute-start | bytes 98312 | tf_op jit(solution)/shard_map/ppermute | solution.py:390
  89.0 5.7 %collective-permute-start.3 = (bf16[16,1024]{1,0:T(8,128)(2,1)S(1)}, bf16[16,1024]{1,0:T(8,128)(2,1)S(1)}, u32[]{:S(2)}, u32[]{:S(2)}) collective-permute-start(bf16[16,1024]{1,0:T(8,128)(2,1)S(1)} %add_convert_fusion.2), channel_id=1, source_target_pairs={{0,6},{1,7},{2,4},{3,5},{4,2},{5,3},{6,0},{7,1},{8,14},{9,15},{10,... | collective-permute-start | bytes 98312 | tf_op jit(solution)/shard_map/ppermute | solution.py:390
  94.7 4.4 %collective-permute-start.4 = (bf16[16,1024]{1,0:T(8,128)(2,1)S(1)}, bf16[16,1024]{1,0:T(8,128)(2,1)S(1)}, u32[]{:S(2)}, u32[]{:S(2)}) collective-permute-start(bf16[16,1024]{1,0:T(8,128)(2,1)S(1)} %add_convert_fusion.1), channel_id=1, source_target_pairs={{0,8},{1,9},{2,10},{3,11},{4,12},{5,13},{6,14},{7,15},{8,0},{9,1},... | collective-permute-start | bytes 98312 | tf_op jit(solution)/shard_map/ppermute | solution.py:390
  99.1 1.3 %collective-permute-start.5 = (bf16[16,1024]{1,0:T(8,128)(2,1)S(1)}, bf16[16,1024]{1,0:T(8,128)(2,1)S(1)}, u32[]{:S(2)}, u32[]{:S(2)}) collective-permute-start(bf16[16,1024]{1,0:T(8,128)(2,1)S(1)} %add_convert_fusion), channel_id=1, source_target_pairs={{0,1},{1,0},{2,3},{3,2},{4,5},{5,4},{6,7},{7,6},{8,9},{9,8},{10,11... | collective-permute-start | bytes 98312 | tf_op jit(solution)/shard_map/ppermute | solution.py:390
  100.4 6.6 %collective-permute-start.6 = (bf16[32,1024]{1,0:T(8,128)(2,1)S(1)}, bf16[32,1024]{1,0:T(8,128)(2,1)S(1)}, u32[]{:S(2)}, u32[]{:S(2)}) collective-permute-start(bf16[32,1024]{1,0:T(8,128)(2,1)S(1)} %pad_maximum_fusion.near_ref), channel_id=1, source_target_pairs={{0,16},{1,17},{2,18},{3,19},{4,20},{5,21},{6,22},{7,23},{8,24},{9,... | collective-permute-start | bytes 196616 | tf_op jit(solution)/shard_map/ppermute | solution.py:390

commit v12 on v10

--- a/solution.py
+++ b/solution.py
@@ -59,7 +59,8 @@
     return jnp.sum(jnp.where(eye, column, 0.0), axis=0, keepdims=True)
 
 
-def targets(lay, ids, slots):
+def targets(lay, experts, ids, slots):
+    ids = rank_of(ids, experts)
     found = []
     kept = slots < lay.capacity
     for group in range(lay.full):
@@ -182,7 +183,8 @@
     count, toks = rows_ref.shape[0], tokens_ref.shape[0]
     row_at = iota((count, toks), 0)
     first, second = [
-        targets(lay, ids_ref[k : k + 1, :], slots_ref[k : k + 1, :]) for k in range(2)
+        targets(lay, count // GROUP, ids_ref[k : k + 1, :], slots_ref[k : k + 1, :])
+        for k in range(2)
     ]
 
     def onehot(at, by):
@@ -234,7 +236,10 @@
     gates_ref[1:2, :] = gates[1]
     cot = cot_ref[...].astype(F32)
     scaled = [(as_column(gate) * cot).astype(BF16) for gate in gates]
-    ranks = [[targets(lay, ids_ref[k : k + 1, :], slots_ref[k : k + 1, :])] for k in range(2)]
+    experts = out_ref.shape[0] // GROUP
+    ranks = [
+        [targets(lay, experts, ids_ref[k : k + 1, :], slots_ref[k : k + 1, :])] for k in range(2)
+    ]
     place(lay, ranks, scaled, out_ref)
 
 
@@ -286,10 +291,10 @@
         pack(lay, total_ref, out_ref)
 
 
-def column_targets(lay, ids_ref, slots_ref):
+def column_targets(lay, experts, ids_ref, slots_ref):
     ids = [as_column(ids_ref[k : k + 1, :].astype(F32)).astype(jnp.int32) for k in range(2)]
     slots = [as_column(slots_ref[k : k + 1, :].astype(F32)).astype(jnp.int32) for k in range(2)]
-    return ids, [targets(lay, ids[k], slots[k]) for k in range(2)]
+    return ids, [targets(lay, experts, ids[k], slots[k]) for k in range(2)]
 
 
 def split_in_two(x):
@@ -312,7 +317,7 @@
 ):
     experts = router_ref.shape[0]
     toks = tokens_ref.shape[0]
-    ids, ranks = column_targets(lay, ids_ref, slots_ref)
+    ids, ranks = column_targets(lay, experts, ids_ref, slots_ref)
     gates = [as_column(gates_ref[k : k + 1, :]) for k in range(2)]
     cot = cot_ref[...].astype(F32)
     choice = [pick(lay, [ranks[k]], message_ref) for k in range(2)]
@@ -336,7 +341,7 @@
 
 
 def grad_kernel(lay, ids_ref, slots_ref, message_ref, back_ref, out_ref):
-    _, ranks = column_targets(lay, ids_ref, slots_ref)
+    _, ranks = column_targets(lay, message_ref.shape[0] // GROUP, ids_ref, slots_ref)
     out_ref[...] = (pick(lay, ranks, message_ref) + back_ref[...]).astype(BF16)
 
 
@@ -379,8 +384,15 @@
     )(*operands)
 
 
-def exchange(x):
-    return lax.all_to_all(x, AXES, split_axis=0, concat_axis=0, tiled=True)
+def rank_of(device, devices):
+    return (device - devices // 4) & (devices - 1)
+
+
+def exchange(x, devices):
+    order = [(rank + devices // 4) % devices for rank in range(devices)]
+    return lax.all_to_all(
+        x, AXES, split_axis=0, concat_axis=0, tiled=True, axis_index_groups=[order]
+    )
 
 
 def from_device(x, bits, devices):
@@ -445,14 +457,14 @@
         2 * place_flops,
         (ids, slots, tokens, router, cotangent),
     )
-    arrived = exchange(sent_tokens)
-    grad_rows = exchange(sent_grads)
+    arrived = exchange(sent_tokens, devices)
+    grad_rows = exchange(sent_grads, devices)
     produced, hidden = expert_call(forward_kernel, lay, arrived, None, in_weight, out_weight)
     produced, grad_rows = lax.optimization_barrier((produced, grad_rows))
-    produced_back = exchange(produced)
+    produced_back = exchange(produced, devices)
     returned = expert_call(backward_kernel, lay, grad_rows, hidden, in_weight, out_weight)
     returned, produced_back = lax.optimization_barrier((returned, produced_back))
-    returned_back = exchange(returned)
+    returned_back = exchange(returned, devices)
 
     mixed, router_back, partial_grad = call(
         functools.partial(mix_kernel, lay),

time: 107 us -> 107 us (level)
  no operation moved by 1% of the time
where the time goes in v12:
time: 107 us
  waiting for transfers between devices  41.1 us (38%)
  Pallas kernels  37.5 us (35%)
  starting transfers between devices  26.4 us (25%)
    pallas_call x2, Pallas kernels, expert_call(): pl.pallas_call(functools.partial(kernel, lay), grid=(ff // tile,), in_spe...  29.9 us
    all_to_all x4, waiting for transfers between devices, exchange(): lax.all_to_all(x, AXES, split_axis=0, concat_axis=0, tiled=True, axis_ind...  29 us
    all_to_all x4, starting transfers between devices, exchange(): lax.all_to_all(x, AXES, split_axis=0, concat_axis=0, tiled=True, axis_ind...  18.2 us
    ppermute x7, waiting for transfers between devices, from_device(): return lax.ppermute(x, AXES, [(d, d ^ bits) for d in range(devices)])  12.1 us
    ppermute x7, starting transfers between devices, from_device(): return lax.ppermute(x, AXES, [(d, d ^ bits) for d in range(devices)])  8.21 us
    pallas_call x3, Pallas kernels, call(): pl.pallas_call(kernel, out_shape=out_shape, compiler_params=pltpu.Compile...  5.44 us
    pallas_call x1, Pallas kernels, on_device(): pl.pallas_call(functools.partial(send_tokens_kernel, lay), out_shape=mess...  2.16 us
  transfers between devices with their start and end apart: 11, of which 10 were waited for; matrix products, arithmetic and copies ran while one was open for 0% of the time, Pallas kernels for 33%

profile of v12, /device:TPU:0, one launch (start us, length us, event | category | flops | bytes accessed | tf_op | source)
XLA Modules:
  0.0 106.6 jit_solution(18034945360070847140)
XLA Ops:
  0.6 2.2 %shard_map.95 = bf16[256,1536]{1,0:T(8,128)(2,1)} custom-call(s32[2,128]{1,0:T(2,128)} %bitcast.17, s32[2,128]{1,0:T(2,128)} %bitcast.21, bf16[128,1024]{1,0:T(8,128)(2,1)} %tokens_ref.3), custom_call_target="tpu_custom_call" | custom-call | flops 134217728 | bytes 1048576 | tf_op jit(solution)/shard_map/pallas_call | solution.py:436
  2.8 7.3 %all-to-all-start = ((bf16[32,8,1536]{2,1,0:T(8,128)(2,1)}), bf16[32,8,1536]{2,1,0:T(8,128)(2,1)S(1)}, u32[]{:S(2)}, u32[]{:S(2)}) async-start(bf16[32,8,1536]{2,1,0:T(8,128)(2,1)} %bitcast.25), calls=%async_computation | async-start | bytes 1572864 | tf_op jit(solution)/shard_map/all_to_all | solution.py:393
  10.1 2.9 %shard_map.94 = (bf16[256,1536]{1,0:T(8,128)(2,1)}, f32[2,128]{1,0:T(2,128)}) custom-call(s32[2,128]{1,0:T(2,128)} %bitcast.18, s32[2,128]{1,0:T(2,128)} %bitcast.22, bf16[128,1024]{1,0:T(8,128)(2,1)} %tokens_ref.3, bf16[32,1024]{1,0:T(8,128)(2,1)} %bitcast.15, bf16[128,1024]{1,0:T(8,128)(2,1)} %cot_ref.3), custom_call_target="tpu_custom_call" | custom-call | flops 268435456 | bytes 1379328 | tf_op jit(solution)/shard_map/pallas_call | solution.py:351
  13.0 17.8 %all-to-all-done = bf16[32,8,1536]{2,1,0:T(8,128)(2,1)S(1)} async-done(((bf16[32,8,1536]{2,1,0:T(8,128)(2,1)}), bf16[32,8,1536]{2,1,0:T(8,128)(2,1)S(1)}, u32[]{:S(2)}, u32[]{:S(2)}) %all-to-all-start) | async-done | bytes 786464 | tf_op jit(solution)/shard_map/all_to_all | solution.py:393
  30.7 0.0 copy-start.6
  30.7 3.6 %all-to-all-start.1 = ((bf16[32,8,1536]{2,1,0:T(8,128)(2,1)}), bf16[32,8,1536]{2,1,0:T(8,128)(2,1)S(1)}, u32[]{:S(2)}, u32[]{:S(2)}) async-start(bf16[32,8,1536]{2,1,0:T(8,128)(2,1)} %bitcast.29), calls=%async_computation.1 | async-start | bytes 1572864 | tf_op jit(solution)/shard_map/all_to_all | solution.py:393
  34.4 0.0 copy-done.6
  34.4 14.7 %shard_map.96 = (bf16[256,1536]{1,0:T(8,128)(2,1)}, bf16[384,4096]{1,0:T(8,128)(2,1)}) custom-call(bf16[256,1536]{1,0:T(8,128)(2,1)} %bitcast.27, bf16[1,1024,4096]{2,1,0:T(8,128)(2,1)} %win_ref.3, bf16[1,4096,1024]{2,1,0:T(8,128)(2,1)} %wout_ref.3), custom_call_target="tpu_custom_call" | custom-call | flops 6442450944 | bytes 21495808 | tf_op jit(solution)/shard_map/pallas_call | solution.py:371
  49.1 5.9 %all-to-all-done.1 = bf16[32,8,1536]{2,1,0:T(8,128)(2,1)S(1)} async-done(((bf16[32,8,1536]{2,1,0:T(8,128)(2,1)}), bf16[32,8,1536]{2,1,0:T(8,128)(2,1)S(1)}, u32[]{:S(2)}, u32[]{:S(2)}) %all-to-all-start.1) | async-done | bytes 786464 | tf_op jit(solution)/shard_map/all_to_all | solution.py:393
  55.0 0.0 copy-start.7
  55.0 3.6 %all-to-all-start.2 = ((bf16[32,8,1536]{2,1,0:T(8,128)(2,1)}), bf16[32,8,1536]{2,1,0:T(8,128)(2,1)S(1)}, u32[]{:S(2)}, u32[]{:S(2)}) async-start(bf16[32,8,1536]{2,1,0:T(8,128)(2,1)} %bitcast.30), calls=%async_computation.2 | async-start | bytes 1572864 | tf_op jit(solution)/shard_map/all_to_all | solution.py:393
  58.6 0.0 copy-done.7
  58.6 0.0 copy-start
  58.6 0.0 copy-start.1
  58.6 0.0 copy-start.2
  58.7 0.0 copy-start.3
  58.7 0.0 copy-start.4
  58.7 0.0 copy-start.5
  58.7 15.1 %shard_map.97 = bf16[256,1536]{1,0:T(8,128)(2,1)} custom-call(bf16[256,1536]{1,0:T(8,128)(2,1)} %bitcast.28, bf16[384,4096]{1,0:T(8,128)(2,1)} %get-tuple-element.20.hidden_ref, bf16[1,1024,4096]{2,1,0:T(8,128)(2,1)} %win_ref.3, bf16[1,4096,1024]{2,1,0:T(8,128)(2,1)} %wout_ref.3), custom_call_target="tpu_custom_call" | custom-call | flops 6442450944 | bytes 21495808 | tf_op jit(solution)/shard_map/pallas_call | solution.py:371
  73.8 5.4 %all-to-all-done.2 = bf16[32,8,1536]{2,1,0:T(8,128)(2,1)S(1)} async-done(((bf16[32,8,1536]{2,1,0:T(8,128)(2,1)}), bf16[32,8,1536]{2,1,0:T(8,128)(2,1)S(1)}, u32[]{:S(2)}, u32[]{:S(2)}) %all-to-all-start.2) | async-done | bytes 786464 | tf_op jit(solution)/shard_map/all_to_all | solution.py:393
  79.2 3.6 %all-to-all-start.3 = ((bf16[32,8,1536]{2,1,0:T(8,128)(2,1)}), bf16[32,8,1536]{2,1,0:T(8,128)(2,1)S(1)}, u32[]{:S(2)}, u32[]{:S(2)}) async-start(bf16[32,8,1536]{2,1,0:T(8,128)(2,1)} %bitcast.26), calls=%async_computation.3 | async-start | bytes 1572864 | tf_op jit(solution)/shard_map/all_to_all | solution.py:393
  82.9 0.0 copy-done
  82.9 0.0 copy-done.1
  82.9 0.0 copy-done.2
  82.9 0.0 copy-done.3
  82.9 0.0 copy-done.4
  82.9 0.0 copy-done.5
  82.9 1.5 %shard_map.98 = (bf16[128,1024]{1,0:T(8,128)(2,1)}, f32[128,1024]{1,0:T(8,128)S(1)}, f32[32,1024]{1,0:T(8,128)S(1)}) custom-call(s32[2,128]{1,0:T(2,128)S(1)} %bitcast.19, s32[2,128]{1,0:T(2,128)S(1)} %bitcast.23, f32[2,128]{1,0:T(2,128)S(1)} %copy-done.5, bf16[256,1536]{1,0:T(8,128)(2,1)S(1)} %bitcast.14, bf16[128,1024]{1,0:T(8,128)(2,1)S(1)} %copy-done.1, ...), custom_call_target="tpu_custom_call" | custom-call | flops 268435456 | bytes 2296832 | tf_op jit(solution)/shard_map/pallas_call | solution.py:351
  84.4 0.2 collective-permute-start
  84.7 1.0 collective-permute-done
  85.7 1.8 %collective-permute-start.1 = (bf16[16,1024]{1,0:T(8,128)(2,1)S(1)}, bf16[16,1024]{1,0:T(8,128)(2,1)S(1)}, u32[]{:S(2)}, u32[]{:S(2)}) collective-permute-start(bf16[16,1024]{1,0:T(8,128)(2,1)S(1)} %add_convert_fusion.2), channel_id=1, source_target_pairs={{0,2},{1,3},{2,0},{3,1},{4,6},{5,7},{6,4},{7,5},{8,10},{9,11},{10,... | collective-permute-start | bytes 98312 | tf_op jit(solution)/shard_map/ppermute | solution.py:399
  87.5 1.5 %collective-permute-start.2 = (bf16[16,1024]{1,0:T(8,128)(2,1)S(1)}, bf16[16,1024]{1,0:T(8,128)(2,1)S(1)}, u32[]{:S(2)}, u32[]{:S(2)}) collective-permute-start(bf16[16,1024]{1,0:T(8,128)(2,1)S(1)} %add_convert_fusion.2), channel_id=1, source_target_pairs={{0,4},{1,5},{2,6},{3,7},{4,0},{5,1},{6,2},{7,3},{8,12},{9,13},{10,... | collective-permute-start | bytes 98312 | tf_op jit(solution)/shard_map/ppermute | solution.py:399
  89.0 0.3 collective-permute-start.3
  89.2 2.4 %collective-permute-done.1 = bf16[16,1024]{1,0:T(8,128)(2,1)S(1)} collective-permute-done((bf16[16,1024]{1,0:T(8,128)(2,1)S(1)}, bf16[16,1024]{1,0:T(8,128)(2,1)S(1)}, u32[]{:S(2)}, u32[]{:S(2)}) %collective-permute-start.1) | collective-permute-done | bytes 32800 | tf_op jit(solution)/shard_map/ppermute | solution.py:399
  91.6 0.9 collective-permute-done.2
  92.5 2.2 %collective-permute-done.3 = bf16[16,1024]{1,0:T(8,128)(2,1)S(1)} collective-permute-done((bf16[16,1024]{1,0:T(8,128)(2,1)S(1)}, bf16[16,1024]{1,0:T(8,128)(2,1)S(1)}, u32[]{:S(2)}, u32[]{:S(2)}) %collective-permute-start.3) | collective-permute-done | bytes 32800 | tf_op jit(solution)/shard_map/ppermute | solution.py:399
  94.7 1.9 %collective-permute-start.4 = (bf16[16,1024]{1,0:T(8,128)(2,1)S(1)}, bf16[16,1024]{1,0:T(8,128)(2,1)S(1)}, u32[]{:S(2)}, u32[]{:S(2)}) collective-permute-start(bf16[16,1024]{1,0:T(8,128)(2,1)S(1)} %add_convert_fusion.1), channel_id=1, source_target_pairs={{0,8},{1,9},{2,10},{3,11},{4,12},{5,13},{6,14},{7,15},{8,0},{9,1},... | collective-permute-start | bytes 98312 | tf_op jit(solution)/shard_map/ppermute | solution.py:399
  96.6 2.5 %collective-permute-done.4 = bf16[16,1024]{1,0:T(8,128)(2,1)S(1)} collective-permute-done((bf16[16,1024]{1,0:T(8,128)(2,1)S(1)}, bf16[16,1024]{1,0:T(8,128)(2,1)S(1)}, u32[]{:S(2)}, u32[]{:S(2)}) %collective-permute-start.4) | collective-permute-done | bytes 32800 | tf_op jit(solution)/shard_map/ppermute | solution.py:399
  99.1 2.4 %collective-permute-start.5 = (bf16[16,1024]{1,0:T(8,128)(2,1)S(1)}, bf16[16,1024]{1,0:T(8,128)(2,1)S(1)}, u32[]{:S(2)}, u32[]{:S(2)}) collective-permute-start(bf16[16,1024]{1,0:T(8,128)(2,1)S(1)} %add_convert_fusion), channel_id=1, source_target_pairs={{0,16},{1,17},{2,18},{3,19},{4,20},{5,21},{6,22},{7,23},{8,24},{9,... | collective-permute-start | bytes 98312 | tf_op jit(solution)/shard_map/ppermute | solution.py:399
  101.6 3.0 %collective-permute-done.5 = bf16[16,1024]{1,0:T(8,128)(2,1)S(1)} collective-permute-done((bf16[16,1024]{1,0:T(8,128)(2,1)S(1)}, bf16[16,1024]{1,0:T(8,128)(2,1)S(1)}, u32[]{:S(2)}, u32[]{:S(2)}) %collective-permute-start.5) | collective-permute-done | bytes 32800 | tf_op jit(solution)/shard_map/ppermute | solution.py:399
  104.5 0.0 all-to-all-done.3
  104.6 0.1 collective-permute-start.6
  104.6 1.1 %shard_map.99 = bf16[128,1024]{1,0:T(8,128)(2,1)} custom-call(s32[2,128]{1,0:T(2,128)S(1)} %bitcast.20, s32[2,128]{1,0:T(2,128)S(1)} %bitcast.24, bf16[256,1536]{1,0:T(8,128)(2,1)S(1)} %bitcast.13, f32[128,1024]{1,0:T(8,128)S(1)} %get-tuple-element.27.back_ref), custom_call_target="tpu_custom_call" | custom-call | flops 134217728 | bytes 1574912 | tf_op jit(solution)/shard_map/pallas_call | solution.py:351
  105.7 0.1 collective-permute-done.6
  105.9 0.7 maximum_bitcast_fusion
  (6 shorter events, 0.1 us)
Async XLA Ops:
  2.8 27.9 %all-to-all-start = ((bf16[32,8,1536]{2,1,0:T(8,128)(2,1)}), bf16[32,8,1536]{2,1,0:T(8,128)(2,1)S(1)}, u32[]{:S(2)}, u32[]{:S(2)}) async-start(bf16[32,8,1536]{2,1,0:T(8,128)(2,1)} %bitcast.25), calls=%async_computation | async-start | bytes 1572864 | tf_op jit(solution)/shard_map/all_to_all | solution.py:393
  30.7 3.6 %copy-start.6 = (bf16[32,8,1536]{2,1,0:T(8,128)(2,1)}, bf16[32,8,1536]{2,1,0:T(8,128)(2,1)S(1)}, u32[]{:S(2)}) copy-start(bf16[32,8,1536]{2,1,0:T(8,128)(2,1)S(1)} %all-to-all-done) | copy-start | bytes 2359300
  30.7 24.2 %all-to-all-start.1 = ((bf16[32,8,1536]{2,1,0:T(8,128)(2,1)}), bf16[32,8,1536]{2,1,0:T(8,128)(2,1)S(1)}, u32[]{:S(2)}, u32[]{:S(2)}) async-start(bf16[32,8,1536]{2,1,0:T(8,128)(2,1)} %bitcast.29), calls=%async_computation.1 | async-start | bytes 1572864 | tf_op jit(solution)/shard_map/all_to_all | solution.py:393
  55.0 3.6 %copy-start.7 = (bf16[32,8,1536]{2,1,0:T(8,128)(2,1)}, bf16[32,8,1536]{2,1,0:T(8,128)(2,1)S(1)}, u32[]{:S(2)}) copy-start(bf16[32,8,1536]{2,1,0:T(8,128)(2,1)S(1)} %all-to-all-done.1) | copy-start | bytes 2359300
  55.0 24.2 %all-to-all-start.2 = ((bf16[32,8,1536]{2,1,0:T(8,128)(2,1)}), bf16[32,8,1536]{2,1,0:T(8,128)(2,1)S(1)}, u32[]{:S(2)}, u32[]{:S(2)}) async-start(bf16[32,8,1536]{2,1,0:T(8,128)(2,1)} %bitcast.30), calls=%async_computation.2 | async-start | bytes 1572864 | tf_op jit(solution)/shard_map/all_to_all | solution.py:393
  58.6 24.3 %copy-start = (bf16[128,1024]{1,0:T(8,128)(2,1)S(1)}, bf16[128,1024]{1,0:T(8,128)(2,1)}, u32[]{:S(2)}) copy-start(bf16[128,1024]{1,0:T(8,128)(2,1)} %tokens_ref.3) | copy-start | bytes 786436
  58.6 24.3 %copy-start.1 = (bf16[128,1024]{1,0:T(8,128)(2,1)S(1)}, bf16[128,1024]{1,0:T(8,128)(2,1)}, u32[]{:S(2)}) copy-start(bf16[128,1024]{1,0:T(8,128)(2,1)} %cot_ref.3) | copy-start | bytes 786436
  58.6 24.3 %copy-start.2 = (bf16[1024,32]{0,1:T(8,128)(2,1)S(1)}, bf16[1024,32]{0,1:T(8,128)(2,1)}, u32[]{:S(2)}) copy-start(bf16[1024,32]{0,1:T(8,128)(2,1)} %param.8) | copy-start | bytes 196612
  58.7 24.2 %copy-start.3 = (s32[128,2]{0,1:T(2,128)S(1)}, s32[128,2]{0,1:T(2,128)}, u32[]{:S(2)}) copy-start(s32[128,2]{0,1:T(2,128)} %param.11) | copy-start | bytes 3076
  58.7 24.2 %copy-start.4 = (s32[128,2]{0,1:T(2,128)S(1)}, s32[128,2]{0,1:T(2,128)}, u32[]{:S(2)}) copy-start(s32[128,2]{0,1:T(2,128)} %param.12) | copy-start | bytes 3076
  58.7 24.2 %copy-start.5 = (f32[2,128]{1,0:T(2,128)S(1)}, f32[2,128]{1,0:T(2,128)}, u32[]{:S(2)}) copy-start(f32[2,128]{1,0:T(2,128)} %get-tuple-element.16.gates_ref) | copy-start | bytes 3076
  79.2 25.3 %all-to-all-start.3 = ((bf16[32,8,1536]{2,1,0:T(8,128)(2,1)}), bf16[32,8,1536]{2,1,0:T(8,128)(2,1)S(1)}, u32[]{:S(2)}, u32[]{:S(2)}) async-start(bf16[32,8,1536]{2,1,0:T(8,128)(2,1)} %bitcast.26), calls=%async_computation.3 | async-start | bytes 1572864 | tf_op jit(solution)/shard_map/all_to_all | solution.py:393
  84.4 1.3 %collective-permute-start = (f32[16,1024]{1,0:T(8,128)S(1)}, f32[16,1024]{1,0:T(8,128)S(1)}, u32[]{:S(2)}, u32[]{:S(2)}) collective-permute-start(f32[16,1024]{1,0:T(8,128)S(1)} %constant_dynamic-slice_fusion), channel_id=1, source_target_pairs={{0,1},{1,0},{2,3},{3,2},{4,5},{5,4},{6,7},{7,6},{8,9},{9,8},{10,11... | collective-permute-start | bytes 196616 | tf_op jit(solution)/shard_map/ppermute | solution.py:399
  85.7 6.0 %collective-permute-start.1 = (bf16[16,1024]{1,0:T(8,128)(2,1)S(1)}, bf16[16,1024]{1,0:T(8,128)(2,1)S(1)}, u32[]{:S(2)}, u32[]{:S(2)}) collective-permute-start(bf16[16,1024]{1,0:T(8,128)(2,1)S(1)} %add_convert_fusion.2), channel_id=1, source_target_pairs={{0,2},{1,3},{2,0},{3,1},{4,6},{5,7},{6,4},{7,5},{8,10},{9,11},{10,... | collective-permute-start | bytes 98312 | tf_op jit(solution)/shard_map/ppermute | solution.py:399
  87.5 5.0 %collective-permute-start.2 = (bf16[16,1024]{1,0:T(8,128)(2,1)S(1)}, bf16[16,1024]{1,0:T(8,128)(2,1)S(1)}, u32[]{:S(2)}, u32[]{:S(2)}) collective-permute-start(bf16[16,1024]{1,0:T(8,128)(2,1)S(1)} %add_convert_fusion.2), channel_id=1, source_target_pairs={{0,4},{1,5},{2,6},{3,7},{4,0},{5,1},{6,2},{7,3},{8,12},{9,13},{10,... | collective-permute-start | bytes 98312 | tf_op jit(solution)/shard_map/ppermute | solution.py:399
  89.0 5.7 %collective-permute-start.3 = (bf16[16,1024]{1,0:T(8,128)(2,1)S(1)}, bf16[16,1024]{1,0:T(8,128)(2,1)S(1)}, u32[]{:S(2)}, u32[]{:S(2)}) collective-permute-start(bf16[16,1024]{1,0:T(8,128)(2,1)S(1)} %add_convert_fusion.2), channel_id=1, source_target_pairs={{0,6},{1,7},{2,4},{3,5},{4,2},{5,3},{6,0},{7,1},{8,14},{9,15},{10,... | collective-permute-start | bytes 98312 | tf_op jit(solution)/shard_map/ppermute | solution.py:399
  94.7 4.4 %collective-permute-start.4 = (bf16[16,1024]{1,0:T(8,128)(2,1)S(1)}, bf16[16,1024]{1,0:T(8,128)(2,1)S(1)}, u32[]{:S(2)}, u32[]{:S(2)}) collective-permute-start(bf16[16,1024]{1,0:T(8,128)(2,1)S(1)} %add_convert_fusion.1), channel_id=1, source_target_pairs={{0,8},{1,9},{2,10},{3,11},{4,12},{5,13},{6,14},{7,15},{8,0},{9,1},... | collective-permute-start | bytes 98312 | tf_op jit(solution)/shard_map/ppermute | solution.py:399
  99.1 5.4 %collective-permute-start.5 = (bf16[16,1024]{1,0:T(8,128)(2,1)S(1)}, bf16[16,1024]{1,0:T(8,128)(2,1)S(1)}, u32[]{:S(2)}, u32[]{:S(2)}) collective-permute-start(bf16[16,1024]{1,0:T(8,128)(2,1)S(1)} %add_convert_fusion), channel_id=1, source_target_pairs={{0,16},{1,17},{2,18},{3,19},{4,20},{5,21},{6,22},{7,23},{8,24},{9,... | collective-permute-start | bytes 98312 | tf_op jit(solution)/shard_map/ppermute | solution.py:399
  104.6 1.3 %collective-permute-start.6 = (f32[16,1024]{1,0:T(8,128)S(1)}, f32[16,1024]{1,0:T(8,128)S(1)}, u32[]{:S(2)}, u32[]{:S(2)}) collective-permute-start(f32[16,1024]{1,0:T(8,128)S(1)} %convert_add_fusion), channel_id=1, source_target_pairs={{0,1},{1,0},{2,3},{3,2},{4,5},{5,4},{6,7},{7,6},{8,9},{9,8},{10,11... | collective-permute-start | bytes 196616 | tf_op jit(solution)/shard_map/ppermute | solution.py:399

commit v13 on v10

--- a/solution.py
+++ b/solution.py
@@ -403,8 +403,11 @@
     bit = PLANE
     while bit < devices:
         sent = own.astype(BF16)
-        own = sent.astype(F32) + from_device(sent, bit, devices).astype(F32)
-        bit *= 2
+        steps = (1, 2, 3) if 2 * bit < devices else (1,)
+        terms = [sent] + [from_device(sent, step * bit, devices) for step in steps]
+        terms = [term.astype(F32) for term in terms]
+        own = sum_of_pairs(*terms) if len(terms) == 4 else terms[0] + terms[1]
+        bit *= 4
     beside, own = lax.optimization_barrier((beside, own))
     other = from_device(own, 1, devices)
     first = core == 0

time: 107 us -> 109 us (1.019)
  waiting for transfers between devices: 41.1 us -> 42.4 us
    ppermute x7 -> x8, waiting for transfers between devices: 12.1 us -> 13.4 us  [from_device(): return lax.ppermute(x, AXES, [(d, d ^ bits) for d in range(devices)])]
    ppermute x7 -> x8, starting transfers between devices: 8.21 us -> 8.33 us  [from_device(): return lax.ppermute(x, AXES, [(d, d ^ bits) for d in range(devices)])]
  transfers between devices with their start and end apart: 11 -> 12, of which waited for: 10 -> 9; matrix products, arithmetic and copies ran while one was open for 0% -> 0% of each run, Pallas kernels for 33% -> 33%
where the time goes in v13:
time: 109 us; the launch traced here: 108 us
  waiting for transfers between devices  42.4 us (39%)
  Pallas kernels  37.4 us (34%)
  starting transfers between devices  26.5 us (24%)
    pallas_call x2, Pallas kernels, expert_call(): pl.pallas_call(functools.partial(kernel, lay), grid=(ff // tile,), in_spe...  29.8 us
    all_to_all x4, waiting for transfers between devices, exchange(): return lax.all_to_all(x, AXES, split_axis=0, concat_axis=0, tiled=True)  29.1 us
    all_to_all x4, starting transfers between devices, exchange(): return lax.all_to_all(x, AXES, split_axis=0, concat_axis=0, tiled=True)  18.2 us
    ppermute x8, waiting for transfers between devices, from_device(): return lax.ppermute(x, AXES, [(d, d ^ bits) for d in range(devices)])  13.4 us
    ppermute x8, starting transfers between devices, from_device(): return lax.ppermute(x, AXES, [(d, d ^ bits) for d in range(devices)])  8.33 us
    pallas_call x3, Pallas kernels, call(): pl.pallas_call(kernel, out_shape=out_shape, compiler_params=pltpu.Compile...  5.43 us
  transfers between devices with their start and end apart: 12, of which 9 were waited for; matrix products, arithmetic and copies ran while one was open for 0% of the time, Pallas kernels for 33%

profile of v13, /device:TPU:0, one launch (start us, length us, event | category | flops | bytes accessed | tf_op | source)
XLA Modules:
  0.0 108.0 jit_solution(3336194071671056436)
XLA Ops:
  0.6 2.2 %shard_map.95 = bf16[256,1536]{1,0:T(8,128)(2,1)} custom-call(s32[2,128]{1,0:T(2,128)} %bitcast.17, s32[2,128]{1,0:T(2,128)} %bitcast.21, bf16[128,1024]{1,0:T(8,128)(2,1)} %tokens_ref.3), custom_call_target="tpu_custom_call" | custom-call | flops 134217728 | bytes 1048576 | tf_op jit(solution)/shard_map/pallas_call | solution.py:427
  2.8 7.3 %all-to-all-start = ((bf16[32,8,1536]{2,1,0:T(8,128)(2,1)}), bf16[32,8,1536]{2,1,0:T(8,128)(2,1)S(1)}, u32[]{:S(2)}, u32[]{:S(2)}) async-start(bf16[32,8,1536]{2,1,0:T(8,128)(2,1)} %bitcast.25), calls=%async_computation | async-start | bytes 1572864 | tf_op jit(solution)/shard_map/all_to_all | solution.py:383
  10.1 2.9 %shard_map.94 = (bf16[256,1536]{1,0:T(8,128)(2,1)}, f32[2,128]{1,0:T(2,128)}) custom-call(s32[2,128]{1,0:T(2,128)} %bitcast.18, s32[2,128]{1,0:T(2,128)} %bitcast.22, bf16[128,1024]{1,0:T(8,128)(2,1)} %tokens_ref.3, bf16[32,1024]{1,0:T(8,128)(2,1)} %bitcast.15, bf16[128,1024]{1,0:T(8,128)(2,1)} %cot_ref.3), custom_call_target="tpu_custom_call" | custom-call | flops 268435456 | bytes 1379328 | tf_op jit(solution)/shard_map/pallas_call | solution.py:346
  13.0 17.8 %all-to-all-done = bf16[32,8,1536]{2,1,0:T(8,128)(2,1)S(1)} async-done(((bf16[32,8,1536]{2,1,0:T(8,128)(2,1)}), bf16[32,8,1536]{2,1,0:T(8,128)(2,1)S(1)}, u32[]{:S(2)}, u32[]{:S(2)}) %all-to-all-start) | async-done | bytes 786464 | tf_op jit(solution)/shard_map/all_to_all | solution.py:383
  30.7 0.0 copy-start.6
  30.7 3.6 %all-to-all-start.1 = ((bf16[32,8,1536]{2,1,0:T(8,128)(2,1)}), bf16[32,8,1536]{2,1,0:T(8,128)(2,1)S(1)}, u32[]{:S(2)}, u32[]{:S(2)}) async-start(bf16[32,8,1536]{2,1,0:T(8,128)(2,1)} %bitcast.29), calls=%async_computation.1 | async-start | bytes 1572864 | tf_op jit(solution)/shard_map/all_to_all | solution.py:383
  34.4 0.0 copy-done.6
  34.4 14.7 %shard_map.96 = (bf16[256,1536]{1,0:T(8,128)(2,1)}, bf16[384,4096]{1,0:T(8,128)(2,1)}) custom-call(bf16[256,1536]{1,0:T(8,128)(2,1)} %bitcast.27, bf16[1,1024,4096]{2,1,0:T(8,128)(2,1)} %win_ref.3, bf16[1,4096,1024]{2,1,0:T(8,128)(2,1)} %wout_ref.3), custom_call_target="tpu_custom_call" | custom-call | flops 6442450944 | bytes 21495808 | tf_op jit(solution)/shard_map/pallas_call | solution.py:366
  49.1 5.9 %all-to-all-done.1 = bf16[32,8,1536]{2,1,0:T(8,128)(2,1)S(1)} async-done(((bf16[32,8,1536]{2,1,0:T(8,128)(2,1)}), bf16[32,8,1536]{2,1,0:T(8,128)(2,1)S(1)}, u32[]{:S(2)}, u32[]{:S(2)}) %all-to-all-start.1) | async-done | bytes 786464 | tf_op jit(solution)/shard_map/all_to_all | solution.py:383
  55.0 0.0 copy-start.7
  55.0 3.6 %all-to-all-start.2 = ((bf16[32,8,1536]{2,1,0:T(8,128)(2,1)}), bf16[32,8,1536]{2,1,0:T(8,128)(2,1)S(1)}, u32[]{:S(2)}, u32[]{:S(2)}) async-start(bf16[32,8,1536]{2,1,0:T(8,128)(2,1)} %bitcast.30), calls=%async_computation.2 | async-start | bytes 1572864 | tf_op jit(solution)/shard_map/all_to_all | solution.py:383
  58.6 0.0 copy-done.7
  58.6 0.0 copy-start
  58.6 0.0 copy-start.1
  58.6 0.0 copy-start.2
  58.6 0.0 copy-start.3
  58.7 0.0 copy-start.4
  58.7 0.0 copy-start.5
  58.7 15.1 %shard_map.97 = bf16[256,1536]{1,0:T(8,128)(2,1)} custom-call(bf16[256,1536]{1,0:T(8,128)(2,1)} %bitcast.28, bf16[384,4096]{1,0:T(8,128)(2,1)} %get-tuple-element.20.hidden_ref, bf16[1,1024,4096]{2,1,0:T(8,128)(2,1)} %win_ref.3, bf16[1,4096,1024]{2,1,0:T(8,128)(2,1)} %wout_ref.3), custom_call_target="tpu_custom_call" | custom-call | flops 6442450944 | bytes 21495808 | tf_op jit(solution)/shard_map/pallas_call | solution.py:366
  73.8 5.4 %all-to-all-done.2 = bf16[32,8,1536]{2,1,0:T(8,128)(2,1)S(1)} async-done(((bf16[32,8,1536]{2,1,0:T(8,128)(2,1)}), bf16[32,8,1536]{2,1,0:T(8,128)(2,1)S(1)}, u32[]{:S(2)}, u32[]{:S(2)}) %all-to-all-start.2) | async-done | bytes 786464 | tf_op jit(solution)/shard_map/all_to_all | solution.py:383
  79.2 3.6 %all-to-all-start.3 = ((bf16[32,8,1536]{2,1,0:T(8,128)(2,1)}), bf16[32,8,1536]{2,1,0:T(8,128)(2,1)S(1)}, u32[]{:S(2)}, u32[]{:S(2)}) async-start(bf16[32,8,1536]{2,1,0:T(8,128)(2,1)} %bitcast.26), calls=%async_computation.3 | async-start | bytes 1572864 | tf_op jit(solution)/shard_map/all_to_all | solution.py:383
  82.9 0.0 copy-done
  82.9 0.0 copy-done.1
  82.9 0.0 copy-done.2
  82.9 0.0 copy-done.3
  82.9 0.0 copy-done.4
  82.9 0.0 copy-done.5
  82.9 1.5 %shard_map.98 = (bf16[128,1024]{1,0:T(8,128)(2,1)}, f32[128,1024]{1,0:T(8,128)S(1)}, f32[32,1024]{1,0:T(8,128)S(1)}) custom-call(s32[2,128]{1,0:T(2,128)S(1)} %bitcast.19, s32[2,128]{1,0:T(2,128)S(1)} %bitcast.23, f32[2,128]{1,0:T(2,128)S(1)} %copy-done.5, bf16[256,1536]{1,0:T(8,128)(2,1)S(1)} %bitcast.14, bf16[128,1024]{1,0:T(8,128)(2,1)S(1)} %copy-done.1, ...), custom_call_target="tpu_custom_call" | custom-call | flops 268435456 | bytes 2296832 | tf_op jit(solution)/shard_map/pallas_call | solution.py:346
  84.4 0.3 collective-permute-start
  84.6 1.0 collective-permute-done
  85.7 1.8 %collective-permute-start.1 = (bf16[16,1024]{1,0:T(8,128)(2,1)S(1)}, bf16[16,1024]{1,0:T(8,128)(2,1)S(1)}, u32[]{:S(2)}, u32[]{:S(2)}) collective-permute-start(bf16[16,1024]{1,0:T(8,128)(2,1)S(1)} %add_convert_fusion.1), channel_id=1, source_target_pairs={{0,2},{1,3},{2,0},{3,1},{4,6},{5,7},{6,4},{7,5},{8,10},{9,11},{10,... | collective-permute-start | bytes 98312 | tf_op jit(solution)/shard_map/ppermute | solution.py:387
  87.5 1.5 %collective-permute-start.2 = (bf16[16,1024]{1,0:T(8,128)(2,1)S(1)}, bf16[16,1024]{1,0:T(8,128)(2,1)S(1)}, u32[]{:S(2)}, u32[]{:S(2)}) collective-permute-start(bf16[16,1024]{1,0:T(8,128)(2,1)S(1)} %add_convert_fusion.1), channel_id=1, source_target_pairs={{0,4},{1,5},{2,6},{3,7},{4,0},{5,1},{6,2},{7,3},{8,12},{9,13},{10,... | collective-permute-start | bytes 98312 | tf_op jit(solution)/shard_map/ppermute | solution.py:387
  89.0 0.3 collective-permute-start.3
  89.2 2.4 %collective-permute-done.1 = bf16[16,1024]{1,0:T(8,128)(2,1)S(1)} collective-permute-done((bf16[16,1024]{1,0:T(8,128)(2,1)S(1)}, bf16[16,1024]{1,0:T(8,128)(2,1)S(1)}, u32[]{:S(2)}, u32[]{:S(2)}) %collective-permute-start.1) | collective-permute-done | bytes 32800 | tf_op jit(solution)/shard_map/ppermute | solution.py:387
  91.6 0.9 collective-permute-done.2
  92.5 2.2 %collective-permute-done.3 = bf16[16,1024]{1,0:T(8,128)(2,1)S(1)} collective-permute-done((bf16[16,1024]{1,0:T(8,128)(2,1)S(1)}, bf16[16,1024]{1,0:T(8,128)(2,1)S(1)}, u32[]{:S(2)}, u32[]{:S(2)}) %collective-permute-start.3) | collective-permute-done | bytes 32800 | tf_op jit(solution)/shard_map/ppermute | solution.py:387
  94.7 1.9 %collective-permute-start.4 = (bf16[16,1024]{1,0:T(8,128)(2,1)S(1)}, bf16[16,1024]{1,0:T(8,128)(2,1)S(1)}, u32[]{:S(2)}, u32[]{:S(2)}) collective-permute-start(bf16[16,1024]{1,0:T(8,128)(2,1)S(1)} %add_convert_fusion), channel_id=1, source_target_pairs={{0,8},{1,9},{2,10},{3,11},{4,12},{5,13},{6,14},{7,15},{8,0},{9,1},... | collective-permute-start | bytes 98312 | tf_op jit(solution)/shard_map/ppermute | solution.py:387
  96.6 1.9 %collective-permute-start.5 = (bf16[16,1024]{1,0:T(8,128)(2,1)S(1)}, bf16[16,1024]{1,0:T(8,128)(2,1)S(1)}, u32[]{:S(2)}, u32[]{:S(2)}) collective-permute-start(bf16[16,1024]{1,0:T(8,128)(2,1)S(1)} %add_convert_fusion), channel_id=1, source_target_pairs={{0,16},{1,17},{2,18},{3,19},{4,20},{5,21},{6,22},{7,23},{8,24},{9,... | collective-permute-start | bytes 98312 | tf_op jit(solution)/shard_map/ppermute | solution.py:387
  98.5 0.6 collective-permute-start.6
  99.2 0.0 collective-permute-done.4
  99.2 6.8 %collective-permute-done.5 = bf16[16,1024]{1,0:T(8,128)(2,1)S(1)} collective-permute-done((bf16[16,1024]{1,0:T(8,128)(2,1)S(1)}, bf16[16,1024]{1,0:T(8,128)(2,1)S(1)}, u32[]{:S(2)}, u32[]{:S(2)}) %collective-permute-start.5) | collective-permute-done | bytes 32800 | tf_op jit(solution)/shard_map/ppermute | solution.py:387
  105.9 0.0 collective-permute-done.6
  106.0 0.0 all-to-all-done.3
  106.0 0.1 collective-permute-start.7
  106.0 1.1 %shard_map.99 = bf16[128,1024]{1,0:T(8,128)(2,1)} custom-call(s32[2,128]{1,0:T(2,128)S(1)} %bitcast.20, s32[2,128]{1,0:T(2,128)S(1)} %bitcast.24, bf16[256,1536]{1,0:T(8,128)(2,1)S(1)} %bitcast.13, f32[128,1024]{1,0:T(8,128)S(1)} %get-tuple-element.27.back_ref), custom_call_target="tpu_custom_call" | custom-call | flops 134217728 | bytes 1574912 | tf_op jit(solution)/shard_map/pallas_call | solution.py:346
  107.1 0.1 collective-permute-done.7
  107.3 0.7 maximum_bitcast_fusion
  (5 shorter events, 0.1 us)
Async XLA Ops:
  2.8 27.9 %all-to-all-start = ((bf16[32,8,1536]{2,1,0:T(8,128)(2,1)}), bf16[32,8,1536]{2,1,0:T(8,128)(2,1)S(1)}, u32[]{:S(2)}, u32[]{:S(2)}) async-start(bf16[32,8,1536]{2,1,0:T(8,128)(2,1)} %bitcast.25), calls=%async_computation | async-start | bytes 1572864 | tf_op jit(solution)/shard_map/all_to_all | solution.py:383
  30.7 3.6 %copy-start.6 = (bf16[32,8,1536]{2,1,0:T(8,128)(2,1)}, bf16[32,8,1536]{2,1,0:T(8,128)(2,1)S(1)}, u32[]{:S(2)}) copy-start(bf16[32,8,1536]{2,1,0:T(8,128)(2,1)S(1)} %all-to-all-done) | copy-start | bytes 2359300
  30.7 24.2 %all-to-all-start.1 = ((bf16[32,8,1536]{2,1,0:T(8,128)(2,1)}), bf16[32,8,1536]{2,1,0:T(8,128)(2,1)S(1)}, u32[]{:S(2)}, u32[]{:S(2)}) async-start(bf16[32,8,1536]{2,1,0:T(8,128)(2,1)} %bitcast.29), calls=%async_computation.1 | async-start | bytes 1572864 | tf_op jit(solution)/shard_map/all_to_all | solution.py:383
  55.0 3.6 %copy-start.7 = (bf16[32,8,1536]{2,1,0:T(8,128)(2,1)}, bf16[32,8,1536]{2,1,0:T(8,128)(2,1)S(1)}, u32[]{:S(2)}) copy-start(bf16[32,8,1536]{2,1,0:T(8,128)(2,1)S(1)} %all-to-all-done.1) | copy-start | bytes 2359300
  55.0 24.2 %all-to-all-start.2 = ((bf16[32,8,1536]{2,1,0:T(8,128)(2,1)}), bf16[32,8,1536]{2,1,0:T(8,128)(2,1)S(1)}, u32[]{:S(2)}, u32[]{:S(2)}) async-start(bf16[32,8,1536]{2,1,0:T(8,128)(2,1)} %bitcast.30), calls=%async_computation.2 | async-start | bytes 1572864 | tf_op jit(solution)/shard_map/all_to_all | solution.py:383
  58.6 24.3 %copy-start = (bf16[128,1024]{1,0:T(8,128)(2,1)S(1)}, bf16[128,1024]{1,0:T(8,128)(2,1)}, u32[]{:S(2)}) copy-start(bf16[128,1024]{1,0:T(8,128)(2,1)} %tokens_ref.3) | copy-start | bytes 786436
  58.6 24.3 %copy-start.1 = (bf16[128,1024]{1,0:T(8,128)(2,1)S(1)}, bf16[128,1024]{1,0:T(8,128)(2,1)}, u32[]{:S(2)}) copy-start(bf16[128,1024]{1,0:T(8,128)(2,1)} %cot_ref.3) | copy-start | bytes 786436
  58.6 24.3 %copy-start.2 = (bf16[1024,32]{0,1:T(8,128)(2,1)S(1)}, bf16[1024,32]{0,1:T(8,128)(2,1)}, u32[]{:S(2)}) copy-start(bf16[1024,32]{0,1:T(8,128)(2,1)} %param.8) | copy-start | bytes 196612
  58.6 24.2 %copy-start.3 = (s32[128,2]{0,1:T(2,128)S(1)}, s32[128,2]{0,1:T(2,128)}, u32[]{:S(2)}) copy-start(s32[128,2]{0,1:T(2,128)} %param.11) | copy-start | bytes 3076
  58.7 24.2 %copy-start.4 = (s32[128,2]{0,1:T(2,128)S(1)}, s32[128,2]{0,1:T(2,128)}, u32[]{:S(2)}) copy-start(s32[128,2]{0,1:T(2,128)} %param.12) | copy-start | bytes 3076
  58.7 24.2 %copy-start.5 = (f32[2,128]{1,0:T(2,128)S(1)}, f32[2,128]{1,0:T(2,128)}, u32[]{:S(2)}) copy-start(f32[2,128]{1,0:T(2,128)} %get-tuple-element.16.gates_ref) | copy-start | bytes 3076
  79.2 26.7 %all-to-all-start.3 = ((bf16[32,8,1536]{2,1,0:T(8,128)(2,1)}), bf16[32,8,1536]{2,1,0:T(8,128)(2,1)S(1)}, u32[]{:S(2)}, u32[]{:S(2)}) async-start(bf16[32,8,1536]{2,1,0:T(8,128)(2,1)} %bitcast.26), calls=%async_computation.3 | async-start | bytes 1572864 | tf_op jit(solution)/shard_map/all_to_all | solution.py:383
  84.4 1.3 %collective-permute-start = (f32[16,1024]{1,0:T(8,128)S(1)}, f32[16,1024]{1,0:T(8,128)S(1)}, u32[]{:S(2)}, u32[]{:S(2)}) collective-permute-start(f32[16,1024]{1,0:T(8,128)S(1)} %constant_dynamic-slice_fusion), channel_id=1, source_target_pairs={{0,1},{1,0},{2,3},{3,2},{4,5},{5,4},{6,7},{7,6},{8,9},{9,8},{10,11... | collective-permute-start | bytes 196616 | tf_op jit(solution)/shard_map/ppermute | solution.py:387
  85.7 6.0 %collective-permute-start.1 = (bf16[16,1024]{1,0:T(8,128)(2,1)S(1)}, bf16[16,1024]{1,0:T(8,128)(2,1)S(1)}, u32[]{:S(2)}, u32[]{:S(2)}) collective-permute-start(bf16[16,1024]{1,0:T(8,128)(2,1)S(1)} %add_convert_fusion.1), channel_id=1, source_target_pairs={{0,2},{1,3},{2,0},{3,1},{4,6},{5,7},{6,4},{7,5},{8,10},{9,11},{10,... | collective-permute-start | bytes 98312 | tf_op jit(solution)/shard_map/ppermute | solution.py:387
  87.5 5.0 %collective-permute-start.2 = (bf16[16,1024]{1,0:T(8,128)(2,1)S(1)}, bf16[16,1024]{1,0:T(8,128)(2,1)S(1)}, u32[]{:S(2)}, u32[]{:S(2)}) collective-permute-start(bf16[16,1024]{1,0:T(8,128)(2,1)S(1)} %add_convert_fusion.1), channel_id=1, source_target_pairs={{0,4},{1,5},{2,6},{3,7},{4,0},{5,1},{6,2},{7,3},{8,12},{9,13},{10,... | collective-permute-start | bytes 98312 | tf_op jit(solution)/shard_map/ppermute | solution.py:387
  89.0 5.7 %collective-permute-start.3 = (bf16[16,1024]{1,0:T(8,128)(2,1)S(1)}, bf16[16,1024]{1,0:T(8,128)(2,1)S(1)}, u32[]{:S(2)}, u32[]{:S(2)}) collective-permute-start(bf16[16,1024]{1,0:T(8,128)(2,1)S(1)} %add_convert_fusion.1), channel_id=1, source_target_pairs={{0,6},{1,7},{2,4},{3,5},{4,2},{5,3},{6,0},{7,1},{8,14},{9,15},{10,... | collective-permute-start | bytes 98312 | tf_op jit(solution)/shard_map/ppermute | solution.py:387
  94.7 4.5 %collective-permute-start.4 = (bf16[16,1024]{1,0:T(8,128)(2,1)S(1)}, bf16[16,1024]{1,0:T(8,128)(2,1)S(1)}, u32[]{:S(2)}, u32[]{:S(2)}) collective-permute-start(bf16[16,1024]{1,0:T(8,128)(2,1)S(1)} %add_convert_fusion), channel_id=1, source_target_pairs={{0,8},{1,9},{2,10},{3,11},{4,12},{5,13},{6,14},{7,15},{8,0},{9,1},... | collective-permute-start | bytes 98312 | tf_op jit(solution)/shard_map/ppermute | solution.py:387
  96.6 9.3 %collective-permute-start.5 = (bf16[16,1024]{1,0:T(8,128)(2,1)S(1)}, bf16[16,1024]{1,0:T(8,128)(2,1)S(1)}, u32[]{:S(2)}, u32[]{:S(2)}) collective-permute-start(bf16[16,1024]{1,0:T(8,128)(2,1)S(1)} %add_convert_fusion), channel_id=1, source_target_pairs={{0,16},{1,17},{2,18},{3,19},{4,20},{5,21},{6,22},{7,23},{8,24},{9,... | collective-permute-start | bytes 98312 | tf_op jit(solution)/shard_map/ppermute | solution.py:387
  98.5 7.4 %collective-permute-start.6 = (bf16[16,1024]{1,0:T(8,128)(2,1)S(1)}, bf16[16,1024]{1,0:T(8,128)(2,1)S(1)}, u32[]{:S(2)}, u32[]{:S(2)}) collective-permute-start(bf16[16,1024]{1,0:T(8,128)(2,1)S(1)} %add_convert_fusion), channel_id=1, source_target_pairs={{0,24},{1,25},{2,26},{3,27},{4,28},{5,29},{6,30},{7,31},{8,16},{9,... | collective-permute-start | bytes 98312 | tf_op jit(solution)/shard_map/ppermute | solution.py:387
  106.0 1.3 %collective-permute-start.7 = (f32[16,1024]{1,0:T(8,128)S(1)}, f32[16,1024]{1,0:T(8,128)S(1)}, u32[]{:S(2)}, u32[]{:S(2)}) collective-permute-start(f32[16,1024]{1,0:T(8,128)S(1)} %add_add_fusion), channel_id=1, source_target_pairs={{0,1},{1,0},{2,3},{3,2},{4,5},{5,4},{6,7},{7,6},{8,9},{9,8},{10,11... | collective-permute-start | bytes 196616 | tf_op jit(solution)/shard_map/ppermute | solution.py:387

commit v14 on v10

--- a/solution.py
+++ b/solution.py
@@ -100,27 +100,26 @@
         ).astype(BF16)
 
 
-def pick(lay, ranks, message_ref):
-    count = message_ref.shape[0]
-    toks = ranks[0][0].shape[0]
+def row_onehots(lay, ranks, count):
+    toks = ranks[0].shape[0]
     row_at = iota((toks, count), 1)
-
-    def onehot(rows):
-        hit = functools.reduce(jnp.logical_or, [row_at == row for row in rows])
-        return jnp.where(hit, 1.0, 0.0).astype(BF16)
-
-    whole = [onehot([t[group] for t in ranks]) for group in range(lay.full)]
+    rows = list(ranks[: lay.full])
+    if lay.rest:
+        rows += [shifted(ranks[lay.full], cut * lay.rest) for cut in range(lay.cuts)]
+    return [jnp.where(row_at == row, 1.0, 0.0).astype(BF16) for row in rows]
+
+
+def pick(lay, hots, message_ref):
     pieces = []
     for cut in range(lay.cuts):
         left = cut * lay.piece
         total = None
         for group in range(lay.full):
             start = group * lay.width + left
-            term = dot(whole[group], message_ref[:, start : start + lay.piece])
+            term = dot(hots[group], message_ref[:, start : start + lay.piece])
             total = term if total is None else total + term
         if lay.rest:
-            hot = onehot([shifted(t[lay.full], cut * lay.rest) for t in ranks])
-            term = dot(hot, message_ref[:, lay.base : lay.base + lay.piece])
+            term = dot(hots[lay.full + cut], message_ref[:, lay.base : lay.base + lay.piece])
             total = term if total is None else total + term
         pieces.append(total)
     return jnp.concatenate(pieces, axis=1) if len(pieces) > 1 else pieces[0]
@@ -309,13 +308,18 @@
     mixed_ref,
     back_ref,
     partial_ref,
+    hots_ref,
 ):
     experts = router_ref.shape[0]
     toks = tokens_ref.shape[0]
     ids, ranks = column_targets(lay, ids_ref, slots_ref)
     gates = [as_column(gates_ref[k : k + 1, :]) for k in range(2)]
     cot = cot_ref[...].astype(F32)
-    choice = [pick(lay, [ranks[k]], message_ref) for k in range(2)]
+    count = message_ref.shape[0]
+    hots = [row_onehots(lay, ranks[k], count) for k in range(2)]
+    choice = [pick(lay, hots[k], message_ref) for k in range(2)]
+    for at, (one, two) in enumerate(zip(*hots)):
+        hots_ref[:, at * count : (at + 1) * count] = one + two
     mixed_ref[...] = (gates[0] * choice[0] + gates[1] * choice[1]).astype(BF16)
     actions = [jnp.sum(choice[k] * cot, axis=1, keepdims=True) for k in range(2)]
     slope = gates[0] * gates[1] * (actions[0] - actions[1])
@@ -335,9 +339,10 @@
     partial_ref[...] = (dot(high, tokens) + dot(low, tokens)) * (1.0 / toks)
 
 
-def grad_kernel(lay, ids_ref, slots_ref, message_ref, back_ref, out_ref):
-    _, ranks = column_targets(lay, ids_ref, slots_ref)
-    out_ref[...] = (pick(lay, ranks, message_ref) + back_ref[...]).astype(BF16)
+def grad_kernel(lay, hots_ref, message_ref, back_ref, out_ref):
+    count = message_ref.shape[0]
+    hots = [hots_ref[:, at : at + count] for at in range(0, hots_ref.shape[1], count)]
+    out_ref[...] = (pick(lay, hots, message_ref) + back_ref[...]).astype(BF16)
 
 
 def call(kernel, out_shape, flops, args, vmem_bytes=VMEM_BYTES):
@@ -454,12 +459,14 @@
     returned, produced_back = lax.optimization_barrier((returned, produced_back))
     returned_back = exchange(returned)
 
-    mixed, router_back, partial_grad = call(
+    hot_columns = experts * GROUP * (lay.full + (lay.cuts if lay.rest else 0))
+    mixed, router_back, partial_grad, hots = call(
         functools.partial(mix_kernel, lay),
         [
             jax.ShapeDtypeStruct((tok_rows, model_width), BF16),
             jax.ShapeDtypeStruct((tok_rows, model_width), F32),
             jax.ShapeDtypeStruct((experts, model_width), F32),
+            jax.ShapeDtypeStruct((tok_rows, hot_columns), BF16),
         ],
         2 * place_flops,
         (ids, slots, gates, produced_back, cotangent, tokens, router),
@@ -470,7 +477,7 @@
         functools.partial(grad_kernel, lay),
         jax.ShapeDtypeStruct((tok_rows, model_width), BF16),
         place_flops,
-        (ids, slots, returned_back, router_back),
+        (hots, returned_back, router_back),
         SMALL_VMEM_BYTES,
     )
     return (mixed, grad_tokens, grad_router.T)

time: 107 us -> 108 us (level)
  no operation moved by 1% of the time
where the time goes in v14:
time: 108 us; the launch traced here: 107 us
  waiting for transfers between devices  41.2 us (38%)
  Pallas kernels  37.4 us (35%)
  starting transfers between devices  26.4 us (24%)
    pallas_call x2, Pallas kernels, expert_call(): pl.pallas_call(functools.partial(kernel, lay), grid=(ff // tile,), in_spe...  29.8 us
    all_to_all x4, waiting for transfers between devices, exchange(): return lax.all_to_all(x, AXES, split_axis=0, concat_axis=0, tiled=True)  29.1 us
    all_to_all x4, starting transfers between devices, exchange(): return lax.all_to_all(x, AXES, split_axis=0, concat_axis=0, tiled=True)  18.2 us
    ppermute x7, waiting for transfers between devices, from_device(): return lax.ppermute(x, AXES, [(d, d ^ bits) for d in range(devices)])  12.1 us
    ppermute x7, starting transfers between devices, from_device(): return lax.ppermute(x, AXES, [(d, d ^ bits) for d in range(devices)])  8.19 us
    pallas_call x3, Pallas kernels, call(): pl.pallas_call(kernel, out_shape=out_shape, compiler_params=pltpu.Compile...  5.4 us
    pallas_call x1, Pallas kernels, on_device(): pl.pallas_call(functools.partial(send_tokens_kernel, lay), out_shape=mess...  2.16 us
  transfers between devices with their start and end apart: 11, of which 10 were waited for; matrix products, arithmetic and copies ran while one was open for 0% of the time, Pallas kernels for 33%

profile of v14, /device:TPU:0, one launch (start us, length us, event | category | flops | bytes accessed | tf_op | source)
XLA Modules:
  0.0 107.5 jit_solution(2468207253117246561)
XLA Ops:
  0.6 2.2 %shard_map.95 = bf16[256,1536]{1,0:T(8,128)(2,1)} custom-call(s32[2,128]{1,0:T(2,128)} %bitcast.17, s32[2,128]{1,0:T(2,128)} %bitcast.20, bf16[128,1024]{1,0:T(8,128)(2,1)} %tokens_ref.3), custom_call_target="tpu_custom_call" | custom-call | flops 134217728 | bytes 1048576 | tf_op jit(solution)/shard_map/pallas_call | solution.py:429
  2.8 7.3 %all-to-all-start = ((bf16[32,8,1536]{2,1,0:T(8,128)(2,1)}), bf16[32,8,1536]{2,1,0:T(8,128)(2,1)S(1)}, u32[]{:S(2)}, u32[]{:S(2)}) async-start(bf16[32,8,1536]{2,1,0:T(8,128)(2,1)} %bitcast.23), calls=%async_computation | async-start | bytes 1572864 | tf_op jit(solution)/shard_map/all_to_all | solution.py:388
  10.1 2.9 %shard_map.94 = (bf16[256,1536]{1,0:T(8,128)(2,1)}, f32[2,128]{1,0:T(2,128)}) custom-call(s32[2,128]{1,0:T(2,128)} %bitcast.18, s32[2,128]{1,0:T(2,128)} %bitcast.21, bf16[128,1024]{1,0:T(8,128)(2,1)} %tokens_ref.3, bf16[32,1024]{1,0:T(8,128)(2,1)} %bitcast.15, bf16[128,1024]{1,0:T(8,128)(2,1)} %cot_ref.3), custom_call_target="tpu_custom_call" | custom-call | flops 268435456 | bytes 1379328 | tf_op jit(solution)/shard_map/pallas_call | solution.py:351
  13.0 17.8 %all-to-all-done = bf16[32,8,1536]{2,1,0:T(8,128)(2,1)S(1)} async-done(((bf16[32,8,1536]{2,1,0:T(8,128)(2,1)}), bf16[32,8,1536]{2,1,0:T(8,128)(2,1)S(1)}, u32[]{:S(2)}, u32[]{:S(2)}) %all-to-all-start) | async-done | bytes 786464 | tf_op jit(solution)/shard_map/all_to_all | solution.py:388
  30.7 0.0 copy-start.6
  30.7 3.6 %all-to-all-start.1 = ((bf16[32,8,1536]{2,1,0:T(8,128)(2,1)}), bf16[32,8,1536]{2,1,0:T(8,128)(2,1)S(1)}, u32[]{:S(2)}, u32[]{:S(2)}) async-start(bf16[32,8,1536]{2,1,0:T(8,128)(2,1)} %bitcast.27), calls=%async_computation.1 | async-start | bytes 1572864 | tf_op jit(solution)/shard_map/all_to_all | solution.py:388
  34.4 0.0 copy-done.6
  34.4 14.7 %shard_map.96 = (bf16[256,1536]{1,0:T(8,128)(2,1)}, bf16[384,4096]{1,0:T(8,128)(2,1)}) custom-call(bf16[256,1536]{1,0:T(8,128)(2,1)} %bitcast.25, bf16[1,1024,4096]{2,1,0:T(8,128)(2,1)} %win_ref.3, bf16[1,4096,1024]{2,1,0:T(8,128)(2,1)} %wout_ref.3), custom_call_target="tpu_custom_call" | custom-call | flops 6442450944 | bytes 21495808 | tf_op jit(solution)/shard_map/pallas_call | solution.py:371
  49.1 5.9 %all-to-all-done.1 = bf16[32,8,1536]{2,1,0:T(8,128)(2,1)S(1)} async-done(((bf16[32,8,1536]{2,1,0:T(8,128)(2,1)}), bf16[32,8,1536]{2,1,0:T(8,128)(2,1)S(1)}, u32[]{:S(2)}, u32[]{:S(2)}) %all-to-all-start.1) | async-done | bytes 786464 | tf_op jit(solution)/shard_map/all_to_all | solution.py:388
  55.0 0.0 copy-start.7
  55.0 0.9 copy-done.7
  55.9 3.6 %all-to-all-start.2 = ((bf16[32,8,1536]{2,1,0:T(8,128)(2,1)}), bf16[32,8,1536]{2,1,0:T(8,128)(2,1)S(1)}, u32[]{:S(2)}, u32[]{:S(2)}) async-start(bf16[32,8,1536]{2,1,0:T(8,128)(2,1)} %bitcast.28), calls=%async_computation.2 | async-start | bytes 1572864 | tf_op jit(solution)/shard_map/all_to_all | solution.py:388
  59.5 0.0 copy-start
  59.5 0.0 copy-start.1
  59.5 0.0 copy-start.2
  59.6 0.0 copy-start.3
  59.6 0.0 copy-start.4
  59.6 0.0 copy-start.5
  59.6 15.1 %shard_map.97 = bf16[256,1536]{1,0:T(8,128)(2,1)} custom-call(bf16[256,1536]{1,0:T(8,128)(2,1)} %bitcast.26, bf16[384,4096]{1,0:T(8,128)(2,1)} %get-tuple-element.21.hidden_ref, bf16[1,1024,4096]{2,1,0:T(8,128)(2,1)} %win_ref.3, bf16[1,4096,1024]{2,1,0:T(8,128)(2,1)} %wout_ref.3), custom_call_target="tpu_custom_call" | custom-call | flops 6442450944 | bytes 21495808 | tf_op jit(solution)/shard_map/pallas_call | solution.py:371
  74.7 5.4 %all-to-all-done.2 = bf16[32,8,1536]{2,1,0:T(8,128)(2,1)S(1)} async-done(((bf16[32,8,1536]{2,1,0:T(8,128)(2,1)}), bf16[32,8,1536]{2,1,0:T(8,128)(2,1)S(1)}, u32[]{:S(2)}, u32[]{:S(2)}) %all-to-all-start.2) | async-done | bytes 786464 | tf_op jit(solution)/shard_map/all_to_all | solution.py:388
  80.1 3.6 %all-to-all-start.3 = ((bf16[32,8,1536]{2,1,0:T(8,128)(2,1)}), bf16[32,8,1536]{2,1,0:T(8,128)(2,1)S(1)}, u32[]{:S(2)}, u32[]{:S(2)}) async-start(bf16[32,8,1536]{2,1,0:T(8,128)(2,1)} %bitcast.24), calls=%async_computation.3 | async-start | bytes 1572864 | tf_op jit(solution)/shard_map/all_to_all | solution.py:388
  83.8 0.0 copy-done
  83.8 0.0 copy-done.1
  83.8 0.0 copy-done.2
  83.8 0.0 copy-done.3
  83.8 0.0 copy-done.4
  83.8 0.0 copy-done.5
  83.8 1.5 %shard_map.98 = (bf16[128,1024]{1,0:T(8,128)(2,1)}, f32[128,1024]{1,0:T(8,128)S(1)}, f32[32,1024]{1,0:T(8,128)S(1)}, bf16[128,768]{1,0:T(8,128)(2,1)S(1)}) custom-call(s32[2,128]{1,0:T(2,128)S(1)} %bitcast.19, s32[2,128]{1,0:T(2,128)S(1)} %bitcast.22, f32[2,128]{1,0:T(2,128)S(1)} %copy-done.5, bf16[256,1536]{1,0:T(8,128)(2,1)S(1)} %bitcast.14, ...), custom_call_target="tpu_custom_call" | custom-call | flops 268435456 | bytes 2493440 | tf_op jit(solution)/shard_map/pallas_call | solution.py:351
  85.4 0.3 collective-permute-start
  85.6 1.0 collective-permute-done
  86.6 1.8 %collective-permute-start.1 = (bf16[16,1024]{1,0:T(8,128)(2,1)S(1)}, bf16[16,1024]{1,0:T(8,128)(2,1)S(1)}, u32[]{:S(2)}, u32[]{:S(2)}) collective-permute-start(bf16[16,1024]{1,0:T(8,128)(2,1)S(1)} %add_convert_fusion.2), channel_id=1, source_target_pairs={{0,2},{1,3},{2,0},{3,1},{4,6},{5,7},{6,4},{7,5},{8,10},{9,11},{10,... | collective-permute-start | bytes 98312 | tf_op jit(solution)/shard_map/ppermute | solution.py:392
  88.5 1.5 %collective-permute-start.2 = (bf16[16,1024]{1,0:T(8,128)(2,1)S(1)}, bf16[16,1024]{1,0:T(8,128)(2,1)S(1)}, u32[]{:S(2)}, u32[]{:S(2)}) collective-permute-start(bf16[16,1024]{1,0:T(8,128)(2,1)S(1)} %add_convert_fusion.2), channel_id=1, source_target_pairs={{0,4},{1,5},{2,6},{3,7},{4,0},{5,1},{6,2},{7,3},{8,12},{9,13},{10,... | collective-permute-start | bytes 98312 | tf_op jit(solution)/shard_map/ppermute | solution.py:392
  89.9 0.3 collective-permute-start.3
  90.2 2.4 %collective-permute-done.1 = bf16[16,1024]{1,0:T(8,128)(2,1)S(1)} collective-permute-done((bf16[16,1024]{1,0:T(8,128)(2,1)S(1)}, bf16[16,1024]{1,0:T(8,128)(2,1)S(1)}, u32[]{:S(2)}, u32[]{:S(2)}) %collective-permute-start.1) | collective-permute-done | bytes 32800 | tf_op jit(solution)/shard_map/ppermute | solution.py:392
  92.6 1.0 collective-permute-done.2
  93.5 2.1 %collective-permute-done.3 = bf16[16,1024]{1,0:T(8,128)(2,1)S(1)} collective-permute-done((bf16[16,1024]{1,0:T(8,128)(2,1)S(1)}, bf16[16,1024]{1,0:T(8,128)(2,1)S(1)}, u32[]{:S(2)}, u32[]{:S(2)}) %collective-permute-start.3) | collective-permute-done | bytes 32800 | tf_op jit(solution)/shard_map/ppermute | solution.py:392
  95.7 1.9 %collective-permute-start.4 = (bf16[16,1024]{1,0:T(8,128)(2,1)S(1)}, bf16[16,1024]{1,0:T(8,128)(2,1)S(1)}, u32[]{:S(2)}, u32[]{:S(2)}) collective-permute-start(bf16[16,1024]{1,0:T(8,128)(2,1)S(1)} %add_convert_fusion.1), channel_id=1, source_target_pairs={{0,8},{1,9},{2,10},{3,11},{4,12},{5,13},{6,14},{7,15},{8,0},{9,1},... | collective-permute-start | bytes 98312 | tf_op jit(solution)/shard_map/ppermute | solution.py:392
  97.6 2.5 %collective-permute-done.4 = bf16[16,1024]{1,0:T(8,128)(2,1)S(1)} collective-permute-done((bf16[16,1024]{1,0:T(8,128)(2,1)S(1)}, bf16[16,1024]{1,0:T(8,128)(2,1)S(1)}, u32[]{:S(2)}, u32[]{:S(2)}) %collective-permute-start.4) | collective-permute-done | bytes 32800 | tf_op jit(solution)/shard_map/ppermute | solution.py:392
  100.0 2.4 %collective-permute-start.5 = (bf16[16,1024]{1,0:T(8,128)(2,1)S(1)}, bf16[16,1024]{1,0:T(8,128)(2,1)S(1)}, u32[]{:S(2)}, u32[]{:S(2)}) collective-permute-start(bf16[16,1024]{1,0:T(8,128)(2,1)S(1)} %add_convert_fusion), channel_id=1, source_target_pairs={{0,16},{1,17},{2,18},{3,19},{4,20},{5,21},{6,22},{7,23},{8,24},{9,... | collective-permute-start | bytes 98312 | tf_op jit(solution)/shard_map/ppermute | solution.py:392
  102.5 3.0 %collective-permute-done.5 = bf16[16,1024]{1,0:T(8,128)(2,1)S(1)} collective-permute-done((bf16[16,1024]{1,0:T(8,128)(2,1)S(1)}, bf16[16,1024]{1,0:T(8,128)(2,1)S(1)}, u32[]{:S(2)}, u32[]{:S(2)}) %collective-permute-start.5) | collective-permute-done | bytes 32800 | tf_op jit(solution)/shard_map/ppermute | solution.py:392
  105.5 0.0 all-to-all-done.3
  105.5 0.1 collective-permute-start.6
  105.5 1.0 shard_map.99
  106.6 0.2 collective-permute-done.6
  106.8 0.7 maximum_bitcast_fusion
  (6 shorter events, 0.1 us)
Async XLA Ops:
  2.8 27.9 %all-to-all-start = ((bf16[32,8,1536]{2,1,0:T(8,128)(2,1)}), bf16[32,8,1536]{2,1,0:T(8,128)(2,1)S(1)}, u32[]{:S(2)}, u32[]{:S(2)}) async-start(bf16[32,8,1536]{2,1,0:T(8,128)(2,1)} %bitcast.23), calls=%async_computation | async-start | bytes 1572864 | tf_op jit(solution)/shard_map/all_to_all | solution.py:388
  30.7 3.6 %copy-start.6 = (bf16[32,8,1536]{2,1,0:T(8,128)(2,1)}, bf16[32,8,1536]{2,1,0:T(8,128)(2,1)S(1)}, u32[]{:S(2)}) copy-start(bf16[32,8,1536]{2,1,0:T(8,128)(2,1)S(1)} %all-to-all-done) | copy-start | bytes 2359300
  30.7 24.2 %all-to-all-start.1 = ((bf16[32,8,1536]{2,1,0:T(8,128)(2,1)}), bf16[32,8,1536]{2,1,0:T(8,128)(2,1)S(1)}, u32[]{:S(2)}, u32[]{:S(2)}) async-start(bf16[32,8,1536]{2,1,0:T(8,128)(2,1)} %bitcast.27), calls=%async_computation.1 | async-start | bytes 1572864 | tf_op jit(solution)/shard_map/all_to_all | solution.py:388
  55.0 0.9 copy-start.7
  55.9 24.2 %all-to-all-start.2 = ((bf16[32,8,1536]{2,1,0:T(8,128)(2,1)}), bf16[32,8,1536]{2,1,0:T(8,128)(2,1)S(1)}, u32[]{:S(2)}, u32[]{:S(2)}) async-start(bf16[32,8,1536]{2,1,0:T(8,128)(2,1)} %bitcast.28), calls=%async_computation.2 | async-start | bytes 1572864 | tf_op jit(solution)/shard_map/all_to_all | solution.py:388
  59.5 24.3 %copy-start = (bf16[128,1024]{1,0:T(8,128)(2,1)S(1)}, bf16[128,1024]{1,0:T(8,128)(2,1)}, u32[]{:S(2)}) copy-start(bf16[128,1024]{1,0:T(8,128)(2,1)} %tokens_ref.3) | copy-start | bytes 786436
  59.5 24.3 %copy-start.1 = (bf16[128,1024]{1,0:T(8,128)(2,1)S(1)}, bf16[128,1024]{1,0:T(8,128)(2,1)}, u32[]{:S(2)}) copy-start(bf16[128,1024]{1,0:T(8,128)(2,1)} %cot_ref.3) | copy-start | bytes 786436
  59.5 24.3 %copy-start.2 = (bf16[1024,32]{0,1:T(8,128)(2,1)S(1)}, bf16[1024,32]{0,1:T(8,128)(2,1)}, u32[]{:S(2)}) copy-start(bf16[1024,32]{0,1:T(8,128)(2,1)} %param.8) | copy-start | bytes 196612
  59.6 24.3 %copy-start.3 = (s32[128,2]{0,1:T(2,128)S(1)}, s32[128,2]{0,1:T(2,128)}, u32[]{:S(2)}) copy-start(s32[128,2]{0,1:T(2,128)} %param.11) | copy-start | bytes 3076
  59.6 24.3 %copy-start.4 = (s32[128,2]{0,1:T(2,128)S(1)}, s32[128,2]{0,1:T(2,128)}, u32[]{:S(2)}) copy-start(s32[128,2]{0,1:T(2,128)} %param.12) | copy-start | bytes 3076
  59.6 24.3 %copy-start.5 = (f32[2,128]{1,0:T(2,128)S(1)}, f32[2,128]{1,0:T(2,128)}, u32[]{:S(2)}) copy-start(f32[2,128]{1,0:T(2,128)} %get-tuple-element.17.gates_ref) | copy-start | bytes 3076
  80.1 25.3 %all-to-all-start.3 = ((bf16[32,8,1536]{2,1,0:T(8,128)(2,1)}), bf16[32,8,1536]{2,1,0:T(8,128)(2,1)S(1)}, u32[]{:S(2)}, u32[]{:S(2)}) async-start(bf16[32,8,1536]{2,1,0:T(8,128)(2,1)} %bitcast.24), calls=%async_computation.3 | async-start | bytes 1572864 | tf_op jit(solution)/shard_map/all_to_all | solution.py:388
  85.4 1.3 %collective-permute-start = (f32[16,1024]{1,0:T(8,128)S(1)}, f32[16,1024]{1,0:T(8,128)S(1)}, u32[]{:S(2)}, u32[]{:S(2)}) collective-permute-start(f32[16,1024]{1,0:T(8,128)S(1)} %constant_dynamic-slice_fusion), channel_id=1, source_target_pairs={{0,1},{1,0},{2,3},{3,2},{4,5},{5,4},{6,7},{7,6},{8,9},{9,8},{10,11... | collective-permute-start | bytes 196616 | tf_op jit(solution)/shard_map/ppermute | solution.py:392
  86.6 5.9 %collective-permute-start.1 = (bf16[16,1024]{1,0:T(8,128)(2,1)S(1)}, bf16[16,1024]{1,0:T(8,128)(2,1)S(1)}, u32[]{:S(2)}, u32[]{:S(2)}) collective-permute-start(bf16[16,1024]{1,0:T(8,128)(2,1)S(1)} %add_convert_fusion.2), channel_id=1, source_target_pairs={{0,2},{1,3},{2,0},{3,1},{4,6},{5,7},{6,4},{7,5},{8,10},{9,11},{10,... | collective-permute-start | bytes 98312 | tf_op jit(solution)/shard_map/ppermute | solution.py:392
  88.5 5.1 %collective-permute-start.2 = (bf16[16,1024]{1,0:T(8,128)(2,1)S(1)}, bf16[16,1024]{1,0:T(8,128)(2,1)S(1)}, u32[]{:S(2)}, u32[]{:S(2)}) collective-permute-start(bf16[16,1024]{1,0:T(8,128)(2,1)S(1)} %add_convert_fusion.2), channel_id=1, source_target_pairs={{0,4},{1,5},{2,6},{3,7},{4,0},{5,1},{6,2},{7,3},{8,12},{9,13},{10,... | collective-permute-start | bytes 98312 | tf_op jit(solution)/shard_map/ppermute | solution.py:392
  89.9 5.7 %collective-permute-start.3 = (bf16[16,1024]{1,0:T(8,128)(2,1)S(1)}, bf16[16,1024]{1,0:T(8,128)(2,1)S(1)}, u32[]{:S(2)}, u32[]{:S(2)}) collective-permute-start(bf16[16,1024]{1,0:T(8,128)(2,1)S(1)} %add_convert_fusion.2), channel_id=1, source_target_pairs={{0,6},{1,7},{2,4},{3,5},{4,2},{5,3},{6,0},{7,1},{8,14},{9,15},{10,... | collective-permute-start | bytes 98312 | tf_op jit(solution)/shard_map/ppermute | solution.py:392
  95.7 4.4 %collective-permute-start.4 = (bf16[16,1024]{1,0:T(8,128)(2,1)S(1)}, bf16[16,1024]{1,0:T(8,128)(2,1)S(1)}, u32[]{:S(2)}, u32[]{:S(2)}) collective-permute-start(bf16[16,1024]{1,0:T(8,128)(2,1)S(1)} %add_convert_fusion.1), channel_id=1, source_target_pairs={{0,8},{1,9},{2,10},{3,11},{4,12},{5,13},{6,14},{7,15},{8,0},{9,1},... | collective-permute-start | bytes 98312 | tf_op jit(solution)/shard_map/ppermute | solution.py:392
  100.0 5.4 %collective-permute-start.5 = (bf16[16,1024]{1,0:T(8,128)(2,1)S(1)}, bf16[16,1024]{1,0:T(8,128)(2,1)S(1)}, u32[]{:S(2)}, u32[]{:S(2)}) collective-permute-start(bf16[16,1024]{1,0:T(8,128)(2,1)S(1)} %add_convert_fusion), channel_id=1, source_target_pairs={{0,16},{1,17},{2,18},{3,19},{4,20},{5,21},{6,22},{7,23},{8,24},{9,... | collective-permute-start | bytes 98312 | tf_op jit(solution)/shard_map/ppermute | solution.py:392
  105.5 1.3 %collective-permute-start.6 = (f32[16,1024]{1,0:T(8,128)S(1)}, f32[16,1024]{1,0:T(8,128)S(1)}, u32[]{:S(2)}, u32[]{:S(2)}) collective-permute-start(f32[16,1024]{1,0:T(8,128)S(1)} %convert_add_fusion), channel_id=1, source_target_pairs={{0,1},{1,0},{2,3},{3,2},{4,5},{5,4},{6,7},{7,6},{8,9},{9,8},{10,11... | collective-permute-start | bytes 196616 | tf_op jit(solution)/shard_map/ppermute | solution.py:392

commit v15 on v12

--- a/solution.py
+++ b/solution.py
@@ -385,11 +385,12 @@
 
 
 def rank_of(device, devices):
-    return (device - devices // 4) & (devices - 1)
+    half = devices // 2
+    return (device & (half - 1)) * 2 + jnp.where(device >= half, 1, 0)
 
 
 def exchange(x, devices):
-    order = [(rank + devices // 4) % devices for rank in range(devices)]
+    order = [rank // 2 + rank % 2 * (devices // 2) for rank in range(devices)]
     return lax.all_to_all(
         x, AXES, split_axis=0, concat_axis=0, tiled=True, axis_index_groups=[order]
     )

time: 107 us -> 108 us (level)
  starting transfers between devices: 26.4 us -> 27.6 us
  transfers between devices with their start and end apart: 11 -> 11, of which waited for: 10 -> 7; matrix products, arithmetic and copies ran while one was open for 0% -> 0% of each run, Pallas kernels for 33% -> 33%
where the time goes in v15:
time: 108 us; the launch traced here: 107 us
  waiting for transfers between devices  40.7 us (38%)
  Pallas kernels  37.5 us (35%)
  starting transfers between devices  27.6 us (26%)
    pallas_call x2, Pallas kernels, expert_call(): pl.pallas_call(functools.partial(kernel, lay), grid=(ff // tile,), in_spe...  29.9 us
    all_to_all x4, waiting for transfers between devices, exchange(): lax.all_to_all(x, AXES, split_axis=0, concat_axis=0, tiled=True, axis_ind...  28.7 us
    all_to_all x4, starting transfers between devices, exchange(): lax.all_to_all(x, AXES, split_axis=0, concat_axis=0, tiled=True, axis_ind...  18.3 us
    ppermute x7, waiting for transfers between devices, from_device(): return lax.ppermute(x, AXES, [(d, d ^ bits) for d in range(devices)])  12 us
    ppermute x7, starting transfers between devices, from_device(): return lax.ppermute(x, AXES, [(d, d ^ bits) for d in range(devices)])  9.29 us
    pallas_call x3, Pallas kernels, call(): pl.pallas_call(kernel, out_shape=out_shape, compiler_params=pltpu.Compile...  5.47 us
    pallas_call x1, Pallas kernels, on_device(): pl.pallas_call(functools.partial(send_tokens_kernel, lay), out_shape=mess...  2.17 us
  transfers between devices with their start and end apart: 11, of which 7 were waited for; matrix products, arithmetic and copies ran while one was open for 0% of the time, Pallas kernels for 33%

profile of v15, /device:TPU:0, one launch (start us, length us, event | category | flops | bytes accessed | tf_op | source)
XLA Modules:
  0.0 107.4 jit_solution(9228647615863517630)
XLA Ops:
  0.6 2.2 %shard_map.95 = bf16[256,1536]{1,0:T(8,128)(2,1)} custom-call(s32[2,128]{1,0:T(2,128)} %bitcast.17, s32[2,128]{1,0:T(2,128)} %bitcast.21, bf16[128,1024]{1,0:T(8,128)(2,1)} %tokens_ref.3), custom_call_target="tpu_custom_call" | custom-call | flops 134217728 | bytes 1048576 | tf_op jit(solution)/shard_map/pallas_call | solution.py:437
  2.8 7.3 %all-to-all-start = ((bf16[32,8,1536]{2,1,0:T(8,128)(2,1)}), bf16[32,8,1536]{2,1,0:T(8,128)(2,1)S(1)}, u32[]{:S(2)}, u32[]{:S(2)}) async-start(bf16[32,8,1536]{2,1,0:T(8,128)(2,1)} %bitcast.25), calls=%async_computation | async-start | bytes 1572864 | tf_op jit(solution)/shard_map/all_to_all | solution.py:394
  10.1 2.9 %shard_map.94 = (bf16[256,1536]{1,0:T(8,128)(2,1)}, f32[2,128]{1,0:T(2,128)}) custom-call(s32[2,128]{1,0:T(2,128)} %bitcast.18, s32[2,128]{1,0:T(2,128)} %bitcast.22, bf16[128,1024]{1,0:T(8,128)(2,1)} %tokens_ref.3, bf16[32,1024]{1,0:T(8,128)(2,1)} %bitcast.15, bf16[128,1024]{1,0:T(8,128)(2,1)} %cot_ref.3), custom_call_target="tpu_custom_call" | custom-call | flops 268435456 | bytes 1379328 | tf_op jit(solution)/shard_map/pallas_call | solution.py:351
  13.0 17.6 %all-to-all-done = bf16[32,8,1536]{2,1,0:T(8,128)(2,1)S(1)} async-done(((bf16[32,8,1536]{2,1,0:T(8,128)(2,1)}), bf16[32,8,1536]{2,1,0:T(8,128)(2,1)S(1)}, u32[]{:S(2)}, u32[]{:S(2)}) %all-to-all-start) | async-done | bytes 786464 | tf_op jit(solution)/shard_map/all_to_all | solution.py:394
  30.6 0.0 copy-start.6
  30.6 3.7 %all-to-all-start.1 = ((bf16[32,8,1536]{2,1,0:T(8,128)(2,1)}), bf16[32,8,1536]{2,1,0:T(8,128)(2,1)S(1)}, u32[]{:S(2)}, u32[]{:S(2)}) async-start(bf16[32,8,1536]{2,1,0:T(8,128)(2,1)} %bitcast.29), calls=%async_computation.1 | async-start | bytes 1572864 | tf_op jit(solution)/shard_map/all_to_all | solution.py:394
  34.3 0.0 copy-done.6
  34.3 14.7 %shard_map.96 = (bf16[256,1536]{1,0:T(8,128)(2,1)}, bf16[384,4096]{1,0:T(8,128)(2,1)}) custom-call(bf16[256,1536]{1,0:T(8,128)(2,1)} %bitcast.27, bf16[1,1024,4096]{2,1,0:T(8,128)(2,1)} %win_ref.3, bf16[1,4096,1024]{2,1,0:T(8,128)(2,1)} %wout_ref.3), custom_call_target="tpu_custom_call" | custom-call | flops 6442450944 | bytes 21495808 | tf_op jit(solution)/shard_map/pallas_call | solution.py:371
  49.0 5.8 %all-to-all-done.1 = bf16[32,8,1536]{2,1,0:T(8,128)(2,1)S(1)} async-done(((bf16[32,8,1536]{2,1,0:T(8,128)(2,1)}), bf16[32,8,1536]{2,1,0:T(8,128)(2,1)S(1)}, u32[]{:S(2)}, u32[]{:S(2)}) %all-to-all-start.1) | async-done | bytes 786464 | tf_op jit(solution)/shard_map/all_to_all | solution.py:394
  54.8 0.0 copy-start.7
  54.8 3.7 %all-to-all-start.2 = ((bf16[32,8,1536]{2,1,0:T(8,128)(2,1)}), bf16[32,8,1536]{2,1,0:T(8,128)(2,1)S(1)}, u32[]{:S(2)}, u32[]{:S(2)}) async-start(bf16[32,8,1536]{2,1,0:T(8,128)(2,1)} %bitcast.30), calls=%async_computation.2 | async-start | bytes 1572864 | tf_op jit(solution)/shard_map/all_to_all | solution.py:394
  58.5 0.0 copy-done.7
  58.5 0.0 copy-start
  58.5 0.0 copy-start.1
  58.5 0.0 copy-start.2
  58.6 0.0 copy-start.3
  58.6 0.0 copy-start.4
  58.6 0.0 copy-start.5
  58.6 15.1 %shard_map.97 = bf16[256,1536]{1,0:T(8,128)(2,1)} custom-call(bf16[256,1536]{1,0:T(8,128)(2,1)} %bitcast.28, bf16[384,4096]{1,0:T(8,128)(2,1)} %get-tuple-element.20.hidden_ref, bf16[1,1024,4096]{2,1,0:T(8,128)(2,1)} %win_ref.3, bf16[1,4096,1024]{2,1,0:T(8,128)(2,1)} %wout_ref.3), custom_call_target="tpu_custom_call" | custom-call | flops 6442450944 | bytes 21495808 | tf_op jit(solution)/shard_map/pallas_call | solution.py:371
  73.7 5.3 %all-to-all-done.2 = bf16[32,8,1536]{2,1,0:T(8,128)(2,1)S(1)} async-done(((bf16[32,8,1536]{2,1,0:T(8,128)(2,1)}), bf16[32,8,1536]{2,1,0:T(8,128)(2,1)S(1)}, u32[]{:S(2)}, u32[]{:S(2)}) %all-to-all-start.2) | async-done | bytes 786464 | tf_op jit(solution)/shard_map/all_to_all | solution.py:394
  79.0 3.7 %all-to-all-start.3 = ((bf16[32,8,1536]{2,1,0:T(8,128)(2,1)}), bf16[32,8,1536]{2,1,0:T(8,128)(2,1)S(1)}, u32[]{:S(2)}, u32[]{:S(2)}) async-start(bf16[32,8,1536]{2,1,0:T(8,128)(2,1)} %bitcast.26), calls=%async_computation.3 | async-start | bytes 1572864 | tf_op jit(solution)/shard_map/all_to_all | solution.py:394
  82.7 0.0 copy-done
  82.7 0.0 copy-done.1
  82.7 0.0 copy-done.2
  82.7 0.0 copy-done.3
  82.8 0.0 copy-done.4
  82.8 0.0 copy-done.5
  82.8 1.5 %shard_map.98 = (bf16[128,1024]{1,0:T(8,128)(2,1)}, f32[128,1024]{1,0:T(8,128)S(1)}, f32[32,1024]{1,0:T(8,128)S(1)}) custom-call(s32[2,128]{1,0:T(2,128)S(1)} %bitcast.19, s32[2,128]{1,0:T(2,128)S(1)} %bitcast.23, f32[2,128]{1,0:T(2,128)S(1)} %copy-done.5, bf16[256,1536]{1,0:T(8,128)(2,1)S(1)} %bitcast.14, bf16[128,1024]{1,0:T(8,128)(2,1)S(1)} %copy-done.1, ...), custom_call_target="tpu_custom_call" | custom-call | flops 268435456 | bytes 2296832 | tf_op jit(solution)/shard_map/pallas_call | solution.py:351
  84.3 0.3 collective-permute-start
  84.5 1.0 collective-permute-done
  85.5 1.8 %collective-permute-start.1 = (bf16[16,1024]{1,0:T(8,128)(2,1)S(1)}, bf16[16,1024]{1,0:T(8,128)(2,1)S(1)}, u32[]{:S(2)}, u32[]{:S(2)}) collective-permute-start(bf16[16,1024]{1,0:T(8,128)(2,1)S(1)} %add_convert_fusion.2), channel_id=1, source_target_pairs={{0,2},{1,3},{2,0},{3,1},{4,6},{5,7},{6,4},{7,5},{8,10},{9,11},{10,... | collective-permute-start | bytes 98312 | tf_op jit(solution)/shard_map/ppermute | solution.py:400
  87.4 1.5 %collective-permute-start.2 = (bf16[16,1024]{1,0:T(8,128)(2,1)S(1)}, bf16[16,1024]{1,0:T(8,128)(2,1)S(1)}, u32[]{:S(2)}, u32[]{:S(2)}) collective-permute-start(bf16[16,1024]{1,0:T(8,128)(2,1)S(1)} %add_convert_fusion.2), channel_id=1, source_target_pairs={{0,4},{1,5},{2,6},{3,7},{4,0},{5,1},{6,2},{7,3},{8,12},{9,13},{10,... | collective-permute-start | bytes 98312 | tf_op jit(solution)/shard_map/ppermute | solution.py:400
  88.8 0.3 collective-permute-start.3
  89.1 5.3 %collective-permute-done.1 = bf16[16,1024]{1,0:T(8,128)(2,1)S(1)} collective-permute-done((bf16[16,1024]{1,0:T(8,128)(2,1)S(1)}, bf16[16,1024]{1,0:T(8,128)(2,1)S(1)}, u32[]{:S(2)}, u32[]{:S(2)}) %collective-permute-start.1) | collective-permute-done | bytes 32800 | tf_op jit(solution)/shard_map/ppermute | solution.py:400
  94.4 0.0 collective-permute-done.2
  94.4 0.0 collective-permute-done.3
  94.4 1.9 %collective-permute-start.4 = (bf16[16,1024]{1,0:T(8,128)(2,1)S(1)}, bf16[16,1024]{1,0:T(8,128)(2,1)S(1)}, u32[]{:S(2)}, u32[]{:S(2)}) collective-permute-start(bf16[16,1024]{1,0:T(8,128)(2,1)S(1)} %add_convert_fusion.1), channel_id=1, source_target_pairs={{0,8},{1,9},{2,10},{3,11},{4,12},{5,13},{6,14},{7,15},{8,0},{9,1},... | collective-permute-start | bytes 98312 | tf_op jit(solution)/shard_map/ppermute | solution.py:400
  96.2 2.4 %collective-permute-done.4 = bf16[16,1024]{1,0:T(8,128)(2,1)S(1)} collective-permute-done((bf16[16,1024]{1,0:T(8,128)(2,1)S(1)}, bf16[16,1024]{1,0:T(8,128)(2,1)S(1)}, u32[]{:S(2)}, u32[]{:S(2)}) %collective-permute-start.4) | collective-permute-done | bytes 32800 | tf_op jit(solution)/shard_map/ppermute | solution.py:400
  98.6 2.8 %collective-permute-start.5 = (bf16[16,1024]{1,0:T(8,128)(2,1)S(1)}, bf16[16,1024]{1,0:T(8,128)(2,1)S(1)}, u32[]{:S(2)}, u32[]{:S(2)}) collective-permute-start(bf16[16,1024]{1,0:T(8,128)(2,1)S(1)} %add_convert_fusion), channel_id=1, source_target_pairs={{0,16},{1,17},{2,18},{3,19},{4,20},{5,21},{6,22},{7,23},{8,24},{9,... | collective-permute-start | bytes 98312 | tf_op jit(solution)/shard_map/ppermute | solution.py:400
  101.4 3.3 %collective-permute-done.5 = bf16[16,1024]{1,0:T(8,128)(2,1)S(1)} collective-permute-done((bf16[16,1024]{1,0:T(8,128)(2,1)S(1)}, bf16[16,1024]{1,0:T(8,128)(2,1)S(1)}, u32[]{:S(2)}, u32[]{:S(2)}) %collective-permute-start.5) | collective-permute-done | bytes 32800 | tf_op jit(solution)/shard_map/ppermute | solution.py:400
  104.7 0.0 all-to-all-done.3
  104.8 0.9 collective-permute-start.6
  105.6 1.1 %shard_map.99 = bf16[128,1024]{1,0:T(8,128)(2,1)} custom-call(s32[2,128]{1,0:T(2,128)S(1)} %bitcast.20, s32[2,128]{1,0:T(2,128)S(1)} %bitcast.24, bf16[256,1536]{1,0:T(8,128)(2,1)S(1)} %bitcast.13, f32[128,1024]{1,0:T(8,128)S(1)} %get-tuple-element.27.back_ref), custom_call_target="tpu_custom_call" | custom-call | flops 134217728 | bytes 1574912 | tf_op jit(solution)/shard_map/pallas_call | solution.py:351
  106.7 0.0 collective-permute-done.6
  106.8 0.7 maximum_bitcast_fusion
  (6 shorter events, 0.1 us)
Async XLA Ops:
  2.8 27.8 %all-to-all-start = ((bf16[32,8,1536]{2,1,0:T(8,128)(2,1)}), bf16[32,8,1536]{2,1,0:T(8,128)(2,1)S(1)}, u32[]{:S(2)}, u32[]{:S(2)}) async-start(bf16[32,8,1536]{2,1,0:T(8,128)(2,1)} %bitcast.25), calls=%async_computation | async-start | bytes 1572864 | tf_op jit(solution)/shard_map/all_to_all | solution.py:394
  30.6 3.7 %copy-start.6 = (bf16[32,8,1536]{2,1,0:T(8,128)(2,1)}, bf16[32,8,1536]{2,1,0:T(8,128)(2,1)S(1)}, u32[]{:S(2)}) copy-start(bf16[32,8,1536]{2,1,0:T(8,128)(2,1)S(1)} %all-to-all-done) | copy-start | bytes 2359300
  30.6 24.2 %all-to-all-start.1 = ((bf16[32,8,1536]{2,1,0:T(8,128)(2,1)}), bf16[32,8,1536]{2,1,0:T(8,128)(2,1)S(1)}, u32[]{:S(2)}, u32[]{:S(2)}) async-start(bf16[32,8,1536]{2,1,0:T(8,128)(2,1)} %bitcast.29), calls=%async_computation.1 | async-start | bytes 1572864 | tf_op jit(solution)/shard_map/all_to_all | solution.py:394
  54.8 3.7 %copy-start.7 = (bf16[32,8,1536]{2,1,0:T(8,128)(2,1)}, bf16[32,8,1536]{2,1,0:T(8,128)(2,1)S(1)}, u32[]{:S(2)}) copy-start(bf16[32,8,1536]{2,1,0:T(8,128)(2,1)S(1)} %all-to-all-done.1) | copy-start | bytes 2359300
  54.8 24.2 %all-to-all-start.2 = ((bf16[32,8,1536]{2,1,0:T(8,128)(2,1)}), bf16[32,8,1536]{2,1,0:T(8,128)(2,1)S(1)}, u32[]{:S(2)}, u32[]{:S(2)}) async-start(bf16[32,8,1536]{2,1,0:T(8,128)(2,1)} %bitcast.30), calls=%async_computation.2 | async-start | bytes 1572864 | tf_op jit(solution)/shard_map/all_to_all | solution.py:394
  58.5 24.2 %copy-start = (bf16[128,1024]{1,0:T(8,128)(2,1)S(1)}, bf16[128,1024]{1,0:T(8,128)(2,1)}, u32[]{:S(2)}) copy-start(bf16[128,1024]{1,0:T(8,128)(2,1)} %tokens_ref.3) | copy-start | bytes 786436
  58.5 24.2 %copy-start.1 = (bf16[128,1024]{1,0:T(8,128)(2,1)S(1)}, bf16[128,1024]{1,0:T(8,128)(2,1)}, u32[]{:S(2)}) copy-start(bf16[128,1024]{1,0:T(8,128)(2,1)} %cot_ref.3) | copy-start | bytes 786436
  58.5 24.2 %copy-start.2 = (bf16[1024,32]{0,1:T(8,128)(2,1)S(1)}, bf16[1024,32]{0,1:T(8,128)(2,1)}, u32[]{:S(2)}) copy-start(bf16[1024,32]{0,1:T(8,128)(2,1)} %param.8) | copy-start | bytes 196612
  58.6 24.2 %copy-start.3 = (s32[128,2]{0,1:T(2,128)S(1)}, s32[128,2]{0,1:T(2,128)}, u32[]{:S(2)}) copy-start(s32[128,2]{0,1:T(2,128)} %param.11) | copy-start | bytes 3076
  58.6 24.2 %copy-start.4 = (s32[128,2]{0,1:T(2,128)S(1)}, s32[128,2]{0,1:T(2,128)}, u32[]{:S(2)}) copy-start(s32[128,2]{0,1:T(2,128)} %param.12) | copy-start | bytes 3076
  58.6 24.2 %copy-start.5 = (f32[2,128]{1,0:T(2,128)S(1)}, f32[2,128]{1,0:T(2,128)}, u32[]{:S(2)}) copy-start(f32[2,128]{1,0:T(2,128)} %get-tuple-element.16.gates_ref) | copy-start | bytes 3076
  79.0 25.7 %all-to-all-start.3 = ((bf16[32,8,1536]{2,1,0:T(8,128)(2,1)}), bf16[32,8,1536]{2,1,0:T(8,128)(2,1)S(1)}, u32[]{:S(2)}, u32[]{:S(2)}) async-start(bf16[32,8,1536]{2,1,0:T(8,128)(2,1)} %bitcast.26), calls=%async_computation.3 | async-start | bytes 1572864 | tf_op jit(solution)/shard_map/all_to_all | solution.py:394
  84.3 1.3 %collective-permute-start = (f32[16,1024]{1,0:T(8,128)S(1)}, f32[16,1024]{1,0:T(8,128)S(1)}, u32[]{:S(2)}, u32[]{:S(2)}) collective-permute-start(f32[16,1024]{1,0:T(8,128)S(1)} %constant_dynamic-slice_fusion), channel_id=1, source_target_pairs={{0,1},{1,0},{2,3},{3,2},{4,5},{5,4},{6,7},{7,6},{8,9},{9,8},{10,11... | collective-permute-start | bytes 196616 | tf_op jit(solution)/shard_map/ppermute | solution.py:400
  85.5 8.8 %collective-permute-start.1 = (bf16[16,1024]{1,0:T(8,128)(2,1)S(1)}, bf16[16,1024]{1,0:T(8,128)(2,1)S(1)}, u32[]{:S(2)}, u32[]{:S(2)}) collective-permute-start(bf16[16,1024]{1,0:T(8,128)(2,1)S(1)} %add_convert_fusion.2), channel_id=1, source_target_pairs={{0,2},{1,3},{2,0},{3,1},{4,6},{5,7},{6,4},{7,5},{8,10},{9,11},{10,... | collective-permute-start | bytes 98312 | tf_op jit(solution)/shard_map/ppermute | solution.py:400
  87.4 7.0 %collective-permute-start.2 = (bf16[16,1024]{1,0:T(8,128)(2,1)S(1)}, bf16[16,1024]{1,0:T(8,128)(2,1)S(1)}, u32[]{:S(2)}, u32[]{:S(2)}) collective-permute-start(bf16[16,1024]{1,0:T(8,128)(2,1)S(1)} %add_convert_fusion.2), channel_id=1, source_target_pairs={{0,4},{1,5},{2,6},{3,7},{4,0},{5,1},{6,2},{7,3},{8,12},{9,13},{10,... | collective-permute-start | bytes 98312 | tf_op jit(solution)/shard_map/ppermute | solution.py:400
  88.8 5.5 %collective-permute-start.3 = (bf16[16,1024]{1,0:T(8,128)(2,1)S(1)}, bf16[16,1024]{1,0:T(8,128)(2,1)S(1)}, u32[]{:S(2)}, u32[]{:S(2)}) collective-permute-start(bf16[16,1024]{1,0:T(8,128)(2,1)S(1)} %add_convert_fusion.2), channel_id=1, source_target_pairs={{0,6},{1,7},{2,4},{3,5},{4,2},{5,3},{6,0},{7,1},{8,14},{9,15},{10,... | collective-permute-start | bytes 98312 | tf_op jit(solution)/shard_map/ppermute | solution.py:400
  94.4 4.2 %collective-permute-start.4 = (bf16[16,1024]{1,0:T(8,128)(2,1)S(1)}, bf16[16,1024]{1,0:T(8,128)(2,1)S(1)}, u32[]{:S(2)}, u32[]{:S(2)}) collective-permute-start(bf16[16,1024]{1,0:T(8,128)(2,1)S(1)} %add_convert_fusion.1), channel_id=1, source_target_pairs={{0,8},{1,9},{2,10},{3,11},{4,12},{5,13},{6,14},{7,15},{8,0},{9,1},... | collective-permute-start | bytes 98312 | tf_op jit(solution)/shard_map/ppermute | solution.py:400
  98.6 6.1 %collective-permute-start.5 = (bf16[16,1024]{1,0:T(8,128)(2,1)S(1)}, bf16[16,1024]{1,0:T(8,128)(2,1)S(1)}, u32[]{:S(2)}, u32[]{:S(2)}) collective-permute-start(bf16[16,1024]{1,0:T(8,128)(2,1)S(1)} %add_convert_fusion), channel_id=1, source_target_pairs={{0,16},{1,17},{2,18},{3,19},{4,20},{5,21},{6,22},{7,23},{8,24},{9,... | collective-permute-start | bytes 98312 | tf_op jit(solution)/shard_map/ppermute | solution.py:400
  104.8 2.0 %collective-permute-start.6 = (f32[16,1024]{1,0:T(8,128)S(1)}, f32[16,1024]{1,0:T(8,128)S(1)}, u32[]{:S(2)}, u32[]{:S(2)}) collective-permute-start(f32[16,1024]{1,0:T(8,128)S(1)} %convert_add_fusion), channel_id=1, source_target_pairs={{0,1},{1,0},{2,3},{3,2},{4,5},{5,4},{6,7},{7,6},{8,9},{9,8},{10,11... | collective-permute-start | bytes 196616 | tf_op jit(solution)/shard_map/ppermute | solution.py:400

commit v16 on v10

--- a/solution.py
+++ b/solution.py
@@ -407,8 +407,8 @@
         bit *= 2
     beside, own = lax.optimization_barrier((beside, own))
     other = from_device(own, 1, devices)
-    first = core == 0
-    total = jnp.concatenate([jnp.where(first, own, other), jnp.where(first, other, own)], axis=0)
+    mine = lax.broadcasted_iota(jnp.int32, (2, 1, 1), 0) == core
+    total = jnp.where(mine, own[None], other[None]).reshape(x.shape)
     return total, beside
 
 

time: 107 us -> 108 us (level)
  transfers between devices with their start and end apart: 11 -> 11, of which waited for: 10 -> 9; matrix products, arithmetic and copies ran while one was open for 0% -> 0% of each run, Pallas kernels for 33% -> 33%
where the time goes in v16:
time: 108 us; the launch traced here: 107 us
  waiting for transfers between devices  40.9 us (38%)
  Pallas kernels  37.5 us (35%)
  starting transfers between devices  26.4 us (24%)
    pallas_call x2, Pallas kernels, expert_call(): pl.pallas_call(functools.partial(kernel, lay), grid=(ff // tile,), in_spe...  29.9 us
    all_to_all x4, waiting for transfers between devices, exchange(): return lax.all_to_all(x, AXES, split_axis=0, concat_axis=0, tiled=True)  29 us
    all_to_all x4, starting transfers between devices, exchange(): return lax.all_to_all(x, AXES, split_axis=0, concat_axis=0, tiled=True)  18.2 us
    ppermute x7, waiting for transfers between devices, from_device(): return lax.ppermute(x, AXES, [(d, d ^ bits) for d in range(devices)])  11.9 us
    ppermute x7, starting transfers between devices, from_device(): return lax.ppermute(x, AXES, [(d, d ^ bits) for d in range(devices)])  8.22 us
    pallas_call x3, Pallas kernels, call(): pl.pallas_call(kernel, out_shape=out_shape, compiler_params=pltpu.Compile...  5.43 us
  transfers between devices with their start and end apart: 11, of which 9 were waited for; matrix products, arithmetic and copies ran while one was open for 0% of the time, Pallas kernels for 33%

profile of v16, /device:TPU:0, one launch (start us, length us, event | category | flops | bytes accessed | tf_op | source)
XLA Modules:
  0.0 106.6 jit_solution(10083424473114733604)
XLA Ops:
  0.6 2.1 %shard_map.95 = bf16[256,1536]{1,0:T(8,128)(2,1)} custom-call(s32[2,128]{1,0:T(2,128)} %bitcast.20, s32[2,128]{1,0:T(2,128)} %bitcast.24, bf16[128,1024]{1,0:T(8,128)(2,1)} %tokens_ref.3), custom_call_target="tpu_custom_call" | custom-call | flops 134217728 | bytes 1048576 | tf_op jit(solution)/shard_map/pallas_call | solution.py:424
  2.8 7.3 %all-to-all-start = ((bf16[32,8,1536]{2,1,0:T(8,128)(2,1)}), bf16[32,8,1536]{2,1,0:T(8,128)(2,1)S(1)}, u32[]{:S(2)}, u32[]{:S(2)}) async-start(bf16[32,8,1536]{2,1,0:T(8,128)(2,1)} %bitcast.28), calls=%async_computation | async-start | bytes 1572864 | tf_op jit(solution)/shard_map/all_to_all | solution.py:383
  10.1 2.9 %shard_map.94 = (bf16[256,1536]{1,0:T(8,128)(2,1)}, f32[2,128]{1,0:T(2,128)}) custom-call(s32[2,128]{1,0:T(2,128)} %bitcast.21, s32[2,128]{1,0:T(2,128)} %bitcast.25, bf16[128,1024]{1,0:T(8,128)(2,1)} %tokens_ref.3, bf16[32,1024]{1,0:T(8,128)(2,1)} %bitcast.18, bf16[128,1024]{1,0:T(8,128)(2,1)} %cot_ref.3), custom_call_target="tpu_custom_call" | custom-call | flops 268435456 | bytes 1379328 | tf_op jit(solution)/shard_map/pallas_call | solution.py:346
  12.9 17.8 %all-to-all-done = bf16[32,8,1536]{2,1,0:T(8,128)(2,1)S(1)} async-done(((bf16[32,8,1536]{2,1,0:T(8,128)(2,1)}), bf16[32,8,1536]{2,1,0:T(8,128)(2,1)S(1)}, u32[]{:S(2)}, u32[]{:S(2)}) %all-to-all-start) | async-done | bytes 786464 | tf_op jit(solution)/shard_map/all_to_all | solution.py:383
  30.7 0.0 copy-start.6
  30.7 3.6 %all-to-all-start.1 = ((bf16[32,8,1536]{2,1,0:T(8,128)(2,1)}), bf16[32,8,1536]{2,1,0:T(8,128)(2,1)S(1)}, u32[]{:S(2)}, u32[]{:S(2)}) async-start(bf16[32,8,1536]{2,1,0:T(8,128)(2,1)} %bitcast.32), calls=%async_computation.1 | async-start | bytes 1572864 | tf_op jit(solution)/shard_map/all_to_all | solution.py:383
  34.3 0.0 copy-done.6
  34.3 14.8 %shard_map.96 = (bf16[256,1536]{1,0:T(8,128)(2,1)}, bf16[384,4096]{1,0:T(8,128)(2,1)}) custom-call(bf16[256,1536]{1,0:T(8,128)(2,1)} %bitcast.30, bf16[1,1024,4096]{2,1,0:T(8,128)(2,1)} %win_ref.3, bf16[1,4096,1024]{2,1,0:T(8,128)(2,1)} %wout_ref.3), custom_call_target="tpu_custom_call" | custom-call | flops 6442450944 | bytes 21495808 | tf_op jit(solution)/shard_map/pallas_call | solution.py:366
  49.1 5.8 %all-to-all-done.1 = bf16[32,8,1536]{2,1,0:T(8,128)(2,1)S(1)} async-done(((bf16[32,8,1536]{2,1,0:T(8,128)(2,1)}), bf16[32,8,1536]{2,1,0:T(8,128)(2,1)S(1)}, u32[]{:S(2)}, u32[]{:S(2)}) %all-to-all-start.1) | async-done | bytes 786464 | tf_op jit(solution)/shard_map/all_to_all | solution.py:383
  55.0 0.0 copy-start.7
  55.0 3.6 %all-to-all-start.2 = ((bf16[32,8,1536]{2,1,0:T(8,128)(2,1)}), bf16[32,8,1536]{2,1,0:T(8,128)(2,1)S(1)}, u32[]{:S(2)}, u32[]{:S(2)}) async-start(bf16[32,8,1536]{2,1,0:T(8,128)(2,1)} %bitcast.33), calls=%async_computation.2 | async-start | bytes 1572864 | tf_op jit(solution)/shard_map/all_to_all | solution.py:383
  58.6 0.0 copy-done.7
  58.6 0.0 copy-start
  58.6 0.0 copy-start.1
  58.6 0.0 copy-start.2
  58.6 0.0 copy-start.3
  58.6 0.0 copy-start.4
  58.7 0.0 copy-start.5
  58.7 15.1 %shard_map.97 = bf16[256,1536]{1,0:T(8,128)(2,1)} custom-call(bf16[256,1536]{1,0:T(8,128)(2,1)} %bitcast.31, bf16[384,4096]{1,0:T(8,128)(2,1)} %get-tuple-element.20.hidden_ref, bf16[1,1024,4096]{2,1,0:T(8,128)(2,1)} %win_ref.3, bf16[1,4096,1024]{2,1,0:T(8,128)(2,1)} %wout_ref.3), custom_call_target="tpu_custom_call" | custom-call | flops 6442450944 | bytes 21495808 | tf_op jit(solution)/shard_map/pallas_call | solution.py:366
  73.8 5.4 %all-to-all-done.2 = bf16[32,8,1536]{2,1,0:T(8,128)(2,1)S(1)} async-done(((bf16[32,8,1536]{2,1,0:T(8,128)(2,1)}), bf16[32,8,1536]{2,1,0:T(8,128)(2,1)S(1)}, u32[]{:S(2)}, u32[]{:S(2)}) %all-to-all-start.2) | async-done | bytes 786464 | tf_op jit(solution)/shard_map/all_to_all | solution.py:383
  79.2 3.6 %all-to-all-start.3 = ((bf16[32,8,1536]{2,1,0:T(8,128)(2,1)}), bf16[32,8,1536]{2,1,0:T(8,128)(2,1)S(1)}, u32[]{:S(2)}, u32[]{:S(2)}) async-start(bf16[32,8,1536]{2,1,0:T(8,128)(2,1)} %bitcast.29), calls=%async_computation.3 | async-start | bytes 1572864 | tf_op jit(solution)/shard_map/all_to_all | solution.py:383
  82.8 0.0 copy-done
  82.9 0.0 copy-done.1
  82.9 0.0 copy-done.2
  82.9 0.0 copy-done.3
  82.9 0.0 copy-done.4
  82.9 0.0 copy-done.5
  82.9 1.5 %shard_map.98 = (bf16[128,1024]{1,0:T(8,128)(2,1)}, f32[128,1024]{1,0:T(8,128)S(1)}, f32[32,1024]{1,0:T(8,128)S(1)}) custom-call(s32[2,128]{1,0:T(2,128)S(1)} %bitcast.22, s32[2,128]{1,0:T(2,128)S(1)} %bitcast.26, f32[2,128]{1,0:T(2,128)S(1)} %copy-done.5, bf16[256,1536]{1,0:T(8,128)(2,1)S(1)} %bitcast.17, bf16[128,1024]{1,0:T(8,128)(2,1)S(1)} %copy-done.1, ...), custom_call_target="tpu_custom_call" | custom-call | flops 268435456 | bytes 2296832 | tf_op jit(solution)/shard_map/pallas_call | solution.py:346
  84.4 0.3 collective-permute-start
  84.6 1.0 collective-permute-done
  85.6 1.8 %collective-permute-start.1 = (bf16[16,1024]{1,0:T(8,128)(2,1)S(1)}, bf16[16,1024]{1,0:T(8,128)(2,1)S(1)}, u32[]{:S(2)}, u32[]{:S(2)}) collective-permute-start(bf16[16,1024]{1,0:T(8,128)(2,1)S(1)} %add_convert_fusion.2), channel_id=1, source_target_pairs={{0,2},{1,3},{2,0},{3,1},{4,6},{5,7},{6,4},{7,5},{8,10},{9,11},{10,... | collective-permute-start | bytes 98312 | tf_op jit(solution)/shard_map/ppermute | solution.py:387
  87.5 1.5 %collective-permute-start.2 = (bf16[16,1024]{1,0:T(8,128)(2,1)S(1)}, bf16[16,1024]{1,0:T(8,128)(2,1)S(1)}, u32[]{:S(2)}, u32[]{:S(2)}) collective-permute-start(bf16[16,1024]{1,0:T(8,128)(2,1)S(1)} %add_convert_fusion.2), channel_id=1, source_target_pairs={{0,4},{1,5},{2,6},{3,7},{4,0},{5,1},{6,2},{7,3},{8,12},{9,13},{10,... | collective-permute-start | bytes 98312 | tf_op jit(solution)/shard_map/ppermute | solution.py:387
  88.9 0.3 collective-permute-start.3
  89.2 2.4 %collective-permute-done.1 = bf16[16,1024]{1,0:T(8,128)(2,1)S(1)} collective-permute-done((bf16[16,1024]{1,0:T(8,128)(2,1)S(1)}, bf16[16,1024]{1,0:T(8,128)(2,1)S(1)}, u32[]{:S(2)}, u32[]{:S(2)}) %collective-permute-start.1) | collective-permute-done | bytes 32800 | tf_op jit(solution)/shard_map/ppermute | solution.py:387
  91.6 0.9 collective-permute-done.2
  92.5 2.2 %collective-permute-done.3 = bf16[16,1024]{1,0:T(8,128)(2,1)S(1)} collective-permute-done((bf16[16,1024]{1,0:T(8,128)(2,1)S(1)}, bf16[16,1024]{1,0:T(8,128)(2,1)S(1)}, u32[]{:S(2)}, u32[]{:S(2)}) %collective-permute-start.3) | collective-permute-done | bytes 32800 | tf_op jit(solution)/shard_map/ppermute | solution.py:387
  94.7 1.9 %collective-permute-start.4 = (bf16[16,1024]{1,0:T(8,128)(2,1)S(1)}, bf16[16,1024]{1,0:T(8,128)(2,1)S(1)}, u32[]{:S(2)}, u32[]{:S(2)}) collective-permute-start(bf16[16,1024]{1,0:T(8,128)(2,1)S(1)} %add_convert_fusion.1), channel_id=1, source_target_pairs={{0,8},{1,9},{2,10},{3,11},{4,12},{5,13},{6,14},{7,15},{8,0},{9,1},... | collective-permute-start | bytes 98312 | tf_op jit(solution)/shard_map/ppermute | solution.py:387
  96.6 2.5 %collective-permute-done.4 = bf16[16,1024]{1,0:T(8,128)(2,1)S(1)} collective-permute-done((bf16[16,1024]{1,0:T(8,128)(2,1)S(1)}, bf16[16,1024]{1,0:T(8,128)(2,1)S(1)}, u32[]{:S(2)}, u32[]{:S(2)}) %collective-permute-start.4) | collective-permute-done | bytes 32800 | tf_op jit(solution)/shard_map/ppermute | solution.py:387
  99.1 2.4 %collective-permute-start.5 = (bf16[16,1024]{1,0:T(8,128)(2,1)S(1)}, bf16[16,1024]{1,0:T(8,128)(2,1)S(1)}, u32[]{:S(2)}, u32[]{:S(2)}) collective-permute-start(bf16[16,1024]{1,0:T(8,128)(2,1)S(1)} %add_convert_fusion), channel_id=1, source_target_pairs={{0,16},{1,17},{2,18},{3,19},{4,20},{5,21},{6,22},{7,23},{8,24},{9,... | collective-permute-start | bytes 98312 | tf_op jit(solution)/shard_map/ppermute | solution.py:387
  101.5 3.0 %collective-permute-done.5 = bf16[16,1024]{1,0:T(8,128)(2,1)S(1)} collective-permute-done((bf16[16,1024]{1,0:T(8,128)(2,1)S(1)}, bf16[16,1024]{1,0:T(8,128)(2,1)S(1)}, u32[]{:S(2)}, u32[]{:S(2)}) %collective-permute-start.5) | collective-permute-done | bytes 32800 | tf_op jit(solution)/shard_map/ppermute | solution.py:387
  104.5 0.0 all-to-all-done.3
  104.5 0.1 collective-permute-start.6
  104.6 0.1 broadcast_in_dim.34
  104.7 0.1 broadcast_in_dim.35
  104.8 1.1 %shard_map.99 = bf16[128,1024]{1,0:T(8,128)(2,1)} custom-call(s32[2,128]{1,0:T(2,128)S(1)} %bitcast.23, s32[2,128]{1,0:T(2,128)S(1)} %bitcast.27, bf16[256,1536]{1,0:T(8,128)(2,1)S(1)} %bitcast.16, f32[128,1024]{1,0:T(8,128)S(1)} %get-tuple-element.27.back_ref), custom_call_target="tpu_custom_call" | custom-call | flops 134217728 | bytes 1574912 | tf_op jit(solution)/shard_map/pallas_call | solution.py:346
  105.9 0.0 collective-permute-done.6
  105.9 0.7 bitcast_select_fusion
  (6 shorter events, 0.1 us)
Async XLA Ops:
  2.8 27.9 %all-to-all-start = ((bf16[32,8,1536]{2,1,0:T(8,128)(2,1)}), bf16[32,8,1536]{2,1,0:T(8,128)(2,1)S(1)}, u32[]{:S(2)}, u32[]{:S(2)}) async-start(bf16[32,8,1536]{2,1,0:T(8,128)(2,1)} %bitcast.28), calls=%async_computation | async-start | bytes 1572864 | tf_op jit(solution)/shard_map/all_to_all | solution.py:383
  30.7 3.6 %copy-start.6 = (bf16[32,8,1536]{2,1,0:T(8,128)(2,1)}, bf16[32,8,1536]{2,1,0:T(8,128)(2,1)S(1)}, u32[]{:S(2)}) copy-start(bf16[32,8,1536]{2,1,0:T(8,128)(2,1)S(1)} %all-to-all-done) | copy-start | bytes 2359300
  30.7 24.2 %all-to-all-start.1 = ((bf16[32,8,1536]{2,1,0:T(8,128)(2,1)}), bf16[32,8,1536]{2,1,0:T(8,128)(2,1)S(1)}, u32[]{:S(2)}, u32[]{:S(2)}) async-start(bf16[32,8,1536]{2,1,0:T(8,128)(2,1)} %bitcast.32), calls=%async_computation.1 | async-start | bytes 1572864 | tf_op jit(solution)/shard_map/all_to_all | solution.py:383
  55.0 3.6 %copy-start.7 = (bf16[32,8,1536]{2,1,0:T(8,128)(2,1)}, bf16[32,8,1536]{2,1,0:T(8,128)(2,1)S(1)}, u32[]{:S(2)}) copy-start(bf16[32,8,1536]{2,1,0:T(8,128)(2,1)S(1)} %all-to-all-done.1) | copy-start | bytes 2359300
  55.0 24.2 %all-to-all-start.2 = ((bf16[32,8,1536]{2,1,0:T(8,128)(2,1)}), bf16[32,8,1536]{2,1,0:T(8,128)(2,1)S(1)}, u32[]{:S(2)}, u32[]{:S(2)}) async-start(bf16[32,8,1536]{2,1,0:T(8,128)(2,1)} %bitcast.33), calls=%async_computation.2 | async-start | bytes 1572864 | tf_op jit(solution)/shard_map/all_to_all | solution.py:383
  58.6 24.3 %copy-start = (bf16[128,1024]{1,0:T(8,128)(2,1)S(1)}, bf16[128,1024]{1,0:T(8,128)(2,1)}, u32[]{:S(2)}) copy-start(bf16[128,1024]{1,0:T(8,128)(2,1)} %tokens_ref.3) | copy-start | bytes 786436
  58.6 24.3 %copy-start.1 = (bf16[128,1024]{1,0:T(8,128)(2,1)S(1)}, bf16[128,1024]{1,0:T(8,128)(2,1)}, u32[]{:S(2)}) copy-start(bf16[128,1024]{1,0:T(8,128)(2,1)} %cot_ref.3) | copy-start | bytes 786436
  58.6 24.3 %copy-start.2 = (bf16[1024,32]{0,1:T(8,128)(2,1)S(1)}, bf16[1024,32]{0,1:T(8,128)(2,1)}, u32[]{:S(2)}) copy-start(bf16[1024,32]{0,1:T(8,128)(2,1)} %param.8) | copy-start | bytes 196612
  58.6 24.2 %copy-start.3 = (s32[128,2]{0,1:T(2,128)S(1)}, s32[128,2]{0,1:T(2,128)}, u32[]{:S(2)}) copy-start(s32[128,2]{0,1:T(2,128)} %param.11) | copy-start | bytes 3076
  58.6 24.2 %copy-start.4 = (s32[128,2]{0,1:T(2,128)S(1)}, s32[128,2]{0,1:T(2,128)}, u32[]{:S(2)}) copy-start(s32[128,2]{0,1:T(2,128)} %param.12) | copy-start | bytes 3076
  58.7 24.2 %copy-start.5 = (f32[2,128]{1,0:T(2,128)S(1)}, f32[2,128]{1,0:T(2,128)}, u32[]{:S(2)}) copy-start(f32[2,128]{1,0:T(2,128)} %get-tuple-element.16.gates_ref) | copy-start | bytes 3076
  79.2 25.3 %all-to-all-start.3 = ((bf16[32,8,1536]{2,1,0:T(8,128)(2,1)}), bf16[32,8,1536]{2,1,0:T(8,128)(2,1)S(1)}, u32[]{:S(2)}, u32[]{:S(2)}) async-start(bf16[32,8,1536]{2,1,0:T(8,128)(2,1)} %bitcast.29), calls=%async_computation.3 | async-start | bytes 1572864 | tf_op jit(solution)/shard_map/all_to_all | solution.py:383
  84.4 1.3 %collective-permute-start = (f32[16,1024]{1,0:T(8,128)S(1)}, f32[16,1024]{1,0:T(8,128)S(1)}, u32[]{:S(2)}, u32[]{:S(2)}) collective-permute-start(f32[16,1024]{1,0:T(8,128)S(1)} %constant_dynamic-slice_fusion), channel_id=1, source_target_pairs={{0,1},{1,0},{2,3},{3,2},{4,5},{5,4},{6,7},{7,6},{8,9},{9,8},{10,11... | collective-permute-start | bytes 196616 | tf_op jit(solution)/shard_map/ppermute | solution.py:387
  85.6 6.0 %collective-permute-start.1 = (bf16[16,1024]{1,0:T(8,128)(2,1)S(1)}, bf16[16,1024]{1,0:T(8,128)(2,1)S(1)}, u32[]{:S(2)}, u32[]{:S(2)}) collective-permute-start(bf16[16,1024]{1,0:T(8,128)(2,1)S(1)} %add_convert_fusion.2), channel_id=1, source_target_pairs={{0,2},{1,3},{2,0},{3,1},{4,6},{5,7},{6,4},{7,5},{8,10},{9,11},{10,... | collective-permute-start | bytes 98312 | tf_op jit(solution)/shard_map/ppermute | solution.py:387
  87.5 5.0 %collective-permute-start.2 = (bf16[16,1024]{1,0:T(8,128)(2,1)S(1)}, bf16[16,1024]{1,0:T(8,128)(2,1)S(1)}, u32[]{:S(2)}, u32[]{:S(2)}) collective-permute-start(bf16[16,1024]{1,0:T(8,128)(2,1)S(1)} %add_convert_fusion.2), channel_id=1, source_target_pairs={{0,4},{1,5},{2,6},{3,7},{4,0},{5,1},{6,2},{7,3},{8,12},{9,13},{10,... | collective-permute-start | bytes 98312 | tf_op jit(solution)/shard_map/ppermute | solution.py:387
  88.9 5.7 %collective-permute-start.3 = (bf16[16,1024]{1,0:T(8,128)(2,1)S(1)}, bf16[16,1024]{1,0:T(8,128)(2,1)S(1)}, u32[]{:S(2)}, u32[]{:S(2)}) collective-permute-start(bf16[16,1024]{1,0:T(8,128)(2,1)S(1)} %add_convert_fusion.2), channel_id=1, source_target_pairs={{0,6},{1,7},{2,4},{3,5},{4,2},{5,3},{6,0},{7,1},{8,14},{9,15},{10,... | collective-permute-start | bytes 98312 | tf_op jit(solution)/shard_map/ppermute | solution.py:387
  94.7 4.4 %collective-permute-start.4 = (bf16[16,1024]{1,0:T(8,128)(2,1)S(1)}, bf16[16,1024]{1,0:T(8,128)(2,1)S(1)}, u32[]{:S(2)}, u32[]{:S(2)}) collective-permute-start(bf16[16,1024]{1,0:T(8,128)(2,1)S(1)} %add_convert_fusion.1), channel_id=1, source_target_pairs={{0,8},{1,9},{2,10},{3,11},{4,12},{5,13},{6,14},{7,15},{8,0},{9,1},... | collective-permute-start | bytes 98312 | tf_op jit(solution)/shard_map/ppermute | solution.py:387
  99.1 5.4 %collective-permute-start.5 = (bf16[16,1024]{1,0:T(8,128)(2,1)S(1)}, bf16[16,1024]{1,0:T(8,128)(2,1)S(1)}, u32[]{:S(2)}, u32[]{:S(2)}) collective-permute-start(bf16[16,1024]{1,0:T(8,128)(2,1)S(1)} %add_convert_fusion), channel_id=1, source_target_pairs={{0,16},{1,17},{2,18},{3,19},{4,20},{5,21},{6,22},{7,23},{8,24},{9,... | collective-permute-start | bytes 98312 | tf_op jit(solution)/shard_map/ppermute | solution.py:387
  104.5 1.4 %collective-permute-start.6 = (f32[16,1024]{1,0:T(8,128)S(1)}, f32[16,1024]{1,0:T(8,128)S(1)}, u32[]{:S(2)}, u32[]{:S(2)}) collective-permute-start(f32[16,1024]{1,0:T(8,128)S(1)} %convert_add_fusion), channel_id=1, source_target_pairs={{0,1},{1,0},{2,3},{3,2},{4,5},{5,4},{6,7},{7,6},{8,9},{9,8},{10,11... | collective-permute-start | bytes 196616 | tf_op jit(solution)/shard_map/ppermute | solution.py:387

commit v17 on v10

--- a/solution.py
+++ b/solution.py
@@ -396,7 +396,7 @@
     core = lax.axis_index("inner") % 2
     own = lax.dynamic_slice_in_dim(x, core * half, half, 0)
     other = lax.dynamic_slice_in_dim(x, (1 - core) * half, half, 0)
-    own = own + from_device(other, 1, devices)
+    own = own + from_device(other.astype(BF16), 1, devices).astype(F32)
     sent = own.astype(BF16)
     terms = [sent] + [from_device(sent, bits, devices) for bits in (2, 4, 6)]
     own = sum_of_pairs(*[term.astype(F32) for term in terms])

time: 107 us -> 107 us (level)
  no operation moved by 1% of the time
where the time goes in v17:
time: 107 us
  waiting for transfers between devices  41.1 us (38%)
  Pallas kernels  37.5 us (35%)
  starting transfers between devices  26.4 us (25%)
    pallas_call x2, Pallas kernels, expert_call(): pl.pallas_call(functools.partial(kernel, lay), grid=(ff // tile,), in_spe...  29.9 us
    all_to_all x4, waiting for transfers between devices, exchange(): return lax.all_to_all(x, AXES, split_axis=0, concat_axis=0, tiled=True)  29 us
    all_to_all x4, starting transfers between devices, exchange(): return lax.all_to_all(x, AXES, split_axis=0, concat_axis=0, tiled=True)  18.2 us
    ppermute x7, waiting for transfers between devices, from_device(): return lax.ppermute(x, AXES, [(d, d ^ bits) for d in range(devices)])  12 us
    ppermute x7, starting transfers between devices, from_device(): return lax.ppermute(x, AXES, [(d, d ^ bits) for d in range(devices)])  8.24 us
    pallas_call x3, Pallas kernels, call(): pl.pallas_call(kernel, out_shape=out_shape, compiler_params=pltpu.Compile...  5.43 us
    pallas_call x1, Pallas kernels, on_device(): pl.pallas_call(functools.partial(send_tokens_kernel, lay), out_shape=mess...  2.16 us
  transfers between devices with their start and end apart: 11, of which 10 were waited for; matrix products, arithmetic and copies ran while one was open for 0% of the time, Pallas kernels for 33%

profile of v17, /device:TPU:0, one launch (start us, length us, event | category | flops | bytes accessed | tf_op | source)
XLA Modules:
  0.0 106.6 jit_solution(16467237784323239418)
XLA Ops:
  0.6 2.2 %shard_map.95 = bf16[256,1536]{1,0:T(8,128)(2,1)} custom-call(s32[2,128]{1,0:T(2,128)} %bitcast.17, s32[2,128]{1,0:T(2,128)} %bitcast.21, bf16[128,1024]{1,0:T(8,128)(2,1)} %tokens_ref.3), custom_call_target="tpu_custom_call" | custom-call | flops 134217728 | bytes 1048576 | tf_op jit(solution)/shard_map/pallas_call | solution.py:424
  2.8 7.3 %all-to-all-start = ((bf16[32,8,1536]{2,1,0:T(8,128)(2,1)}), bf16[32,8,1536]{2,1,0:T(8,128)(2,1)S(1)}, u32[]{:S(2)}, u32[]{:S(2)}) async-start(bf16[32,8,1536]{2,1,0:T(8,128)(2,1)} %bitcast.25), calls=%async_computation | async-start | bytes 1572864 | tf_op jit(solution)/shard_map/all_to_all | solution.py:383
  10.1 2.9 %shard_map.94 = (bf16[256,1536]{1,0:T(8,128)(2,1)}, f32[2,128]{1,0:T(2,128)}) custom-call(s32[2,128]{1,0:T(2,128)} %bitcast.18, s32[2,128]{1,0:T(2,128)} %bitcast.22, bf16[128,1024]{1,0:T(8,128)(2,1)} %tokens_ref.3, bf16[32,1024]{1,0:T(8,128)(2,1)} %bitcast.15, bf16[128,1024]{1,0:T(8,128)(2,1)} %cot_ref.3), custom_call_target="tpu_custom_call" | custom-call | flops 268435456 | bytes 1379328 | tf_op jit(solution)/shard_map/pallas_call | solution.py:346
  13.0 17.8 %all-to-all-done = bf16[32,8,1536]{2,1,0:T(8,128)(2,1)S(1)} async-done(((bf16[32,8,1536]{2,1,0:T(8,128)(2,1)}), bf16[32,8,1536]{2,1,0:T(8,128)(2,1)S(1)}, u32[]{:S(2)}, u32[]{:S(2)}) %all-to-all-start) | async-done | bytes 786464 | tf_op jit(solution)/shard_map/all_to_all | solution.py:383
  30.7 0.0 copy-start.6
  30.7 3.6 %all-to-all-start.1 = ((bf16[32,8,1536]{2,1,0:T(8,128)(2,1)}), bf16[32,8,1536]{2,1,0:T(8,128)(2,1)S(1)}, u32[]{:S(2)}, u32[]{:S(2)}) async-start(bf16[32,8,1536]{2,1,0:T(8,128)(2,1)} %bitcast.29), calls=%async_computation.1 | async-start | bytes 1572864 | tf_op jit(solution)/shard_map/all_to_all | solution.py:383
  34.4 0.0 copy-done.6
  34.4 14.7 %shard_map.96 = (bf16[256,1536]{1,0:T(8,128)(2,1)}, bf16[384,4096]{1,0:T(8,128)(2,1)}) custom-call(bf16[256,1536]{1,0:T(8,128)(2,1)} %bitcast.27, bf16[1,1024,4096]{2,1,0:T(8,128)(2,1)} %win_ref.3, bf16[1,4096,1024]{2,1,0:T(8,128)(2,1)} %wout_ref.3), custom_call_target="tpu_custom_call" | custom-call | flops 6442450944 | bytes 21495808 | tf_op jit(solution)/shard_map/pallas_call | solution.py:366
  49.1 5.9 %all-to-all-done.1 = bf16[32,8,1536]{2,1,0:T(8,128)(2,1)S(1)} async-done(((bf16[32,8,1536]{2,1,0:T(8,128)(2,1)}), bf16[32,8,1536]{2,1,0:T(8,128)(2,1)S(1)}, u32[]{:S(2)}, u32[]{:S(2)}) %all-to-all-start.1) | async-done | bytes 786464 | tf_op jit(solution)/shard_map/all_to_all | solution.py:383
  55.0 0.0 copy-start.7
  55.0 3.6 %all-to-all-start.2 = ((bf16[32,8,1536]{2,1,0:T(8,128)(2,1)}), bf16[32,8,1536]{2,1,0:T(8,128)(2,1)S(1)}, u32[]{:S(2)}, u32[]{:S(2)}) async-start(bf16[32,8,1536]{2,1,0:T(8,128)(2,1)} %bitcast.30), calls=%async_computation.2 | async-start | bytes 1572864 | tf_op jit(solution)/shard_map/all_to_all | solution.py:383
  58.6 0.0 copy-done.7
  58.6 0.0 copy-start
  58.6 0.0 copy-start.1
  58.6 0.0 copy-start.2
  58.7 0.0 copy-start.3
  58.7 0.0 copy-start.4
  58.7 0.0 copy-start.5
  58.7 15.1 %shard_map.97 = bf16[256,1536]{1,0:T(8,128)(2,1)} custom-call(bf16[256,1536]{1,0:T(8,128)(2,1)} %bitcast.28, bf16[384,4096]{1,0:T(8,128)(2,1)} %get-tuple-element.20.hidden_ref, bf16[1,1024,4096]{2,1,0:T(8,128)(2,1)} %win_ref.3, bf16[1,4096,1024]{2,1,0:T(8,128)(2,1)} %wout_ref.3), custom_call_target="tpu_custom_call" | custom-call | flops 6442450944 | bytes 21495808 | tf_op jit(solution)/shard_map/pallas_call | solution.py:366
  73.8 5.4 %all-to-all-done.2 = bf16[32,8,1536]{2,1,0:T(8,128)(2,1)S(1)} async-done(((bf16[32,8,1536]{2,1,0:T(8,128)(2,1)}), bf16[32,8,1536]{2,1,0:T(8,128)(2,1)S(1)}, u32[]{:S(2)}, u32[]{:S(2)}) %all-to-all-start.2) | async-done | bytes 786464 | tf_op jit(solution)/shard_map/all_to_all | solution.py:383
  79.2 3.6 %all-to-all-start.3 = ((bf16[32,8,1536]{2,1,0:T(8,128)(2,1)}), bf16[32,8,1536]{2,1,0:T(8,128)(2,1)S(1)}, u32[]{:S(2)}, u32[]{:S(2)}) async-start(bf16[32,8,1536]{2,1,0:T(8,128)(2,1)} %bitcast.26), calls=%async_computation.3 | async-start | bytes 1572864 | tf_op jit(solution)/shard_map/all_to_all | solution.py:383
  82.9 0.0 copy-done
  82.9 0.0 copy-done.1
  82.9 0.0 copy-done.2
  82.9 0.0 copy-done.3
  82.9 0.0 copy-done.4
  82.9 0.0 copy-done.5
  82.9 1.5 %shard_map.98 = (bf16[128,1024]{1,0:T(8,128)(2,1)}, f32[128,1024]{1,0:T(8,128)S(1)}, f32[32,1024]{1,0:T(8,128)S(1)}) custom-call(s32[2,128]{1,0:T(2,128)S(1)} %bitcast.19, s32[2,128]{1,0:T(2,128)S(1)} %bitcast.23, f32[2,128]{1,0:T(2,128)S(1)} %copy-done.5, bf16[256,1536]{1,0:T(8,128)(2,1)S(1)} %bitcast.14, bf16[128,1024]{1,0:T(8,128)(2,1)S(1)} %copy-done.1, ...), custom_call_target="tpu_custom_call" | custom-call | flops 268435456 | bytes 2296832 | tf_op jit(solution)/shard_map/pallas_call | solution.py:346
  84.4 0.3 collective-permute-start
  84.7 1.0 collective-permute-done
  85.6 1.8 %collective-permute-start.1 = (bf16[16,1024]{1,0:T(8,128)(2,1)S(1)}, bf16[16,1024]{1,0:T(8,128)(2,1)S(1)}, u32[]{:S(2)}, u32[]{:S(2)}) collective-permute-start(bf16[16,1024]{1,0:T(8,128)(2,1)S(1)} %add_convert_fusion.2), channel_id=1, source_target_pairs={{0,2},{1,3},{2,0},{3,1},{4,6},{5,7},{6,4},{7,5},{8,10},{9,11},{10,... | collective-permute-start | bytes 98312 | tf_op jit(solution)/shard_map/ppermute | solution.py:387
  87.5 1.5 %collective-permute-start.2 = (bf16[16,1024]{1,0:T(8,128)(2,1)S(1)}, bf16[16,1024]{1,0:T(8,128)(2,1)S(1)}, u32[]{:S(2)}, u32[]{:S(2)}) collective-permute-start(bf16[16,1024]{1,0:T(8,128)(2,1)S(1)} %add_convert_fusion.2), channel_id=1, source_target_pairs={{0,4},{1,5},{2,6},{3,7},{4,0},{5,1},{6,2},{7,3},{8,12},{9,13},{10,... | collective-permute-start | bytes 98312 | tf_op jit(solution)/shard_map/ppermute | solution.py:387
  88.9 0.3 collective-permute-start.3
  89.2 2.5 %collective-permute-done.1 = bf16[16,1024]{1,0:T(8,128)(2,1)S(1)} collective-permute-done((bf16[16,1024]{1,0:T(8,128)(2,1)S(1)}, bf16[16,1024]{1,0:T(8,128)(2,1)S(1)}, u32[]{:S(2)}, u32[]{:S(2)}) %collective-permute-start.1) | collective-permute-done | bytes 32800 | tf_op jit(solution)/shard_map/ppermute | solution.py:387
  91.6 0.8 collective-permute-done.2
  92.4 2.3 %collective-permute-done.3 = bf16[16,1024]{1,0:T(8,128)(2,1)S(1)} collective-permute-done((bf16[16,1024]{1,0:T(8,128)(2,1)S(1)}, bf16[16,1024]{1,0:T(8,128)(2,1)S(1)}, u32[]{:S(2)}, u32[]{:S(2)}) %collective-permute-start.3) | collective-permute-done | bytes 32800 | tf_op jit(solution)/shard_map/ppermute | solution.py:387
  94.7 1.9 %collective-permute-start.4 = (bf16[16,1024]{1,0:T(8,128)(2,1)S(1)}, bf16[16,1024]{1,0:T(8,128)(2,1)S(1)}, u32[]{:S(2)}, u32[]{:S(2)}) collective-permute-start(bf16[16,1024]{1,0:T(8,128)(2,1)S(1)} %add_convert_fusion.1), channel_id=1, source_target_pairs={{0,8},{1,9},{2,10},{3,11},{4,12},{5,13},{6,14},{7,15},{8,0},{9,1},... | collective-permute-start | bytes 98312 | tf_op jit(solution)/shard_map/ppermute | solution.py:387
  96.6 2.5 %collective-permute-done.4 = bf16[16,1024]{1,0:T(8,128)(2,1)S(1)} collective-permute-done((bf16[16,1024]{1,0:T(8,128)(2,1)S(1)}, bf16[16,1024]{1,0:T(8,128)(2,1)S(1)}, u32[]{:S(2)}, u32[]{:S(2)}) %collective-permute-start.4) | collective-permute-done | bytes 32800 | tf_op jit(solution)/shard_map/ppermute | solution.py:387
  99.1 2.4 %collective-permute-start.5 = (bf16[16,1024]{1,0:T(8,128)(2,1)S(1)}, bf16[16,1024]{1,0:T(8,128)(2,1)S(1)}, u32[]{:S(2)}, u32[]{:S(2)}) collective-permute-start(bf16[16,1024]{1,0:T(8,128)(2,1)S(1)} %add_convert_fusion), channel_id=1, source_target_pairs={{0,16},{1,17},{2,18},{3,19},{4,20},{5,21},{6,22},{7,23},{8,24},{9,... | collective-permute-start | bytes 98312 | tf_op jit(solution)/shard_map/ppermute | solution.py:387
  101.6 3.0 %collective-permute-done.5 = bf16[16,1024]{1,0:T(8,128)(2,1)S(1)} collective-permute-done((bf16[16,1024]{1,0:T(8,128)(2,1)S(1)}, bf16[16,1024]{1,0:T(8,128)(2,1)S(1)}, u32[]{:S(2)}, u32[]{:S(2)}) %collective-permute-start.5) | collective-permute-done | bytes 32800 | tf_op jit(solution)/shard_map/ppermute | solution.py:387
  104.5 0.0 all-to-all-done.3
  104.6 0.1 collective-permute-start.6
  104.6 1.1 %shard_map.99 = bf16[128,1024]{1,0:T(8,128)(2,1)} custom-call(s32[2,128]{1,0:T(2,128)S(1)} %bitcast.20, s32[2,128]{1,0:T(2,128)S(1)} %bitcast.24, bf16[256,1536]{1,0:T(8,128)(2,1)S(1)} %bitcast.13, f32[128,1024]{1,0:T(8,128)S(1)} %get-tuple-element.27.back_ref), custom_call_target="tpu_custom_call" | custom-call | flops 134217728 | bytes 1574912 | tf_op jit(solution)/shard_map/pallas_call | solution.py:346
  105.7 0.1 collective-permute-done.6
  105.9 0.7 maximum_bitcast_fusion
  (6 shorter events, 0.1 us)
Async XLA Ops:
  2.8 27.9 %all-to-all-start = ((bf16[32,8,1536]{2,1,0:T(8,128)(2,1)}), bf16[32,8,1536]{2,1,0:T(8,128)(2,1)S(1)}, u32[]{:S(2)}, u32[]{:S(2)}) async-start(bf16[32,8,1536]{2,1,0:T(8,128)(2,1)} %bitcast.25), calls=%async_computation | async-start | bytes 1572864 | tf_op jit(solution)/shard_map/all_to_all | solution.py:383
  30.7 3.6 %copy-start.6 = (bf16[32,8,1536]{2,1,0:T(8,128)(2,1)}, bf16[32,8,1536]{2,1,0:T(8,128)(2,1)S(1)}, u32[]{:S(2)}) copy-start(bf16[32,8,1536]{2,1,0:T(8,128)(2,1)S(1)} %all-to-all-done) | copy-start | bytes 2359300
  30.7 24.2 %all-to-all-start.1 = ((bf16[32,8,1536]{2,1,0:T(8,128)(2,1)}), bf16[32,8,1536]{2,1,0:T(8,128)(2,1)S(1)}, u32[]{:S(2)}, u32[]{:S(2)}) async-start(bf16[32,8,1536]{2,1,0:T(8,128)(2,1)} %bitcast.29), calls=%async_computation.1 | async-start | bytes 1572864 | tf_op jit(solution)/shard_map/all_to_all | solution.py:383
  55.0 3.6 %copy-start.7 = (bf16[32,8,1536]{2,1,0:T(8,128)(2,1)}, bf16[32,8,1536]{2,1,0:T(8,128)(2,1)S(1)}, u32[]{:S(2)}) copy-start(bf16[32,8,1536]{2,1,0:T(8,128)(2,1)S(1)} %all-to-all-done.1) | copy-start | bytes 2359300
  55.0 24.2 %all-to-all-start.2 = ((bf16[32,8,1536]{2,1,0:T(8,128)(2,1)}), bf16[32,8,1536]{2,1,0:T(8,128)(2,1)S(1)}, u32[]{:S(2)}, u32[]{:S(2)}) async-start(bf16[32,8,1536]{2,1,0:T(8,128)(2,1)} %bitcast.30), calls=%async_computation.2 | async-start | bytes 1572864 | tf_op jit(solution)/shard_map/all_to_all | solution.py:383
  58.6 24.3 %copy-start = (bf16[128,1024]{1,0:T(8,128)(2,1)S(1)}, bf16[128,1024]{1,0:T(8,128)(2,1)}, u32[]{:S(2)}) copy-start(bf16[128,1024]{1,0:T(8,128)(2,1)} %tokens_ref.3) | copy-start | bytes 786436
  58.6 24.3 %copy-start.1 = (bf16[128,1024]{1,0:T(8,128)(2,1)S(1)}, bf16[128,1024]{1,0:T(8,128)(2,1)}, u32[]{:S(2)}) copy-start(bf16[128,1024]{1,0:T(8,128)(2,1)} %cot_ref.3) | copy-start | bytes 786436
  58.6 24.3 %copy-start.2 = (bf16[1024,32]{0,1:T(8,128)(2,1)S(1)}, bf16[1024,32]{0,1:T(8,128)(2,1)}, u32[]{:S(2)}) copy-start(bf16[1024,32]{0,1:T(8,128)(2,1)} %param.8) | copy-start | bytes 196612
  58.7 24.2 %copy-start.3 = (s32[128,2]{0,1:T(2,128)S(1)}, s32[128,2]{0,1:T(2,128)}, u32[]{:S(2)}) copy-start(s32[128,2]{0,1:T(2,128)} %param.11) | copy-start | bytes 3076
  58.7 24.2 %copy-start.4 = (s32[128,2]{0,1:T(2,128)S(1)}, s32[128,2]{0,1:T(2,128)}, u32[]{:S(2)}) copy-start(s32[128,2]{0,1:T(2,128)} %param.12) | copy-start | bytes 3076
  58.7 24.2 %copy-start.5 = (f32[2,128]{1,0:T(2,128)S(1)}, f32[2,128]{1,0:T(2,128)}, u32[]{:S(2)}) copy-start(f32[2,128]{1,0:T(2,128)} %get-tuple-element.16.gates_ref) | copy-start | bytes 3076
  79.2 25.3 %all-to-all-start.3 = ((bf16[32,8,1536]{2,1,0:T(8,128)(2,1)}), bf16[32,8,1536]{2,1,0:T(8,128)(2,1)S(1)}, u32[]{:S(2)}, u32[]{:S(2)}) async-start(bf16[32,8,1536]{2,1,0:T(8,128)(2,1)} %bitcast.26), calls=%async_computation.3 | async-start | bytes 1572864 | tf_op jit(solution)/shard_map/all_to_all | solution.py:383
  84.4 1.2 %collective-permute-start = (bf16[16,1024]{1,0:T(8,128)(2,1)S(1)}, bf16[16,1024]{1,0:T(8,128)(2,1)S(1)}, u32[]{:S(2)}, u32[]{:S(2)}) collective-permute-start(bf16[16,1024]{1,0:T(8,128)(2,1)S(1)} %dynamic-slice_convert_fusion), channel_id=1, source_target_pairs={{0,1},{1,0},{2,3},{3,2},{4,5},{5,4},{6,7},{7,6},{8,9},{9,8},{10,11... | collective-permute-start | bytes 98312 | tf_op jit(solution)/shard_map/ppermute | solution.py:387
  85.6 6.0 %collective-permute-start.1 = (bf16[16,1024]{1,0:T(8,128)(2,1)S(1)}, bf16[16,1024]{1,0:T(8,128)(2,1)S(1)}, u32[]{:S(2)}, u32[]{:S(2)}) collective-permute-start(bf16[16,1024]{1,0:T(8,128)(2,1)S(1)} %add_convert_fusion.2), channel_id=1, source_target_pairs={{0,2},{1,3},{2,0},{3,1},{4,6},{5,7},{6,4},{7,5},{8,10},{9,11},{10,... | collective-permute-start | bytes 98312 | tf_op jit(solution)/shard_map/ppermute | solution.py:387
  87.5 4.9 %collective-permute-start.2 = (bf16[16,1024]{1,0:T(8,128)(2,1)S(1)}, bf16[16,1024]{1,0:T(8,128)(2,1)S(1)}, u32[]{:S(2)}, u32[]{:S(2)}) collective-permute-start(bf16[16,1024]{1,0:T(8,128)(2,1)S(1)} %add_convert_fusion.2), channel_id=1, source_target_pairs={{0,4},{1,5},{2,6},{3,7},{4,0},{5,1},{6,2},{7,3},{8,12},{9,13},{10,... | collective-permute-start | bytes 98312 | tf_op jit(solution)/shard_map/ppermute | solution.py:387
  88.9 5.8 %collective-permute-start.3 = (bf16[16,1024]{1,0:T(8,128)(2,1)S(1)}, bf16[16,1024]{1,0:T(8,128)(2,1)S(1)}, u32[]{:S(2)}, u32[]{:S(2)}) collective-permute-start(bf16[16,1024]{1,0:T(8,128)(2,1)S(1)} %add_convert_fusion.2), channel_id=1, source_target_pairs={{0,6},{1,7},{2,4},{3,5},{4,2},{5,3},{6,0},{7,1},{8,14},{9,15},{10,... | collective-permute-start | bytes 98312 | tf_op jit(solution)/shard_map/ppermute | solution.py:387
  94.7 4.4 %collective-permute-start.4 = (bf16[16,1024]{1,0:T(8,128)(2,1)S(1)}, bf16[16,1024]{1,0:T(8,128)(2,1)S(1)}, u32[]{:S(2)}, u32[]{:S(2)}) collective-permute-start(bf16[16,1024]{1,0:T(8,128)(2,1)S(1)} %add_convert_fusion.1), channel_id=1, source_target_pairs={{0,8},{1,9},{2,10},{3,11},{4,12},{5,13},{6,14},{7,15},{8,0},{9,1},... | collective-permute-start | bytes 98312 | tf_op jit(solution)/shard_map/ppermute | solution.py:387
  99.1 5.4 %collective-permute-start.5 = (bf16[16,1024]{1,0:T(8,128)(2,1)S(1)}, bf16[16,1024]{1,0:T(8,128)(2,1)S(1)}, u32[]{:S(2)}, u32[]{:S(2)}) collective-permute-start(bf16[16,1024]{1,0:T(8,128)(2,1)S(1)} %add_convert_fusion), channel_id=1, source_target_pairs={{0,16},{1,17},{2,18},{3,19},{4,20},{5,21},{6,22},{7,23},{8,24},{9,... | collective-permute-start | bytes 98312 | tf_op jit(solution)/shard_map/ppermute | solution.py:387
  104.6 1.3 %collective-permute-start.6 = (f32[16,1024]{1,0:T(8,128)S(1)}, f32[16,1024]{1,0:T(8,128)S(1)}, u32[]{:S(2)}, u32[]{:S(2)}) collective-permute-start(f32[16,1024]{1,0:T(8,128)S(1)} %convert_add_fusion), channel_id=1, source_target_pairs={{0,1},{1,0},{2,3},{3,2},{4,5},{5,4},{6,7},{7,6},{8,9},{9,8},{10,11... | collective-permute-start | bytes 196616 | tf_op jit(solution)/shard_map/ppermute | solution.py:387
